TPU v7x, 256 devices: a whole 4x4x8 slice. The times are simulated.
256 devices in a mesh: row: 16 (over z, core), col: 8 (over y, x_hi), batch: 2 (over x_lo).
Axes of the slice: x: 4 (x_hi: 2, x_lo: 2; x = x_hi * 2 + x_lo), y: 4, z: 8, core: 2. Of those that a mesh axis runs over, the one named last changes fastest.
Arguments:
- fine: bfloat16 [2, 1024, 1536], P('batch', 'row'), may hold values from -6 to 6
- conv_w: bfloat16 [5, 1536, 1536], P(None, 'col'), may hold values from -0.0625 to 0.0625
- proj_a: bfloat16 [1536, 128], P('col'), may hold values from -0.15625 to 0.15625
- proj_b: bfloat16 [1536, 128], P('col'), may hold values from -0.15625 to 0.15625
- pair_in: bfloat16 [2, 512, 512, 128], P('batch', 'row', 'col'), may hold values from -6 to 6
- pair_w: bfloat16 [3, 3, 128, 128], replicated, may hold values from -0.1875 to 0.1875
- cotangent: bfloat16 [2, 512, 512, 128], P('batch', 'row', 'col'), may hold values from -1.5 to 1.5
Outputs:
- pair_out: bfloat16 [2, 512, 512, 128], P('batch', 'row', 'col')
- grad_fine: bfloat16 [2, 1024, 1536], P('batch', 'row', 'col')
- grad_pair_w: float32 [3, 3, 128, 128], replicated
All inputs are finite; a program needn't handle non-finite values.
Results may differ from a plain program's by a relative error of at most 0.025.
Values may be sent and summed in bfloat16 or wider, within the bound.
No kernel may reach another device: no remote copies, remote signals or barrier semaphores. Data moves between devices by JAX's collectives and lax.ppermute only.
A program may use at most 128 MiB of HBM per device.

v0:
```python
import jax
import jax.numpy as jnp
from jax import lax
from jax.sharding import PartitionSpec as P


def padded(shard, sides, width):
    for axis, dim in sides:
        count, length = (lax.axis_size(axis), shard.shape[dim])
        up = [(i, (i + 1) % count) for i in range(count - 1)]
        down = [(j, i) for i, j in up]
        last = lax.slice_in_dim(shard, length - width, length, axis=dim)
        leading = lax.slice_in_dim(shard, 0, width, axis=dim)
        before = lax.ppermute(last, axis, up)
        after = lax.ppermute(leading, axis, down)
        shard = jnp.concatenate([before, shard, after], axis=dim)
    return shard


def local(fine, conv_w, proj_a, proj_b, pair_in, pair_w, cotangent):
    seqs = fine.shape[0]
    chans = fine.shape[2]
    outchans = conv_w.shape[1]
    rows_here = pair_in.shape[1]
    cols_here = pair_in.shape[2]
    pairs = pair_in.shape[3]
    extended = padded(fine, (("row", 1),), 2)
    grouped = extended.reshape(seqs, rows_here + 2, 2, chans)
    windows = [
        grouped[:, 0:rows_here, 0],
        grouped[:, 0:rows_here, 1],
        grouped[:, 1 : rows_here + 1, 0],
        grouped[:, 1 : rows_here + 1, 1],
        grouped[:, 2 : rows_here + 2, 0],
    ]
    seq_acc = jnp.zeros((seqs * rows_here, outchans), jnp.float32)
    for index in range(5):
        seq_acc = seq_acc + lax.dot_general(
            windows[index].reshape(-1, chans),
            conv_w[index],
            (((1,), (1,)), ((), ())),
            preferred_element_type=jnp.float32,
        )
    seq = seq_acc.astype(jnp.bfloat16)
    part_row = jnp.dot(seq, proj_a, preferred_element_type=jnp.float32).reshape(
        seqs, rows_here, pairs
    )
    part_col = jnp.dot(seq, proj_b, preferred_element_type=jnp.float32).reshape(
        seqs, rows_here, pairs
    )
    rowp, colp_here = (
        lax.psum(part_row.astype(jnp.bfloat16), "col").astype(jnp.float32),
        lax.psum(part_col.astype(jnp.bfloat16), "col").astype(jnp.float32),
    )
    colp_all = lax.all_gather(colp_here, "row", axis=1, tiled=True)
    col_start = lax.axis_index("col") * cols_here
    colp = lax.dynamic_slice_in_dim(colp_all, col_start, cols_here, 1)
    zeta = (pair_in.astype(jnp.float32) + rowp[:, :, None, :] * colp[:, None, :, :]).astype(
        jnp.bfloat16
    )
    zeta_ext = padded(zeta, (("row", 1), ("col", 2)), 1)
    hidden = jnp.zeros((seqs * rows_here * cols_here, pairs), jnp.float32)
    for down in range(3):
        for across in range(3):
            piece = zeta_ext[:, down : down + rows_here, across : across + cols_here].reshape(
                -1, pairs
            )
            hidden = hidden + jnp.dot(
                piece, pair_w[down, across], preferred_element_type=jnp.float32
            )
    hidden = hidden.reshape(seqs, rows_here, cols_here, pairs)
    pair_out = (zeta.astype(jnp.float32) + jax.nn.silu(hidden)).astype(jnp.bfloat16)
    sigma = jax.nn.sigmoid(hidden)
    qgrad = (cotangent.astype(jnp.float32) * sigma * (1.0 + hidden * (1.0 - sigma))).astype(
        jnp.bfloat16
    )
    qgrad_ext = padded(qgrad, (("row", 1), ("col", 2)), 1)
    flat_q = qgrad.reshape(-1, pairs)
    zgrad = cotangent.astype(jnp.float32).reshape(-1, pairs)
    wgrads = []
    for down in range(3):
        for across in range(3):
            back = qgrad_ext[
                :, 2 - down : 2 - down + rows_here, 2 - across : 2 - across + cols_here
            ].reshape(-1, pairs)
            zgrad = zgrad + lax.dot_general(
                back,
                pair_w[down, across],
                (((1,), (1,)), ((), ())),
                preferred_element_type=jnp.float32,
            )
            piece = zeta_ext[:, down : down + rows_here, across : across + cols_here].reshape(
                -1, pairs
            )
            wgrads.append(
                lax.dot_general(
                    piece, flat_q, (((0,), (0,)), ((), ())), preferred_element_type=jnp.float32
                )
            )
    local_wgrad = jnp.stack(wgrads).reshape(3, 3, pairs, pairs)
    grad_pair_w = lax.psum(local_wgrad, ("row", "col", "batch")) / colp_all.shape[1]
    zgrad = zgrad.reshape(seqs, rows_here, cols_here, pairs)
    row_part = jnp.sum(zgrad * colp[:, None, :, :], axis=2)
    col_part = jnp.sum(zgrad * rowp[:, :, None, :], axis=1)
    blank = jnp.zeros(colp_all.shape, jnp.float32)
    full_col = lax.dynamic_update_slice_in_dim(blank, col_part, col_start, 1)
    summed = lax.psum_scatter(full_col.astype(jnp.bfloat16), "row", scatter_dimension=1, tiled=True)
    rowg, colg = (
        lax.psum(row_part.astype(jnp.bfloat16), "col").astype(jnp.float32),
        lax.psum(summed, "col").astype(jnp.float32),
    )
    seqg = (
        jnp.dot(
            rowg.reshape(-1, pairs),
            proj_a.T.astype(jnp.float32),
            preferred_element_type=jnp.float32,
        )
        + jnp.dot(
            colg.reshape(-1, pairs),
            proj_b.T.astype(jnp.float32),
            preferred_element_type=jnp.float32,
        )
    ).astype(jnp.bfloat16)
    seqg_ext = padded(seqg.reshape(seqs, rows_here, outchans), (("row", 1),), 1)
    flat_seqg = seqg_ext.reshape(-1, outchans)
    taps = [
        jnp.dot(flat_seqg, conv_w[index], preferred_element_type=jnp.float32).reshape(
            seqs, rows_here + 2, chans
        )
        for index in range(5)
    ]
    even = taps[0][:, 2 : rows_here + 2] + taps[2][:, 1 : rows_here + 1] + taps[4][:, 0:rows_here]
    odd = taps[1][:, 2 : rows_here + 2] + taps[3][:, 1 : rows_here + 1]
    partial_fine = jnp.stack((even, odd), axis=2).reshape(seqs, 2 * rows_here, chans)
    grad_fine = lax.psum_scatter(
        partial_fine.astype(jnp.bfloat16), "col", scatter_dimension=2, tiled=True
    )
    return (pair_out, grad_fine, grad_pair_w)


def solution(mesh):
    return jax.shard_map(
        local,
        mesh=mesh,
        in_specs=(
            P("batch", "row", None),
            P(None, "col", None),
            P("col", None),
            P("col", None),
            P("batch", "row", "col", None),
            P(),
            P("batch", "row", "col", None),
        ),
        out_specs=(P("batch", "row", "col", None), P("batch", "row", "col"), P()),
        check_vma=False,
    )
```

profile of v0, /device:TPU:2, one launch (start us, length us, event | category | flops | bytes accessed | tf_op | source)
XLA Modules:
  0.0 489.9 jit_solution(15385938031064166951)
XLA Ops:
  8.1 0.8 fusion.122
  8.8 1.7 collective-permute-start
  10.6 1.3 collective-permute-start.1
  11.9 3.5 collective-permute-done.1
  15.3 1.0 pad_maximum_fusion.6
  16.5 0.5 fusion.121
  17.0 1.6 fusion.25
  18.6 1.3 convolution_add_fusion.18
  20.2 0.3 convolution_add_fusion.16
  21.1 41.3 %all-reduce.1 = (bf16[1,32,128]{2,1,0:T(8,128)(2,1)S(1)}, bf16[32,128]{1,0:T(8,128)(2,1)S(1)}) all-reduce(bf16[1,32,128]{2,1,0:T(8,128)(2,1)S(1)} %fusion.15, bf16[32,128]{1,0:T(8,128)(2,1)S(1)} %convolution_convert_fusion.1), channel_id=1, replica_groups=mesh['row'=16,'col'=8,'batch'=2] {'col'}, use_global_device_ids=true, to_apply=%region_1.0 | all-reduce | flops 8192 | bytes 32768 | tf_op jit(solution)/shard_map/psum | solution.py:53
  62.4 21.1 %all_gather.3 = f32[1,512,128]{2,1,0:T(8,128)S(1)} all-gather(f32[1,32,128]{2,1,0:T(8,128)S(1)} %convert_element_type.80), channel_id=1, replica_groups=mesh['row'=16,'col'=8,'batch'=2] {'row'}, dimensions={1}, use_global_device_ids=true | all-gather | bytes 278528 | tf_op jit(solution)/shard_map/all_gather | solution.py:55
  83.7 2.4 collective-permute-start.2
  86.0 1.3 collective-permute-start.3
  87.4 1.8 collective-permute-done.3
  89.2 1.3 collective-permute-start.4
  90.5 1.3 collective-permute-start.5
  92.1 5.5 %collective-permute-done.5 = bf16[1,34,1,128]{3,2,1,0:T(2,128)(2,1)S(1)} collective-permute-done((bf16[1,34,1,128]{3,2,1,0:T(2,128)(2,1)S(1)}, bf16[1,34,1,128]{3,2,1,0:T(2,128)(2,1)S(1)}, u32[]{:S(2)}, u32[]{:S(2)}) %collective-permute-start.5) | collective-permute-done | bytes 8736 | tf_op jit(solution)/shard_map/ppermute | solution.py:15
  97.6 0.3 maximum_maximum_fusion
  97.9 0.6 fusion.117
  100.8 0.7 copy-done.3
  101.6 1.4 multiply_convert_fusion
  103.0 0.3 fusion.11
  103.4 0.3 fusion.10
  103.7 0.3 fusion.9
  104.0 0.3 fusion.8
  104.4 0.3 fusion.7
  104.7 2.8 collective-permute-start.6
  107.5 1.3 collective-permute-start.7
  108.8 0.3 fusion.6
  109.2 2.1 collective-permute-done.7
  111.3 1.3 collective-permute-start.8
  112.6 6.4 %collective-permute-start.9 = (bf16[1,34,1,128]{3,2,1,0:T(2,128)(2,1)S(1)}, bf16[1,34,1,128]{3,2,1,0:T(2,128)(2,1)S(1)}, u32[]{:S(2)}, u32[]{:S(2)}) collective-permute-start(bf16[1,34,1,128]{3,2,1,0:T(2,128)(2,1)S(1)} %get-tuple-element.26), channel_id=1, source_target_pairs={{0,2},{2,4},{4,6},{6,8},{8,10},{10,12},{12,14},{1,3},{3,5},{5,7},{... | collective-permute-start | bytes 26120 | tf_op jit(solution)/shard_map/ppermute | solution.py:14
  119.1 1.3 collective-permute-done.9
  120.4 0.4 pad_maximum_fusion.1
  120.8 0.4 fusion.115
  121.2 0.3 fusion.116
  121.8 0.3 fusion.69
  122.1 0.3 convolution_add_fusion.6
  122.4 0.3 fusion.1
  122.7 0.3 convolution_add_fusion.4
  123.3 0.3 convolution_add_fusion.2
  123.6 0.3 convolution_add_fusion.1
  123.9 0.3 fusion
  124.5 0.6 copy-done.6
  125.2 0.3 fusion.5
  125.6 0.4 fusion.4
  125.9 59.7 %reduce-scatter.5.cloned.1.call-done = bf16[1,32,128]{2,1,0:T(8,128)(2,1)} async-done(((bf16[1,512,128]{2,1,0:T(8,128)(2,1)}), bf16[1,32,128]{2,1,0:T(8,128)(2,1)}) %reduce-scatter.5.cloned.1.call-update) | async-done | bytes 8208 | tf_op jit(solution)/shard_map/reduce_scatter | solution.py:107
  185.6 40.9 %all-reduce = (bf16[32,128]{1,0:T(8,128)(2,1)S(1)}, bf16[32,128]{1,0:T(8,128)(2,1)S(1)}) all-reduce(bf16[32,128]{1,0:T(8,128)(2,1)S(1)} %get-tuple-element.4, bf16[32,128]{1,0:T(8,128)(2,1)} %bitcast.285), channel_id=1, replica_groups=mesh['row'=16,'col'=8,'batch'=2] {'col'}, use_global_device_ids=true, to_apply=%region_3.4 | all-reduce | flops 8192 | bytes 32768 | tf_op jit(solution)/shard_map/psum | solution.py:109
  226.8 1.3 collective-permute-start.10
  228.2 1.3 collective-permute-start.11
  229.5 0.3 fusion.3
  229.8 0.8 copy-done.5
  230.7 0.5 collective-permute-done.11
  231.2 1.3 convolution_bitcast_fusion.4
  232.4 1.3 convolution_bitcast_fusion.3
  233.7 1.3 convolution_bitcast_fusion.2
  235.1 1.3 convolution_bitcast_fusion.1
  236.4 1.3 convolution_bitcast_fusion
  238.0 0.6 copy.13
  238.6 0.8 copy.42
  239.4 239.5 %all-reduce.4.cloned.1.call-done = f32[3,3,128,128]{3,2,1,0:T(8,128)} async-done(((f32[3,3,128,128]{3,2,1,0:T(8,128)}), f32[3,3,128,128]{3,2,1,0:T(8,128)}) %all-reduce.4.cloned.1.call-update) | async-done | bytes 589840 | tf_op jit(solution)/shard_map/psum | solution.py:101
  478.9 1.9 broadcast_multiply_fusion
  480.9 0.9 reshape_bitcast_fusion
  481.7 0.7 copy.14
  (63 shorter events, 5.7 us)
Async XLA Ops:
  8.0 12.9 %copy-start = (bf16[192,128]{1,0:T(8,128)(2,1)S(1)}, bf16[192,128]{1,0:T(8,128)(2,1)}, u32[]{:S(2)}) copy-start(bf16[192,128]{1,0:T(8,128)(2,1)} %param.9) | copy-start | bytes 147460
  8.0 177.6 %reduce-scatter.5.cloned.1.call-start = ((), (), s32[]{:S(2)}) async-start(), calls=%async_computation.2 | async-start | bytes 139264 | tf_op jit(solution)/shard_map/reduce_scatter | solution.py:107
  8.8 3.1 collective-permute-start
  10.6 4.8 collective-permute-start.1
  16.5 3.5 copy-start.1
  19.9 1.0 copy-start.7
  20.0 63.5 %copy-start.2 = (bf16[1,32,64,128]{3,2,1,0:T(8,128)(2,1)S(1)}, bf16[1,32,64,128]{3,2,1,0:T(8,128)(2,1)}, u32[]{:S(2)}) copy-start(bf16[1,32,64,128]{3,2,1,0:T(8,128)(2,1)} %param.11) | copy-start | bytes 1572868
  83.6 8.2 %copy-start.4 = (bf16[3,3,128,128]{3,2,1,0:T(8,128)(2,1)S(1)}, bf16[3,3,128,128]{3,2,1,0:T(8,128)(2,1)}, u32[]{:S(2)}) copy-start(bf16[3,3,128,128]{3,2,1,0:T(8,128)(2,1)} %param.12) | copy-start | bytes 884740
  83.7 3.7 collective-permute-start.2
  86.0 3.1 collective-permute-start.3
  89.2 3.0 collective-permute-start.4
  90.5 7.1 %collective-permute-start.5 = (bf16[1,34,1,128]{3,2,1,0:T(2,128)(2,1)S(1)}, bf16[1,34,1,128]{3,2,1,0:T(2,128)(2,1)S(1)}, u32[]{:S(2)}, u32[]{:S(2)}) collective-permute-start(bf16[1,34,1,128]{3,2,1,0:T(2,128)(2,1)S(1)} %get-tuple-element.30), channel_id=1, source_target_pairs={{2,0},{4,2},{6,4},{8,6},{10,8},{12,10},{14,12},{3,1},{5,3},{7,5},{... | collective-permute-start | bytes 26120 | tf_op jit(solution)/shard_map/ppermute | solution.py:15
  100.5 1.0 copy-start.3
  104.7 4.4 collective-permute-start.6
  107.5 3.8 collective-permute-start.7
  111.3 7.8 %collective-permute-start.8 = (bf16[1,34,1,128]{3,2,1,0:T(2,128)(2,1)S(1)}, bf16[1,34,1,128]{3,2,1,0:T(2,128)(2,1)S(1)}, u32[]{:S(2)}, u32[]{:S(2)}) collective-permute-start(bf16[1,34,1,128]{3,2,1,0:T(2,128)(2,1)S(1)} %get-tuple-element.25), channel_id=1, source_target_pairs={{2,0},{4,2},{6,4},{8,6},{10,8},{12,10},{14,12},{3,1},{5,3},{7,5},{... | collective-permute-start | bytes 26120 | tf_op jit(solution)/shard_map/ppermute | solution.py:15
  112.6 7.8 %collective-permute-start.9 = (bf16[1,34,1,128]{3,2,1,0:T(2,128)(2,1)S(1)}, bf16[1,34,1,128]{3,2,1,0:T(2,128)(2,1)S(1)}, u32[]{:S(2)}, u32[]{:S(2)}) collective-permute-start(bf16[1,34,1,128]{3,2,1,0:T(2,128)(2,1)S(1)} %get-tuple-element.26), channel_id=1, source_target_pairs={{0,2},{2,4},{4,6},{6,8},{8,10},{10,12},{12,14},{1,3},{3,5},{5,7},{... | collective-permute-start | bytes 26120 | tf_op jit(solution)/shard_map/ppermute | solution.py:14
  124.5 0.7 copy-start.6
  125.2 353.8 %all-reduce.4.cloned.1.call-start = ((), (), s32[]{:S(2)}) async-start(), calls=%async_computation.3 | async-start | bytes 1179648 | tf_op jit(solution)/shard_map/psum | solution.py:101
  226.8 3.9 collective-permute-start.10
  228.2 3.0 collective-permute-start.11
  229.8 0.8 copy-start.5
  230.6 250.2 %reduce-scatter.7.cloned.1.call-start = ((), (), s32[]{:S(2)}) async-start(), calls=%async_computation.4 | async-start | bytes 442368
Sparse Core Ops, SparseCore 0:
  125.3 60.2 reduce-scatter.4
  239.6 73.1 reduce-scatter.6
Sparse Core Ops, SparseCore 1:
  230.7 248.2 all-reduce.3
where the time goes:
time: 492 us; the launch traced here: 490 us
  waiting for transfers between devices  314 us (64%)
  blocking collectives  103 us (21%)
  starting transfers between devices  23.7 us (5%)
  matrix products  18.9 us (4%)
  between operations  16.1 us (3%)
  local copies, waits for them, and re-layouts  8.22 us (2%)
  other arithmetic  5.8 us (1%)
    psum x1, waiting for transfers between devices, local(): lax.psum(local_wgrad, ('row', 'col', 'batch')) / colp_all.shape[1]  239 us
    reduce_scatter x1, waiting for transfers between devices, local(): lax.psum_scatter(full_col.astype(jnp.bfloat16), 'row', scatter_dimension=...  59.7 us
    psum x1, blocking collectives, local(): lax.psum(part_col.astype(jnp.bfloat16), 'col').astype(jnp.float32)  41.3 us
    psum x1, blocking collectives, local(): lax.psum(row_part.astype(jnp.bfloat16), 'col').astype(jnp.float32)  40.9 us
    all_gather x1, blocking collectives, local(): colp_all = lax.all_gather(colp_here, 'row', axis=1, tiled=True)  21.1 us
    ppermute x6, starting transfers between devices, padded(): before = lax.ppermute(last, axis, up)  15.8 us
    ppermute x6, waiting for transfers between devices, padded(): after = lax.ppermute(leading, axis, down)  13.3 us
  transfers between devices with their start and end apart: 15, of which 8 were waited for; matrix products, arithmetic and copies ran while one was open for 2% of the time, Pallas kernels for 0%

commit v1 on v0

v1 whole, which is shorter than its diff:
```python
import jax
import jax.numpy as jnp
from jax import lax
from jax.sharding import PartitionSpec as P

BF = jnp.bfloat16
F32 = jnp.float32
WIDE = 80


def shift(x, axis, step):
    count = lax.axis_size(axis)
    return lax.ppermute(x, axis, [(i, (i + step) % count) for i in range(count)])


def flip(x, axis, bit):
    count = lax.axis_size(axis)
    return lax.ppermute(x, axis, [(i, i ^ bit) for i in range(count)])


def ring(x, step):
    pairs = [(4 * y + p, 4 * y + (p + step) % 4) for y in range(4) for p in range(4)]
    return lax.ppermute(x, ("col", "batch"), pairs)


def up(x):
    return x.astype(F32)


def sum_y(x):
    across, left, right = shift(x, "col", 4), shift(x, "col", 2), shift(x, "col", 6)
    return ((up(x) + up(across)) + (up(left) + up(right))).astype(BF)


def sum_x(x):
    across, left, right = flip(x, "col", 1), ring(x, 1), ring(x, 3)
    return ((up(x) + up(across)) + (up(left) + up(right))).astype(BF)


def sum_flip(x, axis, bit):
    return (up(x) + up(flip(x, axis, bit))).astype(BF)


def turned(x, step):
    return jnp.roll(x, -step, axis=1)


def pair_block(pair_ext, cot_ext, rowp, colp, row_ok, col_ok, pair_w):
    chans = pair_ext.shape[-1]
    ok = row_ok[:, None, None] & col_ok[None, :, None]
    zeta = jnp.where(ok, up(pair_ext) + rowp[:, None, :] * colp[None, :, :], 0.0).astype(BF)
    cot = jnp.where(ok[1:37], up(cot_ext), 0.0)
    z3 = jnp.concatenate([turned(zeta, -1), zeta, turned(zeta, 1)], axis=-1)
    hidden = 0.0
    for down in range(3):
        hidden = hidden + jnp.dot(
            z3[down : down + 36].reshape(-1, 3 * chans),
            pair_w[down].reshape(3 * chans, chans),
            preferred_element_type=F32,
        )
    hidden = hidden.reshape(36, WIDE, chans)
    sigma = jax.nn.sigmoid(hidden)
    own_h = hidden[2:34, :64]
    out = (up(zeta[3:35, :64]) + own_h * sigma[2:34, :64]).astype(BF)
    q = (cot * sigma * (1.0 + hidden * (1.0 - sigma))).astype(BF)
    q3 = jnp.concatenate([turned(q, 1), q, turned(q, -1)], axis=-1)
    zgrad = cot[1:35].reshape(-1, chans)
    flat_q = q[2:34, :64].reshape(-1, chans)
    wgrads = []
    for down in range(3):
        zgrad = zgrad + jnp.dot(
            q3[2 - down : 36 - down].reshape(-1, 3 * chans),
            jnp.swapaxes(pair_w[down], 1, 2).reshape(3 * chans, chans),
            preferred_element_type=F32,
        )
        wgrads.append(
            lax.dot_general(
                z3[down + 2 : down + 34, :64].reshape(-1, 3 * chans),
                flat_q,
                (((0,), (0,)), ((), ())),
                preferred_element_type=F32,
            )
        )
    zgrad = zgrad.reshape(34, WIDE, chans)
    row_part = jnp.sum(zgrad[:, :64] * colp[None, :64, :], axis=1)
    row_part = jnp.where(row_ok[2:36, None], row_part, 0.0)
    col_part = jnp.sum(zgrad[1:33] * rowp[3:35, None, :], axis=0)
    col_part = jnp.where(col_ok[:, None], col_part, 0.0)
    return out, jnp.concatenate(wgrads), row_part, col_part


def local(fine, conv_w, proj_a, proj_b, pair_in, pair_w, cotangent):
    chans, outchans, pairs = fine.shape[2], conv_w.shape[1], pair_in.shape[3]
    row, col = lax.axis_index("row"), lax.axis_index("col")
    core, zpos = row % 2, row // 2
    first, last = row == 0, row == 15
    row_bins = 32 * row - 3 + jnp.arange(38)
    row_ok = (row_bins >= 0) & (row_bins < 512)
    place = jnp.arange(WIDE)
    bins = 64 * col + jnp.where(place < 72, place, place - WIDE)
    col_ok = (bins >= 0) & (bins < 512)

    fine = fine[0]
    before = jnp.where(first, 0, shift(fine[-8:], "row", 1))
    after = jnp.where(last, 0, shift(fine[:8], "row", -1))
    grouped = jnp.concatenate([before, fine, after]).reshape(40, 2, chans)
    seq = 0.0
    for tap in range(5):
        seq = seq + lax.dot_general(
            grouped[tap // 2 : tap // 2 + 38, tap % 2],
            conv_w[tap],
            (((1,), (1,)), ((), ())),
            preferred_element_type=F32,
        )
    seq = jnp.where(row_ok[:, None], seq, 0.0).astype(BF)
    proj = jnp.concatenate([proj_a, proj_b], axis=1)
    part = jnp.dot(seq, proj, preferred_element_type=F32).astype(BF)
    both = up(sum_flip(sum_y(part), "col", 1))
    rowp, colp_here = both[:, :pairs], both[:, pairs:].astype(BF)

    mine = jnp.where(core == 0, colp_here[:35], colp_here[3:])
    other = flip(mine, "row", 1)
    colp = jnp.concatenate(
        [jnp.where(core == 0, mine, other), jnp.where(core == 0, other, mine)]
    )
    apart = zpos ^ col
    for bit in (4, 2, 1):
        colp = jnp.where((apart & (2 * bit - 1)) == bit, flip(colp, "row", 2 * bit), colp)
    colp = up(jnp.concatenate([colp[3:], jnp.zeros((10, pairs), BF), colp[:3]]))

    pair, cot = pair_in[0], cotangent[0]
    left = shift(jnp.concatenate([pair[:, 61:], cot[:, 62:]], axis=1), "col", 1)
    right = shift(jnp.concatenate([pair[:, :3], cot[:, :2]], axis=1), "col", -1)
    pair_ext = jnp.concatenate(
        [pair, right[:, :3], jnp.zeros((32, 10, pairs), BF), left[:, :3]], axis=1
    )
    cot_ext = jnp.concatenate(
        [cot, right[:, 3:], jnp.zeros((32, 12, pairs), BF), left[:, 3:]], axis=1
    )
    top = shift(jnp.concatenate([pair_ext[29:], cot_ext[30:]]), "row", 1)
    bottom = shift(jnp.concatenate([pair_ext[:3], cot_ext[:2]]), "row", -1)
    pair_ext = jnp.concatenate([top[:3], pair_ext, bottom[:3]])
    cot_ext = jnp.concatenate([top[3:], cot_ext, bottom[3:]])

    out, wgrad, row_part, col_part = pair_block(
        pair_ext, cot_ext, rowp, colp, row_ok, col_ok, pair_w
    )

    half = wgrad.shape[0] // 2
    keep = jnp.where(core == 0, wgrad[:half], wgrad[half:])
    send = jnp.where(core == 0, wgrad[half:], wgrad[:half]).astype(BF)
    total = (keep + up(flip(send, "row", 1))).astype(BF)
    total = sum_x(sum_y(total))
    for bit in (2, 4, 8):
        total = sum_flip(total, "row", bit)
    theirs = flip(total, "row", 1)
    total = jnp.concatenate([jnp.where(core == 0, total, theirs), jnp.where(core == 0, theirs, total)])
    grad_pair_w = up(total).reshape(3, 3, pairs, pairs) / 512.0

    line = jnp.concatenate([col_part[-1:], col_part[:65]])
    keep = jnp.where(core == 0, line[:34], line[32:])
    send = jnp.where(core == 0, line[32:], line[:34]).astype(BF)
    colg = (keep + up(flip(send, "row", 1))).astype(BF)
    for bit in (2, 4, 8):
        colg = sum_flip(colg, "row", bit)
    colg = jnp.where(zpos == col, colg, 0)
    sums = jnp.concatenate([row_part.astype(BF), colg], axis=1)
    sums = sum_flip(sum_y(sums), "col", 1)
    seqg = lax.dot_general(sums, proj, (((1,), (1,)), ((), ())), preferred_element_type=F32).astype(BF)
    taps = [jnp.dot(seqg, conv_w[tap], preferred_element_type=F32) for tap in range(5)]
    even = taps[0][2:] + taps[2][1:33] + taps[4][:32]
    odd = taps[1][2:] + taps[3][1:33]
    parts = jnp.stack((even, odd), axis=1).astype(BF).reshape(64, 8, outchans)
    parts = lax.all_to_all(parts.transpose(1, 0, 2), "col", 0, 0, tiled=True)
    grad_fine = jnp.sum(up(parts), axis=0).astype(BF)
    return out[None], grad_fine[None], grad_pair_w


def solution(mesh):
    return jax.shard_map(
        local,
        mesh=mesh,
        in_specs=(
            P("batch", "row", None),
            P(None, "col", None),
            P("col", None),
            P("col", None),
            P("batch", "row", "col", None),
            P(),
            P("batch", "row", "col", None),
        ),
        out_specs=(P("batch", "row", "col", None), P("batch", "row", "col"), P()),
        check_vma=False,
    )
```

time: 492 us -> 157 us (0.32)
  waiting for transfers between devices: 314 us -> 51.9 us
  blocking collectives: 103 us -> 0 us
  starting transfers between devices: 23.7 us -> 63.1 us
  between operations: 16.1 us -> 1.31 us
  matrix products: 18.9 us -> 10.5 us
  local copies, waits for them, and re-layouts: 8.22 us -> 16.5 us
  other arithmetic: 5.8 us -> 12.5 us
    psum x1 -> x0, waiting for transfers between devices: 239 us -> none  [local(): lax.psum(local_wgrad, ('row', 'col', 'batch')) / colp_all.shape[1]]
    psum x2 -> x0, blocking collectives: 82.2 us -> none  [the longest x1 41.3 us: local(): lax.psum(part_col.astype(jnp.bfloat16), 'col').astype(jnp.float32)]
    reduce_scatter x1 -> x0, waiting for transfers between devices: 59.7 us -> none  [local(): lax.psum_scatter(full_col.astype(jnp.bfloat16), 'row', scatter_dimension=...]
    ppermute x12 -> x33, starting transfers between devices: 23.6 us -> 58.7 us  [the longest x16 29.4 us: flip(): return lax.ppermute(x, axis, [(i, i ^ bit) for i in range(count)])]
    ppermute x12 -> x33, waiting for transfers between devices: 14.6 us -> 46.5 us  [the longest x16 34.7 us: flip(): return lax.ppermute(x, axis, [(i, i ^ bit) for i in range(count)])]
    all_gather x1 -> x0, blocking collectives: 21.1 us -> none  [local(): colp_all = lax.all_gather(colp_here, 'row', axis=1, tiled=True)]
    dot_general x41 -> x20, matrix products: 18.9 us -> 10.5 us  [the longest x3 2.2 us: pair_block(): jnp.dot(z3[down:down + 36].reshape(-1, 3 * chans), pair_w[down].reshape(3...]
    slice x8 -> x30, local copies, waits for them, and re-layouts: 2.59 us -> 8.13 us  [the longest x2 1.81 us: local(): right = shift(jnp.concatenate([pair[:, :3], cot[:, :2]], axis=1), 'col', -1)]
  transfers between devices with their start and end apart: 15 -> 34, of which waited for: 8 -> 20; matrix products, arithmetic and copies ran while one was open for 2% -> 15% of each run, Pallas kernels for 0% -> 0%
where the time goes in v1:
time: 157 us; the launch traced here: 156 us
  starting transfers between devices  63.1 us (40%)
  waiting for transfers between devices  51.9 us (33%)
  local copies, waits for them, and re-layouts  16.5 us (11%)
  other arithmetic  12.5 us (8%)
  matrix products  10.5 us (7%)
    ppermute x16, waiting for transfers between devices, flip(): return lax.ppermute(x, axis, [(i, i ^ bit) for i in range(count)])  34.7 us
    ppermute x16, starting transfers between devices, flip(): return lax.ppermute(x, axis, [(i, i ^ bit) for i in range(count)])  29.4 us
    ppermute x15, starting transfers between devices, shift(): lax.ppermute(x, axis, [(i, (i + step) % count) for i in range(count)])  27.2 us
    ppermute x15, waiting for transfers between devices, shift(): lax.ppermute(x, axis, [(i, (i + step) % count) for i in range(count)])  10.8 us
    all_to_all x1, waiting for transfers between devices, local(): parts = lax.all_to_all(parts.transpose(1, 0, 2), 'col', 0, 0, tiled=True)  5.38 us
    all_to_all x1, starting transfers between devices, local(): parts = lax.all_to_all(parts.transpose(1, 0, 2), 'col', 0, 0, tiled=True)  4.36 us
    transpose x4, local copies, waits for them, and re-layouts, pair_block(): jnp.swapaxes(pair_w[down], 1, 2).reshape(3 * chans, chans)  3.95 us
  transfers between devices with their start and end apart: 34, of which 20 were waited for; matrix products, arithmetic and copies ran while one was open for 15% of the time, Pallas kernels for 0%

profile of v1, /device:TPU:2, one launch (start us, length us, event | category | flops | bytes accessed | tf_op | source)
XLA Modules:
  0.0 155.9 jit_solution(1688654560559717013)
XLA Ops:
  0.6 0.9 slice_bitcast_fusion.1
  1.6 5.3 %collective-permute-start.5 = (bf16[8,1536]{1,0:T(8,128)(2,1)S(1)}, bf16[8,1536]{1,0:T(8,128)(2,1)S(1)}, u32[]{:S(2)}, u32[]{:S(2)}) collective-permute-start(bf16[8,1536]{1,0:T(8,128)(2,1)S(1)} %get-tuple-element.40), channel_id=1, source_target_pairs={{0,240},{16,0},{32,16},{48,32},{64,48},{80,64},{96,80},{112,96},{1... | collective-permute-start | bytes 73736 | tf_op jit(solution)/shard_map/ppermute | solution.py:13
  6.9 0.9 fusion.98
  7.8 0.9 fusion.97
  9.3 2.1 %collective-permute-start.1 = (bf16[32,5,128]{2,1,0:T(8,128)(2,1)}, bf16[32,5,128]{2,1,0:T(8,128)(2,1)}, u32[]{:S(2)}, u32[]{:S(2)}) collective-permute-start(bf16[32,5,128]{2,1,0:T(8,128)(2,1)} %pad_maximum_fusion.11), channel_id=1, source_target_pairs={{0,2},{2,4},{4,6},{6,8},{8,10},{10,12},{12,14},{14,0},{1,3},{3,5},... | collective-permute-start | bytes 122888 | tf_op jit(solution)/shard_map/ppermute | solution.py:13
  11.5 0.8 constant_dynamic-update-slice_fusion.1
  12.3 0.8 constant_dynamic-update-slice_fusion
  13.7 0.9 pad_maximum_fusion.2
  14.8 1.3 fusion.99
  17.0 0.9 convolution_add_fusion.9
  17.9 1.4 convolution_convert_fusion.1
  19.3 3.1 %collective-permute-start.8 = (bf16[38,256]{1,0:T(8,128)(2,1)S(1)}, bf16[38,256]{1,0:T(8,128)(2,1)S(1)}, u32[]{:S(2)}, u32[]{:S(2)}) collective-permute-start(bf16[38,256]{1,0:T(8,128)(2,1)S(1)} %convolution_convert_fusion.1), channel_id=1, source_target_pairs={{0,12},{2,14},{4,0},{6,2},{8,4},{10,6},{12,8},{14,10},{1,13},{3,15... | collective-permute-start | bytes 58376 | tf_op jit(solution)/shard_map/ppermute | solution.py:13
  22.4 2.2 %collective-permute-start.6 = (bf16[38,256]{1,0:T(8,128)(2,1)S(1)}, bf16[38,256]{1,0:T(8,128)(2,1)S(1)}, u32[]{:S(2)}, u32[]{:S(2)}) collective-permute-start(bf16[38,256]{1,0:T(8,128)(2,1)S(1)} %convolution_convert_fusion.1), channel_id=1, source_target_pairs={{0,8},{2,10},{4,12},{6,14},{8,0},{10,2},{12,4},{14,6},{1,9},{3,11}... | collective-permute-start | bytes 58376 | tf_op jit(solution)/shard_map/ppermute | solution.py:13
  24.7 3.0 %collective-permute-start = (bf16[32,5,128]{2,1,0:T(8,128)(2,1)S(1)}, bf16[32,5,128]{2,1,0:T(8,128)(2,1)S(1)}, u32[]{:S(2)}, u32[]{:S(2)}) collective-permute-start(bf16[32,5,128]{2,1,0:T(8,128)(2,1)S(1)} %pad_maximum_fusion.10), channel_id=1, source_target_pairs={{0,14},{2,0},{4,2},{6,4},{8,6},{10,8},{12,10},{14,12},{1,15},{3,1}... | collective-permute-start | bytes 122888 | tf_op jit(solution)/shard_map/ppermute | solution.py:13
  27.7 1.5 collective-permute-start.9
  29.2 1.7 %slice_bitcast_fusion.2 = (bf16[3,128,128]{1,2,0:T(8,128)(2,1)S(1)}, bf16[3,128,128]{1,2,0:T(8,128)(2,1)S(1)}, bf16[3,128,128]{1,2,0:T(8,128)(2,1)S(1)}, bf16[1,...) fusion(bf16[3,3,128,128]{3,2,1,0:T(8,128)(2,1)} %param.12), kind=kLoop, calls=%fused_computation.160 | loop fusion | bytes 884736 | tf_op jit(solution)/shard_map/transpose | solution.py:73
  31.0 2.1 %collective-permute-done.9 = bf16[38,256]{1,0:T(8,128)(2,1)S(1)} collective-permute-done((bf16[38,256]{1,0:T(8,128)(2,1)S(1)}, bf16[38,256]{1,0:T(8,128)(2,1)S(1)}, u32[]{:S(2)}, u32[]{:S(2)}) %collective-permute-start.9) | collective-permute-done | bytes 19488 | tf_op jit(solution)/shard_map/ppermute | solution.py:18
  33.2 1.1 collective-permute-done.10
  34.4 4.9 %collective-permute-start.11 = (bf16[70,128]{1,0:T(8,128)(2,1)S(1)}, bf16[70,128]{1,0:T(8,128)(2,1)S(1)}, u32[]{:S(2)}, u32[]{:S(2)}) collective-permute-start(bf16[70,128]{1,0:T(8,128)(2,1)S(1)} %pad_maximum_fusion.14), channel_id=1, source_target_pairs={{0,128},{16,144},{32,160},{48,176},{64,192},{80,208},{96,224},{112... | collective-permute-start | bytes 53768 | tf_op jit(solution)/shard_map/ppermute | solution.py:18
  39.5 2.7 %collective-permute-done.11 = bf16[70,128]{1,0:T(8,128)(2,1)S(1)} collective-permute-done((bf16[70,128]{1,0:T(8,128)(2,1)S(1)}, bf16[70,128]{1,0:T(8,128)(2,1)S(1)}, u32[]{:S(2)}, u32[]{:S(2)}) %collective-permute-start.11) | collective-permute-done | bytes 17952 | tf_op jit(solution)/shard_map/ppermute | solution.py:18
  42.4 0.7 copy.20
  43.2 0.7 copy.18
  43.9 0.7 copy.19
  44.8 0.9 slice.352
  45.6 0.9 slice.350
  47.0 1.8 %collective-permute-start.13 = (bf16[70,128]{1,0:T(8,128)(2,1)S(1)}, bf16[70,128]{1,0:T(8,128)(2,1)S(1)}, u32[]{:S(2)}, u32[]{:S(2)}) collective-permute-start(bf16[70,128]{1,0:T(8,128)(2,1)S(1)} %broadcast_select_fusion.6), channel_id=1, source_target_pairs={{0,32},{16,48},{32,0},{48,16},{64,96},{80,112},{96,64},{112,80},{1... | collective-permute-start | bytes 53768 | tf_op jit(solution)/shard_map/ppermute | solution.py:18
  48.9 2.9 %collective-permute-start.3 = (bf16[5,80,128]{2,1,0:T(8,128)(2,1)S(1)}, bf16[5,80,128]{2,1,0:T(8,128)(2,1)S(1)}, u32[]{:S(2)}, u32[]{:S(2)}) collective-permute-start(bf16[5,80,128]{2,1,0:T(8,128)(2,1)S(1)} %get-tuple-element.12), channel_id=1, source_target_pairs={{0,240},{16,0},{32,16},{48,32},{64,48},{80,64},{96,80},{112,96},{1... | collective-permute-start | bytes 307208 | tf_op jit(solution)/shard_map/ppermute | solution.py:13
  52.0 2.2 %collective-permute-done.2 = bf16[5,80,128]{2,1,0:T(8,128)(2,1)S(1)} collective-permute-done((bf16[5,80,128]{2,1,0:T(8,128)(2,1)S(1)}, bf16[5,80,128]{2,1,0:T(8,128)(2,1)S(1)}, u32[]{:S(2)}, u32[]{:S(2)}) %collective-permute-start.2) | collective-permute-done | bytes 102432 | tf_op jit(solution)/shard_map/ppermute | solution.py:13
  54.3 1.6 %select_convert_fusion = bf16[38,80,128]{2,1,0:T(8,128)(2,1)S(1)} fusion(bf16[3,80,128]{2,1,0:T(8,128)(2,1)S(1)} %slice.354, bf16[32,3,128]{2,1,0:T(4,128)(2,1)S(1)} %slice.350, bf16[32,10,128]{2,1,0:T(8,128)(2,1)S(1)} %broadcast_in_dim.96, bf16[32,3,128]{2,1,0:T(4,128)(2,1)S(1)} %slice.347, bf16[32,64,128]{2,1,0:T(8,128)(2,1)S(1)} %bitcast.121, ...), kind=kLoop, calls=%fused_computation.20 | loop fusion | flops 6225920 | bytes 1619936 | tf_op jit(solution)/shard_map/convert_element_type | solution.py:51
  56.3 0.7 maximum_maximum_fusion
  57.6 0.7 fusion.100
  58.4 0.7 convolution_add_fusion.4
  59.2 0.7 convolution_add_fusion.3
  60.0 2.6 %multiply_convert_fusion = (bf16[36,80,128]{2,1,0:T(8,128)(2,1)S(1)}, f32[36,80,128]{2,1,0:T(8,128)}, f32[36,80,128]{2,1,0:T(8,128)S(1)}) fusion(f32[36,80,128]{2,1,0:T(8,128)S(1)} %bitcast.109, bf16[2,80,128]{2,1,0:T(8,128)(2,1)S(1)} %slice.377, bf16[32,2,128]{2,1,0:T(2,128)(2,1)S(1)} %slice.352, bf16[32,12,128]{2,1,0:T(8,128)(2,1)S(1)} %broadcast_in_dim.97, ...), kind=kLoop, calls=%fused_computation.21 | loop fusion | flops 8110080 | bytes 5901120 | tf_op jit(solution)/shard_map/convert_element_type | solution.py:65
  63.2 0.8 maximum_maximum_fusion.1
  69.8 3.0 %collective-permute-done.15 = bf16[34,128]{1,0:T(8,128)(2,1)S(1)} collective-permute-done((bf16[34,128]{1,0:T(8,128)(2,1)S(1)}, bf16[34,128]{1,0:T(8,128)(2,1)S(1)}, u32[]{:S(2)}, u32[]{:S(2)}) %collective-permute-start.15) | collective-permute-done | bytes 8736 | tf_op jit(solution)/shard_map/ppermute | solution.py:18
  72.9 3.1 %collective-permute-start.16 = (bf16[34,128]{1,0:T(8,128)(2,1)S(1)}, bf16[34,128]{1,0:T(8,128)(2,1)S(1)}, u32[]{:S(2)}, u32[]{:S(2)}) collective-permute-start(bf16[34,128]{1,0:T(8,128)(2,1)S(1)} %add_convert_fusion.13), channel_id=1, source_target_pairs={{0,64},{16,80},{32,96},{48,112},{64,0},{80,16},{96,32},{112,48},{1... | collective-permute-start | bytes 26120 | tf_op jit(solution)/shard_map/ppermute | solution.py:18
  76.0 1.6 %collective-permute-done.16 = bf16[34,128]{1,0:T(8,128)(2,1)S(1)} collective-permute-done((bf16[34,128]{1,0:T(8,128)(2,1)S(1)}, bf16[34,128]{1,0:T(8,128)(2,1)S(1)}, u32[]{:S(2)}, u32[]{:S(2)}) %collective-permute-start.16) | collective-permute-done | bytes 8736 | tf_op jit(solution)/shard_map/ppermute | solution.py:18
  77.7 4.3 %collective-permute-start.17 = (bf16[34,128]{1,0:T(8,128)(2,1)S(1)}, bf16[34,128]{1,0:T(8,128)(2,1)S(1)}, u32[]{:S(2)}, u32[]{:S(2)}) collective-permute-start(bf16[34,128]{1,0:T(8,128)(2,1)S(1)} %add_convert_fusion.12), channel_id=1, source_target_pairs={{0,128},{16,144},{32,160},{48,176},{64,192},{80,208},{96,224},{112... | collective-permute-start | bytes 26120 | tf_op jit(solution)/shard_map/ppermute | solution.py:18
  82.1 3.5 %collective-permute-done.17 = bf16[34,128]{1,0:T(8,128)(2,1)S(1)} collective-permute-done((bf16[34,128]{1,0:T(8,128)(2,1)S(1)}, bf16[34,128]{1,0:T(8,128)(2,1)S(1)}, u32[]{:S(2)}, u32[]{:S(2)}) %collective-permute-start.17) | collective-permute-done | bytes 8736 | tf_op jit(solution)/shard_map/ppermute | solution.py:18
  86.3 4.1 %collective-permute-start.18 = (bf16[34,256]{1,0:T(8,128)(2,1)S(1)}, bf16[34,256]{1,0:T(8,128)(2,1)S(1)}, u32[]{:S(2)}, u32[]{:S(2)}) collective-permute-start(bf16[34,256]{1,0:T(8,128)(2,1)S(1)} %pad_maximum_fusion.13), channel_id=1, source_target_pairs={{0,8},{2,10},{4,12},{6,14},{8,0},{10,2},{12,4},{14,6},{1,9},{3,11}... | collective-permute-start | bytes 52232 | tf_op jit(solution)/shard_map/ppermute | solution.py:13
  91.1 1.2 collective-permute-done.18
  92.3 1.8 %collective-permute-done.20 = bf16[34,256]{1,0:T(8,128)(2,1)S(1)} collective-permute-done((bf16[34,256]{1,0:T(8,128)(2,1)S(1)}, bf16[34,256]{1,0:T(8,128)(2,1)S(1)}, u32[]{:S(2)}, u32[]{:S(2)}) %collective-permute-start.20) | collective-permute-done | bytes 17440 | tf_op jit(solution)/shard_map/ppermute | solution.py:13
  94.2 1.2 collective-permute-start.21
  95.5 4.1 %collective-permute-done.21 = bf16[34,256]{1,0:T(8,128)(2,1)S(1)} collective-permute-done((bf16[34,256]{1,0:T(8,128)(2,1)S(1)}, bf16[34,256]{1,0:T(8,128)(2,1)S(1)}, u32[]{:S(2)}, u32[]{:S(2)}) %collective-permute-start.21) | collective-permute-done | bytes 17440 | tf_op jit(solution)/shard_map/ppermute | solution.py:18
  100.0 1.4 collective-permute-start.25
  102.1 1.5 collective-permute-start.23
  103.8 3.0 %collective-permute-done.25 = bf16[576,128]{1,0:T(8,128)(2,1)S(1)} collective-permute-done((bf16[576,128]{1,0:T(8,128)(2,1)S(1)}, bf16[576,128]{1,0:T(8,128)(2,1)S(1)}, u32[]{:S(2)}, u32[]{:S(2)}) %collective-permute-start.25) | collective-permute-done | bytes 147488 | tf_op jit(solution)/shard_map/ppermute | solution.py:13
  106.8 2.6 %collective-permute-done.24 = bf16[576,128]{1,0:T(8,128)(2,1)S(1)} collective-permute-done((bf16[576,128]{1,0:T(8,128)(2,1)S(1)}, bf16[576,128]{1,0:T(8,128)(2,1)S(1)}, u32[]{:S(2)}, u32[]{:S(2)}) %collective-permute-start.24) | collective-permute-done | bytes 147488 | tf_op jit(solution)/shard_map/ppermute | solution.py:13
  109.5 1.5 collective-permute-start.28
  111.6 3.3 %collective-permute-start.26 = (bf16[576,128]{1,0:T(8,128)(2,1)S(1)}, bf16[576,128]{1,0:T(8,128)(2,1)S(1)}, u32[]{:S(2)}, u32[]{:S(2)}) collective-permute-start(bf16[576,128]{1,0:T(8,128)(2,1)S(1)} %add_convert_fusion.4), channel_id=1, source_target_pairs={{0,2},{2,0},{4,6},{6,4},{8,10},{10,8},{12,14},{14,12},{1,3},{3,1},... | collective-permute-start | bytes 442376 | tf_op jit(solution)/shard_map/ppermute | solution.py:18
  115.1 1.0 collective-permute-done.27
  116.1 2.1 %collective-permute-done.26 = bf16[576,128]{1,0:T(8,128)(2,1)S(1)} collective-permute-done((bf16[576,128]{1,0:T(8,128)(2,1)S(1)}, bf16[576,128]{1,0:T(8,128)(2,1)S(1)}, u32[]{:S(2)}, u32[]{:S(2)}) %collective-permute-start.26) | collective-permute-done | bytes 147488 | tf_op jit(solution)/shard_map/ppermute | solution.py:18
  118.3 2.0 %collective-permute-start.29 = (bf16[576,128]{1,0:T(8,128)(2,1)S(1)}, bf16[576,128]{1,0:T(8,128)(2,1)S(1)}, u32[]{:S(2)}, u32[]{:S(2)}) collective-permute-start(bf16[576,128]{1,0:T(8,128)(2,1)S(1)} %add_convert_fusion.3), channel_id=1, source_target_pairs={{0,32},{16,48},{32,0},{48,16},{64,96},{80,112},{96,64},{112,80},{1... | collective-permute-start | bytes 442376 | tf_op jit(solution)/shard_map/ppermute | solution.py:18
  120.5 4.3 %collective-permute-done.29 = bf16[576,128]{1,0:T(8,128)(2,1)S(1)} collective-permute-done((bf16[576,128]{1,0:T(8,128)(2,1)S(1)}, bf16[576,128]{1,0:T(8,128)(2,1)S(1)}, u32[]{:S(2)}, u32[]{:S(2)}) %collective-permute-start.29) | collective-permute-done | bytes 147488 | tf_op jit(solution)/shard_map/ppermute | solution.py:18
  124.8 2.5 %collective-permute-start.30 = (bf16[576,128]{1,0:T(8,128)(2,1)S(1)}, bf16[576,128]{1,0:T(8,128)(2,1)S(1)}, u32[]{:S(2)}, u32[]{:S(2)}) collective-permute-start(bf16[576,128]{1,0:T(8,128)(2,1)S(1)} %add_convert_fusion.2), channel_id=1, source_target_pairs={{0,64},{16,80},{32,96},{48,112},{64,0},{80,16},{96,32},{112,48},{1... | collective-permute-start | bytes 442376 | tf_op jit(solution)/shard_map/ppermute | solution.py:18
  127.5 8.2 %collective-permute-done.30 = bf16[576,128]{1,0:T(8,128)(2,1)S(1)} collective-permute-done((bf16[576,128]{1,0:T(8,128)(2,1)S(1)}, bf16[576,128]{1,0:T(8,128)(2,1)S(1)}, u32[]{:S(2)}, u32[]{:S(2)}) %collective-permute-start.30) | collective-permute-done | bytes 147488 | tf_op jit(solution)/shard_map/ppermute | solution.py:18
  135.8 4.1 %collective-permute-start.31 = (bf16[576,128]{1,0:T(8,128)(2,1)S(1)}, bf16[576,128]{1,0:T(8,128)(2,1)S(1)}, u32[]{:S(2)}, u32[]{:S(2)}) collective-permute-start(bf16[576,128]{1,0:T(8,128)(2,1)S(1)} %add_convert_fusion.1), channel_id=1, source_target_pairs={{0,128},{16,144},{32,160},{48,176},{64,192},{80,208},{96,224},{112... | collective-permute-start | bytes 442376 | tf_op jit(solution)/shard_map/ppermute | solution.py:18
  140.4 0.8 copy.22
  141.2 4.4 %all-to-all-start = ((bf16[8,64,192]{2,1,0:T(8,128)(2,1)}), bf16[8,64,192]{2,1,0:T(8,128)(2,1)S(1)}, u32[]{:S(2)}, u32[]{:S(2)}) async-start(bf16[8,64,192]{2,1,0:T(8,128)(2,1)} %copy.22), calls=%async_computation | async-start | bytes 524288 | tf_op jit(solution)/shard_map/all_to_all | solution.py:174
  145.5 1.0 collective-permute-done.31
  146.7 2.3 %fusion.38 = bf16[1,32,64,128]{3,2,1,0:T(8,128)(2,1)} fusion(f32[36,80,128]{2,1,0:T(8,128)} %get-tuple-element.10, f32[36,80,128]{2,1,0:T(8,128)S(1)} %bitcast.110, bf16[38,80,128]{2,1,0:T(8,128)(2,1)S(1)} %select_convert_fusion), kind=kLoop, calls=%fused_computation.55 | loop fusion | flops 1048576 | bytes 3145728 | tf_op jit(solution)/shard_map/broadcast_in_dim | solution.py:176
  148.9 5.4 %all-to-all-done = bf16[8,64,192]{2,1,0:T(8,128)(2,1)S(1)} async-done(((bf16[8,64,192]{2,1,0:T(8,128)(2,1)}), bf16[8,64,192]{2,1,0:T(8,128)(2,1)S(1)}, u32[]{:S(2)}, u32[]{:S(2)}) %all-to-all-start) | async-done | bytes 196640 | tf_op jit(solution)/shard_map/all_to_all | solution.py:174
  155.0 0.9 convert_multiply_fusion
  (136 shorter events, 16.9 us)
Async XLA Ops:
  0.6 15.4 %copy-start = (bf16[5,192,1536]{2,1,0:T(8,128)(2,1)S(1)}, bf16[5,192,1536]{2,1,0:T(8,128)(2,1)}, u32[]{:S(2)}) copy-start(bf16[5,192,1536]{2,1,0:T(8,128)(2,1)} %param.8) | copy-start | bytes 8847364
  1.6 11.6 %collective-permute-start.4 = (bf16[8,1536]{1,0:T(8,128)(2,1)S(1)}, bf16[8,1536]{1,0:T(8,128)(2,1)S(1)}, u32[]{:S(2)}, u32[]{:S(2)}) collective-permute-start(bf16[8,1536]{1,0:T(8,128)(2,1)S(1)} %get-tuple-element.39), channel_id=1, source_target_pairs={{0,16},{16,32},{32,48},{48,64},{64,80},{80,96},{96,112},{112,128},... | collective-permute-start | bytes 73736 | tf_op jit(solution)/shard_map/ppermute | solution.py:13
  1.6 11.6 %collective-permute-start.5 = (bf16[8,1536]{1,0:T(8,128)(2,1)S(1)}, bf16[8,1536]{1,0:T(8,128)(2,1)S(1)}, u32[]{:S(2)}, u32[]{:S(2)}) collective-permute-start(bf16[8,1536]{1,0:T(8,128)(2,1)S(1)} %get-tuple-element.40), channel_id=1, source_target_pairs={{0,240},{16,0},{32,16},{48,32},{64,48},{80,64},{96,80},{112,96},{1... | collective-permute-start | bytes 73736 | tf_op jit(solution)/shard_map/ppermute | solution.py:13
  9.3 35.4 %collective-permute-start.1 = (bf16[32,5,128]{2,1,0:T(8,128)(2,1)}, bf16[32,5,128]{2,1,0:T(8,128)(2,1)}, u32[]{:S(2)}, u32[]{:S(2)}) collective-permute-start(bf16[32,5,128]{2,1,0:T(8,128)(2,1)} %pad_maximum_fusion.11), channel_id=1, source_target_pairs={{0,2},{2,4},{4,6},{6,8},{8,10},{10,12},{12,14},{14,0},{1,3},{3,5},... | collective-permute-start | bytes 122888 | tf_op jit(solution)/shard_map/ppermute | solution.py:13
  13.1 0.6 copy-start.9
  17.0 31.9 %copy-start.2 = (bf16[1,32,64,128]{3,2,1,0:T(8,128)(2,1)S(1)}, bf16[1,32,64,128]{3,2,1,0:T(8,128)(2,1)}, u32[]{:S(2)}) copy-start(bf16[1,32,64,128]{3,2,1,0:T(8,128)(2,1)} %param.11) | copy-start | bytes 1572868
  19.3 29.5 %copy-start.3 = (bf16[1,32,64,128]{3,2,1,0:T(8,128)(2,1)S(1)}, bf16[1,32,64,128]{3,2,1,0:T(8,128)(2,1)}, u32[]{:S(2)}) copy-start(bf16[1,32,64,128]{3,2,1,0:T(8,128)(2,1)} %param.13) | copy-start | bytes 1572868
  19.3 8.3 %collective-permute-start.8 = (bf16[38,256]{1,0:T(8,128)(2,1)S(1)}, bf16[38,256]{1,0:T(8,128)(2,1)S(1)}, u32[]{:S(2)}, u32[]{:S(2)}) collective-permute-start(bf16[38,256]{1,0:T(8,128)(2,1)S(1)} %convolution_convert_fusion.1), channel_id=1, source_target_pairs={{0,12},{2,14},{4,0},{6,2},{8,4},{10,6},{12,8},{14,10},{1,13},{3,15... | collective-permute-start | bytes 58376 | tf_op jit(solution)/shard_map/ppermute | solution.py:13
  22.4 5.2 %collective-permute-start.7 = (bf16[38,256]{1,0:T(8,128)(2,1)S(1)}, bf16[38,256]{1,0:T(8,128)(2,1)S(1)}, u32[]{:S(2)}, u32[]{:S(2)}) collective-permute-start(bf16[38,256]{1,0:T(8,128)(2,1)S(1)} %convolution_convert_fusion.1), channel_id=1, source_target_pairs={{0,4},{2,6},{4,8},{6,10},{8,12},{10,14},{12,0},{14,2},{1,5},{3,7},... | collective-permute-start | bytes 58376 | tf_op jit(solution)/shard_map/ppermute | solution.py:13
  22.4 5.3 %collective-permute-start.6 = (bf16[38,256]{1,0:T(8,128)(2,1)S(1)}, bf16[38,256]{1,0:T(8,128)(2,1)S(1)}, u32[]{:S(2)}, u32[]{:S(2)}) collective-permute-start(bf16[38,256]{1,0:T(8,128)(2,1)S(1)} %convolution_convert_fusion.1), channel_id=1, source_target_pairs={{0,8},{2,10},{4,12},{6,14},{8,0},{10,2},{12,4},{14,6},{1,9},{3,11}... | collective-permute-start | bytes 58376 | tf_op jit(solution)/shard_map/ppermute | solution.py:13
  24.7 21.8 %collective-permute-start = (bf16[32,5,128]{2,1,0:T(8,128)(2,1)S(1)}, bf16[32,5,128]{2,1,0:T(8,128)(2,1)S(1)}, u32[]{:S(2)}, u32[]{:S(2)}) collective-permute-start(bf16[32,5,128]{2,1,0:T(8,128)(2,1)S(1)} %pad_maximum_fusion.10), channel_id=1, source_target_pairs={{0,14},{2,0},{4,2},{6,4},{8,6},{10,8},{12,10},{14,12},{1,15},{3,1}... | collective-permute-start | bytes 122888 | tf_op jit(solution)/shard_map/ppermute | solution.py:13
  27.7 5.4 %collective-permute-start.9 = (bf16[38,256]{1,0:T(8,128)(2,1)S(1)}, bf16[38,256]{1,0:T(8,128)(2,1)S(1)}, u32[]{:S(2)}, u32[]{:S(2)}) collective-permute-start(bf16[38,256]{1,0:T(8,128)(2,1)S(1)} %add_convert_fusion.9), channel_id=1, source_target_pairs={{0,2},{2,0},{4,6},{6,4},{8,10},{10,8},{12,14},{14,12},{1,3},{3,1},... | collective-permute-start | bytes 58376 | tf_op jit(solution)/shard_map/ppermute | solution.py:18
  33.1 1.3 collective-permute-start.10
  34.4 7.8 %collective-permute-start.11 = (bf16[70,128]{1,0:T(8,128)(2,1)S(1)}, bf16[70,128]{1,0:T(8,128)(2,1)S(1)}, u32[]{:S(2)}, u32[]{:S(2)}) collective-permute-start(bf16[70,128]{1,0:T(8,128)(2,1)S(1)} %pad_maximum_fusion.14), channel_id=1, source_target_pairs={{0,128},{16,144},{32,160},{48,176},{64,192},{80,208},{96,224},{112... | collective-permute-start | bytes 53768 | tf_op jit(solution)/shard_map/ppermute | solution.py:18
  42.2 4.7 %collective-permute-start.12 = (bf16[70,128]{1,0:T(8,128)(2,1)S(1)}, bf16[70,128]{1,0:T(8,128)(2,1)S(1)}, u32[]{:S(2)}, u32[]{:S(2)}) collective-permute-start(bf16[70,128]{1,0:T(8,128)(2,1)S(1)} %broadcast_select_fusion.5), channel_id=1, source_target_pairs={{0,64},{16,80},{32,96},{48,112},{64,0},{80,16},{96,32},{112,48},{1... | collective-permute-start | bytes 53768 | tf_op jit(solution)/shard_map/ppermute | solution.py:18
  47.0 4.9 %collective-permute-start.13 = (bf16[70,128]{1,0:T(8,128)(2,1)S(1)}, bf16[70,128]{1,0:T(8,128)(2,1)S(1)}, u32[]{:S(2)}, u32[]{:S(2)}) collective-permute-start(bf16[70,128]{1,0:T(8,128)(2,1)S(1)} %broadcast_select_fusion.6), channel_id=1, source_target_pairs={{0,32},{16,48},{32,0},{48,16},{64,96},{80,112},{96,64},{112,80},{1... | collective-permute-start | bytes 53768 | tf_op jit(solution)/shard_map/ppermute | solution.py:18
  48.9 5.3 %collective-permute-start.2 = (bf16[5,80,128]{2,1,0:T(8,128)(2,1)S(1)}, bf16[5,80,128]{2,1,0:T(8,128)(2,1)S(1)}, u32[]{:S(2)}, u32[]{:S(2)}) collective-permute-start(bf16[5,80,128]{2,1,0:T(8,128)(2,1)S(1)} %get-tuple-element.11), channel_id=1, source_target_pairs={{0,16},{16,32},{32,48},{48,64},{64,80},{80,96},{96,112},{112,128},... | collective-permute-start | bytes 307208 | tf_op jit(solution)/shard_map/ppermute | solution.py:13
  48.9 5.3 %collective-permute-start.3 = (bf16[5,80,128]{2,1,0:T(8,128)(2,1)S(1)}, bf16[5,80,128]{2,1,0:T(8,128)(2,1)S(1)}, u32[]{:S(2)}, u32[]{:S(2)}) collective-permute-start(bf16[5,80,128]{2,1,0:T(8,128)(2,1)S(1)} %get-tuple-element.12), channel_id=1, source_target_pairs={{0,240},{16,0},{32,16},{48,32},{64,48},{80,64},{96,80},{112,96},{1... | collective-permute-start | bytes 307208 | tf_op jit(solution)/shard_map/ppermute | solution.py:13
  52.0 4.2 %copy-start.8 = (f32[80,128]{1,0:T(8,128)}, f32[80,128]{1,0:T(8,128)S(1)}, u32[]{:S(2)}) copy-start(f32[80,128]{1,0:T(8,128)S(1)} %maximum_convert_fusion) | copy-start | bytes 122884
  58.3 0.9 copy-start.4
  64.1 0.9 copy-start.7
  64.9 0.9 copy-start.6
  65.8 0.9 copy-start.5
  67.8 1.3 collective-permute-start.14
  69.1 6.8 %slice-start = ((f32[80,128]{1,0:T(8,128)}), f32[64,128]{1,0:T(8,128)S(1)}, s32[]{:S(2)}) async-start(f32[80,128]{1,0:T(8,128)} %copy-done.8), calls=%async_computation.1 | async-start | bytes 65536 | tf_op jit(solution)/shard_map/slice | solution.py:85
  69.1 3.8 %collective-permute-start.15 = (bf16[34,128]{1,0:T(8,128)(2,1)S(1)}, bf16[34,128]{1,0:T(8,128)(2,1)S(1)}, u32[]{:S(2)}, u32[]{:S(2)}) collective-permute-start(bf16[34,128]{1,0:T(8,128)(2,1)S(1)} %add_convert_fusion.14), channel_id=1, source_target_pairs={{0,32},{16,48},{32,0},{48,16},{64,96},{80,112},{96,64},{112,80},{1... | collective-permute-start | bytes 26120 | tf_op jit(solution)/shard_map/ppermute | solution.py:18
  72.9 4.8 %collective-permute-start.16 = (bf16[34,128]{1,0:T(8,128)(2,1)S(1)}, bf16[34,128]{1,0:T(8,128)(2,1)S(1)}, u32[]{:S(2)}, u32[]{:S(2)}) collective-permute-start(bf16[34,128]{1,0:T(8,128)(2,1)S(1)} %add_convert_fusion.13), channel_id=1, source_target_pairs={{0,64},{16,80},{32,96},{48,112},{64,0},{80,16},{96,32},{112,48},{1... | collective-permute-start | bytes 26120 | tf_op jit(solution)/shard_map/ppermute | solution.py:18
  77.7 7.9 %collective-permute-start.17 = (bf16[34,128]{1,0:T(8,128)(2,1)S(1)}, bf16[34,128]{1,0:T(8,128)(2,1)S(1)}, u32[]{:S(2)}, u32[]{:S(2)}) collective-permute-start(bf16[34,128]{1,0:T(8,128)(2,1)S(1)} %add_convert_fusion.12), channel_id=1, source_target_pairs={{0,128},{16,144},{32,160},{48,176},{64,192},{80,208},{96,224},{112... | collective-permute-start | bytes 26120 | tf_op jit(solution)/shard_map/ppermute | solution.py:18
  85.6 14.0 %copy-start.10 = (bf16[192,256]{1,0:T(8,128)(2,1)S(1)}, bf16[192,256]{1,0:T(8,128)(2,1)}, u32[]{:S(2)}) copy-start(bf16[192,256]{1,0:T(8,128)(2,1)} %copy-done.9) | copy-start | bytes 294916
  85.6 14.1 %copy-start.1 = (bf16[5,192,1536]{2,1,0:T(8,128)(2,1)S(1)}, bf16[5,192,1536]{2,1,0:T(8,128)(2,1)}, u32[]{:S(2)}) copy-start(bf16[5,192,1536]{2,1,0:T(8,128)(2,1)} %param.8) | copy-start | bytes 8847364
  85.6 5.5 %collective-permute-start.19 = (bf16[34,256]{1,0:T(8,128)(2,1)S(1)}, bf16[34,256]{1,0:T(8,128)(2,1)S(1)}, u32[]{:S(2)}, u32[]{:S(2)}) collective-permute-start(bf16[34,256]{1,0:T(8,128)(2,1)S(1)} %pad_maximum_fusion.13), channel_id=1, source_target_pairs={{0,4},{2,6},{4,8},{6,10},{8,12},{10,14},{12,0},{14,2},{1,5},{3,7},... | collective-permute-start | bytes 52232 | tf_op jit(solution)/shard_map/ppermute | solution.py:13
  86.3 6.0 %collective-permute-start.18 = (bf16[34,256]{1,0:T(8,128)(2,1)S(1)}, bf16[34,256]{1,0:T(8,128)(2,1)S(1)}, u32[]{:S(2)}, u32[]{:S(2)}) collective-permute-start(bf16[34,256]{1,0:T(8,128)(2,1)S(1)} %pad_maximum_fusion.13), channel_id=1, source_target_pairs={{0,8},{2,10},{4,12},{6,14},{8,0},{10,2},{12,4},{14,6},{1,9},{3,11}... | collective-permute-start | bytes 52232 | tf_op jit(solution)/shard_map/ppermute | solution.py:13
  90.4 3.8 %collective-permute-start.20 = (bf16[34,256]{1,0:T(8,128)(2,1)S(1)}, bf16[34,256]{1,0:T(8,128)(2,1)S(1)}, u32[]{:S(2)}, u32[]{:S(2)}) collective-permute-start(bf16[34,256]{1,0:T(8,128)(2,1)S(1)} %pad_maximum_fusion.13), channel_id=1, source_target_pairs={{0,12},{2,14},{4,0},{6,2},{8,4},{10,6},{12,8},{14,10},{1,13},{3,15... | collective-permute-start | bytes 52232 | tf_op jit(solution)/shard_map/ppermute | solution.py:13
  94.2 5.4 %collective-permute-start.21 = (bf16[34,256]{1,0:T(8,128)(2,1)S(1)}, bf16[34,256]{1,0:T(8,128)(2,1)S(1)}, u32[]{:S(2)}, u32[]{:S(2)}) collective-permute-start(bf16[34,256]{1,0:T(8,128)(2,1)S(1)} %add_convert_fusion.7), channel_id=1, source_target_pairs={{0,2},{2,0},{4,6},{6,4},{8,10},{10,8},{12,14},{14,12},{1,3},{3,1},... | collective-permute-start | bytes 52232 | tf_op jit(solution)/shard_map/ppermute | solution.py:18
  95.4 4.6 %collective-permute-start.22 = (bf16[576,128]{1,0:T(8,128)(2,1)S(1)}, bf16[576,128]{1,0:T(8,128)(2,1)S(1)}, u32[]{:S(2)}, u32[]{:S(2)}) collective-permute-start(bf16[576,128]{1,0:T(8,128)(2,1)S(1)} %select_convert_fusion.1), channel_id=1, source_target_pairs={{0,16},{16,0},{32,48},{48,32},{64,80},{80,64},{96,112},{112,96},{1... | collective-permute-start | bytes 442376 | tf_op jit(solution)/shard_map/ppermute | solution.py:18
  100.0 6.8 %collective-permute-start.25 = (bf16[576,128]{1,0:T(8,128)(2,1)S(1)}, bf16[576,128]{1,0:T(8,128)(2,1)S(1)}, u32[]{:S(2)}, u32[]{:S(2)}) collective-permute-start(bf16[576,128]{1,0:T(8,128)(2,1)S(1)} %add_convert_fusion.5), channel_id=1, source_target_pairs={{0,12},{2,14},{4,0},{6,2},{8,4},{10,6},{12,8},{14,10},{1,13},{3,15... | collective-permute-start | bytes 442376 | tf_op jit(solution)/shard_map/ppermute | solution.py:13
  101.4 7.9 %collective-permute-start.24 = (bf16[576,128]{1,0:T(8,128)(2,1)S(1)}, bf16[576,128]{1,0:T(8,128)(2,1)S(1)}, u32[]{:S(2)}, u32[]{:S(2)}) collective-permute-start(bf16[576,128]{1,0:T(8,128)(2,1)S(1)} %add_convert_fusion.5), channel_id=1, source_target_pairs={{0,4},{2,6},{4,8},{6,10},{8,12},{10,14},{12,0},{14,2},{1,5},{3,7},... | collective-permute-start | bytes 442376 | tf_op jit(solution)/shard_map/ppermute | solution.py:13
  102.1 7.3 %collective-permute-start.23 = (bf16[576,128]{1,0:T(8,128)(2,1)S(1)}, bf16[576,128]{1,0:T(8,128)(2,1)S(1)}, u32[]{:S(2)}, u32[]{:S(2)}) collective-permute-start(bf16[576,128]{1,0:T(8,128)(2,1)S(1)} %add_convert_fusion.5), channel_id=1, source_target_pairs={{0,8},{2,10},{4,12},{6,14},{8,0},{10,2},{12,4},{14,6},{1,9},{3,11}... | collective-permute-start | bytes 442376 | tf_op jit(solution)/shard_map/ppermute | solution.py:13
  109.5 5.6 %collective-permute-start.28 = (bf16[576,128]{1,0:T(8,128)(2,1)S(1)}, bf16[576,128]{1,0:T(8,128)(2,1)S(1)}, u32[]{:S(2)}, u32[]{:S(2)}) collective-permute-start(bf16[576,128]{1,0:T(8,128)(2,1)S(1)} %add_convert_fusion.4), channel_id=1, source_target_pairs={{0,3},{1,0},{2,1},{3,2},{4,7},{5,4},{6,5},{7,6},{8,11},{9,8},{10,9... | collective-permute-start | bytes 442376 | tf_op jit(solution)/shard_map/ppermute | solution.py:23
  111.0 5.1 %collective-permute-start.27 = (bf16[576,128]{1,0:T(8,128)(2,1)S(1)}, bf16[576,128]{1,0:T(8,128)(2,1)S(1)}, u32[]{:S(2)}, u32[]{:S(2)}) collective-permute-start(bf16[576,128]{1,0:T(8,128)(2,1)S(1)} %add_convert_fusion.4), channel_id=1, source_target_pairs={{0,1},{1,2},{2,3},{3,0},{4,5},{5,6},{6,7},{7,4},{8,9},{9,10},{10,1... | collective-permute-start | bytes 442376 | tf_op jit(solution)/shard_map/ppermute | solution.py:23
  111.6 6.6 %collective-permute-start.26 = (bf16[576,128]{1,0:T(8,128)(2,1)S(1)}, bf16[576,128]{1,0:T(8,128)(2,1)S(1)}, u32[]{:S(2)}, u32[]{:S(2)}) collective-permute-start(bf16[576,128]{1,0:T(8,128)(2,1)S(1)} %add_convert_fusion.4), channel_id=1, source_target_pairs={{0,2},{2,0},{4,6},{6,4},{8,10},{10,8},{12,14},{14,12},{1,3},{3,1},... | collective-permute-start | bytes 442376 | tf_op jit(solution)/shard_map/ppermute | solution.py:18
  118.3 6.5 %collective-permute-start.29 = (bf16[576,128]{1,0:T(8,128)(2,1)S(1)}, bf16[576,128]{1,0:T(8,128)(2,1)S(1)}, u32[]{:S(2)}, u32[]{:S(2)}) collective-permute-start(bf16[576,128]{1,0:T(8,128)(2,1)S(1)} %add_convert_fusion.3), channel_id=1, source_target_pairs={{0,32},{16,48},{32,0},{48,16},{64,96},{80,112},{96,64},{112,80},{1... | collective-permute-start | bytes 442376 | tf_op jit(solution)/shard_map/ppermute | solution.py:18
  124.8 10.9 %collective-permute-start.30 = (bf16[576,128]{1,0:T(8,128)(2,1)S(1)}, bf16[576,128]{1,0:T(8,128)(2,1)S(1)}, u32[]{:S(2)}, u32[]{:S(2)}) collective-permute-start(bf16[576,128]{1,0:T(8,128)(2,1)S(1)} %add_convert_fusion.2), channel_id=1, source_target_pairs={{0,64},{16,80},{32,96},{48,112},{64,0},{80,16},{96,32},{112,48},{1... | collective-permute-start | bytes 442376 | tf_op jit(solution)/shard_map/ppermute | solution.py:18
  135.8 10.7 %collective-permute-start.31 = (bf16[576,128]{1,0:T(8,128)(2,1)S(1)}, bf16[576,128]{1,0:T(8,128)(2,1)S(1)}, u32[]{:S(2)}, u32[]{:S(2)}) collective-permute-start(bf16[576,128]{1,0:T(8,128)(2,1)S(1)} %add_convert_fusion.1), channel_id=1, source_target_pairs={{0,128},{16,144},{32,160},{48,176},{64,192},{80,208},{96,224},{112... | collective-permute-start | bytes 442376 | tf_op jit(solution)/shard_map/ppermute | solution.py:18
  141.2 13.1 %all-to-all-start = ((bf16[8,64,192]{2,1,0:T(8,128)(2,1)}), bf16[8,64,192]{2,1,0:T(8,128)(2,1)S(1)}, u32[]{:S(2)}, u32[]{:S(2)}) async-start(bf16[8,64,192]{2,1,0:T(8,128)(2,1)} %copy.22), calls=%async_computation | async-start | bytes 524288 | tf_op jit(solution)/shard_map/all_to_all | solution.py:174
  146.6 8.4 %collective-permute-start.32 = (bf16[576,128]{1,0:T(8,128)(2,1)S(1)}, bf16[576,128]{1,0:T(8,128)(2,1)S(1)}, u32[]{:S(2)}, u32[]{:S(2)}) collective-permute-start(bf16[576,128]{1,0:T(8,128)(2,1)S(1)} %add_convert_fusion), channel_id=1, source_target_pairs={{0,16},{16,0},{32,48},{48,32},{64,80},{80,64},{96,112},{112,96},{1... | collective-permute-start | bytes 442376 | tf_op jit(solution)/shard_map/ppermute | solution.py:18

commit v2 on v1

v2 whole, which is shorter than its diff:
```python
import jax
import jax.numpy as jnp
from jax import lax
from jax.experimental import pallas as pl
from jax.experimental.pallas import tpu as pltpu
from jax.sharding import PartitionSpec as P

BF = jnp.bfloat16
F32 = jnp.float32
WIDE = 80
KEPT = 616


def shift(x, axis, step):
    count = lax.axis_size(axis)
    return lax.ppermute(x, axis, [(i, (i + step) % count) for i in range(count)])


def flip(x, axis, bit):
    count = lax.axis_size(axis)
    return lax.ppermute(x, axis, [(i, i ^ bit) for i in range(count)])


def ring(x, step):
    pairs = [(4 * y + p, 4 * y + (p + step) % 4) for y in range(4) for p in range(4)]
    return lax.ppermute(x, ("col", "batch"), pairs)


def up(x):
    return x.astype(F32)


def sum_y(x):
    across, left, right = shift(x, "col", 4), shift(x, "col", 2), shift(x, "col", 6)
    return ((up(x) + up(across)) + (up(left) + up(right))).astype(BF)


def sum_flip(x, axis, bit):
    return (up(x) + up(flip(x, axis, bit))).astype(BF)


def pair_kernel(
    flags, pair, cot, top, bottom, left, right, rowp, colp, weight, turned,
    out, keep, send, rowg,
    zwide, z3, cots, qwide, q3, wgrad, line,
):
    chans = 128
    has_up, has_down, has_left, has_right, core = (flags[i] for i in range(5))
    rows = lax.broadcasted_iota(jnp.int32, (38, 1, 1), 0)
    row_ok = ((rows >= 3) | (has_up > 0)) & ((rows < 35) | (has_down > 0))

    zwide[:, 0:8] = jnp.zeros((38, 8, chans), F32)
    zwide[:, 72:96] = jnp.zeros((38, 24, chans), F32)
    cots[:, 64:80] = jnp.zeros((36, 16, chans), F32)

    def zeta(values, first, count, lo, hi):
        scaled = rowp[first : first + count][:, None, :] * colp[lo:hi][None, :, :]
        return up((up(values) + scaled).astype(BF))

    zwide[0:3, 8:72] = jnp.where(has_up > 0, zeta(top[0:3], 0, 3, 8, 72), 0.0)
    zwide[35:38, 8:72] = jnp.where(has_down > 0, zeta(bottom[0:3], 35, 3, 8, 72), 0.0)
    cots[0:2, 0:64] = jnp.where(has_up > 0, up(top[3:5]), 0.0)
    cots[34:36, 0:64] = jnp.where(has_down > 0, up(bottom[3:5]), 0.0)
    edge = jnp.where(row_ok & (has_left > 0), zeta(left[:, 0:3], 0, 38, 5, 8), 0.0)
    zwide[:, 5:8] = edge
    zwide[:, 85:88] = edge
    edge = jnp.where(row_ok & (has_right > 0), zeta(right[:, 0:3], 0, 38, 72, 75), 0.0)
    zwide[:, 72:75] = edge
    cots[:, 78:80] = jnp.where(row_ok[1:37] & (has_left > 0), up(left[1:37, 3:5]), 0.0)
    cots[:, 64:66] = jnp.where(row_ok[1:37] & (has_right > 0), up(right[1:37, 3:5]), 0.0)
    for at in range(0, 32, 4):
        zwide[at + 3 : at + 7, 8:72] = zeta(pair[at : at + 4], at + 3, 4, 8, 72)
        cots[at + 2 : at + 6, 0:64] = up(cot[at : at + 4])
    zwide[:, 88:89] = zwide[:, 8:9]
    for at in range(0, 38, 2):
        for across in range(3):
            z3[at : at + 2, :, across * chans : (across + 1) * chans] = zwide[
                at : at + 2, 7 + across : 87 + across
            ].astype(BF)

    qwide[:, 0:8] = jnp.zeros((36, 8, chans), F32)
    qwide[:, 88:96] = jnp.zeros((36, 8, chans), F32)
    for at in range(0, 36, 6):
        taps = jnp.concatenate([z3[at + d : at + d + 6].reshape(6 * WIDE, 3 * chans) for d in range(3)], axis=1)
        hidden = jnp.dot(taps, weight[...], preferred_element_type=F32).reshape(6, WIDE, chans)
        sigma = jax.nn.sigmoid(hidden)
        grown = hidden * sigma
        q = cots[at : at + 6] * (sigma + grown * (1.0 - sigma))
        qwide[at : at + 6, 8:88] = up(q.astype(BF))
        lo, hi = max(at, 2), min(at + 6, 34)
        out[lo - 2 : hi - 2] = (
            zwide[lo + 1 : hi + 1, 8:72] + grown[lo - at : hi - at, 0:64]
        ).astype(BF)
    qwide[:, 7:8] = qwide[:, 87:88]
    qwide[:, 88:89] = qwide[:, 8:9]
    for at in range(0, 36, 2):
        for across in range(3):
            q3[at : at + 2, :, across * chans : (across + 1) * chans] = qwide[
                at : at + 2, 9 - across : 89 - across
            ].astype(BF)

    own = q3[2:34, 0:64, chans : 2 * chans].reshape(2048, chans)
    for down in range(3):
        near = z3[down + 2 : down + 34, 0:64].reshape(2048, 3 * chans)
        part = lax.dot_general(own, near, (((0,), (0,)), ((), ())), preferred_element_type=F32)
        for across in range(3):
            at = (3 * down + across) * chans
            wgrad[at : at + chans] = part[:, across * chans : (across + 1) * chans].T

    total = jnp.zeros((WIDE, chans), F32)
    rowg[...] = jnp.zeros((40, chans), BF)
    for at in range(0, 34, 6):
        count = min(6, 34 - at)
        taps = jnp.concatenate(
            [q3[at + 2 - d : at + 2 - d + count].reshape(count * WIDE, 3 * chans) for d in range(3)], axis=1
        )
        zgrad = jnp.dot(taps, turned[...], preferred_element_type=F32).reshape(count, WIDE, chans)
        zgrad = zgrad + cots[at + 1 : at + 1 + count]
        rowg[at : at + count] = jnp.sum(zgrad[:, 0:64] * colp[8:72][None], axis=1).astype(BF)
        for i in range(count):
            if 1 <= at + i < 33:
                total = total + zgrad[i] * rowp[at + i + 2 : at + i + 3]
    rowg[0:1] = jnp.where(has_up > 0, rowg[0:1], 0.0)
    rowg[33:34] = jnp.where(has_down > 0, rowg[33:34], 0.0)
    line[0:1] = jnp.where(has_left > 0, total[79:80], 0.0)
    line[1:65] = total[0:64]
    line[65:66] = jnp.where(has_right > 0, total[64:65], 0.0)
    keep[576:616] = jnp.zeros((40, chans), F32)
    send[576:616] = jnp.zeros((40, chans), BF)
    for mine in range(2):

        @pl.when(core == mine)
        def _(mine=mine):
            keep[0:576] = wgrad[576 * mine : 576 * mine + 576]
            send[0:576] = wgrad[576 - 576 * mine : 1152 - 576 * mine].astype(BF)
            keep[576:610] = line[32 * mine : 32 * mine + 34]
            send[576:610] = line[32 - 32 * mine : 66 - 32 * mine].astype(BF)


def pair_block(flags, pair, cot, top, bottom, left, right, rowp, colp, weight, turned):
    chans = 128
    vmem = pl.BlockSpec(memory_space=pltpu.VMEM)
    return pl.pallas_call(
        pair_kernel,
        out_shape=(
            jax.ShapeDtypeStruct((32, 64, chans), BF),
            jax.ShapeDtypeStruct((KEPT, chans), F32),
            jax.ShapeDtypeStruct((KEPT, chans), BF),
            jax.ShapeDtypeStruct((40, chans), BF),
        ),
        in_specs=[pl.BlockSpec(memory_space=pltpu.SMEM)] + [vmem] * 10,
        out_specs=(vmem,) * 4,
        scratch_shapes=[
            pltpu.VMEM((38, 96, chans), F32),
            pltpu.VMEM((38, WIDE, 3 * chans), BF),
            pltpu.VMEM((36, WIDE, chans), F32),
            pltpu.VMEM((36, 96, chans), F32),
            pltpu.VMEM((36, WIDE, 3 * chans), BF),
            pltpu.VMEM((9 * chans, chans), F32),
            pltpu.VMEM((72, chans), F32),
        ],
        compiler_params=pltpu.CompilerParams(vmem_limit_bytes=40 * 1024 * 1024),
        cost_estimate=pl.CostEstimate(flops=2500000000, bytes_accessed=4000000, transcendentals=700000),
    )(flags, pair, cot, top, bottom, left, right, rowp, colp, weight, turned)


def local(fine, conv_w, proj_a, proj_b, pair_in, pair_w, cotangent):
    chans, outchans, pairs = fine.shape[2], conv_w.shape[1], pair_in.shape[3]
    row, col = lax.axis_index("row"), lax.axis_index("col")
    core, zpos = row % 2, row // 2
    first, last = row == 0, row == 15
    row_bins = 32 * row - 3 + jnp.arange(38)
    row_ok = (row_bins >= 0) & (row_bins < 512)
    flags = jnp.stack([row > 0, row < 15, col > 0, col < 7, core > 0]).astype(jnp.int32)

    fine, pair, cot = fine[0], pair_in[0], cotangent[0]
    before = shift(fine[-8:], "row", 1)
    after = shift(fine[:8], "row", -1)
    top = shift(jnp.concatenate([pair[29:], cot[30:]]), "row", 1)
    bottom = shift(jnp.concatenate([pair[:3], cot[:2]]), "row", -1)
    grouped = jnp.concatenate(
        [jnp.where(first, 0, before), fine, jnp.where(last, 0, after)]
    ).reshape(40, 2, chans)
    seq = 0.0
    for tap in range(5):
        seq = seq + lax.dot_general(
            grouped[tap // 2 : tap // 2 + 38, tap % 2],
            conv_w[tap],
            (((1,), (1,)), ((), ())),
            preferred_element_type=F32,
        )
    seq = jnp.where(row_ok[:, None], seq, 0.0).astype(BF)
    proj = jnp.concatenate([proj_a, proj_b], axis=1)
    part = jnp.dot(seq, proj, preferred_element_type=F32).astype(BF)
    part = jnp.concatenate([part, jnp.zeros((2, 2 * pairs), BF)])

    tall_pair = jnp.concatenate([top[:3], pair, bottom[:3]])
    tall_cot = jnp.concatenate([top[2:], cot, bottom[3:], bottom[4:]])
    left = shift(jnp.concatenate([tall_pair[:, 61:], tall_cot[:, 62:], tall_cot[:, :3]], axis=1), "col", 1)
    right = shift(jnp.concatenate([tall_pair[:, :3], tall_cot[:, :5]], axis=1), "col", -1)

    both = up(sum_flip(sum_y(part), "col", 1))
    rowp, colp_here = both[:, :pairs], both[:, pairs:].astype(BF)

    mine = jnp.where(core == 0, colp_here[:35], colp_here[3:38])
    other = flip(mine, "row", 1)
    colp = jnp.concatenate([jnp.where(core == 0, mine, other), jnp.where(core == 0, other, mine)])
    apart = zpos ^ col
    colp = jnp.where((apart & 4) == 4, flip(colp, "row", 8), colp)
    near = [flip(colp, "row", 2 * k) for k in (1, 2, 3)]
    for k in (1, 2, 3):
        colp = jnp.where((apart & 3) == k, near[k - 1], colp)
    blank = jnp.zeros((10, pairs), BF)
    colp = up(jnp.concatenate([blank[:5], colp[:3], colp[3:], blank, colp[:3], colp[3:4], blank[:7]]))

    weight = pair_w.reshape(9 * pairs, pairs)
    turned = jnp.swapaxes(pair_w, 2, 3).reshape(9 * pairs, pairs)
    out, keep, send, rowg = pair_block(
        flags, pair, cot, top, bottom, left, right, rowp, colp, weight, turned
    )

    total = (keep + up(flip(send, "row", 1))).astype(BF)
    half, colg = total[:576].reshape(4, 144, pairs), total[576:]

    def quarter(k):
        return lax.dynamic_index_in_dim(half, (zpos ^ k) & 3, 0, keepdims=False)

    def joined(k):
        return jnp.concatenate([quarter(k), colg])

    got = [flip(joined(k), "row", 2 * k) for k in (1, 2, 3)]
    total = ((up(joined(0)) + up(got[0])) + (up(got[1]) + up(got[2]))).astype(BF)
    total = sum_flip(total, "row", 8)
    colg = jnp.where(zpos == col, total[144:], 0)
    total = sum_y(jnp.concatenate([total[:144], rowg, colg]))
    across, left, right = flip(total, "col", 1), ring(total[:144], 1), ring(total[:144], 3)
    total = up(total) + up(across)
    sums = total[144:].astype(BF)
    quart = (total[:144] + (up(left) + up(right))).astype(BF)

    near = jnp.stack([quart] + [flip(quart, "row", 2 * k) for k in (1, 2, 3)])
    half = jnp.concatenate([lax.dynamic_index_in_dim(near, (zpos ^ k) & 3, 0, keepdims=False) for k in range(4)])
    theirs = flip(half, "row", 1)
    grad_pair_w = jnp.concatenate([jnp.where(core == 0, half, theirs), jnp.where(core == 0, theirs, half)])
    grad_pair_w = up(grad_pair_w).reshape(3, 3, pairs, pairs) / 512.0

    sums = jnp.concatenate([sums[:34], sums[40:74]], axis=1)
    seqg = lax.dot_general(sums, proj, (((1,), (1,)), ((), ())), preferred_element_type=F32).astype(BF)
    taps = [jnp.dot(seqg, conv_w[tap], preferred_element_type=F32) for tap in range(5)]
    even = taps[0][2:] + taps[2][1:33] + taps[4][:32]
    odd = taps[1][2:] + taps[3][1:33]
    parts = jnp.stack((even, odd), axis=1).astype(BF).reshape(64, 8, outchans)
    parts = lax.all_to_all(parts.transpose(1, 0, 2), "col", 0, 0, tiled=True)
    grad_fine = jnp.sum(up(parts), axis=0).astype(BF)
    return out[None], grad_fine[None], grad_pair_w


def solution(mesh):
    return jax.shard_map(
        local,
        mesh=mesh,
        in_specs=(
            P("batch", "row", None),
            P(None, "col", None),
            P("col", None),
            P("col", None),
            P("batch", "row", "col", None),
            P(),
            P("batch", "row", "col", None),
        ),
        out_specs=(P("batch", "row", "col", None), P("batch", "row", "col"), P()),
        check_vma=False,
    )
```

time: 157 us -> 123 us (0.78)
  waiting for transfers between devices: 51.9 us -> 36.8 us
  local copies, waits for them, and re-layouts: 16.5 us -> 6.82 us
  other arithmetic: 12.5 us -> 3.05 us
  Pallas kernels: 0 us -> 6.4 us
  starting transfers between devices: 63.1 us -> 57.7 us
    ppermute x16, waiting for transfers between devices: 34.7 us -> 20.1 us  [flip(): return lax.ppermute(x, axis, [(i, i ^ bit) for i in range(count)])]
    pallas_call x0 -> x1, Pallas kernels: none -> 6.4 us  [pair_block(): pl.pallas_call(pair_kernel, out_shape=(jax.ShapeDtypeStruct((32, 64, chan...]
    dot_general x9 -> x0, matrix products: 6.16 us -> none  [the longest x3 2.2 us: pair_block(): jnp.dot(z3[down:down + 36].reshape(-1, 3 * chans), pair_w[down].reshape(3...]
    dot_general x5, matrix products: 0.99 us -> 6.42 us  [local(): jnp.dot(seqg, conv_w[tap], preferred_element_type=F32)]
    ppermute x16, starting transfers between devices: 29.4 us -> 24.2 us  [flip(): return lax.ppermute(x, axis, [(i, i ^ bit) for i in range(count)])]
    ppermute x15 -> x12, waiting for transfers between devices: 10.8 us -> 6.37 us  [shift(): lax.ppermute(x, axis, [(i, (i + step) % count) for i in range(count)])]
    slice x29 -> x15, local copies, waits for them, and re-layouts: 6.84 us -> 2.43 us  [the longest x2 1.61 us: local(): bottom = shift(jnp.concatenate([pair[:3], cot[:2]]), 'row', -1)]
    convert_element_type x7 -> x3, other arithmetic: 4.44 us -> 0.06 us  [the longest x1 0.03 us: local(): total = (up(joined(0)) + up(got[0]) + (up(got[1]) + up(got[2]))).astype(BF)]
  transfers between devices with their start and end apart: 34 -> 31, of which waited for: 20 -> 15; matrix products, arithmetic and copies ran while one was open for 15% -> 10% of each run, Pallas kernels for 0% -> 0%
where the time goes in v2:
time: 123 us
  starting transfers between devices  57.7 us (47%)
  waiting for transfers between devices  36.8 us (30%)
  matrix products  10.6 us (9%)
  local copies, waits for them, and re-layouts  6.82 us (6%)
  Pallas kernels  6.4 us (5%)
  other arithmetic  3.05 us (2%)
    ppermute x16, starting transfers between devices, flip(): return lax.ppermute(x, axis, [(i, i ^ bit) for i in range(count)])  24.2 us
    ppermute x12, starting transfers between devices, shift(): lax.ppermute(x, axis, [(i, (i + step) % count) for i in range(count)])  23.8 us
    ppermute x16, waiting for transfers between devices, flip(): return lax.ppermute(x, axis, [(i, i ^ bit) for i in range(count)])  20.1 us
    all_to_all x1, waiting for transfers between devices, local(): parts = lax.all_to_all(parts.transpose(1, 0, 2), 'col', 0, 0, tiled=True)  8.58 us
    all_to_all x1, starting transfers between devices, local(): parts = lax.all_to_all(parts.transpose(1, 0, 2), 'col', 0, 0, tiled=True)  7.69 us
    dot_general x5, matrix products, local(): jnp.dot(seqg, conv_w[tap], preferred_element_type=F32)  6.42 us
    pallas_call x1, Pallas kernels, pair_block(): pl.pallas_call(pair_kernel, out_shape=(jax.ShapeDtypeStruct((32, 64, chan...  6.4 us
    ppermute x12, waiting for transfers between devices, shift(): lax.ppermute(x, axis, [(i, (i + step) % count) for i in range(count)])  6.37 us
  transfers between devices with their start and end apart: 31, of which 15 were waited for; matrix products, arithmetic and copies ran while one was open for 10% of the time, Pallas kernels for 0%

profile of v2, /device:TPU:2, one launch (start us, length us, event | category | flops | bytes accessed | tf_op | source)
XLA Modules:
  0.0 122.5 jit_solution(5956526895170934325)
XLA Ops:
  0.6 0.8 slice_bitcast_fusion.5
  1.4 5.3 %collective-permute-start.5 = (bf16[8,1536]{1,0:T(8,128)(2,1)S(1)}, bf16[8,1536]{1,0:T(8,128)(2,1)S(1)}, u32[]{:S(2)}, u32[]{:S(2)}) collective-permute-start(bf16[8,1536]{1,0:T(8,128)(2,1)S(1)} %get-tuple-element.25), channel_id=1, source_target_pairs={{0,240},{16,0},{32,16},{48,32},{64,48},{80,64},{96,80},{112,96},{1... | collective-permute-start | bytes 73736 | tf_op jit(solution)/shard_map/ppermute | solution.py:16
  6.7 0.8 constant_dynamic-update-slice_fusion.1
  7.5 0.8 slice_bitcast_fusion
  8.3 0.8 slice_bitcast_fusion.2
  9.1 0.8 constant_dynamic-update-slice_fusion
  10.0 1.2 collective-permute-done.4
  11.2 0.9 pad_maximum_fusion
  12.2 0.6 fusion.69
  12.9 1.6 %fusion.18 = f32[38,192]{1,0:T(8,128)S(1)} fusion(bf16[5,192,1536]{2,1,0:T(8,128)(2,1)} %param.8, bf16[38,1,1536]{2,1,0:T(2,128)(2,1)S(1)} %get-tuple-element.23), kind=kOutput, calls=%fused_computation.26 | convolution fusion | flops 22413312 | bytes 735744 | tf_op jit(solution)/shard_map/dot_general | solution.py:186
  14.5 0.3 convolution_add_fusion.6
  14.8 0.3 convolution_add_fusion.5
  15.1 0.3 convolution_add_fusion.4
  15.4 1.5 %convolution_convert_fusion.1 = bf16[38,256]{1,0:T(8,128)(2,1)S(1)} fusion(bf16[192,256]{1,0:T(8,128)(2,1)S(1)} %constant_dynamic-update-slice_fusion, f32[38,192]{1,0:T(8,128)S(1)} %convolution_add_fusion.4, bf16[5,192,1536]{2,1,0:T(8,128)(2,1)} %param.8, bf16[38,1,1536]{2,1,0:T(2,128)(2,1)S(1)} %get-tuple-element.19, pred[38]{0:T(512)(128)(4,1)S(1)} %compare_and_fusion), kind=kOutput, calls=%fused_computation.14 | convolution fusion | flops 26180480 | bytes 853542 | tf_op jit(solution)/shard_map/dot_general | solution.py:194
  16.9 3.3 %collective-permute-start.6 = (bf16[40,256]{1,0:T(8,128)(2,1)S(1)}, bf16[40,256]{1,0:T(8,128)(2,1)S(1)}, u32[]{:S(2)}, u32[]{:S(2)}) collective-permute-start(bf16[40,256]{1,0:T(8,128)(2,1)S(1)} %concatenate.66), channel_id=1, source_target_pairs={{0,8},{2,10},{4,12},{6,14},{8,0},{10,2},{12,4},{14,6},{1,9},{3,11}... | collective-permute-start | bytes 61448 | tf_op jit(solution)/shard_map/ppermute | solution.py:16
  20.2 0.7 collective-permute-start.7
  20.9 2.6 %collective-permute-start.8 = (bf16[40,256]{1,0:T(8,128)(2,1)S(1)}, bf16[40,256]{1,0:T(8,128)(2,1)S(1)}, u32[]{:S(2)}, u32[]{:S(2)}) collective-permute-start(bf16[40,256]{1,0:T(8,128)(2,1)S(1)} %concatenate.66), channel_id=1, source_target_pairs={{0,12},{2,14},{4,0},{6,2},{8,4},{10,6},{12,8},{14,10},{1,13},{3,15... | collective-permute-start | bytes 61448 | tf_op jit(solution)/shard_map/ppermute | solution.py:16
  23.5 1.0 collective-permute-start.1
  24.4 0.8 collective-permute-done.7
  25.2 2.2 %collective-permute-start.9 = (bf16[40,256]{1,0:T(8,128)(2,1)S(1)}, bf16[40,256]{1,0:T(8,128)(2,1)S(1)}, u32[]{:S(2)}, u32[]{:S(2)}) collective-permute-start(bf16[40,256]{1,0:T(8,128)(2,1)S(1)} %add_convert_fusion.5), channel_id=1, source_target_pairs={{0,2},{2,0},{4,6},{6,4},{8,10},{10,8},{12,14},{14,12},{1,3},{3,1},... | collective-permute-start | bytes 61448 | tf_op jit(solution)/shard_map/ppermute | solution.py:21
  27.6 0.2 copy.15
  27.8 2.7 %collective-permute-done.9 = bf16[40,256]{1,0:T(8,128)(2,1)S(1)} collective-permute-done((bf16[40,256]{1,0:T(8,128)(2,1)S(1)}, bf16[40,256]{1,0:T(8,128)(2,1)S(1)}, u32[]{:S(2)}, u32[]{:S(2)}) %collective-permute-start.9) | collective-permute-done | bytes 20512 | tf_op jit(solution)/shard_map/ppermute | solution.py:21
  30.7 1.1 collective-permute-done.10
  31.9 2.0 %collective-permute-start.11 = (bf16[70,128]{1,0:T(8,128)(2,1)S(1)}, bf16[70,128]{1,0:T(8,128)(2,1)S(1)}, u32[]{:S(2)}, u32[]{:S(2)}) collective-permute-start(bf16[70,128]{1,0:T(8,128)(2,1)S(1)} %pad_maximum_fusion.19), channel_id=1, source_target_pairs={{0,128},{16,144},{32,160},{48,176},{64,192},{80,208},{96,224},{112... | collective-permute-start | bytes 53768 | tf_op jit(solution)/shard_map/ppermute | solution.py:21
  34.0 5.7 %collective-permute-done.11 = bf16[70,128]{1,0:T(8,128)(2,1)S(1)} collective-permute-done((bf16[70,128]{1,0:T(8,128)(2,1)S(1)}, bf16[70,128]{1,0:T(8,128)(2,1)S(1)}, u32[]{:S(2)}, u32[]{:S(2)}) %collective-permute-start.11) | collective-permute-done | bytes 17952 | tf_op jit(solution)/shard_map/ppermute | solution.py:21
  39.9 4.3 %collective-permute-start.14 = (bf16[70,128]{1,0:T(8,128)(2,1)S(1)}, bf16[70,128]{1,0:T(8,128)(2,1)S(1)}, u32[]{:S(2)}, u32[]{:S(2)}) collective-permute-start(bf16[70,128]{1,0:T(8,128)(2,1)S(1)} %broadcast_select_fusion.4), channel_id=1, source_target_pairs={{0,32},{16,48},{32,0},{48,16},{64,96},{80,112},{96,64},{112,80},{1... | collective-permute-start | bytes 53768 | tf_op jit(solution)/shard_map/ppermute | solution.py:21
  44.3 2.2 %collective-permute-start.2 = (bf16[38,8,128]{2,1,0:T(8,128)(2,1)S(1)}, bf16[38,8,128]{2,1,0:T(8,128)(2,1)S(1)}, u32[]{:S(2)}, u32[]{:S(2)}) collective-permute-start(bf16[38,8,128]{2,1,0:T(8,128)(2,1)S(1)} %get-tuple-element.12), channel_id=1, source_target_pairs={{0,2},{2,4},{4,6},{6,8},{8,10},{10,12},{12,14},{14,0},{1,3},{3,5},... | collective-permute-start | bytes 233480 | tf_op jit(solution)/shard_map/ppermute | solution.py:16
  46.5 3.5 %collective-permute-start.3 = (bf16[38,8,128]{2,1,0:T(8,128)(2,1)S(1)}, bf16[38,8,128]{2,1,0:T(8,128)(2,1)S(1)}, u32[]{:S(2)}, u32[]{:S(2)}) collective-permute-start(bf16[38,8,128]{2,1,0:T(8,128)(2,1)S(1)} %get-tuple-element.11), channel_id=1, source_target_pairs={{0,14},{2,0},{4,2},{6,4},{8,6},{10,8},{12,10},{14,12},{1,15},{3,1}... | collective-permute-start | bytes 233480 | tf_op jit(solution)/shard_map/ppermute | solution.py:16
  50.1 0.4 concatenate.68
  50.6 2.3 %collective-permute-done.2.left = bf16[38,8,128]{2,1,0:T(8,128)(2,1)S(1)} collective-permute-done((bf16[38,8,128]{2,1,0:T(8,128)(2,1)S(1)}, bf16[38,8,128]{2,1,0:T(8,128)(2,1)S(1)}, u32[]{:S(2)}, u32[]{:S(2)}) %collective-permute-start.2) | collective-permute-done | bytes 77856 | tf_op jit(solution)/shard_map/ppermute | solution.py:16
  52.8 6.4 %shard_map.94 = (bf16[32,64,128]{2,1,0:T(8,128)(2,1)}, f32[616,128]{1,0:T(8,128)S(1)}, bf16[616,128]{1,0:T(8,128)(2,1)S(1)}, bf16[40,128]{1,0:T(8,128)(2,1)S(1)}) custom-call(s32[5]{0:T(128)S(1)} %convert_element_type.119.flags, bf16[32,64,128]{2,1,0:T(8,128)(2,1)S(1)} %bitcast.97, bf16[32,64,128]{2,1,0:T(8,128)(2,1)S(1)} %bitcast.99, ...), custom_call_target="tpu_custom_call" | custom-call | flops 2500000000 | bytes 4000000 | tf_op jit(solution)/shard_map/pallas_call | solution.py:143
  59.2 1.4 %collective-permute-done.15 = bf16[616,128]{1,0:T(8,128)(2,1)S(1)} collective-permute-done((bf16[616,128]{1,0:T(8,128)(2,1)S(1)}, bf16[616,128]{1,0:T(8,128)(2,1)S(1)}, u32[]{:S(2)}, u32[]{:S(2)}) %collective-permute-start.15) | collective-permute-done | bytes 157728 | tf_op jit(solution)/shard_map/ppermute | solution.py:21
  60.7 0.4 collective-permute-start.16
  61.1 0.7 collective-permute-start.17
  61.8 3.4 %collective-permute-start.18 = (bf16[184,128]{1,0:T(8,128)(2,1)S(1)}, bf16[184,128]{1,0:T(8,128)(2,1)S(1)}, u32[]{:S(2)}, u32[]{:S(2)}) collective-permute-start(bf16[184,128]{1,0:T(8,128)(2,1)S(1)} %get-tuple-element.44), channel_id=1, source_target_pairs={{0,96},{16,112},{32,64},{48,80},{64,32},{80,48},{96,0},{112,16},{1... | collective-permute-start | bytes 141320 | tf_op jit(solution)/shard_map/ppermute | solution.py:21
  65.2 0.2 collective-permute-done.16
  65.4 2.7 %collective-permute-done.17 = bf16[184,128]{1,0:T(8,128)(2,1)S(1)} collective-permute-done((bf16[184,128]{1,0:T(8,128)(2,1)S(1)}, bf16[184,128]{1,0:T(8,128)(2,1)S(1)}, u32[]{:S(2)}, u32[]{:S(2)}) %collective-permute-start.17) | collective-permute-done | bytes 47136 | tf_op jit(solution)/shard_map/ppermute | solution.py:21
  68.1 2.5 %collective-permute-start.19 = (bf16[184,128]{1,0:T(8,128)(2,1)S(1)}, bf16[184,128]{1,0:T(8,128)(2,1)S(1)}, u32[]{:S(2)}, u32[]{:S(2)}) collective-permute-start(bf16[184,128]{1,0:T(8,128)(2,1)S(1)} %add_convert_fusion.3), channel_id=1, source_target_pairs={{0,128},{16,144},{32,160},{48,176},{64,192},{80,208},{96,224},{112... | collective-permute-start | bytes 141320 | tf_op jit(solution)/shard_map/ppermute | solution.py:21
  70.6 6.1 %collective-permute-done.19 = bf16[184,128]{1,0:T(8,128)(2,1)S(1)} collective-permute-done((bf16[184,128]{1,0:T(8,128)(2,1)S(1)}, bf16[184,128]{1,0:T(8,128)(2,1)S(1)}, u32[]{:S(2)}, u32[]{:S(2)}) %collective-permute-start.19) | collective-permute-done | bytes 47136 | tf_op jit(solution)/shard_map/ppermute | solution.py:21
  76.8 2.0 %collective-permute-start.20 = (bf16[224,128]{1,0:T(8,128)(2,1)S(1)}, bf16[224,128]{1,0:T(8,128)(2,1)S(1)}, u32[]{:S(2)}, u32[]{:S(2)}) collective-permute-start(bf16[224,128]{1,0:T(8,128)(2,1)S(1)} %pad_maximum_fusion.18), channel_id=1, source_target_pairs={{0,8},{2,10},{4,12},{6,14},{8,0},{10,2},{12,4},{14,6},{1,9},{3,11}... | collective-permute-start | bytes 172040 | tf_op jit(solution)/shard_map/ppermute | solution.py:16
  78.8 1.2 collective-permute-start.21
  80.0 2.0 %collective-permute-start.22 = (bf16[224,128]{1,0:T(8,128)(2,1)S(1)}, bf16[224,128]{1,0:T(8,128)(2,1)S(1)}, u32[]{:S(2)}, u32[]{:S(2)}) collective-permute-start(bf16[224,128]{1,0:T(8,128)(2,1)S(1)} %pad_maximum_fusion.18), channel_id=1, source_target_pairs={{0,12},{2,14},{4,0},{6,2},{8,4},{10,6},{12,8},{14,10},{1,13},{3,15... | collective-permute-start | bytes 172040 | tf_op jit(solution)/shard_map/ppermute | solution.py:16
  82.0 0.5 collective-permute-done.20
  82.5 1.7 %collective-permute-done.21 = bf16[224,128]{1,0:T(8,128)(2,1)S(1)} collective-permute-done((bf16[224,128]{1,0:T(8,128)(2,1)S(1)}, bf16[224,128]{1,0:T(8,128)(2,1)S(1)}, u32[]{:S(2)}, u32[]{:S(2)}) %collective-permute-start.21) | collective-permute-done | bytes 57376 | tf_op jit(solution)/shard_map/ppermute | solution.py:16
  84.2 3.7 %collective-permute-start.23 = (bf16[224,128]{1,0:T(8,128)(2,1)S(1)}, bf16[224,128]{1,0:T(8,128)(2,1)S(1)}, u32[]{:S(2)}, u32[]{:S(2)}) collective-permute-start(bf16[224,128]{1,0:T(8,128)(2,1)S(1)} %add_convert_fusion.1), channel_id=1, source_target_pairs={{0,2},{2,0},{4,6},{6,4},{8,10},{10,8},{12,14},{14,12},{1,3},{3,1},... | collective-permute-start | bytes 172040 | tf_op jit(solution)/shard_map/ppermute | solution.py:21
  87.9 2.0 %collective-permute-start.25 = (bf16[144,128]{1,0:T(8,128)(2,1)S(1)}, bf16[144,128]{1,0:T(8,128)(2,1)S(1)}, u32[]{:S(2)}, u32[]{:S(2)}) collective-permute-start(bf16[144,128]{1,0:T(8,128)(2,1)S(1)} %slice.255), channel_id=1, source_target_pairs={{0,3},{1,0},{2,1},{3,2},{4,7},{5,4},{6,5},{7,6},{8,11},{9,8},{10,9... | collective-permute-start | bytes 110600 | tf_op jit(solution)/shard_map/ppermute | solution.py:26
  89.9 0.1 collective-permute-done.23
  90.1 1.8 %collective-permute-done.24 = bf16[144,128]{1,0:T(8,128)(2,1)S(1)} collective-permute-done((bf16[144,128]{1,0:T(8,128)(2,1)S(1)}, bf16[144,128]{1,0:T(8,128)(2,1)S(1)}, u32[]{:S(2)}, u32[]{:S(2)}) %collective-permute-start.24) | collective-permute-done | bytes 36896 | tf_op jit(solution)/shard_map/ppermute | solution.py:26
  91.9 1.3 %collective-permute-start.26 = (bf16[144,128]{1,0:T(8,128)(2,1)S(1)}, bf16[144,128]{1,0:T(8,128)(2,1)S(1)}, u32[]{:S(2)}, u32[]{:S(2)}) collective-permute-start(bf16[144,128]{1,0:T(8,128)(2,1)S(1)} %fusion.55), channel_id=1, source_target_pairs={{0,32},{16,48},{32,0},{48,16},{64,96},{80,112},{96,64},{112,80},{1... | collective-permute-start | bytes 110600 | tf_op jit(solution)/shard_map/ppermute | solution.py:21
  93.2 2.5 %collective-permute-start.27 = (bf16[144,128]{1,0:T(8,128)(2,1)S(1)}, bf16[144,128]{1,0:T(8,128)(2,1)S(1)}, u32[]{:S(2)}, u32[]{:S(2)}) collective-permute-start(bf16[144,128]{1,0:T(8,128)(2,1)S(1)} %fusion.55), channel_id=1, source_target_pairs={{0,64},{16,80},{32,96},{48,112},{64,0},{80,16},{96,32},{112,48},{1... | collective-permute-start | bytes 110600 | tf_op jit(solution)/shard_map/ppermute | solution.py:21
  95.7 0.9 collective-permute-start.28
  96.6 0.1 convolution_convert_fusion
  96.7 1.3 %fusion.16 = f32[32,1536]{1,0:T(8,128)S(1)} fusion(bf16[5,192,1536]{2,1,0:T(8,128)(2,1)} %param.8, bf16[34,192]{1,0:T(8,128)(2,1)S(1)} %convolution_convert_fusion), kind=kOutput, calls=%fused_computation.24 | convolution fusion | flops 18874368 | bytes 802816 | tf_op jit(solution)/shard_map/dot_general | solution.py:249
  98.0 1.3 %fusion.13 = f32[32,1536]{1,0:T(8,128)S(1)} fusion(bf16[5,192,1536]{2,1,0:T(8,128)(2,1)} %param.8, bf16[34,192]{1,0:T(8,128)(2,1)S(1)} %convolution_convert_fusion), kind=kOutput, calls=%fused_computation.21 | convolution fusion | flops 18874368 | bytes 802816 | tf_op jit(solution)/shard_map/dot_general | solution.py:249
  99.3 1.3 %convolution_add_fusion.2 = f32[32,1536]{1,0:T(8,128)S(1)} fusion(f32[32,1536]{1,0:T(8,128)S(1)} %fusion.16, bf16[5,192,1536]{2,1,0:T(8,128)(2,1)} %param.8, bf16[34,192]{1,0:T(8,128)(2,1)S(1)} %convolution_convert_fusion), kind=kOutput, calls=%fused_computation.2 | convolution fusion | flops 18923520 | bytes 999424 | tf_op jit(solution)/shard_map/dot_general | solution.py:249
  100.6 1.3 %fusion.3 = bf16[32,1,1536]{2,0,1:T(8,128)(2,1)S(1)} fusion(f32[32,1536]{1,0:T(8,128)S(1)} %convolution_add_fusion.2, bf16[5,192,1536]{2,1,0:T(8,128)(2,1)} %param.8, bf16[34,192]{1,0:T(8,128)(2,1)S(1)} %convolution_convert_fusion), kind=kOutput, calls=%fused_computation.6 | convolution fusion | flops 18972672 | bytes 901120 | tf_op jit(solution)/shard_map/dot_general | solution.py:249
  101.9 1.3 %fusion.2 = bf16[32,1,1536]{2,0,1:T(8,128)(2,1)S(1)} fusion(f32[32,1536]{1,0:T(8,128)S(1)} %fusion.13, bf16[5,192,1536]{2,1,0:T(8,128)(2,1)} %param.8, bf16[34,192]{1,0:T(8,128)(2,1)S(1)} %convolution_convert_fusion), kind=kOutput, calls=%fused_computation.5 | convolution fusion | flops 18972672 | bytes 901120 | tf_op jit(solution)/shard_map/dot_general | solution.py:249
  103.2 0.2 copy.16
  103.4 0.3 convert_element_type.149
  103.7 0.8 copy.17
  104.4 7.7 %all-to-all-start = ((bf16[8,64,192]{2,1,0:T(8,128)(2,1)}), bf16[8,64,192]{2,1,0:T(8,128)(2,1)S(1)}, u32[]{:S(2)}, u32[]{:S(2)}) async-start(bf16[8,64,192]{2,1,0:T(8,128)(2,1)} %copy.17), calls=%async_computation | async-start | bytes 524288 | tf_op jit(solution)/shard_map/all_to_all | solution.py:253
  112.4 8.6 %all-to-all-done = bf16[8,64,192]{2,1,0:T(8,128)(2,1)S(1)} async-done(((bf16[8,64,192]{2,1,0:T(8,128)(2,1)}), bf16[8,64,192]{2,1,0:T(8,128)(2,1)S(1)}, u32[]{:S(2)}, u32[]{:S(2)}) %all-to-all-start) | async-done | bytes 196640 | tf_op jit(solution)/shard_map/all_to_all | solution.py:253
  120.9 0.7 reduce_sum.12
  121.7 0.9 convert_multiply_fusion
  (79 shorter events, 1.4 us)
Async XLA Ops:
  1.4 8.6 %collective-permute-start.5 = (bf16[8,1536]{1,0:T(8,128)(2,1)S(1)}, bf16[8,1536]{1,0:T(8,128)(2,1)S(1)}, u32[]{:S(2)}, u32[]{:S(2)}) collective-permute-start(bf16[8,1536]{1,0:T(8,128)(2,1)S(1)} %get-tuple-element.25), channel_id=1, source_target_pairs={{0,240},{16,0},{32,16},{48,32},{64,48},{80,64},{96,80},{112,96},{1... | collective-permute-start | bytes 73736 | tf_op jit(solution)/shard_map/ppermute | solution.py:16
  6.7 4.5 %collective-permute-start.4 = (bf16[8,1536]{1,0:T(8,128)(2,1)S(1)}, bf16[8,1536]{1,0:T(8,128)(2,1)S(1)}, u32[]{:S(2)}, u32[]{:S(2)}) collective-permute-start(bf16[8,1536]{1,0:T(8,128)(2,1)S(1)} %get-tuple-element.24), channel_id=1, source_target_pairs={{0,16},{16,32},{32,48},{48,64},{64,80},{80,96},{96,112},{112,128},... | collective-permute-start | bytes 73736 | tf_op jit(solution)/shard_map/ppermute | solution.py:16
  12.2 2.3 %copy-start.3 = (bf16[5,192,1536]{2,1,0:T(8,128)(2,1)S(1)}, bf16[5,192,1536]{2,1,0:T(8,128)(2,1)}, u32[]{:S(2)}) copy-start(bf16[5,192,1536]{2,1,0:T(8,128)(2,1)} %param.8) | copy-start | bytes 8847364
  12.8 14.8 %copy-start.2 = (bf16[3,3,128,128]{3,2,1,0:T(8,128)(2,1)S(1)}, bf16[3,3,128,128]{3,2,1,0:T(8,128)(2,1)}, u32[]{:S(2)}) copy-start(bf16[3,3,128,128]{3,2,1,0:T(8,128)(2,1)} %param.12) | copy-start | bytes 884740
  12.8 31.3 %copy-start = (bf16[1,32,64,128]{3,2,1,0:T(8,128)(2,1)S(1)}, bf16[1,32,64,128]{3,2,1,0:T(8,128)(2,1)}, u32[]{:S(2)}) copy-start(bf16[1,32,64,128]{3,2,1,0:T(8,128)(2,1)} %param.11) | copy-start | bytes 1572868
  12.9 31.3 %copy-start.1 = (bf16[1,32,64,128]{3,2,1,0:T(8,128)(2,1)S(1)}, bf16[1,32,64,128]{3,2,1,0:T(8,128)(2,1)}, u32[]{:S(2)}) copy-start(bf16[1,32,64,128]{3,2,1,0:T(8,128)(2,1)} %param.13) | copy-start | bytes 1572868
  16.9 7.5 %collective-permute-start.6 = (bf16[40,256]{1,0:T(8,128)(2,1)S(1)}, bf16[40,256]{1,0:T(8,128)(2,1)S(1)}, u32[]{:S(2)}, u32[]{:S(2)}) collective-permute-start(bf16[40,256]{1,0:T(8,128)(2,1)S(1)} %concatenate.66), channel_id=1, source_target_pairs={{0,8},{2,10},{4,12},{6,14},{8,0},{10,2},{12,4},{14,6},{1,9},{3,11}... | collective-permute-start | bytes 61448 | tf_op jit(solution)/shard_map/ppermute | solution.py:16
  20.2 5.0 %collective-permute-start.7 = (bf16[40,256]{1,0:T(8,128)(2,1)S(1)}, bf16[40,256]{1,0:T(8,128)(2,1)S(1)}, u32[]{:S(2)}, u32[]{:S(2)}) collective-permute-start(bf16[40,256]{1,0:T(8,128)(2,1)S(1)} %concatenate.66), channel_id=1, source_target_pairs={{0,4},{2,6},{4,8},{6,10},{8,12},{10,14},{12,0},{14,2},{1,5},{3,7},... | collective-permute-start | bytes 61448 | tf_op jit(solution)/shard_map/ppermute | solution.py:16
  20.9 4.3 %collective-permute-start.8 = (bf16[40,256]{1,0:T(8,128)(2,1)S(1)}, bf16[40,256]{1,0:T(8,128)(2,1)S(1)}, u32[]{:S(2)}, u32[]{:S(2)}) collective-permute-start(bf16[40,256]{1,0:T(8,128)(2,1)S(1)} %concatenate.66), channel_id=1, source_target_pairs={{0,12},{2,14},{4,0},{6,2},{8,4},{10,6},{12,8},{14,10},{1,13},{3,15... | collective-permute-start | bytes 61448 | tf_op jit(solution)/shard_map/ppermute | solution.py:16
  23.5 10.5 %collective-permute-start.1 = (bf16[5,64,128]{2,1,0:T(8,128)(2,1)S(1)}, bf16[5,64,128]{2,1,0:T(8,128)(2,1)S(1)}, u32[]{:S(2)}, u32[]{:S(2)}) collective-permute-start(bf16[5,64,128]{2,1,0:T(8,128)(2,1)S(1)} %pad_maximum_fusion.9), channel_id=1, source_target_pairs={{0,240},{16,0},{32,16},{48,32},{64,48},{80,64},{96,80},{112,96},{1... | collective-permute-start | bytes 245768 | tf_op jit(solution)/shard_map/ppermute | solution.py:16
  25.2 5.4 %collective-permute-start.9 = (bf16[40,256]{1,0:T(8,128)(2,1)S(1)}, bf16[40,256]{1,0:T(8,128)(2,1)S(1)}, u32[]{:S(2)}, u32[]{:S(2)}) collective-permute-start(bf16[40,256]{1,0:T(8,128)(2,1)S(1)} %add_convert_fusion.5), channel_id=1, source_target_pairs={{0,2},{2,0},{4,6},{6,4},{8,10},{10,8},{12,14},{14,12},{1,3},{3,1},... | collective-permute-start | bytes 61448 | tf_op jit(solution)/shard_map/ppermute | solution.py:21
  27.4 6.5 %collective-permute-start = (bf16[5,64,128]{2,1,0:T(8,128)(2,1)S(1)}, bf16[5,64,128]{2,1,0:T(8,128)(2,1)S(1)}, u32[]{:S(2)}, u32[]{:S(2)}) collective-permute-start(bf16[5,64,128]{2,1,0:T(8,128)(2,1)S(1)} %pad_maximum_fusion.8), channel_id=1, source_target_pairs={{0,16},{16,32},{32,48},{48,64},{64,80},{80,96},{96,112},{112,128},... | collective-permute-start | bytes 245768 | tf_op jit(solution)/shard_map/ppermute | solution.py:16
  30.6 1.3 %collective-permute-start.10 = (bf16[35,128]{1,0:T(8,128)(2,1)S(1)}, bf16[35,128]{1,0:T(8,128)(2,1)S(1)}, u32[]{:S(2)}, u32[]{:S(2)}) collective-permute-start(bf16[35,128]{1,0:T(8,128)(2,1)S(1)} %slice_select_fusion.1), channel_id=1, source_target_pairs={{0,16},{16,0},{32,48},{48,32},{64,80},{80,64},{96,112},{112,96},{1... | collective-permute-start | bytes 26888 | tf_op jit(solution)/shard_map/ppermute | solution.py:21
  31.9 7.8 %collective-permute-start.11 = (bf16[70,128]{1,0:T(8,128)(2,1)S(1)}, bf16[70,128]{1,0:T(8,128)(2,1)S(1)}, u32[]{:S(2)}, u32[]{:S(2)}) collective-permute-start(bf16[70,128]{1,0:T(8,128)(2,1)S(1)} %pad_maximum_fusion.19), channel_id=1, source_target_pairs={{0,128},{16,144},{32,160},{48,176},{64,192},{80,208},{96,224},{112... | collective-permute-start | bytes 53768 | tf_op jit(solution)/shard_map/ppermute | solution.py:21
  39.7 10.3 %collective-permute-start.12 = (bf16[70,128]{1,0:T(8,128)(2,1)S(1)}, bf16[70,128]{1,0:T(8,128)(2,1)S(1)}, u32[]{:S(2)}, u32[]{:S(2)}) collective-permute-start(bf16[70,128]{1,0:T(8,128)(2,1)S(1)} %broadcast_select_fusion.4), channel_id=1, source_target_pairs={{0,96},{16,112},{32,64},{48,80},{64,32},{80,48},{96,0},{112,16},{1... | collective-permute-start | bytes 53768 | tf_op jit(solution)/shard_map/ppermute | solution.py:21
  39.8 10.2 %collective-permute-start.13 = (bf16[70,128]{1,0:T(8,128)(2,1)S(1)}, bf16[70,128]{1,0:T(8,128)(2,1)S(1)}, u32[]{:S(2)}, u32[]{:S(2)}) collective-permute-start(bf16[70,128]{1,0:T(8,128)(2,1)S(1)} %broadcast_select_fusion.4), channel_id=1, source_target_pairs={{0,64},{16,80},{32,96},{48,112},{64,0},{80,16},{96,32},{112,48},{1... | collective-permute-start | bytes 53768 | tf_op jit(solution)/shard_map/ppermute | solution.py:21
  39.9 10.1 %collective-permute-start.14 = (bf16[70,128]{1,0:T(8,128)(2,1)S(1)}, bf16[70,128]{1,0:T(8,128)(2,1)S(1)}, u32[]{:S(2)}, u32[]{:S(2)}) collective-permute-start(bf16[70,128]{1,0:T(8,128)(2,1)S(1)} %broadcast_select_fusion.4), channel_id=1, source_target_pairs={{0,32},{16,48},{32,0},{48,16},{64,96},{80,112},{96,64},{112,80},{1... | collective-permute-start | bytes 53768 | tf_op jit(solution)/shard_map/ppermute | solution.py:21
  44.3 8.5 %collective-permute-start.2 = (bf16[38,8,128]{2,1,0:T(8,128)(2,1)S(1)}, bf16[38,8,128]{2,1,0:T(8,128)(2,1)S(1)}, u32[]{:S(2)}, u32[]{:S(2)}) collective-permute-start(bf16[38,8,128]{2,1,0:T(8,128)(2,1)S(1)} %get-tuple-element.12), channel_id=1, source_target_pairs={{0,2},{2,4},{4,6},{6,8},{8,10},{10,12},{12,14},{14,0},{1,3},{3,5},... | collective-permute-start | bytes 233480 | tf_op jit(solution)/shard_map/ppermute | solution.py:16
  46.5 6.3 %collective-permute-start.3 = (bf16[38,8,128]{2,1,0:T(8,128)(2,1)S(1)}, bf16[38,8,128]{2,1,0:T(8,128)(2,1)S(1)}, u32[]{:S(2)}, u32[]{:S(2)}) collective-permute-start(bf16[38,8,128]{2,1,0:T(8,128)(2,1)S(1)} %get-tuple-element.11), channel_id=1, source_target_pairs={{0,14},{2,0},{4,2},{6,4},{8,6},{10,8},{12,10},{14,12},{1,15},{3,1}... | collective-permute-start | bytes 233480 | tf_op jit(solution)/shard_map/ppermute | solution.py:16
  59.2 1.4 %collective-permute-start.15 = (bf16[616,128]{1,0:T(8,128)(2,1)S(1)}, bf16[616,128]{1,0:T(8,128)(2,1)S(1)}, u32[]{:S(2)}, u32[]{:S(2)}) collective-permute-start(bf16[616,128]{1,0:T(8,128)(2,1)S(1)} %get-tuple-element.9), channel_id=1, source_target_pairs={{0,16},{16,0},{32,48},{48,32},{64,80},{80,64},{96,112},{112,96},{1... | collective-permute-start | bytes 473096 | tf_op jit(solution)/shard_map/ppermute | solution.py:21
  60.7 4.7 %collective-permute-start.16 = (bf16[184,128]{1,0:T(8,128)(2,1)S(1)}, bf16[184,128]{1,0:T(8,128)(2,1)S(1)}, u32[]{:S(2)}, u32[]{:S(2)}) collective-permute-start(bf16[184,128]{1,0:T(8,128)(2,1)S(1)} %get-tuple-element.42), channel_id=1, source_target_pairs={{0,32},{16,48},{32,0},{48,16},{64,96},{80,112},{96,64},{112,80},{1... | collective-permute-start | bytes 141320 | tf_op jit(solution)/shard_map/ppermute | solution.py:21
  61.1 7.0 %collective-permute-start.17 = (bf16[184,128]{1,0:T(8,128)(2,1)S(1)}, bf16[184,128]{1,0:T(8,128)(2,1)S(1)}, u32[]{:S(2)}, u32[]{:S(2)}) collective-permute-start(bf16[184,128]{1,0:T(8,128)(2,1)S(1)} %get-tuple-element.43), channel_id=1, source_target_pairs={{0,64},{16,80},{32,96},{48,112},{64,0},{80,16},{96,32},{112,48},{1... | collective-permute-start | bytes 141320 | tf_op jit(solution)/shard_map/ppermute | solution.py:21
  61.8 6.3 %collective-permute-start.18 = (bf16[184,128]{1,0:T(8,128)(2,1)S(1)}, bf16[184,128]{1,0:T(8,128)(2,1)S(1)}, u32[]{:S(2)}, u32[]{:S(2)}) collective-permute-start(bf16[184,128]{1,0:T(8,128)(2,1)S(1)} %get-tuple-element.44), channel_id=1, source_target_pairs={{0,96},{16,112},{32,64},{48,80},{64,32},{80,48},{96,0},{112,16},{1... | collective-permute-start | bytes 141320 | tf_op jit(solution)/shard_map/ppermute | solution.py:21
  68.1 8.6 %collective-permute-start.19 = (bf16[184,128]{1,0:T(8,128)(2,1)S(1)}, bf16[184,128]{1,0:T(8,128)(2,1)S(1)}, u32[]{:S(2)}, u32[]{:S(2)}) collective-permute-start(bf16[184,128]{1,0:T(8,128)(2,1)S(1)} %add_convert_fusion.3), channel_id=1, source_target_pairs={{0,128},{16,144},{32,160},{48,176},{64,192},{80,208},{96,224},{112... | collective-permute-start | bytes 141320 | tf_op jit(solution)/shard_map/ppermute | solution.py:21
  76.8 5.8 %collective-permute-start.20 = (bf16[224,128]{1,0:T(8,128)(2,1)S(1)}, bf16[224,128]{1,0:T(8,128)(2,1)S(1)}, u32[]{:S(2)}, u32[]{:S(2)}) collective-permute-start(bf16[224,128]{1,0:T(8,128)(2,1)S(1)} %pad_maximum_fusion.18), channel_id=1, source_target_pairs={{0,8},{2,10},{4,12},{6,14},{8,0},{10,2},{12,4},{14,6},{1,9},{3,11}... | collective-permute-start | bytes 172040 | tf_op jit(solution)/shard_map/ppermute | solution.py:16
  78.8 5.4 %collective-permute-start.21 = (bf16[224,128]{1,0:T(8,128)(2,1)S(1)}, bf16[224,128]{1,0:T(8,128)(2,1)S(1)}, u32[]{:S(2)}, u32[]{:S(2)}) collective-permute-start(bf16[224,128]{1,0:T(8,128)(2,1)S(1)} %pad_maximum_fusion.18), channel_id=1, source_target_pairs={{0,4},{2,6},{4,8},{6,10},{8,12},{10,14},{12,0},{14,2},{1,5},{3,7},... | collective-permute-start | bytes 172040 | tf_op jit(solution)/shard_map/ppermute | solution.py:16
  80.0 4.2 %collective-permute-start.22 = (bf16[224,128]{1,0:T(8,128)(2,1)S(1)}, bf16[224,128]{1,0:T(8,128)(2,1)S(1)}, u32[]{:S(2)}, u32[]{:S(2)}) collective-permute-start(bf16[224,128]{1,0:T(8,128)(2,1)S(1)} %pad_maximum_fusion.18), channel_id=1, source_target_pairs={{0,12},{2,14},{4,0},{6,2},{8,4},{10,6},{12,8},{14,10},{1,13},{3,15... | collective-permute-start | bytes 172040 | tf_op jit(solution)/shard_map/ppermute | solution.py:16
  84.2 5.8 %collective-permute-start.23 = (bf16[224,128]{1,0:T(8,128)(2,1)S(1)}, bf16[224,128]{1,0:T(8,128)(2,1)S(1)}, u32[]{:S(2)}, u32[]{:S(2)}) collective-permute-start(bf16[224,128]{1,0:T(8,128)(2,1)S(1)} %add_convert_fusion.1), channel_id=1, source_target_pairs={{0,2},{2,0},{4,6},{6,4},{8,10},{10,8},{12,14},{14,12},{1,3},{3,1},... | collective-permute-start | bytes 172040 | tf_op jit(solution)/shard_map/ppermute | solution.py:21
  87.9 4.0 %collective-permute-start.24 = (bf16[144,128]{1,0:T(8,128)(2,1)S(1)}, bf16[144,128]{1,0:T(8,128)(2,1)S(1)}, u32[]{:S(2)}, u32[]{:S(2)}) collective-permute-start(bf16[144,128]{1,0:T(8,128)(2,1)S(1)} %slice.255), channel_id=1, source_target_pairs={{0,1},{1,2},{2,3},{3,0},{4,5},{5,6},{6,7},{7,4},{8,9},{9,10},{10,1... | collective-permute-start | bytes 110600 | tf_op jit(solution)/shard_map/ppermute | solution.py:26
  87.9 4.0 %collective-permute-start.25 = (bf16[144,128]{1,0:T(8,128)(2,1)S(1)}, bf16[144,128]{1,0:T(8,128)(2,1)S(1)}, u32[]{:S(2)}, u32[]{:S(2)}) collective-permute-start(bf16[144,128]{1,0:T(8,128)(2,1)S(1)} %slice.255), channel_id=1, source_target_pairs={{0,3},{1,0},{2,1},{3,2},{4,7},{5,4},{6,5},{7,6},{8,11},{9,8},{10,9... | collective-permute-start | bytes 110600 | tf_op jit(solution)/shard_map/ppermute | solution.py:26
  91.9 20.2 %collective-permute-start.26 = (bf16[144,128]{1,0:T(8,128)(2,1)S(1)}, bf16[144,128]{1,0:T(8,128)(2,1)S(1)}, u32[]{:S(2)}, u32[]{:S(2)}) collective-permute-start(bf16[144,128]{1,0:T(8,128)(2,1)S(1)} %fusion.55), channel_id=1, source_target_pairs={{0,32},{16,48},{32,0},{48,16},{64,96},{80,112},{96,64},{112,80},{1... | collective-permute-start | bytes 110600 | tf_op jit(solution)/shard_map/ppermute | solution.py:21
  93.2 18.9 %collective-permute-start.27 = (bf16[144,128]{1,0:T(8,128)(2,1)S(1)}, bf16[144,128]{1,0:T(8,128)(2,1)S(1)}, u32[]{:S(2)}, u32[]{:S(2)}) collective-permute-start(bf16[144,128]{1,0:T(8,128)(2,1)S(1)} %fusion.55), channel_id=1, source_target_pairs={{0,64},{16,80},{32,96},{48,112},{64,0},{80,16},{96,32},{112,48},{1... | collective-permute-start | bytes 110600 | tf_op jit(solution)/shard_map/ppermute | solution.py:21
  95.7 16.5 %collective-permute-start.28 = (bf16[144,128]{1,0:T(8,128)(2,1)S(1)}, bf16[144,128]{1,0:T(8,128)(2,1)S(1)}, u32[]{:S(2)}, u32[]{:S(2)}) collective-permute-start(bf16[144,128]{1,0:T(8,128)(2,1)S(1)} %fusion.55), channel_id=1, source_target_pairs={{0,96},{16,112},{32,64},{48,80},{64,32},{80,48},{96,0},{112,16},{1... | collective-permute-start | bytes 110600 | tf_op jit(solution)/shard_map/ppermute | solution.py:21
  104.4 16.5 %all-to-all-start = ((bf16[8,64,192]{2,1,0:T(8,128)(2,1)}), bf16[8,64,192]{2,1,0:T(8,128)(2,1)S(1)}, u32[]{:S(2)}, u32[]{:S(2)}) async-start(bf16[8,64,192]{2,1,0:T(8,128)(2,1)} %copy.17), calls=%async_computation | async-start | bytes 524288 | tf_op jit(solution)/shard_map/all_to_all | solution.py:253
  112.3 9.3 %collective-permute-start.29 = (bf16[576,128]{1,0:T(8,128)(2,1)S(1)}, bf16[576,128]{1,0:T(8,128)(2,1)S(1)}, u32[]{:S(2)}, u32[]{:S(2)}) collective-permute-start(bf16[576,128]{1,0:T(8,128)(2,1)S(1)} %pad_maximum_fusion.3), channel_id=1, source_target_pairs={{0,16},{16,0},{32,48},{48,32},{64,80},{80,64},{96,112},{112,96},{1... | collective-permute-start | bytes 442376 | tf_op jit(solution)/shard_map/ppermute | solution.py:21

commit v3 on v2

--- a/solution.py
+++ b/solution.py
@@ -21,11 +21,6 @@
     return lax.ppermute(x, axis, [(i, i ^ bit) for i in range(count)])
 
 
-def ring(x, step):
-    pairs = [(4 * y + p, 4 * y + (p + step) % 4) for y in range(4) for p in range(4)]
-    return lax.ppermute(x, ("col", "batch"), pairs)
-
-
 def up(x):
     return x.astype(F32)
 
@@ -39,15 +34,26 @@
     return (up(x) + up(flip(x, axis, bit))).astype(BF)
 
 
+def taken(x, at):
+    return lax.dynamic_slice(x, (at, 0, 0), (1,) + x.shape[1:], allow_negative_indices=False)[0]
+
+
 def pair_kernel(
-    flags, pair, cot, top, bottom, left, right, rowp, colp, weight, turned,
+    flags, pair, cot, top, bottom, left, right, rowp, bins, weight,
     out, keep, send, rowg,
-    zwide, z3, cots, qwide, q3, wgrad, line,
+    zwide, z3, cots, qwide, q3, wgrad, line, colp, turned,
 ):
     chans = 128
     has_up, has_down, has_left, has_right, core = (flags[i] for i in range(5))
     rows = lax.broadcasted_iota(jnp.int32, (38, 1, 1), 0)
     row_ok = ((rows >= 3) | (has_up > 0)) & ((rows < 35) | (has_down > 0))
+
+    colp[...] = jnp.zeros((96, chans), F32)
+    colp[5:75] = bins[0:70]
+    colp[85:88] = bins[0:3]
+    colp[88:89] = bins[3:4]
+    for at in range(0, 9 * chans, chans):
+        turned[at : at + chans] = up(weight[at : at + chans]).T.astype(BF)
 
     zwide[:, 0:8] = jnp.zeros((38, 8, chans), F32)
     zwide[:, 72:96] = jnp.zeros((38, 24, chans), F32)
@@ -137,9 +143,79 @@
             send[576:610] = line[32 - 32 * mine : 66 - 32 * mine].astype(BF)
 
 
-def pair_block(flags, pair, cot, top, bottom, left, right, rowp, colp, weight, turned):
+def conv_kernel(flags, fine, before, after, conv_w, proj, part, wide):
+    blocks = wide.shape[0]
+    wide[:, 80:88] = jnp.zeros((blocks, 8, 128), F32)
+    for j in range(blocks):
+        lanes = slice(128 * j, 128 * j + 128)
+        wide[j, 0:8] = jnp.where(flags[0] > 0, up(before[:, lanes]), 0.0)
+        wide[j, 8:72] = up(fine[:, lanes])
+        wide[j, 72:80] = jnp.where(flags[1] > 0, up(after[:, lanes]), 0.0)
+    seq = jnp.zeros((40, conv_w.shape[1]), F32)
+    for tap in range(5):
+        window = jnp.concatenate([wide[j, pl.ds(tap, 40, stride=2)] for j in range(blocks)], axis=1)
+        seq = seq + lax.dot_general(
+            window.astype(BF), conv_w[tap], (((1,), (1,)), ((), ())), preferred_element_type=F32
+        )
+    rows = lax.broadcasted_iota(jnp.int32, (40, 1), 0)
+    ok = ((rows >= 3) | (flags[0] > 0)) & ((rows < 35) | (flags[1] > 0)) & (rows < 38)
+    seq = jnp.where(ok, seq, 0.0).astype(BF)
+    part[...] = jnp.dot(seq, proj[...], preferred_element_type=F32).astype(BF)
+
+
+def grad_conv_kernel(sums, proj, conv_w, parts, seqg, whole):
+    pair = jnp.concatenate([sums[0:40], sums[40:80]], axis=1)
+    grad = lax.dot_general(pair, proj[...], (((1,), (1,)), ((), ())), preferred_element_type=F32)
+    seqg[...] = up(grad.astype(BF))
+    ahead, here, behind = (seqg[at : at + 32].astype(BF) for at in (2, 1, 0))
+
+    def times(x, tap):
+        return jnp.dot(x, conv_w[tap], preferred_element_type=F32)
+
+    even = times(ahead, 0) + times(here, 2) + times(behind, 4)
+    odd = times(ahead, 1) + times(here, 3)
+    for j in range(whole.shape[0]):
+        lanes = slice(128 * j, 128 * j + 128)
+        whole[j, pl.ds(0, 32, stride=2)] = even[:, lanes]
+        whole[j, pl.ds(1, 32, stride=2)] = odd[:, lanes]
+    for m in range(4):
+        low, middle, high = (whole[3 * m + i] for i in range(3))
+        parts[2 * m] = jnp.concatenate([low, middle[:, :64]], axis=1).astype(BF)
+        parts[2 * m + 1] = jnp.concatenate([middle[:, 64:], high], axis=1).astype(BF)
+
+
+VMEM = pl.BlockSpec(memory_space=pltpu.VMEM)
+SMEM = pl.BlockSpec(memory_space=pltpu.SMEM)
+
+
+def conv_forward(flags, fine, before, after, conv_w, proj):
+    chans = fine.shape[1]
+    return pl.pallas_call(
+        conv_kernel,
+        out_shape=jax.ShapeDtypeStruct((40, proj.shape[1]), BF),
+        in_specs=[SMEM] + [VMEM] * 5,
+        out_specs=VMEM,
+        scratch_shapes=[pltpu.VMEM((chans // 128, 88, 128), F32)],
+        compiler_params=pltpu.CompilerParams(vmem_limit_bytes=12 * 1024 * 1024),
+        cost_estimate=pl.CostEstimate(flops=120000000, bytes_accessed=3500000, transcendentals=0),
+    )(flags, fine, before, after, conv_w, proj)
+
+
+def conv_backward(sums, proj, conv_w):
+    outchans, chans = conv_w.shape[1:]
+    return pl.pallas_call(
+        grad_conv_kernel,
+        out_shape=jax.ShapeDtypeStruct((8, 64, outchans), BF),
+        in_specs=[VMEM] * 3,
+        out_specs=VMEM,
+        scratch_shapes=[pltpu.VMEM((40, outchans), F32), pltpu.VMEM((chans // 128, 64, 128), F32)],
+        compiler_params=pltpu.CompilerParams(vmem_limit_bytes=12 * 1024 * 1024),
+        cost_estimate=pl.CostEstimate(flops=120000000, bytes_accessed=3500000, transcendentals=0),
+    )(sums, proj, conv_w)
+
+
+def pair_block(flags, pair, cot, top, bottom, left, right, rowp, bins, weight):
     chans = 128
-    vmem = pl.BlockSpec(memory_space=pltpu.VMEM)
     return pl.pallas_call(
         pair_kernel,
         out_shape=(
@@ -148,8 +224,8 @@
             jax.ShapeDtypeStruct((KEPT, chans), BF),
             jax.ShapeDtypeStruct((40, chans), BF),
         ),
-        in_specs=[pl.BlockSpec(memory_space=pltpu.SMEM)] + [vmem] * 10,
-        out_specs=(vmem,) * 4,
+        in_specs=[SMEM] + [VMEM] * 9,
+        out_specs=(VMEM,) * 4,
         scratch_shapes=[
             pltpu.VMEM((38, 96, chans), F32),
             pltpu.VMEM((38, WIDE, 3 * chans), BF),
@@ -158,72 +234,60 @@
             pltpu.VMEM((36, WIDE, 3 * chans), BF),
             pltpu.VMEM((9 * chans, chans), F32),
             pltpu.VMEM((72, chans), F32),
+            pltpu.VMEM((96, chans), F32),
+            pltpu.VMEM((9 * chans, chans), BF),
         ],
-        compiler_params=pltpu.CompilerParams(vmem_limit_bytes=40 * 1024 * 1024),
+        compiler_params=pltpu.CompilerParams(vmem_limit_bytes=24 * 1024 * 1024),
         cost_estimate=pl.CostEstimate(flops=2500000000, bytes_accessed=4000000, transcendentals=700000),
-    )(flags, pair, cot, top, bottom, left, right, rowp, colp, weight, turned)
+    )(flags, pair, cot, top, bottom, left, right, rowp, bins, weight)
 
 
 def local(fine, conv_w, proj_a, proj_b, pair_in, pair_w, cotangent):
-    chans, outchans, pairs = fine.shape[2], conv_w.shape[1], pair_in.shape[3]
+    pairs = pair_in.shape[3]
     row, col = lax.axis_index("row"), lax.axis_index("col")
     core, zpos = row % 2, row // 2
-    first, last = row == 0, row == 15
-    row_bins = 32 * row - 3 + jnp.arange(38)
-    row_ok = (row_bins >= 0) & (row_bins < 512)
-    flags = jnp.stack([row > 0, row < 15, col > 0, col < 7, core > 0]).astype(jnp.int32)
+    place = jnp.arange(8)
+    place, spot, most = place // 2, jnp.where(place < 2, row, jnp.where(place < 4, col, core)), place % 2
+    flags = jnp.where(most == 0, spot > 0, spot < jnp.where(place == 0, 15, 7)).astype(jnp.int32)
 
     fine, pair, cot = fine[0], pair_in[0], cotangent[0]
-    before = shift(fine[-8:], "row", 1)
+    apart = zpos ^ col
+    scalars = (core == 0, (apart & 4) == 4, [(apart & 3) == k for k in (1, 2, 3)], zpos == col, [(zpos ^ k) & 3 for k in range(4)])
+    edge, flags, scalars = lax.optimization_barrier((fine[-8:], flags, scalars))
+    is_first, is_far, is_near, is_root, places = scalars
+    before = shift(edge, "row", 1)
     after = shift(fine[:8], "row", -1)
     top = shift(jnp.concatenate([pair[29:], cot[30:]]), "row", 1)
     bottom = shift(jnp.concatenate([pair[:3], cot[:2]]), "row", -1)
-    grouped = jnp.concatenate(
-        [jnp.where(first, 0, before), fine, jnp.where(last, 0, after)]
-    ).reshape(40, 2, chans)
-    seq = 0.0
-    for tap in range(5):
-        seq = seq + lax.dot_general(
-            grouped[tap // 2 : tap // 2 + 38, tap % 2],
-            conv_w[tap],
-            (((1,), (1,)), ((), ())),
-            preferred_element_type=F32,
-        )
-    seq = jnp.where(row_ok[:, None], seq, 0.0).astype(BF)
     proj = jnp.concatenate([proj_a, proj_b], axis=1)
-    part = jnp.dot(seq, proj, preferred_element_type=F32).astype(BF)
-    part = jnp.concatenate([part, jnp.zeros((2, 2 * pairs), BF)])
+    part = conv_forward(flags, fine, before, after, conv_w, proj)
 
     tall_pair = jnp.concatenate([top[:3], pair, bottom[:3]])
     tall_cot = jnp.concatenate([top[2:], cot, bottom[3:], bottom[4:]])
-    left = shift(jnp.concatenate([tall_pair[:, 61:], tall_cot[:, 62:], tall_cot[:, :3]], axis=1), "col", 1)
-    right = shift(jnp.concatenate([tall_pair[:, :3], tall_cot[:, :5]], axis=1), "col", -1)
+    left = jnp.concatenate([tall_pair[:, 61:], tall_cot[:, 62:], tall_cot[:, :3]], axis=1)
+    right = jnp.concatenate([tall_pair[:, :3], tall_cot[:, :5]], axis=1)
 
     both = up(sum_flip(sum_y(part), "col", 1))
     rowp, colp_here = both[:, :pairs], both[:, pairs:].astype(BF)
 
-    mine = jnp.where(core == 0, colp_here[:35], colp_here[3:38])
+    mine = jnp.where(is_first, colp_here[:35], colp_here[3:38])
     other = flip(mine, "row", 1)
-    colp = jnp.concatenate([jnp.where(core == 0, mine, other), jnp.where(core == 0, other, mine)])
-    apart = zpos ^ col
-    colp = jnp.where((apart & 4) == 4, flip(colp, "row", 8), colp)
+    colp = jnp.concatenate([jnp.where(is_first, mine, other), jnp.where(is_first, other, mine)])
+    colp, left, right = lax.optimization_barrier((colp, left, right))
+    far, left, right = flip(colp, "row", 8), shift(left, "col", 1), shift(right, "col", -1)
+    far, left, right = lax.optimization_barrier((far, left, right))
+    colp = jnp.where(is_far, far, colp)
     near = [flip(colp, "row", 2 * k) for k in (1, 2, 3)]
     for k in (1, 2, 3):
-        colp = jnp.where((apart & 3) == k, near[k - 1], colp)
-    blank = jnp.zeros((10, pairs), BF)
-    colp = up(jnp.concatenate([blank[:5], colp[:3], colp[3:], blank, colp[:3], colp[3:4], blank[:7]]))
-
+        colp = jnp.where(is_near[k - 1], near[k - 1], colp)
     weight = pair_w.reshape(9 * pairs, pairs)
-    turned = jnp.swapaxes(pair_w, 2, 3).reshape(9 * pairs, pairs)
-    out, keep, send, rowg = pair_block(
-        flags, pair, cot, top, bottom, left, right, rowp, colp, weight, turned
-    )
+    out, keep, send, rowg = pair_block(flags, pair, cot, top, bottom, left, right, rowp, up(colp), weight)
 
     total = (keep + up(flip(send, "row", 1))).astype(BF)
     half, colg = total[:576].reshape(4, 144, pairs), total[576:]
 
     def quarter(k):
-        return lax.dynamic_index_in_dim(half, (zpos ^ k) & 3, 0, keepdims=False)
+        return taken(half, places[k])
 
     def joined(k):
         return jnp.concatenate([quarter(k), colg])
@@ -231,26 +295,21 @@
     got = [flip(joined(k), "row", 2 * k) for k in (1, 2, 3)]
     total = ((up(joined(0)) + up(got[0])) + (up(got[1]) + up(got[2]))).astype(BF)
     total = sum_flip(total, "row", 8)
-    colg = jnp.where(zpos == col, total[144:], 0)
+    colg = jnp.where(is_root, total[144:], 0)
     total = sum_y(jnp.concatenate([total[:144], rowg, colg]))
-    across, left, right = flip(total, "col", 1), ring(total[:144], 1), ring(total[:144], 3)
-    total = up(total) + up(across)
-    sums = total[144:].astype(BF)
-    quart = (total[:144] + (up(left) + up(right))).astype(BF)
+    total = sum_flip(total, "col", 1)
+    quart, sums = total[:144], total[144:]
+    parts = conv_backward(sums, proj, conv_w)
+    quart = sum_flip(quart, "batch", 1)
+    parts, quart = lax.optimization_barrier((parts, quart))
+    parts = lax.all_to_all(parts, "col", 0, 0, tiled=True)
 
     near = jnp.stack([quart] + [flip(quart, "row", 2 * k) for k in (1, 2, 3)])
-    half = jnp.concatenate([lax.dynamic_index_in_dim(near, (zpos ^ k) & 3, 0, keepdims=False) for k in range(4)])
+    half = jnp.concatenate([taken(near, places[k]) for k in range(4)])
     theirs = flip(half, "row", 1)
-    grad_pair_w = jnp.concatenate([jnp.where(core == 0, half, theirs), jnp.where(core == 0, theirs, half)])
+    grad_pair_w = jnp.concatenate([jnp.where(is_first, half, theirs), jnp.where(is_first, theirs, half)])
     grad_pair_w = up(grad_pair_w).reshape(3, 3, pairs, pairs) / 512.0
 
-    sums = jnp.concatenate([sums[:34], sums[40:74]], axis=1)
-    seqg = lax.dot_general(sums, proj, (((1,), (1,)), ((), ())), preferred_element_type=F32).astype(BF)
-    taps = [jnp.dot(seqg, conv_w[tap], preferred_element_type=F32) for tap in range(5)]
-    even = taps[0][2:] + taps[2][1:33] + taps[4][:32]
-    odd = taps[1][2:] + taps[3][1:33]
-    parts = jnp.stack((even, odd), axis=1).astype(BF).reshape(64, 8, outchans)
-    parts = lax.all_to_all(parts.transpose(1, 0, 2), "col", 0, 0, tiled=True)
     grad_fine = jnp.sum(up(parts), axis=0).astype(BF)
     return out[None], grad_fine[None], grad_pair_w
 

time: 123 us -> 115 us (0.935)
  waiting for transfers between devices: 36.8 us -> 47.6 us
  matrix products: 10.6 us -> 0 us
  starting transfers between devices: 57.7 us -> 48.4 us
  Pallas kernels: 6.4 us -> 9.79 us
    dot_general x11 -> x0, matrix products: 10.6 us -> none  [the longest x5 6.42 us: local(): jnp.dot(seqg, conv_w[tap], preferred_element_type=F32)]
    ppermute x16 -> x17, waiting for transfers between devices: 20.1 us -> 29.8 us  [flip(): return lax.ppermute(x, axis, [(i, i ^ bit) for i in range(count)])]
    all_to_all x1, starting transfers between devices: 7.69 us -> 3.45 us  [local(): parts = lax.all_to_all(parts, 'col', 0, 0, tiled=True)]
    pallas_call x0 -> x2, Pallas kernels: none -> 3.32 us  [the longest x1 1.69 us: conv_forward(): pl.pallas_call(conv_kernel, out_shape=jax.ShapeDtypeStruct((40, proj.shap...]
    ppermute x12, waiting for transfers between devices: 6.37 us -> 9.14 us  [shift(): lax.ppermute(x, axis, [(i, (i + step) % count) for i in range(count)])]
    unnamed x9 -> x13, local copies, waits for them, and re-layouts: 0.83 us -> 3.58 us
    ppermute x2 -> x0, starting transfers between devices: 2.03 us -> none  [ring(): return lax.ppermute(x, ('col', 'batch'), pairs)]
    ppermute x2 -> x0, waiting for transfers between devices: 1.78 us -> none  [ring(): return lax.ppermute(x, ('col', 'batch'), pairs)]
  transfers between devices with their start and end apart: 31 -> 30, of which waited for: 15 -> 17; matrix products, arithmetic and copies ran while one was open for 10% -> 3% of each run, Pallas kernels for 0% -> 1%
where the time goes in v3:
time: 115 us
  starting transfers between devices  48.4 us (42%)
  waiting for transfers between devices  47.6 us (41%)
  Pallas kernels  9.79 us (9%)
  local copies, waits for them, and re-layouts  6.14 us (5%)
  other arithmetic  2.01 us (2%)
    ppermute x17, waiting for transfers between devices, flip(): return lax.ppermute(x, axis, [(i, i ^ bit) for i in range(count)])  29.8 us
    ppermute x17, starting transfers between devices, flip(): return lax.ppermute(x, axis, [(i, i ^ bit) for i in range(count)])  22.5 us
    ppermute x12, starting transfers between devices, shift(): lax.ppermute(x, axis, [(i, (i + step) % count) for i in range(count)])  22.4 us
    ppermute x12, waiting for transfers between devices, shift(): lax.ppermute(x, axis, [(i, (i + step) % count) for i in range(count)])  9.14 us
    all_to_all x1, waiting for transfers between devices, local(): parts = lax.all_to_all(parts, 'col', 0, 0, tiled=True)  8.58 us
    pallas_call x1, Pallas kernels, pair_block(): pl.pallas_call(pair_kernel, out_shape=(jax.ShapeDtypeStruct((32, 64, chan...  6.47 us
    unnamed x13, local copies, waits for them, and re-layouts  3.58 us
    all_to_all x1, starting transfers between devices, local(): parts = lax.all_to_all(parts, 'col', 0, 0, tiled=True)  3.45 us
  transfers between devices with their start and end apart: 30, of which 17 were waited for; matrix products, arithmetic and copies ran while one was open for 3% of the time, Pallas kernels for 1%

profile of v3, /device:TPU:2, one launch (start us, length us, event | category | flops | bytes accessed | tf_op | source)
XLA Modules:
  0.0 114.9 jit_solution(3447616330845246115)
XLA Ops:
  0.6 0.0 copy-start.2
  0.7 0.8 slice_bitcast_fusion.4
  1.5 5.3 %collective-permute-start.3 = (bf16[8,1536]{1,0:T(8,128)(2,1)S(1)}, bf16[8,1536]{1,0:T(8,128)(2,1)S(1)}, u32[]{:S(2)}, u32[]{:S(2)}) collective-permute-start(bf16[8,1536]{1,0:T(8,128)(2,1)S(1)} %get-tuple-element.59), channel_id=1, source_target_pairs={{0,240},{16,0},{32,16},{48,32},{64,48},{80,64},{96,80},{112,96},{1... | collective-permute-start | bytes 73736 | tf_op jit(solution)/shard_map/ppermute | solution.py:16
  6.8 0.8 constant_dynamic-update-slice_fusion.1
  7.6 0.8 slice_bitcast_fusion
  8.5 0.8 constant_dynamic-update-slice_fusion.proj
  9.3 0.0 collective-permute-done.2.before
  9.3 0.0 copy-start
  9.3 1.8 %copy-done = bf16[5,192,1536]{2,1,0:T(8,128)(2,1)S(1)} copy-done((bf16[5,192,1536]{2,1,0:T(8,128)(2,1)S(1)}, bf16[5,192,1536]{2,1,0:T(8,128)(2,1)}, u32[]{:S(2)}) %copy-start) | copy-done | bytes 2949144
  11.1 0.9 copy-done.4
  12.1 1.7 %shard_map.94 = bf16[40,256]{1,0:T(8,128)(2,1)S(1)} custom-call(s32[8]{0:T(128)S(1)} %select_convert_fusion.1.flags, bf16[64,1536]{1,0:T(8,128)(2,1)S(1)} %bitcast.44, bf16[8,1536]{1,0:T(8,128)(2,1)S(1)} %collective-permute-done.2.before, bf16[8,1536]{1,0:T(8,128)(2,1)S(1)} %collective-permute-done.3.after, bf16[5,192,1536]{2,1,0:T(8,128)(2,1)S(1)} %copy-done, ...), custom_call_target="tpu_custom_call" | custom-call | flops 120000000 | bytes 3500000 | tf_op jit(solution)/shard_map/pallas_call | solution.py:193
  13.7 3.1 %collective-permute-start.6 = (bf16[40,256]{1,0:T(8,128)(2,1)S(1)}, bf16[40,256]{1,0:T(8,128)(2,1)S(1)}, u32[]{:S(2)}, u32[]{:S(2)}) collective-permute-start(bf16[40,256]{1,0:T(8,128)(2,1)S(1)} %shard_map.94), channel_id=1, source_target_pairs={{0,12},{2,14},{4,0},{6,2},{8,4},{10,6},{12,8},{14,10},{1,13},{3,15... | collective-permute-start | bytes 61448 | tf_op jit(solution)/shard_map/ppermute | solution.py:16
  16.8 0.0 collective-permute-start.5
  16.8 2.2 %collective-permute-start.4 = (bf16[40,256]{1,0:T(8,128)(2,1)S(1)}, bf16[40,256]{1,0:T(8,128)(2,1)S(1)}, u32[]{:S(2)}, u32[]{:S(2)}) collective-permute-start(bf16[40,256]{1,0:T(8,128)(2,1)S(1)} %shard_map.94), channel_id=1, source_target_pairs={{0,8},{2,10},{4,12},{6,14},{8,0},{10,2},{12,4},{14,6},{1,9},{3,11}... | collective-permute-start | bytes 61448 | tf_op jit(solution)/shard_map/ppermute | solution.py:16
  19.1 0.0 collective-permute-done.6
  19.1 2.8 %collective-permute-done.5 = bf16[40,256]{1,0:T(8,128)(2,1)S(1)} collective-permute-done((bf16[40,256]{1,0:T(8,128)(2,1)S(1)}, bf16[40,256]{1,0:T(8,128)(2,1)S(1)}, u32[]{:S(2)}, u32[]{:S(2)}) %collective-permute-start.5) | collective-permute-done | bytes 20512 | tf_op jit(solution)/shard_map/ppermute | solution.py:16
  21.8 0.3 collective-permute-done.4
  22.1 2.2 %collective-permute-start.7 = (bf16[40,256]{1,0:T(8,128)(2,1)S(1)}, bf16[40,256]{1,0:T(8,128)(2,1)S(1)}, u32[]{:S(2)}, u32[]{:S(2)}) collective-permute-start(bf16[40,256]{1,0:T(8,128)(2,1)S(1)} %add_convert_fusion.7), channel_id=1, source_target_pairs={{0,2},{2,0},{4,6},{6,4},{8,10},{10,8},{12,14},{14,12},{1,3},{3,1},... | collective-permute-start | bytes 61448 | tf_op jit(solution)/shard_map/ppermute | solution.py:21
  24.4 0.0 collective-permute-start
  24.4 3.1 %collective-permute-done.7 = bf16[40,256]{1,0:T(8,128)(2,1)S(1)} collective-permute-done((bf16[40,256]{1,0:T(8,128)(2,1)S(1)}, bf16[40,256]{1,0:T(8,128)(2,1)S(1)}, u32[]{:S(2)}, u32[]{:S(2)}) %collective-permute-start.7) | collective-permute-done | bytes 20512 | tf_op jit(solution)/shard_map/ppermute | solution.py:21
  27.5 0.1 collective-permute-start.8
  27.7 2.4 %collective-permute-start.1 = (bf16[5,64,128]{2,1,0:T(8,128)(2,1)S(1)}, bf16[5,64,128]{2,1,0:T(8,128)(2,1)S(1)}, u32[]{:S(2)}, u32[]{:S(2)}) collective-permute-start(bf16[5,64,128]{2,1,0:T(8,128)(2,1)S(1)} %pad_maximum_fusion.7), channel_id=1, source_target_pairs={{0,240},{16,0},{32,16},{48,32},{64,48},{80,64},{96,80},{112,96},{1... | collective-permute-start | bytes 245768 | tf_op jit(solution)/shard_map/ppermute | solution.py:16
  30.1 0.0 collective-permute-done.8
  30.1 2.0 %collective-permute-done.1.bottom = bf16[5,64,128]{2,1,0:T(8,128)(2,1)S(1)} collective-permute-done((bf16[5,64,128]{2,1,0:T(8,128)(2,1)S(1)}, bf16[5,64,128]{2,1,0:T(8,128)(2,1)S(1)}, u32[]{:S(2)}, u32[]{:S(2)}) %collective-permute-start.1) | collective-permute-done | bytes 81952 | tf_op jit(solution)/shard_map/ppermute | solution.py:16
  32.1 0.0 collective-permute-done.top
  32.2 0.1 fusion.6
  32.3 2.2 %collective-permute-start.10 = (bf16[38,8,128]{2,1,0:T(8,128)(2,1)S(1)}, bf16[38,8,128]{2,1,0:T(8,128)(2,1)S(1)}, u32[]{:S(2)}, u32[]{:S(2)}) collective-permute-start(bf16[38,8,128]{2,1,0:T(8,128)(2,1)S(1)} %get-tuple-element.31), channel_id=1, source_target_pairs={{0,2},{2,4},{4,6},{6,8},{8,10},{10,12},{12,14},{14,0},{1,3},{3,5},... | collective-permute-start | bytes 233480 | tf_op jit(solution)/shard_map/ppermute | solution.py:16
  34.5 3.5 %collective-permute-start.11 = (bf16[38,8,128]{2,1,0:T(8,128)(2,1)S(1)}, bf16[38,8,128]{2,1,0:T(8,128)(2,1)S(1)}, u32[]{:S(2)}, u32[]{:S(2)}) collective-permute-start(bf16[38,8,128]{2,1,0:T(8,128)(2,1)S(1)} %get-tuple-element.32), channel_id=1, source_target_pairs={{0,14},{2,0},{4,2},{6,4},{8,6},{10,8},{12,10},{14,12},{1,15},{3,1}... | collective-permute-start | bytes 233480 | tf_op jit(solution)/shard_map/ppermute | solution.py:16
  38.0 2.5 %collective-permute-start.9 = (bf16[70,128]{1,0:T(8,128)(2,1)S(1)}, bf16[70,128]{1,0:T(8,128)(2,1)S(1)}, u32[]{:S(2)}, u32[]{:S(2)}) collective-permute-start(bf16[70,128]{1,0:T(8,128)(2,1)S(1)} %pad_maximum_fusion.17), channel_id=1, source_target_pairs={{0,128},{16,144},{32,160},{48,176},{64,192},{80,208},{96,224},{112... | collective-permute-start | bytes 53768 | tf_op jit(solution)/shard_map/ppermute | solution.py:21
  40.5 5.2 %collective-permute-done.9 = bf16[70,128]{1,0:T(8,128)(2,1)S(1)} collective-permute-done((bf16[70,128]{1,0:T(8,128)(2,1)S(1)}, bf16[70,128]{1,0:T(8,128)(2,1)S(1)}, u32[]{:S(2)}, u32[]{:S(2)}) %collective-permute-start.9) | collective-permute-done | bytes 17952 | tf_op jit(solution)/shard_map/ppermute | solution.py:21
  45.7 0.1 collective-permute-start.14
  45.8 0.5 collective-permute-start.13
  46.4 3.8 %collective-permute-start.12 = (bf16[70,128]{1,0:T(8,128)(2,1)S(1)}, bf16[70,128]{1,0:T(8,128)(2,1)S(1)}, u32[]{:S(2)}, u32[]{:S(2)}) collective-permute-start(bf16[70,128]{1,0:T(8,128)(2,1)S(1)} %broadcast_select_fusion.2), channel_id=1, source_target_pairs={{0,96},{16,112},{32,64},{48,80},{64,32},{80,48},{96,0},{112,16},{1... | collective-permute-start | bytes 53768 | tf_op jit(solution)/shard_map/ppermute | solution.py:21
  50.2 0.4 collective-permute-done.13
  50.6 1.7 %collective-permute-done.12 = bf16[70,128]{1,0:T(8,128)(2,1)S(1)} collective-permute-done((bf16[70,128]{1,0:T(8,128)(2,1)S(1)}, bf16[70,128]{1,0:T(8,128)(2,1)S(1)}, u32[]{:S(2)}, u32[]{:S(2)}) %collective-permute-start.12) | collective-permute-done | bytes 17952 | tf_op jit(solution)/shard_map/ppermute | solution.py:21
  52.3 0.0 copy-start.1
  52.3 6.5 %shard_map.95 = (bf16[32,64,128]{2,1,0:T(8,128)(2,1)}, f32[616,128]{1,0:T(8,128)S(1)}, bf16[616,128]{1,0:T(8,128)(2,1)S(1)}, bf16[40,128]{1,0:T(8,128)(2,1)S(1)}) custom-call(s32[8]{0:T(128)S(1)} %select_convert_fusion.1.flags, bf16[32,64,128]{2,1,0:T(8,128)(2,1)S(1)} %bitcast.41, bf16[32,64,128]{2,1,0:T(8,128)(2,1)S(1)} %bitcast.43, ...), custom_call_target="tpu_custom_call" | custom-call | flops 2500000000 | bytes 4000000 | tf_op jit(solution)/shard_map/pallas_call | solution.py:219
  58.8 1.4 %collective-permute-done.15 = bf16[616,128]{1,0:T(8,128)(2,1)S(1)} collective-permute-done((bf16[616,128]{1,0:T(8,128)(2,1)S(1)}, bf16[616,128]{1,0:T(8,128)(2,1)S(1)}, u32[]{:S(2)}, u32[]{:S(2)}) %collective-permute-start.15) | collective-permute-done | bytes 157728 | tf_op jit(solution)/shard_map/ppermute | solution.py:21
  60.3 0.5 collective-permute-start.16
  60.8 3.7 %collective-permute-start.17 = (bf16[184,128]{1,0:T(8,128)(2,1)S(1)}, bf16[184,128]{1,0:T(8,128)(2,1)S(1)}, u32[]{:S(2)}, u32[]{:S(2)}) collective-permute-start(bf16[184,128]{1,0:T(8,128)(2,1)S(1)} %get-tuple-element.74), channel_id=1, source_target_pairs={{0,64},{16,80},{32,96},{48,112},{64,0},{80,16},{96,32},{112,48},{1... | collective-permute-start | bytes 141320 | tf_op jit(solution)/shard_map/ppermute | solution.py:21
  64.4 0.4 collective-permute-start.18
  64.8 2.7 %collective-permute-done.17 = bf16[184,128]{1,0:T(8,128)(2,1)S(1)} collective-permute-done((bf16[184,128]{1,0:T(8,128)(2,1)S(1)}, bf16[184,128]{1,0:T(8,128)(2,1)S(1)}, u32[]{:S(2)}, u32[]{:S(2)}) %collective-permute-start.17) | collective-permute-done | bytes 47136 | tf_op jit(solution)/shard_map/ppermute | solution.py:21
  67.5 2.8 %collective-permute-done.18 = bf16[184,128]{1,0:T(8,128)(2,1)S(1)} collective-permute-done((bf16[184,128]{1,0:T(8,128)(2,1)S(1)}, bf16[184,128]{1,0:T(8,128)(2,1)S(1)}, u32[]{:S(2)}, u32[]{:S(2)}) %collective-permute-start.18) | collective-permute-done | bytes 47136 | tf_op jit(solution)/shard_map/ppermute | solution.py:21
  70.3 2.7 %collective-permute-start.19 = (bf16[184,128]{1,0:T(8,128)(2,1)S(1)}, bf16[184,128]{1,0:T(8,128)(2,1)S(1)}, u32[]{:S(2)}, u32[]{:S(2)}) collective-permute-start(bf16[184,128]{1,0:T(8,128)(2,1)S(1)} %add_convert_fusion.4), channel_id=1, source_target_pairs={{0,128},{16,144},{32,160},{48,176},{64,192},{80,208},{96,224},{112... | collective-permute-start | bytes 141320 | tf_op jit(solution)/shard_map/ppermute | solution.py:21
  73.1 5.8 %collective-permute-done.19 = bf16[184,128]{1,0:T(8,128)(2,1)S(1)} collective-permute-done((bf16[184,128]{1,0:T(8,128)(2,1)S(1)}, bf16[184,128]{1,0:T(8,128)(2,1)S(1)}, u32[]{:S(2)}, u32[]{:S(2)}) %collective-permute-start.19) | collective-permute-done | bytes 47136 | tf_op jit(solution)/shard_map/ppermute | solution.py:21
  78.9 0.1 collective-permute-start.21
  79.0 3.5 %collective-permute-start.20 = (bf16[224,128]{1,0:T(8,128)(2,1)S(1)}, bf16[224,128]{1,0:T(8,128)(2,1)S(1)}, u32[]{:S(2)}, u32[]{:S(2)}) collective-permute-start(bf16[224,128]{1,0:T(8,128)(2,1)S(1)} %pad_maximum_fusion.16), channel_id=1, source_target_pairs={{0,8},{2,10},{4,12},{6,14},{8,0},{10,2},{12,4},{14,6},{1,9},{3,11}... | collective-permute-start | bytes 172040 | tf_op jit(solution)/shard_map/ppermute | solution.py:16
  82.5 0.1 collective-permute-start.22
  82.6 1.8 %collective-permute-done.21 = bf16[224,128]{1,0:T(8,128)(2,1)S(1)} collective-permute-done((bf16[224,128]{1,0:T(8,128)(2,1)S(1)}, bf16[224,128]{1,0:T(8,128)(2,1)S(1)}, u32[]{:S(2)}, u32[]{:S(2)}) %collective-permute-start.21) | collective-permute-done | bytes 57376 | tf_op jit(solution)/shard_map/ppermute | solution.py:16
  84.4 0.9 collective-permute-done.20
  85.2 1.4 %collective-permute-done.22 = bf16[224,128]{1,0:T(8,128)(2,1)S(1)} collective-permute-done((bf16[224,128]{1,0:T(8,128)(2,1)S(1)}, bf16[224,128]{1,0:T(8,128)(2,1)S(1)}, u32[]{:S(2)}, u32[]{:S(2)}) %collective-permute-start.22) | collective-permute-done | bytes 57376 | tf_op jit(solution)/shard_map/ppermute | solution.py:16
  86.7 1.3 %collective-permute-start.23 = (bf16[224,128]{1,0:T(8,128)(2,1)S(1)}, bf16[224,128]{1,0:T(8,128)(2,1)S(1)}, u32[]{:S(2)}, u32[]{:S(2)}) collective-permute-start(bf16[224,128]{1,0:T(8,128)(2,1)S(1)} %add_convert_fusion.2), channel_id=1, source_target_pairs={{0,2},{2,0},{4,6},{6,4},{8,10},{10,8},{12,14},{14,12},{1,3},{3,1},... | collective-permute-start | bytes 172040 | tf_op jit(solution)/shard_map/ppermute | solution.py:21
  88.0 4.5 %collective-permute-done.23 = bf16[224,128]{1,0:T(8,128)(2,1)S(1)} collective-permute-done((bf16[224,128]{1,0:T(8,128)(2,1)S(1)}, bf16[224,128]{1,0:T(8,128)(2,1)S(1)}, u32[]{:S(2)}, u32[]{:S(2)}) %collective-permute-start.23) | collective-permute-done | bytes 57376 | tf_op jit(solution)/shard_map/ppermute | solution.py:21
  92.5 0.2 collective-permute-start.24
  92.7 1.6 %shard_map.96 = bf16[8,64,192]{2,1,0:T(8,128)(2,1)} custom-call(bf16[80,128]{1,0:T(8,128)(2,1)S(1)} %slice.143.sums, bf16[192,256]{1,0:T(8,128)(2,1)S(1)} %constant_dynamic-update-slice_fusion.proj, bf16[5,192,1536]{2,1,0:T(8,128)(2,1)S(1)} %copy-done.1), custom_call_target="tpu_custom_call" | custom-call | flops 120000000 | bytes 3500000 | tf_op jit(solution)/shard_map/pallas_call | solution.py:206
  94.3 2.3 %collective-permute-done.24 = bf16[144,128]{1,0:T(8,128)(2,1)S(1)} collective-permute-done((bf16[144,128]{1,0:T(8,128)(2,1)S(1)}, bf16[144,128]{1,0:T(8,128)(2,1)S(1)}, u32[]{:S(2)}, u32[]{:S(2)}) %collective-permute-start.24) | collective-permute-done | bytes 36896 | tf_op jit(solution)/shard_map/ppermute | solution.py:21
  96.6 0.5 collective-permute-start.27
  97.0 4.0 %collective-permute-start.25 = (bf16[144,128]{1,0:T(8,128)(2,1)S(1)}, bf16[144,128]{1,0:T(8,128)(2,1)S(1)}, u32[]{:S(2)}, u32[]{:S(2)}) collective-permute-start(bf16[144,128]{1,0:T(8,128)(2,1)S(1)} %add_convert_fusion.5), channel_id=1, source_target_pairs={{0,32},{16,48},{32,0},{48,16},{64,96},{80,112},{96,64},{112,80},{1... | collective-permute-start | bytes 110600 | tf_op jit(solution)/shard_map/ppermute | solution.py:21
  101.0 3.4 %all-to-all-start = ((bf16[8,64,192]{2,1,0:T(8,128)(2,1)}), bf16[8,64,192]{2,1,0:T(8,128)(2,1)S(1)}, u32[]{:S(2)}, u32[]{:S(2)}) async-start(bf16[8,64,192]{2,1,0:T(8,128)(2,1)} %shard_map.96), calls=%async_computation | async-start | bytes 524288 | tf_op jit(solution)/shard_map/all_to_all | solution.py:305
  104.6 0.1 collective-permute-start.28
  104.7 8.6 %all-to-all-done = bf16[8,64,192]{2,1,0:T(8,128)(2,1)S(1)} async-done(((bf16[8,64,192]{2,1,0:T(8,128)(2,1)}), bf16[8,64,192]{2,1,0:T(8,128)(2,1)S(1)}, u32[]{:S(2)}, u32[]{:S(2)}) %all-to-all-start) | async-done | bytes 196640 | tf_op jit(solution)/shard_map/all_to_all | solution.py:305
  113.3 0.7 reduce_sum.12
  113.9 0.1 broadcast_select_fusion.1
  114.0 0.9 convert_multiply_fusion
  (53 shorter events, 0.5 us)
Async XLA Ops:
  0.6 31.6 %copy-start.2 = (bf16[1,32,64,128]{3,2,1,0:T(8,128)(2,1)S(1)}, bf16[1,32,64,128]{3,2,1,0:T(8,128)(2,1)}, u32[]{:S(2)}) copy-start(bf16[1,32,64,128]{3,2,1,0:T(8,128)(2,1)} %param.11) | copy-start | bytes 1572868
  1.5 7.8 %collective-permute-start.2 = (bf16[8,1536]{1,0:T(8,128)(2,1)S(1)}, bf16[8,1536]{1,0:T(8,128)(2,1)S(1)}, u32[]{:S(2)}, u32[]{:S(2)}) collective-permute-start(bf16[8,1536]{1,0:T(8,128)(2,1)S(1)} %get-tuple-element.29), channel_id=1, source_target_pairs={{0,16},{16,32},{32,48},{48,64},{64,80},{80,96},{96,112},{112,128},... | collective-permute-start | bytes 73736 | tf_op jit(solution)/shard_map/ppermute | solution.py:16
  1.5 7.8 %collective-permute-start.3 = (bf16[8,1536]{1,0:T(8,128)(2,1)S(1)}, bf16[8,1536]{1,0:T(8,128)(2,1)S(1)}, u32[]{:S(2)}, u32[]{:S(2)}) collective-permute-start(bf16[8,1536]{1,0:T(8,128)(2,1)S(1)} %get-tuple-element.59), channel_id=1, source_target_pairs={{0,240},{16,0},{32,16},{48,32},{64,48},{80,64},{96,80},{112,96},{1... | collective-permute-start | bytes 73736 | tf_op jit(solution)/shard_map/ppermute | solution.py:16
  9.3 1.8 %copy-start = (bf16[5,192,1536]{2,1,0:T(8,128)(2,1)S(1)}, bf16[5,192,1536]{2,1,0:T(8,128)(2,1)}, u32[]{:S(2)}) copy-start(bf16[5,192,1536]{2,1,0:T(8,128)(2,1)} %conv_w.3) | copy-start | bytes 8847364
  11.1 0.9 copy-start.4
  12.1 7.0 %copy-start.3 = (bf16[1,32,64,128]{3,2,1,0:T(8,128)(2,1)S(1)}, bf16[1,32,64,128]{3,2,1,0:T(8,128)(2,1)}, u32[]{:S(2)}) copy-start(bf16[1,32,64,128]{3,2,1,0:T(8,128)(2,1)} %param.13) | copy-start | bytes 1572868
  12.1 40.2 %copy-start.5 = (bf16[3,3,128,128]{3,2,1,0:T(8,128)(2,1)S(1)}, bf16[3,3,128,128]{3,2,1,0:T(8,128)(2,1)}, u32[]{:S(2)}) copy-start(bf16[3,3,128,128]{3,2,1,0:T(8,128)(2,1)} %param.12) | copy-start | bytes 884740
  13.7 5.3 %collective-permute-start.6 = (bf16[40,256]{1,0:T(8,128)(2,1)S(1)}, bf16[40,256]{1,0:T(8,128)(2,1)S(1)}, u32[]{:S(2)}, u32[]{:S(2)}) collective-permute-start(bf16[40,256]{1,0:T(8,128)(2,1)S(1)} %shard_map.94), channel_id=1, source_target_pairs={{0,12},{2,14},{4,0},{6,2},{8,4},{10,6},{12,8},{14,10},{1,13},{3,15... | collective-permute-start | bytes 61448 | tf_op jit(solution)/shard_map/ppermute | solution.py:16
  16.8 5.0 %collective-permute-start.5 = (bf16[40,256]{1,0:T(8,128)(2,1)S(1)}, bf16[40,256]{1,0:T(8,128)(2,1)S(1)}, u32[]{:S(2)}, u32[]{:S(2)}) collective-permute-start(bf16[40,256]{1,0:T(8,128)(2,1)S(1)} %shard_map.94), channel_id=1, source_target_pairs={{0,4},{2,6},{4,8},{6,10},{8,12},{10,14},{12,0},{14,2},{1,5},{3,7},... | collective-permute-start | bytes 61448 | tf_op jit(solution)/shard_map/ppermute | solution.py:16
  16.8 5.3 %collective-permute-start.4 = (bf16[40,256]{1,0:T(8,128)(2,1)S(1)}, bf16[40,256]{1,0:T(8,128)(2,1)S(1)}, u32[]{:S(2)}, u32[]{:S(2)}) collective-permute-start(bf16[40,256]{1,0:T(8,128)(2,1)S(1)} %shard_map.94), channel_id=1, source_target_pairs={{0,8},{2,10},{4,12},{6,14},{8,0},{10,2},{12,4},{14,6},{1,9},{3,11}... | collective-permute-start | bytes 61448 | tf_op jit(solution)/shard_map/ppermute | solution.py:16
  22.1 5.4 %collective-permute-start.7 = (bf16[40,256]{1,0:T(8,128)(2,1)S(1)}, bf16[40,256]{1,0:T(8,128)(2,1)S(1)}, u32[]{:S(2)}, u32[]{:S(2)}) collective-permute-start(bf16[40,256]{1,0:T(8,128)(2,1)S(1)} %add_convert_fusion.7), channel_id=1, source_target_pairs={{0,2},{2,0},{4,6},{6,4},{8,10},{10,8},{12,14},{14,12},{1,3},{3,1},... | collective-permute-start | bytes 61448 | tf_op jit(solution)/shard_map/ppermute | solution.py:21
  24.4 7.8 %collective-permute-start = (bf16[5,64,128]{2,1,0:T(8,128)(2,1)S(1)}, bf16[5,64,128]{2,1,0:T(8,128)(2,1)S(1)}, u32[]{:S(2)}, u32[]{:S(2)}) collective-permute-start(bf16[5,64,128]{2,1,0:T(8,128)(2,1)S(1)} %pad_maximum_fusion.6), channel_id=1, source_target_pairs={{0,16},{16,32},{32,48},{48,64},{64,80},{80,96},{96,112},{112,128},... | collective-permute-start | bytes 245768 | tf_op jit(solution)/shard_map/ppermute | solution.py:16
  27.5 2.5 %collective-permute-start.8 = (bf16[35,128]{1,0:T(8,128)(2,1)S(1)}, bf16[35,128]{1,0:T(8,128)(2,1)S(1)}, u32[]{:S(2)}, u32[]{:S(2)}) collective-permute-start(bf16[35,128]{1,0:T(8,128)(2,1)S(1)} %slice_select_fusion.1), channel_id=1, source_target_pairs={{0,16},{16,0},{32,48},{48,32},{64,80},{80,64},{96,112},{112,96},{1... | collective-permute-start | bytes 26888 | tf_op jit(solution)/shard_map/ppermute | solution.py:21
  27.7 4.5 %collective-permute-start.1 = (bf16[5,64,128]{2,1,0:T(8,128)(2,1)S(1)}, bf16[5,64,128]{2,1,0:T(8,128)(2,1)S(1)}, u32[]{:S(2)}, u32[]{:S(2)}) collective-permute-start(bf16[5,64,128]{2,1,0:T(8,128)(2,1)S(1)} %pad_maximum_fusion.7), channel_id=1, source_target_pairs={{0,240},{16,0},{32,16},{48,32},{64,48},{80,64},{96,80},{112,96},{1... | collective-permute-start | bytes 245768 | tf_op jit(solution)/shard_map/ppermute | solution.py:16
  32.3 13.4 %collective-permute-start.10 = (bf16[38,8,128]{2,1,0:T(8,128)(2,1)S(1)}, bf16[38,8,128]{2,1,0:T(8,128)(2,1)S(1)}, u32[]{:S(2)}, u32[]{:S(2)}) collective-permute-start(bf16[38,8,128]{2,1,0:T(8,128)(2,1)S(1)} %get-tuple-element.31), channel_id=1, source_target_pairs={{0,2},{2,4},{4,6},{6,8},{8,10},{10,12},{12,14},{14,0},{1,3},{3,5},... | collective-permute-start | bytes 233480 | tf_op jit(solution)/shard_map/ppermute | solution.py:16
  34.5 11.2 %collective-permute-start.11 = (bf16[38,8,128]{2,1,0:T(8,128)(2,1)S(1)}, bf16[38,8,128]{2,1,0:T(8,128)(2,1)S(1)}, u32[]{:S(2)}, u32[]{:S(2)}) collective-permute-start(bf16[38,8,128]{2,1,0:T(8,128)(2,1)S(1)} %get-tuple-element.32), channel_id=1, source_target_pairs={{0,14},{2,0},{4,2},{6,4},{8,6},{10,8},{12,10},{14,12},{1,15},{3,1}... | collective-permute-start | bytes 233480 | tf_op jit(solution)/shard_map/ppermute | solution.py:16
  38.0 7.7 %collective-permute-start.9 = (bf16[70,128]{1,0:T(8,128)(2,1)S(1)}, bf16[70,128]{1,0:T(8,128)(2,1)S(1)}, u32[]{:S(2)}, u32[]{:S(2)}) collective-permute-start(bf16[70,128]{1,0:T(8,128)(2,1)S(1)} %pad_maximum_fusion.17), channel_id=1, source_target_pairs={{0,128},{16,144},{32,160},{48,176},{64,192},{80,208},{96,224},{112... | collective-permute-start | bytes 53768 | tf_op jit(solution)/shard_map/ppermute | solution.py:21
  45.7 4.5 %collective-permute-start.14 = (bf16[70,128]{1,0:T(8,128)(2,1)S(1)}, bf16[70,128]{1,0:T(8,128)(2,1)S(1)}, u32[]{:S(2)}, u32[]{:S(2)}) collective-permute-start(bf16[70,128]{1,0:T(8,128)(2,1)S(1)} %broadcast_select_fusion.2), channel_id=1, source_target_pairs={{0,32},{16,48},{32,0},{48,16},{64,96},{80,112},{96,64},{112,80},{1... | collective-permute-start | bytes 53768 | tf_op jit(solution)/shard_map/ppermute | solution.py:21
  45.8 4.7 %collective-permute-start.13 = (bf16[70,128]{1,0:T(8,128)(2,1)S(1)}, bf16[70,128]{1,0:T(8,128)(2,1)S(1)}, u32[]{:S(2)}, u32[]{:S(2)}) collective-permute-start(bf16[70,128]{1,0:T(8,128)(2,1)S(1)} %broadcast_select_fusion.2), channel_id=1, source_target_pairs={{0,64},{16,80},{32,96},{48,112},{64,0},{80,16},{96,32},{112,48},{1... | collective-permute-start | bytes 53768 | tf_op jit(solution)/shard_map/ppermute | solution.py:21
  46.4 5.9 %collective-permute-start.12 = (bf16[70,128]{1,0:T(8,128)(2,1)S(1)}, bf16[70,128]{1,0:T(8,128)(2,1)S(1)}, u32[]{:S(2)}, u32[]{:S(2)}) collective-permute-start(bf16[70,128]{1,0:T(8,128)(2,1)S(1)} %broadcast_select_fusion.2), channel_id=1, source_target_pairs={{0,96},{16,112},{32,64},{48,80},{64,32},{80,48},{96,0},{112,16},{1... | collective-permute-start | bytes 53768 | tf_op jit(solution)/shard_map/ppermute | solution.py:21
  52.3 40.4 %copy-start.1 = (bf16[5,192,1536]{2,1,0:T(8,128)(2,1)S(1)}, bf16[5,192,1536]{2,1,0:T(8,128)(2,1)}, u32[]{:S(2)}) copy-start(bf16[5,192,1536]{2,1,0:T(8,128)(2,1)} %conv_w.3) | copy-start | bytes 8847364
  58.8 1.4 %collective-permute-start.15 = (bf16[616,128]{1,0:T(8,128)(2,1)S(1)}, bf16[616,128]{1,0:T(8,128)(2,1)S(1)}, u32[]{:S(2)}, u32[]{:S(2)}) collective-permute-start(bf16[616,128]{1,0:T(8,128)(2,1)S(1)} %get-tuple-element.42), channel_id=1, source_target_pairs={{0,16},{16,0},{32,48},{48,32},{64,80},{80,64},{96,112},{112,96},{1... | collective-permute-start | bytes 473096 | tf_op jit(solution)/shard_map/ppermute | solution.py:21
  60.3 4.5 %collective-permute-start.16 = (bf16[184,128]{1,0:T(8,128)(2,1)S(1)}, bf16[184,128]{1,0:T(8,128)(2,1)S(1)}, u32[]{:S(2)}, u32[]{:S(2)}) collective-permute-start(bf16[184,128]{1,0:T(8,128)(2,1)S(1)} %get-tuple-element.73), channel_id=1, source_target_pairs={{0,32},{16,48},{32,0},{48,16},{64,96},{80,112},{96,64},{112,80},{1... | collective-permute-start | bytes 141320 | tf_op jit(solution)/shard_map/ppermute | solution.py:21
  60.8 6.7 %collective-permute-start.17 = (bf16[184,128]{1,0:T(8,128)(2,1)S(1)}, bf16[184,128]{1,0:T(8,128)(2,1)S(1)}, u32[]{:S(2)}, u32[]{:S(2)}) collective-permute-start(bf16[184,128]{1,0:T(8,128)(2,1)S(1)} %get-tuple-element.74), channel_id=1, source_target_pairs={{0,64},{16,80},{32,96},{48,112},{64,0},{80,16},{96,32},{112,48},{1... | collective-permute-start | bytes 141320 | tf_op jit(solution)/shard_map/ppermute | solution.py:21
  64.4 5.9 %collective-permute-start.18 = (bf16[184,128]{1,0:T(8,128)(2,1)S(1)}, bf16[184,128]{1,0:T(8,128)(2,1)S(1)}, u32[]{:S(2)}, u32[]{:S(2)}) collective-permute-start(bf16[184,128]{1,0:T(8,128)(2,1)S(1)} %get-tuple-element.75), channel_id=1, source_target_pairs={{0,96},{16,112},{32,64},{48,80},{64,32},{80,48},{96,0},{112,16},{1... | collective-permute-start | bytes 141320 | tf_op jit(solution)/shard_map/ppermute | solution.py:21
  70.3 8.5 %collective-permute-start.19 = (bf16[184,128]{1,0:T(8,128)(2,1)S(1)}, bf16[184,128]{1,0:T(8,128)(2,1)S(1)}, u32[]{:S(2)}, u32[]{:S(2)}) collective-permute-start(bf16[184,128]{1,0:T(8,128)(2,1)S(1)} %add_convert_fusion.4), channel_id=1, source_target_pairs={{0,128},{16,144},{32,160},{48,176},{64,192},{80,208},{96,224},{112... | collective-permute-start | bytes 141320 | tf_op jit(solution)/shard_map/ppermute | solution.py:21
  78.9 5.5 %collective-permute-start.21 = (bf16[224,128]{1,0:T(8,128)(2,1)S(1)}, bf16[224,128]{1,0:T(8,128)(2,1)S(1)}, u32[]{:S(2)}, u32[]{:S(2)}) collective-permute-start(bf16[224,128]{1,0:T(8,128)(2,1)S(1)} %pad_maximum_fusion.16), channel_id=1, source_target_pairs={{0,4},{2,6},{4,8},{6,10},{8,12},{10,14},{12,0},{14,2},{1,5},{3,7},... | collective-permute-start | bytes 172040 | tf_op jit(solution)/shard_map/ppermute | solution.py:16
  79.0 6.2 %collective-permute-start.20 = (bf16[224,128]{1,0:T(8,128)(2,1)S(1)}, bf16[224,128]{1,0:T(8,128)(2,1)S(1)}, u32[]{:S(2)}, u32[]{:S(2)}) collective-permute-start(bf16[224,128]{1,0:T(8,128)(2,1)S(1)} %pad_maximum_fusion.16), channel_id=1, source_target_pairs={{0,8},{2,10},{4,12},{6,14},{8,0},{10,2},{12,4},{14,6},{1,9},{3,11}... | collective-permute-start | bytes 172040 | tf_op jit(solution)/shard_map/ppermute | solution.py:16
  82.5 4.2 %collective-permute-start.22 = (bf16[224,128]{1,0:T(8,128)(2,1)S(1)}, bf16[224,128]{1,0:T(8,128)(2,1)S(1)}, u32[]{:S(2)}, u32[]{:S(2)}) collective-permute-start(bf16[224,128]{1,0:T(8,128)(2,1)S(1)} %pad_maximum_fusion.16), channel_id=1, source_target_pairs={{0,12},{2,14},{4,0},{6,2},{8,4},{10,6},{12,8},{14,10},{1,13},{3,15... | collective-permute-start | bytes 172040 | tf_op jit(solution)/shard_map/ppermute | solution.py:16
  86.7 5.8 %collective-permute-start.23 = (bf16[224,128]{1,0:T(8,128)(2,1)S(1)}, bf16[224,128]{1,0:T(8,128)(2,1)S(1)}, u32[]{:S(2)}, u32[]{:S(2)}) collective-permute-start(bf16[224,128]{1,0:T(8,128)(2,1)S(1)} %add_convert_fusion.2), channel_id=1, source_target_pairs={{0,2},{2,0},{4,6},{6,4},{8,10},{10,8},{12,14},{14,12},{1,3},{3,1},... | collective-permute-start | bytes 172040 | tf_op jit(solution)/shard_map/ppermute | solution.py:21
  92.5 4.0 %collective-permute-start.24 = (bf16[144,128]{1,0:T(8,128)(2,1)S(1)}, bf16[144,128]{1,0:T(8,128)(2,1)S(1)}, u32[]{:S(2)}, u32[]{:S(2)}) collective-permute-start(bf16[144,128]{1,0:T(8,128)(2,1)S(1)} %slice.144), channel_id=1, source_target_pairs={{0,1},{1,0},{2,3},{3,2},{4,5},{5,4},{6,7},{7,6},{8,9},{9,8},{10,11... | collective-permute-start | bytes 110600 | tf_op jit(solution)/shard_map/ppermute | solution.py:21
  96.6 7.9 %collective-permute-start.27 = (bf16[144,128]{1,0:T(8,128)(2,1)S(1)}, bf16[144,128]{1,0:T(8,128)(2,1)S(1)}, u32[]{:S(2)}, u32[]{:S(2)}) collective-permute-start(bf16[144,128]{1,0:T(8,128)(2,1)S(1)} %add_convert_fusion.5), channel_id=1, source_target_pairs={{0,96},{16,112},{32,64},{48,80},{64,32},{80,48},{96,0},{112,16},{1... | collective-permute-start | bytes 110600 | tf_op jit(solution)/shard_map/ppermute | solution.py:21
  97.0 7.5 %collective-permute-start.26 = (bf16[144,128]{1,0:T(8,128)(2,1)S(1)}, bf16[144,128]{1,0:T(8,128)(2,1)S(1)}, u32[]{:S(2)}, u32[]{:S(2)}) collective-permute-start(bf16[144,128]{1,0:T(8,128)(2,1)S(1)} %add_convert_fusion.5), channel_id=1, source_target_pairs={{0,64},{16,80},{32,96},{48,112},{64,0},{80,16},{96,32},{112,48},{1... | collective-permute-start | bytes 110600 | tf_op jit(solution)/shard_map/ppermute | solution.py:21
  97.0 7.5 %collective-permute-start.25 = (bf16[144,128]{1,0:T(8,128)(2,1)S(1)}, bf16[144,128]{1,0:T(8,128)(2,1)S(1)}, u32[]{:S(2)}, u32[]{:S(2)}) collective-permute-start(bf16[144,128]{1,0:T(8,128)(2,1)S(1)} %add_convert_fusion.5), channel_id=1, source_target_pairs={{0,32},{16,48},{32,0},{48,16},{64,96},{80,112},{96,64},{112,80},{1... | collective-permute-start | bytes 110600 | tf_op jit(solution)/shard_map/ppermute | solution.py:21
  101.0 12.2 %all-to-all-start = ((bf16[8,64,192]{2,1,0:T(8,128)(2,1)}), bf16[8,64,192]{2,1,0:T(8,128)(2,1)S(1)}, u32[]{:S(2)}, u32[]{:S(2)}) async-start(bf16[8,64,192]{2,1,0:T(8,128)(2,1)} %shard_map.96), calls=%async_computation | async-start | bytes 524288 | tf_op jit(solution)/shard_map/all_to_all | solution.py:305
  104.6 9.3 %collective-permute-start.28 = (bf16[576,128]{1,0:T(8,128)(2,1)S(1)}, bf16[576,128]{1,0:T(8,128)(2,1)S(1)}, u32[]{:S(2)}, u32[]{:S(2)}) collective-permute-start(bf16[576,128]{1,0:T(8,128)(2,1)S(1)} %pad_maximum_fusion.1), channel_id=1, source_target_pairs={{0,16},{16,0},{32,48},{48,32},{64,80},{80,64},{96,112},{112,96},{1... | collective-permute-start | bytes 442376 | tf_op jit(solution)/shard_map/ppermute | solution.py:21

commit v4 on v3

--- a/solution.py
+++ b/solution.py
@@ -39,9 +39,9 @@
 
 
 def pair_kernel(
-    flags, pair, cot, top, bottom, left, right, rowp, bins, weight,
+    flags, pair, cot, top, bottom, halos, rowp, bins, weight, turned,
     out, keep, send, rowg,
-    zwide, z3, cots, qwide, q3, wgrad, line, colp, turned,
+    zwide, z3, cots, qwide, q3, wgrad, line, colp, packed, left, right,
 ):
     chans = 128
     has_up, has_down, has_left, has_right, core = (flags[i] for i in range(5))
@@ -52,8 +52,11 @@
     colp[5:75] = bins[0:70]
     colp[85:88] = bins[0:3]
     colp[88:89] = bins[3:4]
-    for at in range(0, 9 * chans, chans):
-        turned[at : at + chans] = up(weight[at : at + chans]).T.astype(BF)
+
+    packed[...] = up(halos[...])
+    for i in range(38):
+        left[i, 0:5] = packed[5 * i : 5 * i + 5]
+        right[i, 0:5] = packed[192 + 5 * i : 197 + 5 * i]
 
     zwide[:, 0:8] = jnp.zeros((38, 8, chans), F32)
     zwide[:, 72:96] = jnp.zeros((38, 24, chans), F32)
@@ -63,10 +66,10 @@
         scaled = rowp[first : first + count][:, None, :] * colp[lo:hi][None, :, :]
         return up((up(values) + scaled).astype(BF))
 
-    zwide[0:3, 8:72] = jnp.where(has_up > 0, zeta(top[0:3], 0, 3, 8, 72), 0.0)
-    zwide[35:38, 8:72] = jnp.where(has_down > 0, zeta(bottom[0:3], 35, 3, 8, 72), 0.0)
-    cots[0:2, 0:64] = jnp.where(has_up > 0, up(top[3:5]), 0.0)
-    cots[34:36, 0:64] = jnp.where(has_down > 0, up(bottom[3:5]), 0.0)
+    zwide[0:3, 8:72] = jnp.where(has_up > 0, zeta(top[3:6], 0, 3, 8, 72), 0.0)
+    zwide[35:38, 8:72] = jnp.where(has_down > 0, zeta(bottom[3:6], 35, 3, 8, 72), 0.0)
+    cots[0:2, 0:64] = jnp.where(has_up > 0, up(top[6:8]), 0.0)
+    cots[34:36, 0:64] = jnp.where(has_down > 0, up(bottom[6:8]), 0.0)
     edge = jnp.where(row_ok & (has_left > 0), zeta(left[:, 0:3], 0, 38, 5, 8), 0.0)
     zwide[:, 5:8] = edge
     zwide[:, 85:88] = edge
@@ -143,14 +146,50 @@
             send[576:610] = line[32 - 32 * mine : 66 - 32 * mine].astype(BF)
 
 
-def conv_kernel(flags, fine, before, after, conv_w, proj, part, wide):
+def run_all(copies):
+    for copy in copies:
+        copy.start()
+    for copy in copies:
+        copy.wait()
+
+
+def turn_kernel(weight, turned):
+    for at in range(0, weight.shape[0], 128):
+        turned[at : at + 128] = up(weight[at : at + 128]).T.astype(BF)
+
+
+def begin_kernel(given, taken):
+    taken[...] = given[...]
+
+
+def ends_kernel(fine, pair, cot, begun, to_next, to_last, sems):
+    copies = []
+
+    def add(source, target):
+        copies.append(pltpu.make_async_copy(source, target, sems.at[len(copies)]))
+
+    blocks = fine.shape[1] // 128
+    for ref, spots, pair_rows, cot_rows in ((to_next, 48, 29, 30), (to_last, 0, 0, 0)):
+        for j in range(blocks):
+            add(fine.at[spots : spots + 16, 128 * j : 128 * j + 128], ref.at[j // 4, 16 * (j % 4) : 16 * (j % 4) + 16])
+        add(pair.at[pair_rows : pair_rows + 3], ref.at[3:6])
+        add(cot.at[cot_rows : cot_rows + 2], ref.at[6:8])
+    run_all(copies)
+
+
+def conv_kernel(
+    flags, fine, top, bottom, conv_w, proj_a, proj_b, pair, cot,
+    to_next, to_last, wide, edge,
+):
     blocks = wide.shape[0]
     wide[:, 80:88] = jnp.zeros((blocks, 8, 128), F32)
     for j in range(blocks):
         lanes = slice(128 * j, 128 * j + 128)
-        wide[j, 0:8] = jnp.where(flags[0] > 0, up(before[:, lanes]), 0.0)
+        spots = up(top[j // 4, 16 * (j % 4) : 16 * (j % 4) + 16])
+        wide[j, 0:8] = jnp.where(flags[0] > 0, spots[8:], 0.0)
         wide[j, 8:72] = up(fine[:, lanes])
-        wide[j, 72:80] = jnp.where(flags[1] > 0, up(after[:, lanes]), 0.0)
+        spots = up(bottom[j // 4, 16 * (j % 4) : 16 * (j % 4) + 16])
+        wide[j, 72:80] = jnp.where(flags[1] > 0, spots[:8], 0.0)
     seq = jnp.zeros((40, conv_w.shape[1]), F32)
     for tap in range(5):
         window = jnp.concatenate([wide[j, pl.ds(tap, 40, stride=2)] for j in range(blocks)], axis=1)
@@ -160,12 +199,31 @@
     rows = lax.broadcasted_iota(jnp.int32, (40, 1), 0)
     ok = ((rows >= 3) | (flags[0] > 0)) & ((rows < 35) | (flags[1] > 0)) & (rows < 38)
     seq = jnp.where(ok, seq, 0.0).astype(BF)
-    part[...] = jnp.dot(seq, proj[...], preferred_element_type=F32).astype(BF)
-
-
-def grad_conv_kernel(sums, proj, conv_w, parts, seqg, whole):
-    pair = jnp.concatenate([sums[0:40], sums[40:80]], axis=1)
-    grad = lax.dot_general(pair, proj[...], (((1,), (1,)), ((), ())), preferred_element_type=F32)
+    rowp = jnp.dot(seq, proj_a[...], preferred_element_type=F32).astype(BF)
+    colp = jnp.dot(seq, proj_b[...], preferred_element_type=F32).astype(BF)
+    for ref in (to_next, to_last):
+        ref[0:40] = rowp
+        ref[40:80] = colp
+
+    edge[...] = jnp.zeros(edge.shape, F32)
+    for ref, pair_cols, cot_cols in ((to_next, (61, 64), (62, 64)), (to_last, (0, 3), (0, 2))):
+        for i in range(38):
+            if i < 3:
+                ours, theirs = top[i + 3 : i + 4], top[i + 5 : i + 6]
+            elif i < 35:
+                ours, theirs = pair[i - 3 : i - 2], cot[i - 3 : i - 2]
+            else:
+                ours, theirs = bottom[i - 32 : i - 31], bottom[min(i - 29, 7) : min(i - 28, 8)]
+            edge[5 * i : 5 * i + 3] = up(ours[0, pair_cols[0] : pair_cols[1]])
+            edge[5 * i + 3 : 5 * i + 5] = up(theirs[0, cot_cols[0] : cot_cols[1]])
+        ref[80:272] = edge[...].astype(BF)
+
+
+def grad_conv_kernel(sums, proj_a, proj_b, conv_w, parts, seqg, whole):
+    grad = sum(
+        lax.dot_general(x, proj[...], (((1,), (1,)), ((), ())), preferred_element_type=F32)
+        for x, proj in ((sums[0:40], proj_a), (sums[40:80], proj_b))
+    )
     seqg[...] = up(grad.astype(BF))
     ahead, here, behind = (seqg[at : at + 32].astype(BF) for at in (2, 1, 0))
 
@@ -188,33 +246,72 @@
 SMEM = pl.BlockSpec(memory_space=pltpu.SMEM)
 
 
-def conv_forward(flags, fine, before, after, conv_w, proj):
-    chans = fine.shape[1]
+HBM = pl.BlockSpec(memory_space=pltpu.HBM)
+
+
+def transposed(weight):
+    return pl.pallas_call(
+        turn_kernel,
+        out_shape=jax.ShapeDtypeStruct(weight.shape, BF),
+        in_specs=[VMEM],
+        out_specs=VMEM,
+        compiler_params=pltpu.CompilerParams(vmem_limit_bytes=4 * 1024 * 1024),
+        cost_estimate=pl.CostEstimate(flops=40000000000, bytes_accessed=600000, transcendentals=0),
+    )(weight)
+
+
+def begin(seed):
+    return pl.pallas_call(
+        begin_kernel,
+        out_shape=jax.ShapeDtypeStruct(seed.shape, seed.dtype),
+        in_specs=[VMEM],
+        out_specs=VMEM,
+        compiler_params=pltpu.CompilerParams(vmem_limit_bytes=1024 * 1024),
+        cost_estimate=pl.CostEstimate(flops=40000000000, bytes_accessed=8192, transcendentals=0),
+    )(seed)
+
+
+def ends(fine, pair, cot, begun):
+    payload = jax.ShapeDtypeStruct((8, 64, 128), BF)
+    return pl.pallas_call(
+        ends_kernel,
+        out_shape=(payload, payload),
+        in_specs=[VMEM] * 4,
+        out_specs=(VMEM, VMEM),
+        scratch_shapes=[pltpu.SemaphoreType.DMA((2 * (fine.shape[1] // 128) + 4,))],
+        compiler_params=pltpu.CompilerParams(vmem_limit_bytes=6 * 1024 * 1024),
+        cost_estimate=pl.CostEstimate(flops=0, bytes_accessed=600000, transcendentals=0),
+    )(fine, pair, cot, begun)
+
+
+def conv_forward(*arrays):
+    chans = arrays[1].shape[1]
+    payload = jax.ShapeDtypeStruct((272, 128), BF)
     return pl.pallas_call(
         conv_kernel,
-        out_shape=jax.ShapeDtypeStruct((40, proj.shape[1]), BF),
-        in_specs=[SMEM] + [VMEM] * 5,
-        out_specs=VMEM,
-        scratch_shapes=[pltpu.VMEM((chans // 128, 88, 128), F32)],
+        out_shape=(payload, payload),
+        in_specs=[SMEM] + [VMEM] * 8,
+        out_specs=(VMEM, VMEM),
+        scratch_shapes=[pltpu.VMEM((chans // 128, 88, 128), F32), pltpu.VMEM((192, 128), F32)],
         compiler_params=pltpu.CompilerParams(vmem_limit_bytes=12 * 1024 * 1024),
         cost_estimate=pl.CostEstimate(flops=120000000, bytes_accessed=3500000, transcendentals=0),
-    )(flags, fine, before, after, conv_w, proj)
-
-
-def conv_backward(sums, proj, conv_w):
+    )(*arrays)
+
+
+def conv_backward(sums, proj_a, proj_b, conv_w):
     outchans, chans = conv_w.shape[1:]
     return pl.pallas_call(
         grad_conv_kernel,
         out_shape=jax.ShapeDtypeStruct((8, 64, outchans), BF),
-        in_specs=[VMEM] * 3,
+        in_specs=[VMEM] * 4,
         out_specs=VMEM,
         scratch_shapes=[pltpu.VMEM((40, outchans), F32), pltpu.VMEM((chans // 128, 64, 128), F32)],
         compiler_params=pltpu.CompilerParams(vmem_limit_bytes=12 * 1024 * 1024),
         cost_estimate=pl.CostEstimate(flops=120000000, bytes_accessed=3500000, transcendentals=0),
-    )(sums, proj, conv_w)
-
-
-def pair_block(flags, pair, cot, top, bottom, left, right, rowp, bins, weight):
+    )(sums, proj_a, proj_b, conv_w)
+
+
+def pair_block(flags, pair, cot, top, bottom, halos, rowp, bins, weight, turned):
     chans = 128
     return pl.pallas_call(
         pair_kernel,
@@ -235,11 +332,13 @@
             pltpu.VMEM((9 * chans, chans), F32),
             pltpu.VMEM((72, chans), F32),
             pltpu.VMEM((96, chans), F32),
-            pltpu.VMEM((9 * chans, chans), BF),
+            pltpu.VMEM((384, chans), F32),
+            pltpu.VMEM((38, 8, chans), F32),
+            pltpu.VMEM((38, 8, chans), F32),
         ],
         compiler_params=pltpu.CompilerParams(vmem_limit_bytes=24 * 1024 * 1024),
         cost_estimate=pl.CostEstimate(flops=2500000000, bytes_accessed=4000000, transcendentals=700000),
-    )(flags, pair, cot, top, bottom, left, right, rowp, bins, weight)
+    )(flags, pair, cot, top, bottom, halos, rowp, bins, weight, turned)
 
 
 def local(fine, conv_w, proj_a, proj_b, pair_in, pair_w, cotangent):
@@ -252,36 +351,31 @@
 
     fine, pair, cot = fine[0], pair_in[0], cotangent[0]
     apart = zpos ^ col
-    scalars = (core == 0, (apart & 4) == 4, [(apart & 3) == k for k in (1, 2, 3)], zpos == col, [(zpos ^ k) & 3 for k in range(4)])
-    edge, flags, scalars = lax.optimization_barrier((fine[-8:], flags, scalars))
-    is_first, is_far, is_near, is_root, places = scalars
-    before = shift(edge, "row", 1)
-    after = shift(fine[:8], "row", -1)
-    top = shift(jnp.concatenate([pair[29:], cot[30:]]), "row", 1)
-    bottom = shift(jnp.concatenate([pair[:3], cot[:2]]), "row", -1)
-    proj = jnp.concatenate([proj_a, proj_b], axis=1)
-    part = conv_forward(flags, fine, before, after, conv_w, proj)
-
-    tall_pair = jnp.concatenate([top[:3], pair, bottom[:3]])
-    tall_cot = jnp.concatenate([top[2:], cot, bottom[3:], bottom[4:]])
-    left = jnp.concatenate([tall_pair[:, 61:], tall_cot[:, 62:], tall_cot[:, :3]], axis=1)
-    right = jnp.concatenate([tall_pair[:, :3], tall_cot[:, :5]], axis=1)
-
-    both = up(sum_flip(sum_y(part), "col", 1))
-    rowp, colp_here = both[:, :pairs], both[:, pairs:].astype(BF)
+    scalars = (core == 0, (apart & 4) == 4, [(apart & 3) == k for k in (1, 2, 3)], zpos == col, [(zpos ^ k) & 3 for k in range(4)], col % 2 == 1)
+    seed, flags, scalars = lax.optimization_barrier((jnp.zeros((8, 128), F32), flags, scalars))
+    is_first, is_far, is_near, is_root, places, is_odd = scalars
+    down, above = ends(fine, pair, cot, begin(seed))
+    top, bottom = shift(down, "row", 1), shift(above, "row", -1)
+    weight = pair_w.reshape(9 * pairs, pairs)
+    top, bottom, turned = lax.optimization_barrier((top, bottom, transposed(weight)))
+    to_next, to_last = conv_forward(flags, fine, top, bottom, conv_w, proj_a, proj_b, pair, cot)
+
+    across, from_last, from_next = shift(to_next[:80], "col", 4), shift(to_next, "col", 2), shift(to_last, "col", -2)
+    both = ((up(to_next[:80]) + up(across)) + (up(from_last[:80]) + up(from_next[:80]))).astype(BF)
+    to_left = jnp.where(is_odd, from_last[80:], to_next[80:])
+    to_right = jnp.where(is_odd, to_last[80:], from_next[80:])
+    other = flip(jnp.concatenate([both, to_left, to_right]), "col", 1)
+    both, halos = up(both) + up(other[:80]), other[80:]
+    rowp, colp_here = both[:40], both[40:].astype(BF)
 
     mine = jnp.where(is_first, colp_here[:35], colp_here[3:38])
     other = flip(mine, "row", 1)
     colp = jnp.concatenate([jnp.where(is_first, mine, other), jnp.where(is_first, other, mine)])
-    colp, left, right = lax.optimization_barrier((colp, left, right))
-    far, left, right = flip(colp, "row", 8), shift(left, "col", 1), shift(right, "col", -1)
-    far, left, right = lax.optimization_barrier((far, left, right))
-    colp = jnp.where(is_far, far, colp)
+    colp = jnp.where(is_far, flip(colp, "row", 8), colp)
     near = [flip(colp, "row", 2 * k) for k in (1, 2, 3)]
     for k in (1, 2, 3):
         colp = jnp.where(is_near[k - 1], near[k - 1], colp)
-    weight = pair_w.reshape(9 * pairs, pairs)
-    out, keep, send, rowg = pair_block(flags, pair, cot, top, bottom, left, right, rowp, up(colp), weight)
+    out, keep, send, rowg = pair_block(flags, pair, cot, top, bottom, halos, rowp, up(colp), weight, turned)
 
     total = (keep + up(flip(send, "row", 1))).astype(BF)
     half, colg = total[:576].reshape(4, 144, pairs), total[576:]
@@ -299,7 +393,7 @@
     total = sum_y(jnp.concatenate([total[:144], rowg, colg]))
     total = sum_flip(total, "col", 1)
     quart, sums = total[:144], total[144:]
-    parts = conv_backward(sums, proj, conv_w)
+    parts = conv_backward(sums, proj_a, proj_b, conv_w)
     quart = sum_flip(quart, "batch", 1)
     parts, quart = lax.optimization_barrier((parts, quart))
     parts = lax.all_to_all(parts, "col", 0, 0, tiled=True)

time: 115 us -> 108 us (0.939)
  local copies, waits for them, and re-layouts: 6.14 us -> 1.31 us
  waiting for transfers between devices: 47.6 us -> 44 us
    ppermute x12 -> x8, starting transfers between devices: 22.4 us -> 15.5 us  [shift(): lax.ppermute(x, axis, [(i, (i + step) % count) for i in range(count)])]
    ppermute x17, starting transfers between devices: 22.5 us -> 29 us  [flip(): return lax.ppermute(x, axis, [(i, i ^ bit) for i in range(count)])]
    ppermute x17, waiting for transfers between devices: 29.8 us -> 25.4 us  [flip(): return lax.ppermute(x, axis, [(i, i ^ bit) for i in range(count)])]
    unnamed x13 -> x14, local copies, waits for them, and re-layouts: 3.58 us -> 1.22 us
    slice x7 -> x3, local copies, waits for them, and re-layouts: 1.66 us -> 0.01 us  [the longest x1 0.01 us: local(): both, halos = (up(both) + up(other[:80]), other[80:])]
    ppermute x12 -> x8, waiting for transfers between devices: 9.14 us -> 10 us  [shift(): lax.ppermute(x, axis, [(i, (i + step) % count) for i in range(count)])]
    pallas_call x1 -> x4, Pallas kernels: 1.69 us -> 2.48 us  [the longest x1 1.78 us: conv_forward(): pl.pallas_call(conv_kernel, out_shape=(payload, payload), in_specs=[SMEM]...]
  transfers between devices with their start and end apart: 30 -> 26, of which waited for: 17 -> 18; matrix products, arithmetic and copies ran while one was open for 3% -> 1% of each run, Pallas kernels for 1% -> 2%
where the time goes in v4:
time: 108 us
  starting transfers between devices  48.9 us (45%)
  waiting for transfers between devices  44 us (41%)
  Pallas kernels  10.6 us (10%)
  other arithmetic  1.92 us (2%)
  local copies, waits for them, and re-layouts  1.31 us (1%)
    ppermute x17, starting transfers between devices, flip(): return lax.ppermute(x, axis, [(i, i ^ bit) for i in range(count)])  29 us
    ppermute x17, waiting for transfers between devices, flip(): return lax.ppermute(x, axis, [(i, i ^ bit) for i in range(count)])  25.4 us
    ppermute x8, starting transfers between devices, shift(): lax.ppermute(x, axis, [(i, (i + step) % count) for i in range(count)])  15.5 us
    ppermute x8, waiting for transfers between devices, shift(): lax.ppermute(x, axis, [(i, (i + step) % count) for i in range(count)])  10 us
    all_to_all x1, waiting for transfers between devices, local(): parts = lax.all_to_all(parts, 'col', 0, 0, tiled=True)  8.58 us
    pallas_call x1, Pallas kernels, pair_block(): pl.pallas_call(pair_kernel, out_shape=(jax.ShapeDtypeStruct((32, 64, chan...  6.49 us
    all_to_all x1, starting transfers between devices, local(): parts = lax.all_to_all(parts, 'col', 0, 0, tiled=True)  4.35 us
  transfers between devices with their start and end apart: 26, of which 18 were waited for; matrix products, arithmetic and copies ran while one was open for 1% of the time, Pallas kernels for 2%

profile of v4, /device:TPU:2, one launch (start us, length us, event | category | flops | bytes accessed | tf_op | source)
XLA Modules:
  0.0 107.7 jit_solution(14556773465227394489)
XLA Ops:
  0.7 0.0 copy-start.1
  0.7 0.0 copy-start.2
  0.7 0.0 copy-start.3
  0.8 0.0 copy-start.6
  0.8 1.0 copy-done.1
  1.8 0.2 copy-done.2
  1.9 0.0 copy-done.3
  2.0 0.5 shard_map.95
  2.5 0.0 collective-permute-start
  2.5 5.3 %collective-permute-start.1 = (bf16[8,64,128]{2,1,0:T(8,128)(2,1)S(1)}, bf16[8,64,128]{2,1,0:T(8,128)(2,1)S(1)}, u32[]{:S(2)}, u32[]{:S(2)}) collective-permute-start(bf16[8,64,128]{2,1,0:T(8,128)(2,1)S(1)} %get-tuple-element.32), channel_id=1, source_target_pairs={{0,240},{16,0},{32,16},{48,32},{64,48},{80,64},{96,80},{112,96},{1... | collective-permute-start | bytes 393224 | tf_op jit(solution)/shard_map/ppermute | solution.py:16
  7.8 0.2 shard_map.96.turned
  8.0 2.4 %collective-permute-done.top = bf16[8,64,128]{2,1,0:T(8,128)(2,1)S(1)} collective-permute-done((bf16[8,64,128]{2,1,0:T(8,128)(2,1)S(1)}, bf16[8,64,128]{2,1,0:T(8,128)(2,1)S(1)}, u32[]{:S(2)}, u32[]{:S(2)}) %collective-permute-start) | collective-permute-done | bytes 131104 | tf_op jit(solution)/shard_map/ppermute | solution.py:16
  10.5 0.0 collective-permute-done.1.bottom
  10.5 1.8 %shard_map.97 = (bf16[272,128]{1,0:T(8,128)(2,1)S(1)}, bf16[272,128]{1,0:T(8,128)(2,1)S(1)}) custom-call(s32[8]{0:T(128)S(1)} %select_convert_fusion.1.flags, bf16[64,1536]{1,0:T(8,128)(2,1)S(1)} %bitcast.35, bf16[8,64,128]{2,1,0:T(8,128)(2,1)S(1)} %collective-permute-done.top, bf16[8,64,128]{2,1,0:T(8,128)(2,1)S(1)} %collective-permute-done.1.bottom, ...), custom_call_target="tpu_custom_call" | custom-call | flops 120000000 | bytes 3500000 | tf_op jit(solution)/shard_map/pallas_call | solution.py:290
  12.3 3.1 %collective-permute-start.4 = (bf16[272,128]{1,0:T(8,128)(2,1)S(1)}, bf16[272,128]{1,0:T(8,128)(2,1)S(1)}, u32[]{:S(2)}, u32[]{:S(2)}) collective-permute-start(bf16[272,128]{1,0:T(8,128)(2,1)S(1)} %get-tuple-element.36), channel_id=1, source_target_pairs={{0,12},{2,14},{4,0},{6,2},{8,4},{10,6},{12,8},{14,10},{1,13},{3,15... | collective-permute-start | bytes 208904 | tf_op jit(solution)/shard_map/ppermute | solution.py:16
  15.4 0.0 collective-permute-start.3
  15.4 2.2 %collective-permute-start.2 = (bf16[80,128]{1,0:T(8,128)(2,1)S(1)}, bf16[80,128]{1,0:T(8,128)(2,1)S(1)}, u32[]{:S(2)}, u32[]{:S(2)}) collective-permute-start(bf16[80,128]{1,0:T(8,128)(2,1)S(1)} %slice.59), channel_id=1, source_target_pairs={{0,8},{2,10},{4,12},{6,14},{8,0},{10,2},{12,4},{14,6},{1,9},{3,11}... | collective-permute-start | bytes 61448 | tf_op jit(solution)/shard_map/ppermute | solution.py:16
  17.6 0.0 collective-permute-done.4
  17.6 3.5 %collective-permute-done.3 = bf16[272,128]{1,0:T(8,128)(2,1)S(1)} collective-permute-done((bf16[272,128]{1,0:T(8,128)(2,1)S(1)}, bf16[272,128]{1,0:T(8,128)(2,1)S(1)}, u32[]{:S(2)}, u32[]{:S(2)}) %collective-permute-start.3) | collective-permute-done | bytes 69664 | tf_op jit(solution)/shard_map/ppermute | solution.py:16
  21.1 0.0 collective-permute-done.2
  21.2 2.2 %collective-permute-start.5 = (bf16[464,128]{1,0:T(8,128)(2,1)S(1)}, bf16[464,128]{1,0:T(8,128)(2,1)S(1)}, u32[]{:S(2)}, u32[]{:S(2)}) collective-permute-start(bf16[464,128]{1,0:T(8,128)(2,1)S(1)} %pad_maximum_fusion.2), channel_id=1, source_target_pairs={{0,2},{2,0},{4,6},{6,4},{8,10},{10,8},{12,14},{14,12},{1,3},{3,1},... | collective-permute-start | bytes 356360 | tf_op jit(solution)/shard_map/ppermute | solution.py:21
  23.4 4.2 %collective-permute-done.5 = bf16[464,128]{1,0:T(8,128)(2,1)S(1)} collective-permute-done((bf16[464,128]{1,0:T(8,128)(2,1)S(1)}, bf16[464,128]{1,0:T(8,128)(2,1)S(1)}, u32[]{:S(2)}, u32[]{:S(2)}) %collective-permute-start.5) | collective-permute-done | bytes 118816 | tf_op jit(solution)/shard_map/ppermute | solution.py:21
  27.6 0.1 collective-permute-start.6
  27.7 1.2 %collective-permute-done.6 = bf16[35,128]{1,0:T(8,128)(2,1)S(1)} collective-permute-done((bf16[35,128]{1,0:T(8,128)(2,1)S(1)}, bf16[35,128]{1,0:T(8,128)(2,1)S(1)}, u32[]{:S(2)}, u32[]{:S(2)}) %collective-permute-start.6) | collective-permute-done | bytes 8992 | tf_op jit(solution)/shard_map/ppermute | solution.py:21
  28.9 4.9 %collective-permute-start.7 = (bf16[70,128]{1,0:T(8,128)(2,1)S(1)}, bf16[70,128]{1,0:T(8,128)(2,1)S(1)}, u32[]{:S(2)}, u32[]{:S(2)}) collective-permute-start(bf16[70,128]{1,0:T(8,128)(2,1)S(1)} %pad_maximum_fusion.8), channel_id=1, source_target_pairs={{0,128},{16,144},{32,160},{48,176},{64,192},{80,208},{96,224},{112... | collective-permute-start | bytes 53768 | tf_op jit(solution)/shard_map/ppermute | solution.py:21
  33.9 2.8 %collective-permute-done.7 = bf16[70,128]{1,0:T(8,128)(2,1)S(1)} collective-permute-done((bf16[70,128]{1,0:T(8,128)(2,1)S(1)}, bf16[70,128]{1,0:T(8,128)(2,1)S(1)}, u32[]{:S(2)}, u32[]{:S(2)}) %collective-permute-start.7) | collective-permute-done | bytes 17952 | tf_op jit(solution)/shard_map/ppermute | solution.py:21
  36.7 0.1 collective-permute-start.10
  36.8 3.1 %collective-permute-start.9 = (bf16[70,128]{1,0:T(8,128)(2,1)S(1)}, bf16[70,128]{1,0:T(8,128)(2,1)S(1)}, u32[]{:S(2)}, u32[]{:S(2)}) collective-permute-start(bf16[70,128]{1,0:T(8,128)(2,1)S(1)} %broadcast_select_fusion.2), channel_id=1, source_target_pairs={{0,64},{16,80},{32,96},{48,112},{64,0},{80,16},{96,32},{112,48},{1... | collective-permute-start | bytes 53768 | tf_op jit(solution)/shard_map/ppermute | solution.py:21
  39.9 1.2 %collective-permute-start.8 = (bf16[70,128]{1,0:T(8,128)(2,1)S(1)}, bf16[70,128]{1,0:T(8,128)(2,1)S(1)}, u32[]{:S(2)}, u32[]{:S(2)}) collective-permute-start(bf16[70,128]{1,0:T(8,128)(2,1)S(1)} %broadcast_select_fusion.2), channel_id=1, source_target_pairs={{0,96},{16,112},{32,64},{48,80},{64,32},{80,48},{96,0},{112,16},{1... | collective-permute-start | bytes 53768 | tf_op jit(solution)/shard_map/ppermute | solution.py:21
  41.2 0.5 collective-permute-done.9
  41.7 3.8 %collective-permute-done.8 = bf16[70,128]{1,0:T(8,128)(2,1)S(1)} collective-permute-done((bf16[70,128]{1,0:T(8,128)(2,1)S(1)}, bf16[70,128]{1,0:T(8,128)(2,1)S(1)}, u32[]{:S(2)}, u32[]{:S(2)}) %collective-permute-start.8) | collective-permute-done | bytes 17952 | tf_op jit(solution)/shard_map/ppermute | solution.py:21
  45.5 6.5 %shard_map.98 = (bf16[32,64,128]{2,1,0:T(8,128)(2,1)}, f32[616,128]{1,0:T(8,128)S(1)}, bf16[616,128]{1,0:T(8,128)(2,1)S(1)}, bf16[40,128]{1,0:T(8,128)(2,1)S(1)}) custom-call(s32[8]{0:T(128)S(1)} %select_convert_fusion.1.flags, bf16[32,64,128]{2,1,0:T(8,128)(2,1)S(1)} %bitcast.30, bf16[32,64,128]{2,1,0:T(8,128)(2,1)S(1)} %bitcast.33, ...), custom_call_target="tpu_custom_call" | custom-call | flops 2500000000 | bytes 4000000 | tf_op jit(solution)/shard_map/pallas_call | solution.py:316
  52.0 1.4 %collective-permute-done.11 = bf16[616,128]{1,0:T(8,128)(2,1)S(1)} collective-permute-done((bf16[616,128]{1,0:T(8,128)(2,1)S(1)}, bf16[616,128]{1,0:T(8,128)(2,1)S(1)}, u32[]{:S(2)}, u32[]{:S(2)}) %collective-permute-start.11) | collective-permute-done | bytes 157728 | tf_op jit(solution)/shard_map/ppermute | solution.py:21
  53.5 0.3 collective-permute-start.12
  53.8 1.8 %collective-permute-start.13 = (bf16[184,128]{1,0:T(8,128)(2,1)S(1)}, bf16[184,128]{1,0:T(8,128)(2,1)S(1)}, u32[]{:S(2)}, u32[]{:S(2)}) collective-permute-start(bf16[184,128]{1,0:T(8,128)(2,1)S(1)} %get-tuple-element.70), channel_id=1, source_target_pairs={{0,64},{16,80},{32,96},{48,112},{64,0},{80,16},{96,32},{112,48},{1... | collective-permute-start | bytes 141320 | tf_op jit(solution)/shard_map/ppermute | solution.py:21
  55.6 2.6 %collective-permute-start.14 = (bf16[184,128]{1,0:T(8,128)(2,1)S(1)}, bf16[184,128]{1,0:T(8,128)(2,1)S(1)}, u32[]{:S(2)}, u32[]{:S(2)}) collective-permute-start(bf16[184,128]{1,0:T(8,128)(2,1)S(1)} %get-tuple-element.71), channel_id=1, source_target_pairs={{0,96},{16,112},{32,64},{48,80},{64,32},{80,48},{96,0},{112,16},{1... | collective-permute-start | bytes 141320 | tf_op jit(solution)/shard_map/ppermute | solution.py:21
  58.2 0.2 collective-permute-done.12
  58.4 1.1 %collective-permute-done.13 = bf16[184,128]{1,0:T(8,128)(2,1)S(1)} collective-permute-done((bf16[184,128]{1,0:T(8,128)(2,1)S(1)}, bf16[184,128]{1,0:T(8,128)(2,1)S(1)}, u32[]{:S(2)}, u32[]{:S(2)}) %collective-permute-start.13) | collective-permute-done | bytes 47136 | tf_op jit(solution)/shard_map/ppermute | solution.py:21
  59.5 2.0 %collective-permute-done.14 = bf16[184,128]{1,0:T(8,128)(2,1)S(1)} collective-permute-done((bf16[184,128]{1,0:T(8,128)(2,1)S(1)}, bf16[184,128]{1,0:T(8,128)(2,1)S(1)}, u32[]{:S(2)}, u32[]{:S(2)}) %collective-permute-start.14) | collective-permute-done | bytes 47136 | tf_op jit(solution)/shard_map/ppermute | solution.py:21
  61.5 4.9 %collective-permute-start.15 = (bf16[184,128]{1,0:T(8,128)(2,1)S(1)}, bf16[184,128]{1,0:T(8,128)(2,1)S(1)}, u32[]{:S(2)}, u32[]{:S(2)}) collective-permute-start(bf16[184,128]{1,0:T(8,128)(2,1)S(1)} %add_convert_fusion.4), channel_id=1, source_target_pairs={{0,128},{16,144},{32,160},{48,176},{64,192},{80,208},{96,224},{112... | collective-permute-start | bytes 141320 | tf_op jit(solution)/shard_map/ppermute | solution.py:21
  66.4 3.2 %collective-permute-done.15 = bf16[184,128]{1,0:T(8,128)(2,1)S(1)} collective-permute-done((bf16[184,128]{1,0:T(8,128)(2,1)S(1)}, bf16[184,128]{1,0:T(8,128)(2,1)S(1)}, u32[]{:S(2)}, u32[]{:S(2)}) %collective-permute-start.15) | collective-permute-done | bytes 47136 | tf_op jit(solution)/shard_map/ppermute | solution.py:21
  69.7 0.2 collective-permute-start.17
  69.8 4.6 %collective-permute-start.16 = (bf16[224,128]{1,0:T(8,128)(2,1)S(1)}, bf16[224,128]{1,0:T(8,128)(2,1)S(1)}, u32[]{:S(2)}, u32[]{:S(2)}) collective-permute-start(bf16[224,128]{1,0:T(8,128)(2,1)S(1)} %pad_maximum_fusion.7), channel_id=1, source_target_pairs={{0,8},{2,10},{4,12},{6,14},{8,0},{10,2},{12,4},{14,6},{1,9},{3,11}... | collective-permute-start | bytes 172040 | tf_op jit(solution)/shard_map/ppermute | solution.py:16
  74.4 0.1 collective-permute-start.18
  74.5 0.6 collective-permute-done.17
  75.1 2.0 %collective-permute-done.16 = bf16[224,128]{1,0:T(8,128)(2,1)S(1)} collective-permute-done((bf16[224,128]{1,0:T(8,128)(2,1)S(1)}, bf16[224,128]{1,0:T(8,128)(2,1)S(1)}, u32[]{:S(2)}, u32[]{:S(2)}) %collective-permute-start.16) | collective-permute-done | bytes 57376 | tf_op jit(solution)/shard_map/ppermute | solution.py:16
  77.2 1.4 %collective-permute-done.18 = bf16[224,128]{1,0:T(8,128)(2,1)S(1)} collective-permute-done((bf16[224,128]{1,0:T(8,128)(2,1)S(1)}, bf16[224,128]{1,0:T(8,128)(2,1)S(1)}, u32[]{:S(2)}, u32[]{:S(2)}) %collective-permute-start.18) | collective-permute-done | bytes 57376 | tf_op jit(solution)/shard_map/ppermute | solution.py:16
  78.6 2.2 %collective-permute-start.19 = (bf16[224,128]{1,0:T(8,128)(2,1)S(1)}, bf16[224,128]{1,0:T(8,128)(2,1)S(1)}, u32[]{:S(2)}, u32[]{:S(2)}) collective-permute-start(bf16[224,128]{1,0:T(8,128)(2,1)S(1)} %add_convert_fusion.2), channel_id=1, source_target_pairs={{0,2},{2,0},{4,6},{6,4},{8,10},{10,8},{12,14},{14,12},{1,3},{3,1},... | collective-permute-start | bytes 172040 | tf_op jit(solution)/shard_map/ppermute | solution.py:21
  80.8 3.6 %collective-permute-done.19 = bf16[224,128]{1,0:T(8,128)(2,1)S(1)} collective-permute-done((bf16[224,128]{1,0:T(8,128)(2,1)S(1)}, bf16[224,128]{1,0:T(8,128)(2,1)S(1)}, u32[]{:S(2)}, u32[]{:S(2)}) %collective-permute-start.19) | collective-permute-done | bytes 57376 | tf_op jit(solution)/shard_map/ppermute | solution.py:21
  84.4 1.0 collective-permute-start.20
  85.4 1.6 %shard_map.99 = bf16[8,64,192]{2,1,0:T(8,128)(2,1)} custom-call(bf16[80,128]{1,0:T(8,128)(2,1)S(1)} %slice.90.sums, bf16[192,128]{1,0:T(8,128)(2,1)S(1)} %copy-done.4, bf16[192,128]{1,0:T(8,128)(2,1)S(1)} %copy-done.5, bf16[5,192,1536]{2,1,0:T(8,128)(2,1)S(1)} %copy-done), custom_call_target="tpu_custom_call" | custom-call | flops 120000000 | bytes 3500000 | tf_op jit(solution)/shard_map/pallas_call | solution.py:303
  87.1 1.4 %collective-permute-done.20 = bf16[144,128]{1,0:T(8,128)(2,1)S(1)} collective-permute-done((bf16[144,128]{1,0:T(8,128)(2,1)S(1)}, bf16[144,128]{1,0:T(8,128)(2,1)S(1)}, u32[]{:S(2)}, u32[]{:S(2)}) %collective-permute-start.20) | collective-permute-done | bytes 36896 | tf_op jit(solution)/shard_map/ppermute | solution.py:21
  88.5 1.9 %collective-permute-start.23 = (bf16[144,128]{1,0:T(8,128)(2,1)S(1)}, bf16[144,128]{1,0:T(8,128)(2,1)S(1)}, u32[]{:S(2)}, u32[]{:S(2)}) collective-permute-start(bf16[144,128]{1,0:T(8,128)(2,1)S(1)} %add_convert_fusion.5), channel_id=1, source_target_pairs={{0,96},{16,112},{32,64},{48,80},{64,32},{80,48},{96,0},{112,16},{1... | collective-permute-start | bytes 110600 | tf_op jit(solution)/shard_map/ppermute | solution.py:21
  90.4 0.0 collective-permute-start.22
  90.4 2.6 %collective-permute-start.21 = (bf16[144,128]{1,0:T(8,128)(2,1)S(1)}, bf16[144,128]{1,0:T(8,128)(2,1)S(1)}, u32[]{:S(2)}, u32[]{:S(2)}) collective-permute-start(bf16[144,128]{1,0:T(8,128)(2,1)S(1)} %add_convert_fusion.5), channel_id=1, source_target_pairs={{0,32},{16,48},{32,0},{48,16},{64,96},{80,112},{96,64},{112,80},{1... | collective-permute-start | bytes 110600 | tf_op jit(solution)/shard_map/ppermute | solution.py:21
  93.0 4.3 %all-to-all-start = ((bf16[8,64,192]{2,1,0:T(8,128)(2,1)}), bf16[8,64,192]{2,1,0:T(8,128)(2,1)S(1)}, u32[]{:S(2)}, u32[]{:S(2)}) async-start(bf16[8,64,192]{2,1,0:T(8,128)(2,1)} %shard_map.99), calls=%async_computation | async-start | bytes 524288 | tf_op jit(solution)/shard_map/all_to_all | solution.py:399
  97.3 0.0 collective-permute-done.23
  97.3 0.0 collective-permute-done.21
  97.4 0.1 collective-permute-start.24
  97.5 8.6 %all-to-all-done = bf16[8,64,192]{2,1,0:T(8,128)(2,1)S(1)} async-done(((bf16[8,64,192]{2,1,0:T(8,128)(2,1)}), bf16[8,64,192]{2,1,0:T(8,128)(2,1)S(1)}, u32[]{:S(2)}, u32[]{:S(2)}) %all-to-all-start) | async-done | bytes 196640 | tf_op jit(solution)/shard_map/all_to_all | solution.py:399
  106.1 0.7 reduce_sum.12
  106.8 0.0 collective-permute-done.24
  106.8 0.1 broadcast_select_fusion.1
  106.8 0.9 convert_multiply_fusion
  (44 shorter events, 0.4 us)
Async XLA Ops:
  0.7 1.0 copy-start.1
  0.7 1.2 %copy-start.2 = (bf16[1,32,64,128]{3,2,1,0:T(8,128)(2,1)S(1)}, bf16[1,32,64,128]{3,2,1,0:T(8,128)(2,1)}, u32[]{:S(2)}) copy-start(bf16[1,32,64,128]{3,2,1,0:T(8,128)(2,1)} %param.13) | copy-start | bytes 1572868
  0.7 1.2 %copy-start.3 = (bf16[1,64,1536]{2,1,0:T(8,128)(2,1)S(1)}, bf16[1,64,1536]{2,1,0:T(8,128)(2,1)}, u32[]{:S(2)}) copy-start(bf16[1,64,1536]{2,1,0:T(8,128)(2,1)} %param.7) | copy-start | bytes 589828
  0.8 7.1 %copy-start.6 = (bf16[3,3,128,128]{3,2,1,0:T(8,128)(2,1)S(1)}, bf16[3,3,128,128]{3,2,1,0:T(8,128)(2,1)}, u32[]{:S(2)}) copy-start(bf16[3,3,128,128]{3,2,1,0:T(8,128)(2,1)} %param.12) | copy-start | bytes 884740
  2.5 8.0 %collective-permute-start = (bf16[8,64,128]{2,1,0:T(8,128)(2,1)S(1)}, bf16[8,64,128]{2,1,0:T(8,128)(2,1)S(1)}, u32[]{:S(2)}, u32[]{:S(2)}) collective-permute-start(bf16[8,64,128]{2,1,0:T(8,128)(2,1)S(1)} %get-tuple-element.31), channel_id=1, source_target_pairs={{0,16},{16,32},{32,48},{48,64},{64,80},{80,96},{96,112},{112,128},... | collective-permute-start | bytes 393224 | tf_op jit(solution)/shard_map/ppermute | solution.py:16
  2.5 7.9 %collective-permute-start.1 = (bf16[8,64,128]{2,1,0:T(8,128)(2,1)S(1)}, bf16[8,64,128]{2,1,0:T(8,128)(2,1)S(1)}, u32[]{:S(2)}, u32[]{:S(2)}) collective-permute-start(bf16[8,64,128]{2,1,0:T(8,128)(2,1)S(1)} %get-tuple-element.32), channel_id=1, source_target_pairs={{0,240},{16,0},{32,16},{48,32},{64,48},{80,64},{96,80},{112,96},{1... | collective-permute-start | bytes 393224 | tf_op jit(solution)/shard_map/ppermute | solution.py:16
  7.8 2.6 %copy-start = (bf16[5,192,1536]{2,1,0:T(8,128)(2,1)S(1)}, bf16[5,192,1536]{2,1,0:T(8,128)(2,1)}, u32[]{:S(2)}) copy-start(bf16[5,192,1536]{2,1,0:T(8,128)(2,1)} %conv_w.3) | copy-start | bytes 8847364
  7.8 2.6 %copy-start.4 = (bf16[192,128]{1,0:T(8,128)(2,1)S(1)}, bf16[192,128]{1,0:T(8,128)(2,1)}, u32[]{:S(2)}) copy-start(bf16[192,128]{1,0:T(8,128)(2,1)} %proj_a.3) | copy-start | bytes 147460
  7.8 2.6 %copy-start.5 = (bf16[192,128]{1,0:T(8,128)(2,1)S(1)}, bf16[192,128]{1,0:T(8,128)(2,1)}, u32[]{:S(2)}) copy-start(bf16[192,128]{1,0:T(8,128)(2,1)} %proj_b.3) | copy-start | bytes 147460
  12.3 5.3 %collective-permute-start.4 = (bf16[272,128]{1,0:T(8,128)(2,1)S(1)}, bf16[272,128]{1,0:T(8,128)(2,1)S(1)}, u32[]{:S(2)}, u32[]{:S(2)}) collective-permute-start(bf16[272,128]{1,0:T(8,128)(2,1)S(1)} %get-tuple-element.36), channel_id=1, source_target_pairs={{0,12},{2,14},{4,0},{6,2},{8,4},{10,6},{12,8},{14,10},{1,13},{3,15... | collective-permute-start | bytes 208904 | tf_op jit(solution)/shard_map/ppermute | solution.py:16
  15.4 5.7 %collective-permute-start.3 = (bf16[272,128]{1,0:T(8,128)(2,1)S(1)}, bf16[272,128]{1,0:T(8,128)(2,1)S(1)}, u32[]{:S(2)}, u32[]{:S(2)}) collective-permute-start(bf16[272,128]{1,0:T(8,128)(2,1)S(1)} %get-tuple-element.35), channel_id=1, source_target_pairs={{0,4},{2,6},{4,8},{6,10},{8,12},{10,14},{12,0},{14,2},{1,5},{3,7},... | collective-permute-start | bytes 208904 | tf_op jit(solution)/shard_map/ppermute | solution.py:16
  15.4 5.8 %collective-permute-start.2 = (bf16[80,128]{1,0:T(8,128)(2,1)S(1)}, bf16[80,128]{1,0:T(8,128)(2,1)S(1)}, u32[]{:S(2)}, u32[]{:S(2)}) collective-permute-start(bf16[80,128]{1,0:T(8,128)(2,1)S(1)} %slice.59), channel_id=1, source_target_pairs={{0,8},{2,10},{4,12},{6,14},{8,0},{10,2},{12,4},{14,6},{1,9},{3,11}... | collective-permute-start | bytes 61448 | tf_op jit(solution)/shard_map/ppermute | solution.py:16
  21.2 6.4 %collective-permute-start.5 = (bf16[464,128]{1,0:T(8,128)(2,1)S(1)}, bf16[464,128]{1,0:T(8,128)(2,1)S(1)}, u32[]{:S(2)}, u32[]{:S(2)}) collective-permute-start(bf16[464,128]{1,0:T(8,128)(2,1)S(1)} %pad_maximum_fusion.2), channel_id=1, source_target_pairs={{0,2},{2,0},{4,6},{6,4},{8,10},{10,8},{12,14},{14,12},{1,3},{3,1},... | collective-permute-start | bytes 356360 | tf_op jit(solution)/shard_map/ppermute | solution.py:21
  27.6 1.3 %collective-permute-start.6 = (bf16[35,128]{1,0:T(8,128)(2,1)S(1)}, bf16[35,128]{1,0:T(8,128)(2,1)S(1)}, u32[]{:S(2)}, u32[]{:S(2)}) collective-permute-start(bf16[35,128]{1,0:T(8,128)(2,1)S(1)} %slice_select_fusion.3), channel_id=1, source_target_pairs={{0,16},{16,0},{32,48},{48,32},{64,80},{80,64},{96,112},{112,96},{1... | collective-permute-start | bytes 26888 | tf_op jit(solution)/shard_map/ppermute | solution.py:21
  28.9 7.8 %collective-permute-start.7 = (bf16[70,128]{1,0:T(8,128)(2,1)S(1)}, bf16[70,128]{1,0:T(8,128)(2,1)S(1)}, u32[]{:S(2)}, u32[]{:S(2)}) collective-permute-start(bf16[70,128]{1,0:T(8,128)(2,1)S(1)} %pad_maximum_fusion.8), channel_id=1, source_target_pairs={{0,128},{16,144},{32,160},{48,176},{64,192},{80,208},{96,224},{112... | collective-permute-start | bytes 53768 | tf_op jit(solution)/shard_map/ppermute | solution.py:21
  36.7 4.5 %collective-permute-start.10 = (bf16[70,128]{1,0:T(8,128)(2,1)S(1)}, bf16[70,128]{1,0:T(8,128)(2,1)S(1)}, u32[]{:S(2)}, u32[]{:S(2)}) collective-permute-start(bf16[70,128]{1,0:T(8,128)(2,1)S(1)} %broadcast_select_fusion.2), channel_id=1, source_target_pairs={{0,32},{16,48},{32,0},{48,16},{64,96},{80,112},{96,64},{112,80},{1... | collective-permute-start | bytes 53768 | tf_op jit(solution)/shard_map/ppermute | solution.py:21
  36.8 4.9 %collective-permute-start.9 = (bf16[70,128]{1,0:T(8,128)(2,1)S(1)}, bf16[70,128]{1,0:T(8,128)(2,1)S(1)}, u32[]{:S(2)}, u32[]{:S(2)}) collective-permute-start(bf16[70,128]{1,0:T(8,128)(2,1)S(1)} %broadcast_select_fusion.2), channel_id=1, source_target_pairs={{0,64},{16,80},{32,96},{48,112},{64,0},{80,16},{96,32},{112,48},{1... | collective-permute-start | bytes 53768 | tf_op jit(solution)/shard_map/ppermute | solution.py:21
  39.9 5.6 %collective-permute-start.8 = (bf16[70,128]{1,0:T(8,128)(2,1)S(1)}, bf16[70,128]{1,0:T(8,128)(2,1)S(1)}, u32[]{:S(2)}, u32[]{:S(2)}) collective-permute-start(bf16[70,128]{1,0:T(8,128)(2,1)S(1)} %broadcast_select_fusion.2), channel_id=1, source_target_pairs={{0,96},{16,112},{32,64},{48,80},{64,32},{80,48},{96,0},{112,16},{1... | collective-permute-start | bytes 53768 | tf_op jit(solution)/shard_map/ppermute | solution.py:21
  52.0 1.4 %collective-permute-start.11 = (bf16[616,128]{1,0:T(8,128)(2,1)S(1)}, bf16[616,128]{1,0:T(8,128)(2,1)S(1)}, u32[]{:S(2)}, u32[]{:S(2)}) collective-permute-start(bf16[616,128]{1,0:T(8,128)(2,1)S(1)} %get-tuple-element.46), channel_id=1, source_target_pairs={{0,16},{16,0},{32,48},{48,32},{64,80},{80,64},{96,112},{112,96},{1... | collective-permute-start | bytes 473096 | tf_op jit(solution)/shard_map/ppermute | solution.py:21
  53.5 4.9 %collective-permute-start.12 = (bf16[184,128]{1,0:T(8,128)(2,1)S(1)}, bf16[184,128]{1,0:T(8,128)(2,1)S(1)}, u32[]{:S(2)}, u32[]{:S(2)}) collective-permute-start(bf16[184,128]{1,0:T(8,128)(2,1)S(1)} %get-tuple-element.69), channel_id=1, source_target_pairs={{0,32},{16,48},{32,0},{48,16},{64,96},{80,112},{96,64},{112,80},{1... | collective-permute-start | bytes 141320 | tf_op jit(solution)/shard_map/ppermute | solution.py:21
  53.8 5.7 %collective-permute-start.13 = (bf16[184,128]{1,0:T(8,128)(2,1)S(1)}, bf16[184,128]{1,0:T(8,128)(2,1)S(1)}, u32[]{:S(2)}, u32[]{:S(2)}) collective-permute-start(bf16[184,128]{1,0:T(8,128)(2,1)S(1)} %get-tuple-element.70), channel_id=1, source_target_pairs={{0,64},{16,80},{32,96},{48,112},{64,0},{80,16},{96,32},{112,48},{1... | collective-permute-start | bytes 141320 | tf_op jit(solution)/shard_map/ppermute | solution.py:21
  55.6 5.9 %collective-permute-start.14 = (bf16[184,128]{1,0:T(8,128)(2,1)S(1)}, bf16[184,128]{1,0:T(8,128)(2,1)S(1)}, u32[]{:S(2)}, u32[]{:S(2)}) collective-permute-start(bf16[184,128]{1,0:T(8,128)(2,1)S(1)} %get-tuple-element.71), channel_id=1, source_target_pairs={{0,96},{16,112},{32,64},{48,80},{64,32},{80,48},{96,0},{112,16},{1... | collective-permute-start | bytes 141320 | tf_op jit(solution)/shard_map/ppermute | solution.py:21
  61.5 8.1 %collective-permute-start.15 = (bf16[184,128]{1,0:T(8,128)(2,1)S(1)}, bf16[184,128]{1,0:T(8,128)(2,1)S(1)}, u32[]{:S(2)}, u32[]{:S(2)}) collective-permute-start(bf16[184,128]{1,0:T(8,128)(2,1)S(1)} %add_convert_fusion.4), channel_id=1, source_target_pairs={{0,128},{16,144},{32,160},{48,176},{64,192},{80,208},{96,224},{112... | collective-permute-start | bytes 141320 | tf_op jit(solution)/shard_map/ppermute | solution.py:21
  69.7 5.5 %collective-permute-start.17 = (bf16[224,128]{1,0:T(8,128)(2,1)S(1)}, bf16[224,128]{1,0:T(8,128)(2,1)S(1)}, u32[]{:S(2)}, u32[]{:S(2)}) collective-permute-start(bf16[224,128]{1,0:T(8,128)(2,1)S(1)} %pad_maximum_fusion.7), channel_id=1, source_target_pairs={{0,4},{2,6},{4,8},{6,10},{8,12},{10,14},{12,0},{14,2},{1,5},{3,7},... | collective-permute-start | bytes 172040 | tf_op jit(solution)/shard_map/ppermute | solution.py:16
  69.8 7.3 %collective-permute-start.16 = (bf16[224,128]{1,0:T(8,128)(2,1)S(1)}, bf16[224,128]{1,0:T(8,128)(2,1)S(1)}, u32[]{:S(2)}, u32[]{:S(2)}) collective-permute-start(bf16[224,128]{1,0:T(8,128)(2,1)S(1)} %pad_maximum_fusion.7), channel_id=1, source_target_pairs={{0,8},{2,10},{4,12},{6,14},{8,0},{10,2},{12,4},{14,6},{1,9},{3,11}... | collective-permute-start | bytes 172040 | tf_op jit(solution)/shard_map/ppermute | solution.py:16
  74.4 4.2 %collective-permute-start.18 = (bf16[224,128]{1,0:T(8,128)(2,1)S(1)}, bf16[224,128]{1,0:T(8,128)(2,1)S(1)}, u32[]{:S(2)}, u32[]{:S(2)}) collective-permute-start(bf16[224,128]{1,0:T(8,128)(2,1)S(1)} %pad_maximum_fusion.7), channel_id=1, source_target_pairs={{0,12},{2,14},{4,0},{6,2},{8,4},{10,6},{12,8},{14,10},{1,13},{3,15... | collective-permute-start | bytes 172040 | tf_op jit(solution)/shard_map/ppermute | solution.py:16
  78.6 5.8 %collective-permute-start.19 = (bf16[224,128]{1,0:T(8,128)(2,1)S(1)}, bf16[224,128]{1,0:T(8,128)(2,1)S(1)}, u32[]{:S(2)}, u32[]{:S(2)}) collective-permute-start(bf16[224,128]{1,0:T(8,128)(2,1)S(1)} %add_convert_fusion.2), channel_id=1, source_target_pairs={{0,2},{2,0},{4,6},{6,4},{8,10},{10,8},{12,14},{14,12},{1,3},{3,1},... | collective-permute-start | bytes 172040 | tf_op jit(solution)/shard_map/ppermute | solution.py:21
  84.4 4.0 %collective-permute-start.20 = (bf16[144,128]{1,0:T(8,128)(2,1)S(1)}, bf16[144,128]{1,0:T(8,128)(2,1)S(1)}, u32[]{:S(2)}, u32[]{:S(2)}) collective-permute-start(bf16[144,128]{1,0:T(8,128)(2,1)S(1)} %slice.91), channel_id=1, source_target_pairs={{0,1},{1,0},{2,3},{3,2},{4,5},{5,4},{6,7},{7,6},{8,9},{9,8},{10,11... | collective-permute-start | bytes 110600 | tf_op jit(solution)/shard_map/ppermute | solution.py:21
  88.5 8.8 %collective-permute-start.23 = (bf16[144,128]{1,0:T(8,128)(2,1)S(1)}, bf16[144,128]{1,0:T(8,128)(2,1)S(1)}, u32[]{:S(2)}, u32[]{:S(2)}) collective-permute-start(bf16[144,128]{1,0:T(8,128)(2,1)S(1)} %add_convert_fusion.5), channel_id=1, source_target_pairs={{0,96},{16,112},{32,64},{48,80},{64,32},{80,48},{96,0},{112,16},{1... | collective-permute-start | bytes 110600 | tf_op jit(solution)/shard_map/ppermute | solution.py:21
  90.4 6.9 %collective-permute-start.22 = (bf16[144,128]{1,0:T(8,128)(2,1)S(1)}, bf16[144,128]{1,0:T(8,128)(2,1)S(1)}, u32[]{:S(2)}, u32[]{:S(2)}) collective-permute-start(bf16[144,128]{1,0:T(8,128)(2,1)S(1)} %add_convert_fusion.5), channel_id=1, source_target_pairs={{0,64},{16,80},{32,96},{48,112},{64,0},{80,16},{96,32},{112,48},{1... | collective-permute-start | bytes 110600 | tf_op jit(solution)/shard_map/ppermute | solution.py:21
  90.4 7.0 %collective-permute-start.21 = (bf16[144,128]{1,0:T(8,128)(2,1)S(1)}, bf16[144,128]{1,0:T(8,128)(2,1)S(1)}, u32[]{:S(2)}, u32[]{:S(2)}) collective-permute-start(bf16[144,128]{1,0:T(8,128)(2,1)S(1)} %add_convert_fusion.5), channel_id=1, source_target_pairs={{0,32},{16,48},{32,0},{48,16},{64,96},{80,112},{96,64},{112,80},{1... | collective-permute-start | bytes 110600 | tf_op jit(solution)/shard_map/ppermute | solution.py:21
  93.0 13.1 %all-to-all-start = ((bf16[8,64,192]{2,1,0:T(8,128)(2,1)}), bf16[8,64,192]{2,1,0:T(8,128)(2,1)S(1)}, u32[]{:S(2)}, u32[]{:S(2)}) async-start(bf16[8,64,192]{2,1,0:T(8,128)(2,1)} %shard_map.99), calls=%async_computation | async-start | bytes 524288 | tf_op jit(solution)/shard_map/all_to_all | solution.py:399
  97.4 9.3 %collective-permute-start.24 = (bf16[576,128]{1,0:T(8,128)(2,1)S(1)}, bf16[576,128]{1,0:T(8,128)(2,1)S(1)}, u32[]{:S(2)}, u32[]{:S(2)}) collective-permute-start(bf16[576,128]{1,0:T(8,128)(2,1)S(1)} %pad_maximum_fusion.1), channel_id=1, source_target_pairs={{0,16},{16,0},{32,48},{48,32},{64,80},{80,64},{96,112},{112,96},{1... | collective-permute-start | bytes 442376 | tf_op jit(solution)/shard_map/ppermute | solution.py:21

commit v5 on v4

--- a/solution.py
+++ b/solution.py
@@ -19,6 +19,27 @@
 def flip(x, axis, bit):
     count = lax.axis_size(axis)
     return lax.ppermute(x, axis, [(i, i ^ bit) for i in range(count)])
+
+
+def spread(x, far):
+    def place(z, core, col):
+        return (z % 8 * 2 + core) * 8 + col
+
+    pairs = {}
+    for col in range(8):
+        pairs[place(col, 0, col)] = place(col + far, 0, col)
+        if far < 4:
+            pairs[place(col, 1, col)] = place(col - far, 1, col)
+    open_ends = set(range(128)) - set(pairs.values())
+    for at in range(128):
+        if at not in pairs and at ^ 8 in open_ends:
+            pairs[at] = at ^ 8
+            open_ends.remove(at ^ 8)
+    for at in range(128):
+        if at not in pairs:
+            pairs[at] = min(end for end in open_ends if end % 8 == at % 8)
+            open_ends.remove(pairs[at])
+    return lax.ppermute(x, ("row", "col"), sorted(pairs.items()))
 
 
 def up(x):
@@ -350,10 +371,13 @@
     flags = jnp.where(most == 0, spot > 0, spot < jnp.where(place == 0, 15, 7)).astype(jnp.int32)
 
     fine, pair, cot = fine[0], pair_in[0], cotangent[0]
-    apart = zpos ^ col
-    scalars = (core == 0, (apart & 4) == 4, [(apart & 3) == k for k in (1, 2, 3)], zpos == col, [(zpos ^ k) & 3 for k in range(4)], col % 2 == 1)
+    apart = (zpos - col) & 7
+    is_there = [jnp.where(core == 0, apart == far, (apart == 8 - far) & (far < 4)) for far in (1, 2, 3, 4)]
+    is_held = (apart == 0) | ((apart <= 4) == (core == 0))
+    scalars = (core == 0, is_there, is_held, zpos == col, [(zpos ^ k) & 3 for k in range(4)], col % 2 == 1)
+    scalars += ([(col // 2 + k) & 3 for k in range(4)], (zpos & 1) == 1, (zpos & 2) == 2)
     seed, flags, scalars = lax.optimization_barrier((jnp.zeros((8, 128), F32), flags, scalars))
-    is_first, is_far, is_near, is_root, places, is_odd = scalars
+    is_first, is_there, is_held, is_root, places, is_odd, ahead, low_bit, high_bit = scalars
     down, above = ends(fine, pair, cot, begin(seed))
     top, bottom = shift(down, "row", 1), shift(above, "row", -1)
     weight = pair_w.reshape(9 * pairs, pairs)
@@ -371,10 +395,10 @@
     mine = jnp.where(is_first, colp_here[:35], colp_here[3:38])
     other = flip(mine, "row", 1)
     colp = jnp.concatenate([jnp.where(is_first, mine, other), jnp.where(is_first, other, mine)])
-    colp = jnp.where(is_far, flip(colp, "row", 8), colp)
-    near = [flip(colp, "row", 2 * k) for k in (1, 2, 3)]
-    for k in (1, 2, 3):
-        colp = jnp.where(is_near[k - 1], near[k - 1], colp)
+    sent = [spread(colp, far) for far in (4, 3, 2, 1)]
+    for far, got in zip((4, 3, 2, 1), sent):
+        colp = jnp.where(is_there[far - 1], got, colp)
+    colp = jnp.where(is_held, colp, flip(colp, "row", 1))
     out, keep, send, rowg = pair_block(flags, pair, cot, top, bottom, halos, rowp, up(colp), weight, turned)
 
     total = (keep + up(flip(send, "row", 1))).astype(BF)
@@ -396,15 +420,21 @@
     parts = conv_backward(sums, proj_a, proj_b, conv_w)
     quart = sum_flip(quart, "batch", 1)
     parts, quart = lax.optimization_barrier((parts, quart))
-    parts = lax.all_to_all(parts, "col", 0, 0, tiled=True)
-
-    near = jnp.stack([quart] + [flip(quart, "row", 2 * k) for k in (1, 2, 3)])
-    half = jnp.concatenate([taken(near, places[k]) for k in range(4)])
+
+    parts = parts.reshape(4, 128, parts.shape[2])
+    got = [shift(taken(parts, ahead[k]), "col", 2 * k) for k in (1, 2, 3)]
+    near = flip(quart, "row", 2)
+    got, near = lax.optimization_barrier((got, near))
+    mine = (up(taken(parts, ahead[0])) + up(got[0])) + (up(got[1]) + up(got[2]))
+    two = jnp.where(low_bit, jnp.concatenate([near, quart]), jnp.concatenate([quart, near]))
+    other = flip(jnp.where(is_odd, mine[:64], mine[64:]).astype(BF), "col", 1)
+    far = flip(two, "row", 4)
+    other, far = lax.optimization_barrier((other, far))
+    half = jnp.where(high_bit, jnp.concatenate([far, two]), jnp.concatenate([two, far]))
     theirs = flip(half, "row", 1)
     grad_pair_w = jnp.concatenate([jnp.where(is_first, half, theirs), jnp.where(is_first, theirs, half)])
     grad_pair_w = up(grad_pair_w).reshape(3, 3, pairs, pairs) / 512.0
-
-    grad_fine = jnp.sum(up(parts), axis=0).astype(BF)
+    grad_fine = (jnp.where(is_odd, mine[64:], mine[:64]) + up(other)).astype(BF)
     return out[None], grad_fine[None], grad_pair_w
 
 

time: 108 us -> 101 us (0.935)
  the two profiles are of different devices: /device:TPU:2 before, /device:TPU:1 now
where the time goes in v5:
time: 101 us
  starting transfers between devices  52.1 us (52%)
  waiting for transfers between devices  35.1 us (35%)
  Pallas kernels  9.89 us (10%)
  other arithmetic  1.91 us (2%)
  local copies, waits for them, and re-layouts  1.31 us (1%)
  between operations  1.05 us (1%)
    ppermute x14, starting transfers between devices, flip(): return lax.ppermute(x, axis, [(i, i ^ bit) for i in range(count)])  33.6 us
    ppermute x14, waiting for transfers between devices, flip(): return lax.ppermute(x, axis, [(i, i ^ bit) for i in range(count)])  18.6 us
    ppermute x11, starting transfers between devices, shift(): lax.ppermute(x, axis, [(i, (i + step) % count) for i in range(count)])  14 us
    ppermute x11, waiting for transfers between devices, shift(): lax.ppermute(x, axis, [(i, (i + step) % count) for i in range(count)])  11.1 us
    pallas_call x1, Pallas kernels, pair_block(): pl.pallas_call(pair_kernel, out_shape=(jax.ShapeDtypeStruct((32, 64, chan...  6.5 us
    ppermute x4, waiting for transfers between devices, spread(): return lax.ppermute(x, ('row', 'col'), sorted(pairs.items()))  5.4 us
    ppermute x4, starting transfers between devices, spread(): return lax.ppermute(x, ('row', 'col'), sorted(pairs.items()))  4.46 us
  transfers between devices with their start and end apart: 29, of which 23 were waited for; matrix products, arithmetic and copies ran while one was open for 1% of the time, Pallas kernels for 1%

profile of v5, /device:TPU:1, one launch (start us, length us, event | category | flops | bytes accessed | tf_op | source)
XLA Modules:
  0.0 101.4 jit_solution(9400752576935001722)
XLA Ops:
  0.8 0.0 copy-start.1
  0.8 0.0 copy-start.2
  0.8 0.0 copy-start.3
  0.8 0.0 copy-start.6
  0.8 1.0 copy-done.1
  1.8 0.2 copy-done.2
  2.0 0.0 copy-done.3
  2.0 0.5 shard_map.95
  2.6 3.0 %collective-permute-start = (bf16[8,64,128]{2,1,0:T(8,128)(2,1)S(1)}, bf16[8,64,128]{2,1,0:T(8,128)(2,1)S(1)}, u32[]{:S(2)}, u32[]{:S(2)}) collective-permute-start(bf16[8,64,128]{2,1,0:T(8,128)(2,1)S(1)} %get-tuple-element.44), channel_id=1, source_target_pairs={{0,16},{16,32},{32,48},{48,64},{64,80},{80,96},{96,112},{112,128},... | collective-permute-start | bytes 393224 | tf_op jit(solution)/shard_map/ppermute | solution.py:16
  5.6 0.2 collective-permute-start.1
  5.9 0.2 shard_map.96.turned
  6.0 1.5 %collective-permute-done.top = bf16[8,64,128]{2,1,0:T(8,128)(2,1)S(1)} collective-permute-done((bf16[8,64,128]{2,1,0:T(8,128)(2,1)S(1)}, bf16[8,64,128]{2,1,0:T(8,128)(2,1)S(1)}, u32[]{:S(2)}, u32[]{:S(2)}) %collective-permute-start) | collective-permute-done | bytes 131104 | tf_op jit(solution)/shard_map/ppermute | solution.py:16
  7.5 2.7 %collective-permute-done.1.bottom = bf16[8,64,128]{2,1,0:T(8,128)(2,1)S(1)} collective-permute-done((bf16[8,64,128]{2,1,0:T(8,128)(2,1)S(1)}, bf16[8,64,128]{2,1,0:T(8,128)(2,1)S(1)}, u32[]{:S(2)}, u32[]{:S(2)}) %collective-permute-start.1) | collective-permute-done | bytes 131104 | tf_op jit(solution)/shard_map/ppermute | solution.py:16
  10.3 1.8 %shard_map.97 = (bf16[272,128]{1,0:T(8,128)(2,1)S(1)}, bf16[272,128]{1,0:T(8,128)(2,1)S(1)}) custom-call(s32[8]{0:T(128)S(1)} %select_convert_fusion.2.flags, bf16[64,1536]{1,0:T(8,128)(2,1)S(1)} %bitcast.36, bf16[8,64,128]{2,1,0:T(8,128)(2,1)S(1)} %collective-permute-done.top, bf16[8,64,128]{2,1,0:T(8,128)(2,1)S(1)} %collective-permute-done.1.bottom, ...), custom_call_target="tpu_custom_call" | custom-call | flops 120000000 | bytes 3500000 | tf_op jit(solution)/shard_map/pallas_call | solution.py:311
  12.1 2.8 %collective-permute-start.4 = (bf16[272,128]{1,0:T(8,128)(2,1)S(1)}, bf16[272,128]{1,0:T(8,128)(2,1)S(1)}, u32[]{:S(2)}, u32[]{:S(2)}) collective-permute-start(bf16[272,128]{1,0:T(8,128)(2,1)S(1)} %get-tuple-element.49), channel_id=1, source_target_pairs={{0,12},{2,14},{4,0},{6,2},{8,4},{10,6},{12,8},{14,10},{1,13},{3,15... | collective-permute-start | bytes 208904 | tf_op jit(solution)/shard_map/ppermute | solution.py:16
  14.9 0.0 collective-permute-start.3
  14.9 1.6 %collective-permute-start.2 = (bf16[80,128]{1,0:T(8,128)(2,1)S(1)}, bf16[80,128]{1,0:T(8,128)(2,1)S(1)}, u32[]{:S(2)}, u32[]{:S(2)}) collective-permute-start(bf16[80,128]{1,0:T(8,128)(2,1)S(1)} %slice.67), channel_id=1, source_target_pairs={{0,8},{2,10},{4,12},{6,14},{8,0},{10,2},{12,4},{14,6},{1,9},{3,11}... | collective-permute-start | bytes 61448 | tf_op jit(solution)/shard_map/ppermute | solution.py:16
  16.6 2.9 %collective-permute-done.3 = bf16[272,128]{1,0:T(8,128)(2,1)S(1)} collective-permute-done((bf16[272,128]{1,0:T(8,128)(2,1)S(1)}, bf16[272,128]{1,0:T(8,128)(2,1)S(1)}, u32[]{:S(2)}, u32[]{:S(2)}) %collective-permute-start.3) | collective-permute-done | bytes 69664 | tf_op jit(solution)/shard_map/ppermute | solution.py:16
  19.6 2.8 %collective-permute-start.5 = (bf16[464,128]{1,0:T(8,128)(2,1)S(1)}, bf16[464,128]{1,0:T(8,128)(2,1)S(1)}, u32[]{:S(2)}, u32[]{:S(2)}) collective-permute-start(bf16[464,128]{1,0:T(8,128)(2,1)S(1)} %pad_maximum_fusion), channel_id=1, source_target_pairs={{0,2},{2,0},{4,6},{6,4},{8,10},{10,8},{12,14},{14,12},{1,3},{3,1},... | collective-permute-start | bytes 356360 | tf_op jit(solution)/shard_map/ppermute | solution.py:21
  22.4 2.4 %collective-permute-done.5 = bf16[464,128]{1,0:T(8,128)(2,1)S(1)} collective-permute-done((bf16[464,128]{1,0:T(8,128)(2,1)S(1)}, bf16[464,128]{1,0:T(8,128)(2,1)S(1)}, u32[]{:S(2)}, u32[]{:S(2)}) %collective-permute-start.5) | collective-permute-done | bytes 118816 | tf_op jit(solution)/shard_map/ppermute | solution.py:21
  24.9 4.4 %collective-permute-start.6 = (bf16[35,128]{1,0:T(8,128)(2,1)S(1)}, bf16[35,128]{1,0:T(8,128)(2,1)S(1)}, u32[]{:S(2)}, u32[]{:S(2)}) collective-permute-start(bf16[35,128]{1,0:T(8,128)(2,1)S(1)} %slice_select_fusion.3), channel_id=1, source_target_pairs={{0,16},{16,0},{32,48},{48,32},{64,80},{80,64},{96,112},{112,96},{1... | collective-permute-start | bytes 26888 | tf_op jit(solution)/shard_map/ppermute | solution.py:21
  29.3 0.8 collective-permute-done.6
  30.1 0.4 collective-permute-start.10
  30.6 4.0 %collective-permute-start.9 = (bf16[70,128]{1,0:T(8,128)(2,1)S(1)}, bf16[70,128]{1,0:T(8,128)(2,1)S(1)}, u32[]{:S(2)}, u32[]{:S(2)}) collective-permute-start(bf16[70,128]{1,0:T(8,128)(2,1)S(1)} %pad_maximum_fusion.6), channel_id=1, source_target_pairs={{0,96},{2,18},{4,20},{6,102},{8,24},{10,26},{12,28},{14,30},{16,17... | collective-permute-start | bytes 53768 | tf_op jit(solution)/shard_map/ppermute | solution.py:42
  34.6 2.1 %collective-permute-done.10 = bf16[70,128]{1,0:T(8,128)(2,1)S(1)} collective-permute-done((bf16[70,128]{1,0:T(8,128)(2,1)S(1)}, bf16[70,128]{1,0:T(8,128)(2,1)S(1)}, u32[]{:S(2)}, u32[]{:S(2)}) %collective-permute-start.10) | collective-permute-done | bytes 17952 | tf_op jit(solution)/shard_map/ppermute | solution.py:42
  36.8 0.2 collective-permute-done.9
  36.9 3.1 %collective-permute-done.8 = bf16[70,128]{1,0:T(8,128)(2,1)S(1)} collective-permute-done((bf16[70,128]{1,0:T(8,128)(2,1)S(1)}, bf16[70,128]{1,0:T(8,128)(2,1)S(1)}, u32[]{:S(2)}, u32[]{:S(2)}) %collective-permute-start.8) | collective-permute-done | bytes 17952 | tf_op jit(solution)/shard_map/ppermute | solution.py:42
  40.0 0.7 collective-permute-start.11
  40.7 0.8 collective-permute-done.11
  41.5 6.5 %shard_map.98 = (bf16[32,64,128]{2,1,0:T(8,128)(2,1)}, f32[616,128]{1,0:T(8,128)S(1)}, bf16[616,128]{1,0:T(8,128)(2,1)S(1)}, bf16[40,128]{1,0:T(8,128)(2,1)S(1)}) custom-call(s32[8]{0:T(128)S(1)} %select_convert_fusion.2.flags, bf16[32,64,128]{2,1,0:T(8,128)(2,1)S(1)} %bitcast.29, bf16[32,64,128]{2,1,0:T(8,128)(2,1)S(1)} %bitcast.32, ...), custom_call_target="tpu_custom_call" | custom-call | flops 2500000000 | bytes 4000000 | tf_op jit(solution)/shard_map/pallas_call | solution.py:337
  48.0 0.3 collective-permute-start.12
  48.4 1.1 %collective-permute-done.12 = bf16[616,128]{1,0:T(8,128)(2,1)S(1)} collective-permute-done((bf16[616,128]{1,0:T(8,128)(2,1)S(1)}, bf16[616,128]{1,0:T(8,128)(2,1)S(1)}, u32[]{:S(2)}, u32[]{:S(2)}) %collective-permute-start.12) | collective-permute-done | bytes 157728 | tf_op jit(solution)/shard_map/ppermute | solution.py:21
  49.6 0.1 collective-permute-start.13
  49.7 0.8 collective-permute-start.14
  50.4 2.8 %collective-permute-start.15 = (bf16[184,128]{1,0:T(8,128)(2,1)S(1)}, bf16[184,128]{1,0:T(8,128)(2,1)S(1)}, u32[]{:S(2)}, u32[]{:S(2)}) collective-permute-start(bf16[184,128]{1,0:T(8,128)(2,1)S(1)} %get-tuple-element.96), channel_id=1, source_target_pairs={{0,96},{16,112},{32,64},{48,80},{64,32},{80,48},{96,0},{112,16},{1... | collective-permute-start | bytes 141320 | tf_op jit(solution)/shard_map/ppermute | solution.py:21
  53.2 0.5 collective-permute-done.14
  53.7 1.6 %collective-permute-done.15 = bf16[184,128]{1,0:T(8,128)(2,1)S(1)} collective-permute-done((bf16[184,128]{1,0:T(8,128)(2,1)S(1)}, bf16[184,128]{1,0:T(8,128)(2,1)S(1)}, u32[]{:S(2)}, u32[]{:S(2)}) %collective-permute-start.15) | collective-permute-done | bytes 47136 | tf_op jit(solution)/shard_map/ppermute | solution.py:21
  55.3 2.5 %collective-permute-start.16 = (bf16[184,128]{1,0:T(8,128)(2,1)S(1)}, bf16[184,128]{1,0:T(8,128)(2,1)S(1)}, u32[]{:S(2)}, u32[]{:S(2)}) collective-permute-start(bf16[184,128]{1,0:T(8,128)(2,1)S(1)} %add_convert_fusion.4), channel_id=1, source_target_pairs={{0,128},{16,144},{32,160},{48,176},{64,192},{80,208},{96,224},{112... | collective-permute-start | bytes 141320 | tf_op jit(solution)/shard_map/ppermute | solution.py:21
  57.8 4.4 %collective-permute-done.16 = bf16[184,128]{1,0:T(8,128)(2,1)S(1)} collective-permute-done((bf16[184,128]{1,0:T(8,128)(2,1)S(1)}, bf16[184,128]{1,0:T(8,128)(2,1)S(1)}, u32[]{:S(2)}, u32[]{:S(2)}) %collective-permute-start.16) | collective-permute-done | bytes 47136 | tf_op jit(solution)/shard_map/ppermute | solution.py:21
  62.3 0.7 collective-permute-start.18
  63.0 0.6 collective-permute-start.17
  63.6 1.9 %collective-permute-start.19 = (bf16[224,128]{1,0:T(8,128)(2,1)S(1)}, bf16[224,128]{1,0:T(8,128)(2,1)S(1)}, u32[]{:S(2)}, u32[]{:S(2)}) collective-permute-start(bf16[224,128]{1,0:T(8,128)(2,1)S(1)} %pad_maximum_fusion.5), channel_id=1, source_target_pairs={{0,12},{2,14},{4,0},{6,2},{8,4},{10,6},{12,8},{14,10},{1,13},{3,15... | collective-permute-start | bytes 172040 | tf_op jit(solution)/shard_map/ppermute | solution.py:16
  65.5 1.1 %collective-permute-done.18 = bf16[224,128]{1,0:T(8,128)(2,1)S(1)} collective-permute-done((bf16[224,128]{1,0:T(8,128)(2,1)S(1)}, bf16[224,128]{1,0:T(8,128)(2,1)S(1)}, u32[]{:S(2)}, u32[]{:S(2)}) %collective-permute-start.18) | collective-permute-done | bytes 57376 | tf_op jit(solution)/shard_map/ppermute | solution.py:16
  66.6 0.9 collective-permute-done.17
  67.5 0.3 collective-permute-done.19
  67.8 5.3 %collective-permute-start.20 = (bf16[224,128]{1,0:T(8,128)(2,1)S(1)}, bf16[224,128]{1,0:T(8,128)(2,1)S(1)}, u32[]{:S(2)}, u32[]{:S(2)}) collective-permute-start(bf16[224,128]{1,0:T(8,128)(2,1)S(1)} %add_convert_fusion.2), channel_id=1, source_target_pairs={{0,2},{2,0},{4,6},{6,4},{8,10},{10,8},{12,14},{14,12},{1,3},{3,1},... | collective-permute-start | bytes 172040 | tf_op jit(solution)/shard_map/ppermute | solution.py:21
  73.1 1.6 %collective-permute-done.20 = bf16[224,128]{1,0:T(8,128)(2,1)S(1)} collective-permute-done((bf16[224,128]{1,0:T(8,128)(2,1)S(1)}, bf16[224,128]{1,0:T(8,128)(2,1)S(1)}, u32[]{:S(2)}, u32[]{:S(2)}) %collective-permute-start.20) | collective-permute-done | bytes 57376 | tf_op jit(solution)/shard_map/ppermute | solution.py:21
  74.7 0.4 collective-permute-start.21
  75.1 0.9 shard_map.99
  76.0 1.9 %collective-permute-done.21 = bf16[144,128]{1,0:T(8,128)(2,1)S(1)} collective-permute-done((bf16[144,128]{1,0:T(8,128)(2,1)S(1)}, bf16[144,128]{1,0:T(8,128)(2,1)S(1)}, u32[]{:S(2)}, u32[]{:S(2)}) %collective-permute-start.21) | collective-permute-done | bytes 36896 | tf_op jit(solution)/shard_map/ppermute | solution.py:21
  77.9 2.2 %collective-permute-start.24 = (bf16[128,192]{1,0:T(8,128)(2,1)S(1)}, bf16[128,192]{1,0:T(8,128)(2,1)S(1)}, u32[]{:S(2)}, u32[]{:S(2)}) collective-permute-start(bf16[128,192]{1,0:T(8,128)(2,1)S(1)} %get-tuple-element.83), channel_id=1, source_target_pairs={{0,12},{2,14},{4,0},{6,2},{8,4},{10,6},{12,8},{14,10},{1,13},{3,15... | collective-permute-start | bytes 147464 | tf_op jit(solution)/shard_map/ppermute | solution.py:16
  80.1 0.2 collective-permute-start.23
  80.4 0.7 collective-permute-start.22
  81.0 1.3 %collective-permute-start.25 = (bf16[144,128]{1,0:T(8,128)(2,1)S(1)}, bf16[144,128]{1,0:T(8,128)(2,1)S(1)}, u32[]{:S(2)}, u32[]{:S(2)}) collective-permute-start(bf16[144,128]{1,0:T(8,128)(2,1)S(1)} %add_convert_fusion.5), channel_id=1, source_target_pairs={{0,32},{16,48},{32,0},{48,16},{64,96},{80,112},{96,64},{112,80},{1... | collective-permute-start | bytes 110600 | tf_op jit(solution)/shard_map/ppermute | solution.py:21
  82.3 1.5 %collective-permute-done.25 = bf16[144,128]{1,0:T(8,128)(2,1)S(1)} collective-permute-done((bf16[144,128]{1,0:T(8,128)(2,1)S(1)}, bf16[144,128]{1,0:T(8,128)(2,1)S(1)}, u32[]{:S(2)}, u32[]{:S(2)}) %collective-permute-start.25) | collective-permute-done | bytes 36896 | tf_op jit(solution)/shard_map/ppermute | solution.py:21
  83.8 1.0 %collective-permute-done.23 = bf16[128,192]{1,0:T(8,128)(2,1)S(1)} collective-permute-done((bf16[128,192]{1,0:T(8,128)(2,1)S(1)}, bf16[128,192]{1,0:T(8,128)(2,1)S(1)}, u32[]{:S(2)}, u32[]{:S(2)}) %collective-permute-start.23) | collective-permute-done | bytes 49184 | tf_op jit(solution)/shard_map/ppermute | solution.py:16
  84.9 0.5 collective-permute-done.22
  85.4 0.4 collective-permute-start.27
  85.9 3.1 %collective-permute-start.26 = (bf16[64,192]{1,0:T(8,128)(2,1)S(1)}, bf16[64,192]{1,0:T(8,128)(2,1)S(1)}, u32[]{:S(2)}, u32[]{:S(2)}) collective-permute-start(bf16[64,192]{1,0:T(8,128)(2,1)S(1)} %select_convert_fusion), channel_id=1, source_target_pairs={{0,2},{2,0},{4,6},{6,4},{8,10},{10,8},{12,14},{14,12},{1,3},{3,1},... | collective-permute-start | bytes 73736 | tf_op jit(solution)/shard_map/ppermute | solution.py:21
  88.9 1.6 %collective-permute-done.26 = bf16[64,192]{1,0:T(8,128)(2,1)S(1)} collective-permute-done((bf16[64,192]{1,0:T(8,128)(2,1)S(1)}, bf16[64,192]{1,0:T(8,128)(2,1)S(1)}, u32[]{:S(2)}, u32[]{:S(2)}) %collective-permute-start.26) | collective-permute-done | bytes 24608 | tf_op jit(solution)/shard_map/ppermute | solution.py:21
  90.6 8.9 %collective-permute-start.28 = (bf16[576,128]{1,0:T(8,128)(2,1)S(1)}, bf16[576,128]{1,0:T(8,128)(2,1)S(1)}, u32[]{:S(2)}, u32[]{:S(2)}) collective-permute-start(bf16[576,128]{1,0:T(8,128)(2,1)S(1)} %maximum_select_fusion), channel_id=1, source_target_pairs={{0,16},{16,0},{32,48},{48,32},{64,80},{80,64},{96,112},{112,96},{1... | collective-permute-start | bytes 442376 | tf_op jit(solution)/shard_map/ppermute | solution.py:21
  99.5 0.6 fusion.1
  100.1 0.4 collective-permute-done.28
  100.5 0.9 convert_multiply_fusion
  (52 shorter events, 0.6 us)
Async XLA Ops:
  0.8 1.0 %copy-start.1 = (bf16[1,32,64,128]{3,2,1,0:T(8,128)(2,1)S(1)}, bf16[1,32,64,128]{3,2,1,0:T(8,128)(2,1)}, u32[]{:S(2)}) copy-start(bf16[1,32,64,128]{3,2,1,0:T(8,128)(2,1)} %param.11) | copy-start | bytes 1572868
  0.8 1.2 %copy-start.2 = (bf16[1,32,64,128]{3,2,1,0:T(8,128)(2,1)S(1)}, bf16[1,32,64,128]{3,2,1,0:T(8,128)(2,1)}, u32[]{:S(2)}) copy-start(bf16[1,32,64,128]{3,2,1,0:T(8,128)(2,1)} %param.13) | copy-start | bytes 1572868
  0.8 1.2 %copy-start.3 = (bf16[1,64,1536]{2,1,0:T(8,128)(2,1)S(1)}, bf16[1,64,1536]{2,1,0:T(8,128)(2,1)}, u32[]{:S(2)}) copy-start(bf16[1,64,1536]{2,1,0:T(8,128)(2,1)} %param.7) | copy-start | bytes 589828
  0.8 5.0 %copy-start.6 = (bf16[3,3,128,128]{3,2,1,0:T(8,128)(2,1)S(1)}, bf16[3,3,128,128]{3,2,1,0:T(8,128)(2,1)}, u32[]{:S(2)}) copy-start(bf16[3,3,128,128]{3,2,1,0:T(8,128)(2,1)} %param.12) | copy-start | bytes 884740
  2.6 5.0 %collective-permute-start = (bf16[8,64,128]{2,1,0:T(8,128)(2,1)S(1)}, bf16[8,64,128]{2,1,0:T(8,128)(2,1)S(1)}, u32[]{:S(2)}, u32[]{:S(2)}) collective-permute-start(bf16[8,64,128]{2,1,0:T(8,128)(2,1)S(1)} %get-tuple-element.44), channel_id=1, source_target_pairs={{0,16},{16,32},{32,48},{48,64},{64,80},{80,96},{96,112},{112,128},... | collective-permute-start | bytes 393224 | tf_op jit(solution)/shard_map/ppermute | solution.py:16
  5.6 4.7 %collective-permute-start.1 = (bf16[8,64,128]{2,1,0:T(8,128)(2,1)S(1)}, bf16[8,64,128]{2,1,0:T(8,128)(2,1)S(1)}, u32[]{:S(2)}, u32[]{:S(2)}) collective-permute-start(bf16[8,64,128]{2,1,0:T(8,128)(2,1)S(1)} %get-tuple-element.45), channel_id=1, source_target_pairs={{0,240},{16,0},{32,16},{48,32},{64,48},{80,64},{96,80},{112,96},{1... | collective-permute-start | bytes 393224 | tf_op jit(solution)/shard_map/ppermute | solution.py:16
  5.8 4.4 %copy-start = (bf16[5,192,1536]{2,1,0:T(8,128)(2,1)S(1)}, bf16[5,192,1536]{2,1,0:T(8,128)(2,1)}, u32[]{:S(2)}) copy-start(bf16[5,192,1536]{2,1,0:T(8,128)(2,1)} %conv_w.3) | copy-start | bytes 8847364
  5.8 4.4 %copy-start.4 = (bf16[192,128]{1,0:T(8,128)(2,1)S(1)}, bf16[192,128]{1,0:T(8,128)(2,1)}, u32[]{:S(2)}) copy-start(bf16[192,128]{1,0:T(8,128)(2,1)} %proj_a.3) | copy-start | bytes 147460
  5.8 4.4 %copy-start.5 = (bf16[192,128]{1,0:T(8,128)(2,1)S(1)}, bf16[192,128]{1,0:T(8,128)(2,1)}, u32[]{:S(2)}) copy-start(bf16[192,128]{1,0:T(8,128)(2,1)} %proj_b.3) | copy-start | bytes 147460
  12.1 4.5 %collective-permute-start.4 = (bf16[272,128]{1,0:T(8,128)(2,1)S(1)}, bf16[272,128]{1,0:T(8,128)(2,1)S(1)}, u32[]{:S(2)}, u32[]{:S(2)}) collective-permute-start(bf16[272,128]{1,0:T(8,128)(2,1)S(1)} %get-tuple-element.49), channel_id=1, source_target_pairs={{0,12},{2,14},{4,0},{6,2},{8,4},{10,6},{12,8},{14,10},{1,13},{3,15... | collective-permute-start | bytes 208904 | tf_op jit(solution)/shard_map/ppermute | solution.py:16
  14.9 4.6 %collective-permute-start.3 = (bf16[272,128]{1,0:T(8,128)(2,1)S(1)}, bf16[272,128]{1,0:T(8,128)(2,1)S(1)}, u32[]{:S(2)}, u32[]{:S(2)}) collective-permute-start(bf16[272,128]{1,0:T(8,128)(2,1)S(1)} %get-tuple-element.48), channel_id=1, source_target_pairs={{0,4},{2,6},{4,8},{6,10},{8,12},{10,14},{12,0},{14,2},{1,5},{3,7},... | collective-permute-start | bytes 208904 | tf_op jit(solution)/shard_map/ppermute | solution.py:16
  14.9 4.6 %collective-permute-start.2 = (bf16[80,128]{1,0:T(8,128)(2,1)S(1)}, bf16[80,128]{1,0:T(8,128)(2,1)S(1)}, u32[]{:S(2)}, u32[]{:S(2)}) collective-permute-start(bf16[80,128]{1,0:T(8,128)(2,1)S(1)} %slice.67), channel_id=1, source_target_pairs={{0,8},{2,10},{4,12},{6,14},{8,0},{10,2},{12,4},{14,6},{1,9},{3,11}... | collective-permute-start | bytes 61448 | tf_op jit(solution)/shard_map/ppermute | solution.py:16
  19.6 5.3 %collective-permute-start.5 = (bf16[464,128]{1,0:T(8,128)(2,1)S(1)}, bf16[464,128]{1,0:T(8,128)(2,1)S(1)}, u32[]{:S(2)}, u32[]{:S(2)}) collective-permute-start(bf16[464,128]{1,0:T(8,128)(2,1)S(1)} %pad_maximum_fusion), channel_id=1, source_target_pairs={{0,2},{2,0},{4,6},{6,4},{8,10},{10,8},{12,14},{14,12},{1,3},{3,1},... | collective-permute-start | bytes 356360 | tf_op jit(solution)/shard_map/ppermute | solution.py:21
  24.9 5.2 %collective-permute-start.6 = (bf16[35,128]{1,0:T(8,128)(2,1)S(1)}, bf16[35,128]{1,0:T(8,128)(2,1)S(1)}, u32[]{:S(2)}, u32[]{:S(2)}) collective-permute-start(bf16[35,128]{1,0:T(8,128)(2,1)S(1)} %slice_select_fusion.3), channel_id=1, source_target_pairs={{0,16},{16,0},{32,48},{48,32},{64,80},{80,64},{96,112},{112,96},{1... | collective-permute-start | bytes 26888 | tf_op jit(solution)/shard_map/ppermute | solution.py:21
  30.1 6.6 %collective-permute-start.10 = (bf16[70,128]{1,0:T(8,128)(2,1)S(1)}, bf16[70,128]{1,0:T(8,128)(2,1)S(1)}, u32[]{:S(2)}, u32[]{:S(2)}) collective-permute-start(bf16[70,128]{1,0:T(8,128)(2,1)S(1)} %pad_maximum_fusion.6), channel_id=1, source_target_pairs={{0,128},{2,18},{4,20},{6,22},{8,24},{10,26},{12,28},{14,30},{16,0}... | collective-permute-start | bytes 53768 | tf_op jit(solution)/shard_map/ppermute | solution.py:42
  30.6 6.4 %collective-permute-start.9 = (bf16[70,128]{1,0:T(8,128)(2,1)S(1)}, bf16[70,128]{1,0:T(8,128)(2,1)S(1)}, u32[]{:S(2)}, u32[]{:S(2)}) collective-permute-start(bf16[70,128]{1,0:T(8,128)(2,1)S(1)} %pad_maximum_fusion.6), channel_id=1, source_target_pairs={{0,96},{2,18},{4,20},{6,102},{8,24},{10,26},{12,28},{14,30},{16,17... | collective-permute-start | bytes 53768 | tf_op jit(solution)/shard_map/ppermute | solution.py:42
  34.6 5.4 %collective-permute-start.8 = (bf16[70,128]{1,0:T(8,128)(2,1)S(1)}, bf16[70,128]{1,0:T(8,128)(2,1)S(1)}, u32[]{:S(2)}, u32[]{:S(2)}) collective-permute-start(bf16[70,128]{1,0:T(8,128)(2,1)S(1)} %pad_maximum_fusion.6), channel_id=1, source_target_pairs={{0,64},{2,18},{4,68},{6,22},{8,24},{10,26},{12,28},{14,30},{16,208... | collective-permute-start | bytes 53768 | tf_op jit(solution)/shard_map/ppermute | solution.py:42
  34.6 5.4 %collective-permute-start.7 = (bf16[70,128]{1,0:T(8,128)(2,1)S(1)}, bf16[70,128]{1,0:T(8,128)(2,1)S(1)}, u32[]{:S(2)}, u32[]{:S(2)}) collective-permute-start(bf16[70,128]{1,0:T(8,128)(2,1)S(1)} %pad_maximum_fusion.6), channel_id=1, source_target_pairs={{0,32},{2,34},{4,20},{6,22},{8,24},{10,26},{12,28},{14,30},{16,240... | collective-permute-start | bytes 53768 | tf_op jit(solution)/shard_map/ppermute | solution.py:42
  40.0 1.5 %collective-permute-start.11 = (bf16[70,128]{1,0:T(8,128)(2,1)S(1)}, bf16[70,128]{1,0:T(8,128)(2,1)S(1)}, u32[]{:S(2)}, u32[]{:S(2)}) collective-permute-start(bf16[70,128]{1,0:T(8,128)(2,1)S(1)} %select_select_fusion), channel_id=1, source_target_pairs={{0,16},{16,0},{32,48},{48,32},{64,80},{80,64},{96,112},{112,96},{1... | collective-permute-start | bytes 53768 | tf_op jit(solution)/shard_map/ppermute | solution.py:21
  48.0 1.4 %collective-permute-start.12 = (bf16[616,128]{1,0:T(8,128)(2,1)S(1)}, bf16[616,128]{1,0:T(8,128)(2,1)S(1)}, u32[]{:S(2)}, u32[]{:S(2)}) collective-permute-start(bf16[616,128]{1,0:T(8,128)(2,1)S(1)} %get-tuple-element.60), channel_id=1, source_target_pairs={{0,16},{16,0},{32,48},{48,32},{64,80},{80,64},{96,112},{112,96},{1... | collective-permute-start | bytes 473096 | tf_op jit(solution)/shard_map/ppermute | solution.py:21
  49.6 3.6 %collective-permute-start.13 = (bf16[184,128]{1,0:T(8,128)(2,1)S(1)}, bf16[184,128]{1,0:T(8,128)(2,1)S(1)}, u32[]{:S(2)}, u32[]{:S(2)}) collective-permute-start(bf16[184,128]{1,0:T(8,128)(2,1)S(1)} %get-tuple-element.94), channel_id=1, source_target_pairs={{0,32},{16,48},{32,0},{48,16},{64,96},{80,112},{96,64},{112,80},{1... | collective-permute-start | bytes 141320 | tf_op jit(solution)/shard_map/ppermute | solution.py:21
  49.7 4.0 %collective-permute-start.14 = (bf16[184,128]{1,0:T(8,128)(2,1)S(1)}, bf16[184,128]{1,0:T(8,128)(2,1)S(1)}, u32[]{:S(2)}, u32[]{:S(2)}) collective-permute-start(bf16[184,128]{1,0:T(8,128)(2,1)S(1)} %get-tuple-element.95), channel_id=1, source_target_pairs={{0,64},{16,80},{32,96},{48,112},{64,0},{80,16},{96,32},{112,48},{1... | collective-permute-start | bytes 141320 | tf_op jit(solution)/shard_map/ppermute | solution.py:21
  50.4 4.8 %collective-permute-start.15 = (bf16[184,128]{1,0:T(8,128)(2,1)S(1)}, bf16[184,128]{1,0:T(8,128)(2,1)S(1)}, u32[]{:S(2)}, u32[]{:S(2)}) collective-permute-start(bf16[184,128]{1,0:T(8,128)(2,1)S(1)} %get-tuple-element.96), channel_id=1, source_target_pairs={{0,96},{16,112},{32,64},{48,80},{64,32},{80,48},{96,0},{112,16},{1... | collective-permute-start | bytes 141320 | tf_op jit(solution)/shard_map/ppermute | solution.py:21
  55.3 6.9 %collective-permute-start.16 = (bf16[184,128]{1,0:T(8,128)(2,1)S(1)}, bf16[184,128]{1,0:T(8,128)(2,1)S(1)}, u32[]{:S(2)}, u32[]{:S(2)}) collective-permute-start(bf16[184,128]{1,0:T(8,128)(2,1)S(1)} %add_convert_fusion.4), channel_id=1, source_target_pairs={{0,128},{16,144},{32,160},{48,176},{64,192},{80,208},{96,224},{112... | collective-permute-start | bytes 141320 | tf_op jit(solution)/shard_map/ppermute | solution.py:21
  62.3 4.3 %collective-permute-start.18 = (bf16[224,128]{1,0:T(8,128)(2,1)S(1)}, bf16[224,128]{1,0:T(8,128)(2,1)S(1)}, u32[]{:S(2)}, u32[]{:S(2)}) collective-permute-start(bf16[224,128]{1,0:T(8,128)(2,1)S(1)} %pad_maximum_fusion.5), channel_id=1, source_target_pairs={{0,4},{2,6},{4,8},{6,10},{8,12},{10,14},{12,0},{14,2},{1,5},{3,7},... | collective-permute-start | bytes 172040 | tf_op jit(solution)/shard_map/ppermute | solution.py:16
  63.0 4.5 %collective-permute-start.17 = (bf16[224,128]{1,0:T(8,128)(2,1)S(1)}, bf16[224,128]{1,0:T(8,128)(2,1)S(1)}, u32[]{:S(2)}, u32[]{:S(2)}) collective-permute-start(bf16[224,128]{1,0:T(8,128)(2,1)S(1)} %pad_maximum_fusion.5), channel_id=1, source_target_pairs={{0,8},{2,10},{4,12},{6,14},{8,0},{10,2},{12,4},{14,6},{1,9},{3,11}... | collective-permute-start | bytes 172040 | tf_op jit(solution)/shard_map/ppermute | solution.py:16
  63.6 4.2 %collective-permute-start.19 = (bf16[224,128]{1,0:T(8,128)(2,1)S(1)}, bf16[224,128]{1,0:T(8,128)(2,1)S(1)}, u32[]{:S(2)}, u32[]{:S(2)}) collective-permute-start(bf16[224,128]{1,0:T(8,128)(2,1)S(1)} %pad_maximum_fusion.5), channel_id=1, source_target_pairs={{0,12},{2,14},{4,0},{6,2},{8,4},{10,6},{12,8},{14,10},{1,13},{3,15... | collective-permute-start | bytes 172040 | tf_op jit(solution)/shard_map/ppermute | solution.py:16
  67.8 6.8 %collective-permute-start.20 = (bf16[224,128]{1,0:T(8,128)(2,1)S(1)}, bf16[224,128]{1,0:T(8,128)(2,1)S(1)}, u32[]{:S(2)}, u32[]{:S(2)}) collective-permute-start(bf16[224,128]{1,0:T(8,128)(2,1)S(1)} %add_convert_fusion.2), channel_id=1, source_target_pairs={{0,2},{2,0},{4,6},{6,4},{8,10},{10,8},{12,14},{14,12},{1,3},{3,1},... | collective-permute-start | bytes 172040 | tf_op jit(solution)/shard_map/ppermute | solution.py:21
  74.7 3.2 %collective-permute-start.21 = (bf16[144,128]{1,0:T(8,128)(2,1)S(1)}, bf16[144,128]{1,0:T(8,128)(2,1)S(1)}, u32[]{:S(2)}, u32[]{:S(2)}) collective-permute-start(bf16[144,128]{1,0:T(8,128)(2,1)S(1)} %slice.101), channel_id=1, source_target_pairs={{0,1},{1,0},{2,3},{3,2},{4,5},{5,4},{6,7},{7,6},{8,9},{9,8},{10,11... | collective-permute-start | bytes 110600 | tf_op jit(solution)/shard_map/ppermute | solution.py:21
  77.9 5.9 %collective-permute-start.24 = (bf16[128,192]{1,0:T(8,128)(2,1)S(1)}, bf16[128,192]{1,0:T(8,128)(2,1)S(1)}, u32[]{:S(2)}, u32[]{:S(2)}) collective-permute-start(bf16[128,192]{1,0:T(8,128)(2,1)S(1)} %get-tuple-element.83), channel_id=1, source_target_pairs={{0,12},{2,14},{4,0},{6,2},{8,4},{10,6},{12,8},{14,10},{1,13},{3,15... | collective-permute-start | bytes 147464 | tf_op jit(solution)/shard_map/ppermute | solution.py:16
  80.1 4.7 %collective-permute-start.23 = (bf16[128,192]{1,0:T(8,128)(2,1)S(1)}, bf16[128,192]{1,0:T(8,128)(2,1)S(1)}, u32[]{:S(2)}, u32[]{:S(2)}) collective-permute-start(bf16[128,192]{1,0:T(8,128)(2,1)S(1)} %get-tuple-element.84), channel_id=1, source_target_pairs={{0,8},{2,10},{4,12},{6,14},{8,0},{10,2},{12,4},{14,6},{1,9},{3,11}... | collective-permute-start | bytes 147464 | tf_op jit(solution)/shard_map/ppermute | solution.py:16
  80.4 5.0 %collective-permute-start.22 = (bf16[128,192]{1,0:T(8,128)(2,1)S(1)}, bf16[128,192]{1,0:T(8,128)(2,1)S(1)}, u32[]{:S(2)}, u32[]{:S(2)}) collective-permute-start(bf16[128,192]{1,0:T(8,128)(2,1)S(1)} %get-tuple-element.85), channel_id=1, source_target_pairs={{0,4},{2,6},{4,8},{6,10},{8,12},{10,14},{12,0},{14,2},{1,5},{3,7},... | collective-permute-start | bytes 147464 | tf_op jit(solution)/shard_map/ppermute | solution.py:16
  81.0 2.8 %collective-permute-start.25 = (bf16[144,128]{1,0:T(8,128)(2,1)S(1)}, bf16[144,128]{1,0:T(8,128)(2,1)S(1)}, u32[]{:S(2)}, u32[]{:S(2)}) collective-permute-start(bf16[144,128]{1,0:T(8,128)(2,1)S(1)} %add_convert_fusion.5), channel_id=1, source_target_pairs={{0,32},{16,48},{32,0},{48,16},{64,96},{80,112},{96,64},{112,80},{1... | collective-permute-start | bytes 110600 | tf_op jit(solution)/shard_map/ppermute | solution.py:21
  85.4 5.1 %collective-permute-start.27 = (bf16[288,128]{1,0:T(8,128)(2,1)S(1)}, bf16[288,128]{1,0:T(8,128)(2,1)S(1)}, u32[]{:S(2)}, u32[]{:S(2)}) collective-permute-start(bf16[288,128]{1,0:T(8,128)(2,1)S(1)} %maximum_select_fusion.1), channel_id=1, source_target_pairs={{0,64},{16,80},{32,96},{48,112},{64,0},{80,16},{96,32},{112,48},{1... | collective-permute-start | bytes 221192 | tf_op jit(solution)/shard_map/ppermute | solution.py:21
  85.9 4.7 %collective-permute-start.26 = (bf16[64,192]{1,0:T(8,128)(2,1)S(1)}, bf16[64,192]{1,0:T(8,128)(2,1)S(1)}, u32[]{:S(2)}, u32[]{:S(2)}) collective-permute-start(bf16[64,192]{1,0:T(8,128)(2,1)S(1)} %select_convert_fusion), channel_id=1, source_target_pairs={{0,2},{2,0},{4,6},{6,4},{8,10},{10,8},{12,14},{14,12},{1,3},{3,1},... | collective-permute-start | bytes 73736 | tf_op jit(solution)/shard_map/ppermute | solution.py:21
  90.6 9.9 %collective-permute-start.28 = (bf16[576,128]{1,0:T(8,128)(2,1)S(1)}, bf16[576,128]{1,0:T(8,128)(2,1)S(1)}, u32[]{:S(2)}, u32[]{:S(2)}) collective-permute-start(bf16[576,128]{1,0:T(8,128)(2,1)S(1)} %maximum_select_fusion), channel_id=1, source_target_pairs={{0,16},{16,0},{32,48},{48,32},{64,80},{80,64},{96,112},{112,96},{1... | collective-permute-start | bytes 442376 | tf_op jit(solution)/shard_map/ppermute | solution.py:21

commit v6 on v5

--- a/solution.py
+++ b/solution.py
@@ -8,6 +8,7 @@
 BF = jnp.bfloat16
 F32 = jnp.float32
 WIDE = 80
+STEP = 3
 KEPT = 616
 
 
@@ -60,7 +61,7 @@
 
 
 def pair_kernel(
-    flags, pair, cot, top, bottom, halos, rowp, bins, weight, turned,
+    flags, pair, cot, top, bottom, halos, rowp, bins, ahead, back,
     out, keep, send, rowg,
     zwide, z3, cots, qwide, q3, wgrad, line, colp, packed, left, right,
 ):
@@ -110,17 +111,23 @@
 
     qwide[:, 0:8] = jnp.zeros((36, 8, chans), F32)
     qwide[:, 88:96] = jnp.zeros((36, 8, chans), F32)
-    for at in range(0, 36, 6):
-        taps = jnp.concatenate([z3[at + d : at + d + 6].reshape(6 * WIDE, 3 * chans) for d in range(3)], axis=1)
-        hidden = jnp.dot(taps, weight[...], preferred_element_type=F32).reshape(6, WIDE, chans)
-        sigma = jax.nn.sigmoid(hidden)
-        grown = hidden * sigma
-        q = cots[at : at + 6] * (sigma + grown * (1.0 - sigma))
-        qwide[at : at + 6, 8:88] = up(q.astype(BF))
-        lo, hi = max(at, 2), min(at + 6, 34)
-        out[lo - 2 : hi - 2] = (
-            zwide[lo + 1 : hi + 1, 8:72] + grown[lo - at : hi - at, 0:64]
-        ).astype(BF)
+
+    def taps(ref, at, count):
+        rows = [jnp.concatenate([ref[at + 2 * i + d] for i in range(count)]) for d in range(4)]
+        return jnp.concatenate(rows, axis=1)
+
+    for at in range(0, 36, 2 * STEP):
+        both = jnp.dot(taps(z3, at, STEP), ahead[...], preferred_element_type=F32)
+        for half in range(2):
+            for i in range(STEP):
+                row = at + 2 * i + half
+                hidden = both[i * WIDE : (i + 1) * WIDE, half * chans : (half + 1) * chans]
+                sigma = jax.nn.sigmoid(hidden)
+                grown = hidden * sigma
+                q = cots[row] * (sigma + grown * (1.0 - sigma))
+                qwide[row, 8:88] = up(q.astype(BF))
+                if 2 <= row < 34:
+                    out[row - 2] = (zwide[row + 1, 8:72] + grown[0:64]).astype(BF)
     qwide[:, 7:8] = qwide[:, 87:88]
     qwide[:, 88:89] = qwide[:, 8:9]
     for at in range(0, 36, 2):
@@ -138,20 +145,20 @@
             wgrad[at : at + chans] = part[:, across * chans : (across + 1) * chans].T
 
     total = jnp.zeros((WIDE, chans), F32)
-    rowg[...] = jnp.zeros((40, chans), BF)
-    for at in range(0, 34, 6):
-        count = min(6, 34 - at)
-        taps = jnp.concatenate(
-            [q3[at + 2 - d : at + 2 - d + count].reshape(count * WIDE, 3 * chans) for d in range(3)], axis=1
-        )
-        zgrad = jnp.dot(taps, turned[...], preferred_element_type=F32).reshape(count, WIDE, chans)
-        zgrad = zgrad + cots[at + 1 : at + 1 + count]
-        rowg[at : at + count] = jnp.sum(zgrad[:, 0:64] * colp[8:72][None], axis=1).astype(BF)
-        for i in range(count):
-            if 1 <= at + i < 33:
-                total = total + zgrad[i] * rowp[at + i + 2 : at + i + 3]
-    rowg[0:1] = jnp.where(has_up > 0, rowg[0:1], 0.0)
-    rowg[33:34] = jnp.where(has_down > 0, rowg[33:34], 0.0)
+    sums = {}
+    for at in range(0, 34, 2 * STEP):
+        count = min(STEP, (34 - at) // 2)
+        both = jnp.dot(taps(q3, at, count), back[...], preferred_element_type=F32)
+        for half in range(2):
+            for i in range(count):
+                row = at + 2 * i + half
+                zgrad = both[i * WIDE : (i + 1) * WIDE, half * chans : (half + 1) * chans] + cots[row + 1]
+                sums[row] = jnp.sum(zgrad[0:64] * colp[8:72], axis=0, keepdims=True)
+                if 1 <= row < 33:
+                    total = total + zgrad * rowp[row + 2 : row + 3]
+    sums[0] = jnp.where(has_up > 0, sums[0], 0.0)
+    sums[33] = jnp.where(has_down > 0, sums[33], 0.0)
+    rowg[...] = jnp.concatenate([sums[row] for row in range(34)] + [jnp.zeros((6, chans), F32)]).astype(BF)
     line[0:1] = jnp.where(has_left > 0, total[79:80], 0.0)
     line[1:65] = total[0:64]
     line[65:66] = jnp.where(has_right > 0, total[64:65], 0.0)
@@ -174,9 +181,23 @@
         copy.wait()
 
 
-def turn_kernel(weight, turned):
-    for at in range(0, weight.shape[0], 128):
-        turned[at : at + 128] = up(weight[at : at + 128]).T.astype(BF)
+def turn_kernel(weight, ahead, back):
+    chans = 128
+    size = 3 * chans
+    for row in range(4):
+        here = slice(size * row, size * row + size)
+        for out in range(2):
+            lanes = slice(chans * out, chans * out + chans)
+            tap = row - out
+            if 0 <= tap < 3:
+                ahead[here, lanes] = weight[size * tap : size * tap + size]
+                for across in range(3):
+                    at = size * (2 - tap) + chans * across
+                    turned = up(weight[at : at + chans]).T.astype(BF)
+                    back[size * row + chans * across : size * row + chans * across + chans, lanes] = turned
+            else:
+                ahead[here, lanes] = jnp.zeros((size, chans), BF)
+                back[here, lanes] = jnp.zeros((size, chans), BF)
 
 
 def begin_kernel(given, taken):
@@ -270,13 +291,14 @@
 HBM = pl.BlockSpec(memory_space=pltpu.HBM)
 
 
-def transposed(weight):
+def two_row_weights(weight):
+    shape = jax.ShapeDtypeStruct((12 * weight.shape[1], 2 * weight.shape[1]), BF)
     return pl.pallas_call(
         turn_kernel,
-        out_shape=jax.ShapeDtypeStruct(weight.shape, BF),
+        out_shape=(shape, shape),
         in_specs=[VMEM],
-        out_specs=VMEM,
-        compiler_params=pltpu.CompilerParams(vmem_limit_bytes=4 * 1024 * 1024),
+        out_specs=(VMEM, VMEM),
+        compiler_params=pltpu.CompilerParams(vmem_limit_bytes=6 * 1024 * 1024),
         cost_estimate=pl.CostEstimate(flops=40000000000, bytes_accessed=600000, transcendentals=0),
     )(weight)
 
@@ -332,7 +354,7 @@
     )(sums, proj_a, proj_b, conv_w)
 
 
-def pair_block(flags, pair, cot, top, bottom, halos, rowp, bins, weight, turned):
+def pair_block(flags, pair, cot, top, bottom, halos, rowp, bins, ahead, back):
     chans = 128
     return pl.pallas_call(
         pair_kernel,
@@ -359,7 +381,7 @@
         ],
         compiler_params=pltpu.CompilerParams(vmem_limit_bytes=24 * 1024 * 1024),
         cost_estimate=pl.CostEstimate(flops=2500000000, bytes_accessed=4000000, transcendentals=700000),
-    )(flags, pair, cot, top, bottom, halos, rowp, bins, weight, turned)
+    )(flags, pair, cot, top, bottom, halos, rowp, bins, ahead, back)
 
 
 def local(fine, conv_w, proj_a, proj_b, pair_in, pair_w, cotangent):
@@ -375,13 +397,13 @@
     is_there = [jnp.where(core == 0, apart == far, (apart == 8 - far) & (far < 4)) for far in (1, 2, 3, 4)]
     is_held = (apart == 0) | ((apart <= 4) == (core == 0))
     scalars = (core == 0, is_there, is_held, zpos == col, [(zpos ^ k) & 3 for k in range(4)], col % 2 == 1)
-    scalars += ([(col // 2 + k) & 3 for k in range(4)], (zpos & 1) == 1, (zpos & 2) == 2)
+    scalars += ([(col // 2 + k) & 3 for k in range(4)],)
     seed, flags, scalars = lax.optimization_barrier((jnp.zeros((8, 128), F32), flags, scalars))
-    is_first, is_there, is_held, is_root, places, is_odd, ahead, low_bit, high_bit = scalars
+    is_first, is_there, is_held, is_root, places, is_odd, ahead = scalars
     down, above = ends(fine, pair, cot, begin(seed))
     top, bottom = shift(down, "row", 1), shift(above, "row", -1)
     weight = pair_w.reshape(9 * pairs, pairs)
-    top, bottom, turned = lax.optimization_barrier((top, bottom, transposed(weight)))
+    top, bottom, weights = lax.optimization_barrier((top, bottom, two_row_weights(weight)))
     to_next, to_last = conv_forward(flags, fine, top, bottom, conv_w, proj_a, proj_b, pair, cot)
 
     across, from_last, from_next = shift(to_next[:80], "col", 4), shift(to_next, "col", 2), shift(to_last, "col", -2)
@@ -399,7 +421,7 @@
     for far, got in zip((4, 3, 2, 1), sent):
         colp = jnp.where(is_there[far - 1], got, colp)
     colp = jnp.where(is_held, colp, flip(colp, "row", 1))
-    out, keep, send, rowg = pair_block(flags, pair, cot, top, bottom, halos, rowp, up(colp), weight, turned)
+    out, keep, send, rowg = pair_block(flags, pair, cot, top, bottom, halos, rowp, up(colp), *weights)
 
     total = (keep + up(flip(send, "row", 1))).astype(BF)
     half, colg = total[:576].reshape(4, 144, pairs), total[576:]
@@ -415,22 +437,23 @@
     total = sum_flip(total, "row", 8)
     colg = jnp.where(is_root, total[144:], 0)
     total = sum_y(jnp.concatenate([total[:144], rowg, colg]))
-    total = sum_flip(total, "col", 1)
-    quart, sums = total[:144], total[144:]
+
+    quart = total[:144]
+    across, others = flip(total, "col", 1), flip(quart, "batch", 1)
+    crossed = lax.ppermute(quart, ("col", "batch"), [(i, i ^ 3) for i in range(16)])
+    sums = (up(total[144:]) + up(across[144:])).astype(BF)
     parts = conv_backward(sums, proj_a, proj_b, conv_w)
-    quart = sum_flip(quart, "batch", 1)
+    quart = ((up(quart) + up(across[:144])) + (up(others) + up(crossed))).astype(BF)
     parts, quart = lax.optimization_barrier((parts, quart))
 
     parts = parts.reshape(4, 128, parts.shape[2])
     got = [shift(taken(parts, ahead[k]), "col", 2 * k) for k in (1, 2, 3)]
-    near = flip(quart, "row", 2)
+    near = [flip(quart, "row", 2 * k) for k in (1, 2, 3)]
     got, near = lax.optimization_barrier((got, near))
     mine = (up(taken(parts, ahead[0])) + up(got[0])) + (up(got[1]) + up(got[2]))
-    two = jnp.where(low_bit, jnp.concatenate([near, quart]), jnp.concatenate([quart, near]))
+    near = jnp.stack([quart] + near)
+    half = jnp.concatenate([taken(near, places[k]) for k in range(4)])
     other = flip(jnp.where(is_odd, mine[:64], mine[64:]).astype(BF), "col", 1)
-    far = flip(two, "row", 4)
-    other, far = lax.optimization_barrier((other, far))
-    half = jnp.where(high_bit, jnp.concatenate([far, two]), jnp.concatenate([two, far]))
     theirs = flip(half, "row", 1)
     grad_pair_w = jnp.concatenate([jnp.where(is_first, half, theirs), jnp.where(is_first, theirs, half)])
     grad_pair_w = up(grad_pair_w).reshape(3, 3, pairs, pairs) / 512.0

time: 101 us -> 98.9 us (0.979)
  the two profiles are of different devices: /device:TPU:1 before, /device:TPU:2 now
where the time goes in v6:
time: 98.9 us; the launch traced here: 97 us
  starting transfers between devices  43.2 us (44%)
  waiting for transfers between devices  40.4 us (41%)
  Pallas kernels  9.12 us (9%)
  other arithmetic  1.93 us (2%)
  local copies, waits for them, and re-layouts  1.32 us (1%)
  between operations  1.09 us (1%)
    ppermute x15, waiting for transfers between devices, flip(): return lax.ppermute(x, axis, [(i, i ^ bit) for i in range(count)])  24.5 us
    ppermute x15, starting transfers between devices, flip(): return lax.ppermute(x, axis, [(i, i ^ bit) for i in range(count)])  20.5 us
    ppermute x11, starting transfers between devices, shift(): lax.ppermute(x, axis, [(i, (i + step) % count) for i in range(count)])  17.7 us
    ppermute x11, waiting for transfers between devices, shift(): lax.ppermute(x, axis, [(i, (i + step) % count) for i in range(count)])  9.48 us
    pallas_call x1, Pallas kernels, pair_block(): pl.pallas_call(pair_kernel, out_shape=(jax.ShapeDtypeStruct((32, 64, chan...  5.57 us
    ppermute x4, waiting for transfers between devices, spread(): return lax.ppermute(x, ('row', 'col'), sorted(pairs.items()))  4.97 us
    ppermute x4, starting transfers between devices, spread(): return lax.ppermute(x, ('row', 'col'), sorted(pairs.items()))  4.93 us
  transfers between devices with their start and end apart: 31, of which 21 were waited for; matrix products, arithmetic and copies ran while one was open for 1% of the time, Pallas kernels for 1%

profile of v6, /device:TPU:2, one launch (start us, length us, event | category | flops | bytes accessed | tf_op | source)
XLA Modules:
  0.0 97.0 jit_solution(13268400516134873288)
XLA Ops:
  0.8 0.0 copy-start.1
  0.8 0.0 copy-start.2
  0.8 0.0 copy-start.3
  0.8 0.0 copy-start.6
  0.8 1.0 %copy-done.1 = bf16[1,32,64,128]{3,2,1,0:T(8,128)(2,1)S(1)} copy-done((bf16[1,32,64,128]{3,2,1,0:T(8,128)(2,1)S(1)}, bf16[1,32,64,128]{3,2,1,0:T(8,128)(2,1)}, u32[]{:S(2)}) %copy-start.1) | copy-done | bytes 524312
  1.8 0.2 copy-done.2
  2.0 0.0 copy-done.3
  2.0 0.5 shard_map.95
  2.6 0.0 collective-permute-start
  2.6 5.3 %collective-permute-start.1 = (bf16[8,64,128]{2,1,0:T(8,128)(2,1)S(1)}, bf16[8,64,128]{2,1,0:T(8,128)(2,1)S(1)}, u32[]{:S(2)}, u32[]{:S(2)}) collective-permute-start(bf16[8,64,128]{2,1,0:T(8,128)(2,1)S(1)} %get-tuple-element.46), channel_id=1, source_target_pairs={{0,240},{16,0},{32,16},{48,32},{64,48},{80,64},{96,80},{112,96},{1... | collective-permute-start | bytes 393224 | tf_op jit(solution)/shard_map/ppermute | solution.py:17
  7.9 0.3 shard_map.96
  8.2 2.3 %collective-permute-done.top = bf16[8,64,128]{2,1,0:T(8,128)(2,1)S(1)} collective-permute-done((bf16[8,64,128]{2,1,0:T(8,128)(2,1)S(1)}, bf16[8,64,128]{2,1,0:T(8,128)(2,1)S(1)}, u32[]{:S(2)}, u32[]{:S(2)}) %collective-permute-start) | collective-permute-done | bytes 131104 | tf_op jit(solution)/shard_map/ppermute | solution.py:17
  10.5 0.0 collective-permute-done.1.bottom
  10.5 1.8 %shard_map.97 = (bf16[272,128]{1,0:T(8,128)(2,1)S(1)}, bf16[272,128]{1,0:T(8,128)(2,1)S(1)}) custom-call(s32[8]{0:T(128)S(1)} %select_convert_fusion.2.flags, bf16[64,1536]{1,0:T(8,128)(2,1)S(1)} %bitcast.48, bf16[8,64,128]{2,1,0:T(8,128)(2,1)S(1)} %collective-permute-done.top, bf16[8,64,128]{2,1,0:T(8,128)(2,1)S(1)} %collective-permute-done.1.bottom, ...), custom_call_target="tpu_custom_call" | custom-call | flops 120000000 | bytes 3500000 | tf_op jit(solution)/shard_map/pallas_call | solution.py:333
  12.3 3.1 %collective-permute-start.4 = (bf16[272,128]{1,0:T(8,128)(2,1)S(1)}, bf16[272,128]{1,0:T(8,128)(2,1)S(1)}, u32[]{:S(2)}, u32[]{:S(2)}) collective-permute-start(bf16[272,128]{1,0:T(8,128)(2,1)S(1)} %get-tuple-element.52), channel_id=1, source_target_pairs={{0,12},{2,14},{4,0},{6,2},{8,4},{10,6},{12,8},{14,10},{1,13},{3,15... | collective-permute-start | bytes 208904 | tf_op jit(solution)/shard_map/ppermute | solution.py:17
  15.4 0.0 collective-permute-start.3
  15.4 2.2 %collective-permute-start.2 = (bf16[80,128]{1,0:T(8,128)(2,1)S(1)}, bf16[80,128]{1,0:T(8,128)(2,1)S(1)}, u32[]{:S(2)}, u32[]{:S(2)}) collective-permute-start(bf16[80,128]{1,0:T(8,128)(2,1)S(1)} %slice.73), channel_id=1, source_target_pairs={{0,8},{2,10},{4,12},{6,14},{8,0},{10,2},{12,4},{14,6},{1,9},{3,11}... | collective-permute-start | bytes 61448 | tf_op jit(solution)/shard_map/ppermute | solution.py:17
  17.6 0.0 collective-permute-done.4
  17.6 3.5 %collective-permute-done.3 = bf16[272,128]{1,0:T(8,128)(2,1)S(1)} collective-permute-done((bf16[272,128]{1,0:T(8,128)(2,1)S(1)}, bf16[272,128]{1,0:T(8,128)(2,1)S(1)}, u32[]{:S(2)}, u32[]{:S(2)}) %collective-permute-start.3) | collective-permute-done | bytes 69664 | tf_op jit(solution)/shard_map/ppermute | solution.py:17
  21.2 2.2 %collective-permute-start.5 = (bf16[464,128]{1,0:T(8,128)(2,1)S(1)}, bf16[464,128]{1,0:T(8,128)(2,1)S(1)}, u32[]{:S(2)}, u32[]{:S(2)}) collective-permute-start(bf16[464,128]{1,0:T(8,128)(2,1)S(1)} %pad_maximum_fusion.2), channel_id=1, source_target_pairs={{0,2},{2,0},{4,6},{6,4},{8,10},{10,8},{12,14},{14,12},{1,3},{3,1},... | collective-permute-start | bytes 356360 | tf_op jit(solution)/shard_map/ppermute | solution.py:22
  23.4 4.2 %collective-permute-done.5 = bf16[464,128]{1,0:T(8,128)(2,1)S(1)} collective-permute-done((bf16[464,128]{1,0:T(8,128)(2,1)S(1)}, bf16[464,128]{1,0:T(8,128)(2,1)S(1)}, u32[]{:S(2)}, u32[]{:S(2)}) %collective-permute-start.5) | collective-permute-done | bytes 118816 | tf_op jit(solution)/shard_map/ppermute | solution.py:22
  27.7 0.1 collective-permute-start.6
  27.8 1.2 %collective-permute-done.6 = bf16[35,128]{1,0:T(8,128)(2,1)S(1)} collective-permute-done((bf16[35,128]{1,0:T(8,128)(2,1)S(1)}, bf16[35,128]{1,0:T(8,128)(2,1)S(1)}, u32[]{:S(2)}, u32[]{:S(2)}) %collective-permute-start.6) | collective-permute-done | bytes 8992 | tf_op jit(solution)/shard_map/ppermute | solution.py:22
  29.0 4.9 %collective-permute-start.10 = (bf16[70,128]{1,0:T(8,128)(2,1)S(1)}, bf16[70,128]{1,0:T(8,128)(2,1)S(1)}, u32[]{:S(2)}, u32[]{:S(2)}) collective-permute-start(bf16[70,128]{1,0:T(8,128)(2,1)S(1)} %pad_maximum_fusion.8), channel_id=1, source_target_pairs={{0,128},{2,18},{4,20},{6,22},{8,24},{10,26},{12,28},{14,30},{16,0}... | collective-permute-start | bytes 53768 | tf_op jit(solution)/shard_map/ppermute | solution.py:43
  33.9 1.4 %collective-permute-done.10 = bf16[70,128]{1,0:T(8,128)(2,1)S(1)} collective-permute-done((bf16[70,128]{1,0:T(8,128)(2,1)S(1)}, bf16[70,128]{1,0:T(8,128)(2,1)S(1)}, u32[]{:S(2)}, u32[]{:S(2)}) %collective-permute-start.10) | collective-permute-done | bytes 17952 | tf_op jit(solution)/shard_map/ppermute | solution.py:43
  35.4 3.5 %collective-permute-done.9 = bf16[70,128]{1,0:T(8,128)(2,1)S(1)} collective-permute-done((bf16[70,128]{1,0:T(8,128)(2,1)S(1)}, bf16[70,128]{1,0:T(8,128)(2,1)S(1)}, u32[]{:S(2)}, u32[]{:S(2)}) %collective-permute-start.9) | collective-permute-done | bytes 17952 | tf_op jit(solution)/shard_map/ppermute | solution.py:43
  38.9 0.2 collective-permute-start.11
  39.1 1.1 %collective-permute-done.11 = bf16[70,128]{1,0:T(8,128)(2,1)S(1)} collective-permute-done((bf16[70,128]{1,0:T(8,128)(2,1)S(1)}, bf16[70,128]{1,0:T(8,128)(2,1)S(1)}, u32[]{:S(2)}, u32[]{:S(2)}) %collective-permute-start.11) | collective-permute-done | bytes 17952 | tf_op jit(solution)/shard_map/ppermute | solution.py:22
  40.2 5.6 %shard_map.98 = (bf16[32,64,128]{2,1,0:T(8,128)(2,1)}, f32[616,128]{1,0:T(8,128)S(1)}, bf16[616,128]{1,0:T(8,128)(2,1)S(1)}, bf16[40,128]{1,0:T(8,128)(2,1)S(1)}) custom-call(s32[8]{0:T(128)S(1)} %select_convert_fusion.2.flags, bf16[32,64,128]{2,1,0:T(8,128)(2,1)S(1)} %bitcast.41, bf16[32,64,128]{2,1,0:T(8,128)(2,1)S(1)} %bitcast.44, ...), custom_call_target="tpu_custom_call" | custom-call | flops 2500000000 | bytes 4000000 | tf_op jit(solution)/shard_map/pallas_call | solution.py:359
  45.8 0.2 collective-permute-start.12
  45.9 1.2 %collective-permute-done.12 = bf16[616,128]{1,0:T(8,128)(2,1)S(1)} collective-permute-done((bf16[616,128]{1,0:T(8,128)(2,1)S(1)}, bf16[616,128]{1,0:T(8,128)(2,1)S(1)}, u32[]{:S(2)}, u32[]{:S(2)}) %collective-permute-start.12) | collective-permute-done | bytes 157728 | tf_op jit(solution)/shard_map/ppermute | solution.py:22
  47.3 0.1 collective-permute-start.13
  47.4 1.3 %collective-permute-start.14 = (bf16[184,128]{1,0:T(8,128)(2,1)S(1)}, bf16[184,128]{1,0:T(8,128)(2,1)S(1)}, u32[]{:S(2)}, u32[]{:S(2)}) collective-permute-start(bf16[184,128]{1,0:T(8,128)(2,1)S(1)} %get-tuple-element.101), channel_id=1, source_target_pairs={{0,64},{16,80},{32,96},{48,112},{64,0},{80,16},{96,32},{112,48},{1... | collective-permute-start | bytes 141320 | tf_op jit(solution)/shard_map/ppermute | solution.py:22
  48.7 3.0 %collective-permute-start.15 = (bf16[184,128]{1,0:T(8,128)(2,1)S(1)}, bf16[184,128]{1,0:T(8,128)(2,1)S(1)}, u32[]{:S(2)}, u32[]{:S(2)}) collective-permute-start(bf16[184,128]{1,0:T(8,128)(2,1)S(1)} %get-tuple-element.102), channel_id=1, source_target_pairs={{0,96},{16,112},{32,64},{48,80},{64,32},{80,48},{96,0},{112,16},{1... | collective-permute-start | bytes 141320 | tf_op jit(solution)/shard_map/ppermute | solution.py:22
  51.8 0.2 collective-permute-done.13
  52.0 2.7 %collective-permute-done.14 = bf16[184,128]{1,0:T(8,128)(2,1)S(1)} collective-permute-done((bf16[184,128]{1,0:T(8,128)(2,1)S(1)}, bf16[184,128]{1,0:T(8,128)(2,1)S(1)}, u32[]{:S(2)}, u32[]{:S(2)}) %collective-permute-start.14) | collective-permute-done | bytes 47136 | tf_op jit(solution)/shard_map/ppermute | solution.py:22
  54.7 2.8 %collective-permute-start.16 = (bf16[184,128]{1,0:T(8,128)(2,1)S(1)}, bf16[184,128]{1,0:T(8,128)(2,1)S(1)}, u32[]{:S(2)}, u32[]{:S(2)}) collective-permute-start(bf16[184,128]{1,0:T(8,128)(2,1)S(1)} %add_convert_fusion.3), channel_id=1, source_target_pairs={{0,128},{16,144},{32,160},{48,176},{64,192},{80,208},{96,224},{112... | collective-permute-start | bytes 141320 | tf_op jit(solution)/shard_map/ppermute | solution.py:22
  57.5 5.8 %collective-permute-done.16 = bf16[184,128]{1,0:T(8,128)(2,1)S(1)} collective-permute-done((bf16[184,128]{1,0:T(8,128)(2,1)S(1)}, bf16[184,128]{1,0:T(8,128)(2,1)S(1)}, u32[]{:S(2)}, u32[]{:S(2)}) %collective-permute-start.16) | collective-permute-done | bytes 47136 | tf_op jit(solution)/shard_map/ppermute | solution.py:22
  63.3 0.8 collective-permute-start.18
  64.1 0.5 collective-permute-start.17
  64.6 2.3 %collective-permute-start.19 = (bf16[224,128]{1,0:T(8,128)(2,1)S(1)}, bf16[224,128]{1,0:T(8,128)(2,1)S(1)}, u32[]{:S(2)}, u32[]{:S(2)}) collective-permute-start(bf16[224,128]{1,0:T(8,128)(2,1)S(1)} %pad_maximum_fusion.7), channel_id=1, source_target_pairs={{0,12},{2,14},{4,0},{6,2},{8,4},{10,6},{12,8},{14,10},{1,13},{3,15... | collective-permute-start | bytes 172040 | tf_op jit(solution)/shard_map/ppermute | solution.py:17
  66.9 1.9 %collective-permute-done.18 = bf16[224,128]{1,0:T(8,128)(2,1)S(1)} collective-permute-done((bf16[224,128]{1,0:T(8,128)(2,1)S(1)}, bf16[224,128]{1,0:T(8,128)(2,1)S(1)}, u32[]{:S(2)}, u32[]{:S(2)}) %collective-permute-start.18) | collective-permute-done | bytes 57376 | tf_op jit(solution)/shard_map/ppermute | solution.py:17
  68.8 1.0 %collective-permute-done.17 = bf16[224,128]{1,0:T(8,128)(2,1)S(1)} collective-permute-done((bf16[224,128]{1,0:T(8,128)(2,1)S(1)}, bf16[224,128]{1,0:T(8,128)(2,1)S(1)}, u32[]{:S(2)}, u32[]{:S(2)}) %collective-permute-start.17) | collective-permute-done | bytes 57376 | tf_op jit(solution)/shard_map/ppermute | solution.py:17
  69.8 0.5 collective-permute-done.19
  70.3 3.2 %collective-permute-start.20 = (bf16[224,128]{1,0:T(8,128)(2,1)S(1)}, bf16[224,128]{1,0:T(8,128)(2,1)S(1)}, u32[]{:S(2)}, u32[]{:S(2)}) collective-permute-start(bf16[224,128]{1,0:T(8,128)(2,1)S(1)} %add_convert_fusion.1), channel_id=1, source_target_pairs={{0,2},{2,0},{4,6},{6,4},{8,10},{10,8},{12,14},{14,12},{1,3},{3,1},... | collective-permute-start | bytes 172040 | tf_op jit(solution)/shard_map/ppermute | solution.py:22
  73.5 1.4 %collective-permute-start.21 = (bf16[144,128]{1,0:T(8,128)(2,1)S(1)}, bf16[144,128]{1,0:T(8,128)(2,1)S(1)}, u32[]{:S(2)}, u32[]{:S(2)}) collective-permute-start(bf16[144,128]{1,0:T(8,128)(2,1)S(1)} %slice.110), channel_id=1, source_target_pairs={{0,1},{1,0},{2,3},{3,2},{4,5},{5,4},{6,7},{7,6},{8,9},{9,8},{10,11... | collective-permute-start | bytes 110600 | tf_op jit(solution)/shard_map/ppermute | solution.py:22
  74.9 1.2 %collective-permute-done.20 = bf16[224,128]{1,0:T(8,128)(2,1)S(1)} collective-permute-done((bf16[224,128]{1,0:T(8,128)(2,1)S(1)}, bf16[224,128]{1,0:T(8,128)(2,1)S(1)}, u32[]{:S(2)}, u32[]{:S(2)}) %collective-permute-start.20) | collective-permute-done | bytes 57376 | tf_op jit(solution)/shard_map/ppermute | solution.py:22
  76.1 0.9 shard_map.99
  77.0 0.4 collective-permute-done.21
  77.4 1.4 %collective-permute-done.22 = bf16[144,128]{1,0:T(8,128)(2,1)S(1)} collective-permute-done((bf16[144,128]{1,0:T(8,128)(2,1)S(1)}, bf16[144,128]{1,0:T(8,128)(2,1)S(1)}, u32[]{:S(2)}, u32[]{:S(2)}) %collective-permute-start.22) | collective-permute-done | bytes 36896 | tf_op jit(solution)/shard_map/ppermute | solution.py:443
  78.9 2.0 %collective-permute-start.28 = (bf16[144,128]{1,0:T(8,128)(2,1)S(1)}, bf16[144,128]{1,0:T(8,128)(2,1)S(1)}, u32[]{:S(2)}, u32[]{:S(2)}) collective-permute-start(bf16[144,128]{1,0:T(8,128)(2,1)S(1)} %add_convert_fusion.4), channel_id=1, source_target_pairs={{0,96},{16,112},{32,64},{48,80},{64,32},{80,48},{96,0},{112,16},{1... | collective-permute-start | bytes 110600 | tf_op jit(solution)/shard_map/ppermute | solution.py:22
  80.8 2.5 %collective-permute-start.25 = (bf16[128,192]{1,0:T(8,128)(2,1)S(1)}, bf16[128,192]{1,0:T(8,128)(2,1)S(1)}, u32[]{:S(2)}, u32[]{:S(2)}) collective-permute-start(bf16[128,192]{1,0:T(8,128)(2,1)S(1)} %get-tuple-element.85), channel_id=1, source_target_pairs={{0,12},{2,14},{4,0},{6,2},{8,4},{10,6},{12,8},{14,10},{1,13},{3,15... | collective-permute-start | bytes 147464 | tf_op jit(solution)/shard_map/ppermute | solution.py:17
  83.3 1.1 %collective-permute-start.24 = (bf16[128,192]{1,0:T(8,128)(2,1)S(1)}, bf16[128,192]{1,0:T(8,128)(2,1)S(1)}, u32[]{:S(2)}, u32[]{:S(2)}) collective-permute-start(bf16[128,192]{1,0:T(8,128)(2,1)S(1)} %get-tuple-element.86), channel_id=1, source_target_pairs={{0,8},{2,10},{4,12},{6,14},{8,0},{10,2},{12,4},{14,6},{1,9},{3,11}... | collective-permute-start | bytes 147464 | tf_op jit(solution)/shard_map/ppermute | solution.py:17
  84.4 0.8 collective-permute-start.27
  85.2 1.7 %collective-permute-start.26 = (bf16[144,128]{1,0:T(8,128)(2,1)S(1)}, bf16[144,128]{1,0:T(8,128)(2,1)S(1)}, u32[]{:S(2)}, u32[]{:S(2)}) collective-permute-start(bf16[144,128]{1,0:T(8,128)(2,1)S(1)} %add_convert_fusion.4), channel_id=1, source_target_pairs={{0,32},{16,48},{32,0},{48,16},{64,96},{80,112},{96,64},{112,80},{1... | collective-permute-start | bytes 110600 | tf_op jit(solution)/shard_map/ppermute | solution.py:22
  86.9 2.4 %collective-permute-done.27 = bf16[144,128]{1,0:T(8,128)(2,1)S(1)} collective-permute-done((bf16[144,128]{1,0:T(8,128)(2,1)S(1)}, bf16[144,128]{1,0:T(8,128)(2,1)S(1)}, u32[]{:S(2)}, u32[]{:S(2)}) %collective-permute-start.27) | collective-permute-done | bytes 36896 | tf_op jit(solution)/shard_map/ppermute | solution.py:22
  89.4 0.2 collective-permute-done.26
  89.6 0.3 collective-permute-done.23
  89.9 1.4 %collective-permute-start.29 = (bf16[64,192]{1,0:T(8,128)(2,1)S(1)}, bf16[64,192]{1,0:T(8,128)(2,1)S(1)}, u32[]{:S(2)}, u32[]{:S(2)}) collective-permute-start(bf16[64,192]{1,0:T(8,128)(2,1)S(1)} %select_convert_fusion), channel_id=1, source_target_pairs={{0,2},{2,0},{4,6},{6,4},{8,10},{10,8},{12,14},{14,12},{1,3},{3,1},... | collective-permute-start | bytes 73736 | tf_op jit(solution)/shard_map/ppermute | solution.py:22
  91.5 0.1 collective-permute-start.30
  91.6 3.9 %collective-permute-done.29 = bf16[64,192]{1,0:T(8,128)(2,1)S(1)} collective-permute-done((bf16[64,192]{1,0:T(8,128)(2,1)S(1)}, bf16[64,192]{1,0:T(8,128)(2,1)S(1)}, u32[]{:S(2)}, u32[]{:S(2)}) %collective-permute-start.29) | collective-permute-done | bytes 24608 | tf_op jit(solution)/shard_map/ppermute | solution.py:22
  95.4 0.6 fusion.1
  96.1 0.1 broadcast_select_fusion.1
  96.1 0.9 convert_multiply_fusion
  (56 shorter events, 0.5 us)
Async XLA Ops:
  0.8 1.0 %copy-start.1 = (bf16[1,32,64,128]{3,2,1,0:T(8,128)(2,1)S(1)}, bf16[1,32,64,128]{3,2,1,0:T(8,128)(2,1)}, u32[]{:S(2)}) copy-start(bf16[1,32,64,128]{3,2,1,0:T(8,128)(2,1)} %param.11) | copy-start | bytes 1572868
  0.8 1.2 %copy-start.2 = (bf16[1,32,64,128]{3,2,1,0:T(8,128)(2,1)S(1)}, bf16[1,32,64,128]{3,2,1,0:T(8,128)(2,1)}, u32[]{:S(2)}) copy-start(bf16[1,32,64,128]{3,2,1,0:T(8,128)(2,1)} %param.13) | copy-start | bytes 1572868
  0.8 1.2 %copy-start.3 = (bf16[1,64,1536]{2,1,0:T(8,128)(2,1)S(1)}, bf16[1,64,1536]{2,1,0:T(8,128)(2,1)}, u32[]{:S(2)}) copy-start(bf16[1,64,1536]{2,1,0:T(8,128)(2,1)} %param.7) | copy-start | bytes 589828
  0.8 7.1 %copy-start.6 = (bf16[3,3,128,128]{3,2,1,0:T(8,128)(2,1)S(1)}, bf16[3,3,128,128]{3,2,1,0:T(8,128)(2,1)}, u32[]{:S(2)}) copy-start(bf16[3,3,128,128]{3,2,1,0:T(8,128)(2,1)} %param.12) | copy-start | bytes 884740
  2.6 8.0 %collective-permute-start = (bf16[8,64,128]{2,1,0:T(8,128)(2,1)S(1)}, bf16[8,64,128]{2,1,0:T(8,128)(2,1)S(1)}, u32[]{:S(2)}, u32[]{:S(2)}) collective-permute-start(bf16[8,64,128]{2,1,0:T(8,128)(2,1)S(1)} %get-tuple-element.45), channel_id=1, source_target_pairs={{0,16},{16,32},{32,48},{48,64},{64,80},{80,96},{96,112},{112,128},... | collective-permute-start | bytes 393224 | tf_op jit(solution)/shard_map/ppermute | solution.py:17
  2.6 7.9 %collective-permute-start.1 = (bf16[8,64,128]{2,1,0:T(8,128)(2,1)S(1)}, bf16[8,64,128]{2,1,0:T(8,128)(2,1)S(1)}, u32[]{:S(2)}, u32[]{:S(2)}) collective-permute-start(bf16[8,64,128]{2,1,0:T(8,128)(2,1)S(1)} %get-tuple-element.46), channel_id=1, source_target_pairs={{0,240},{16,0},{32,16},{48,32},{64,48},{80,64},{96,80},{112,96},{1... | collective-permute-start | bytes 393224 | tf_op jit(solution)/shard_map/ppermute | solution.py:17
  7.9 2.6 %copy-start = (bf16[5,192,1536]{2,1,0:T(8,128)(2,1)S(1)}, bf16[5,192,1536]{2,1,0:T(8,128)(2,1)}, u32[]{:S(2)}) copy-start(bf16[5,192,1536]{2,1,0:T(8,128)(2,1)} %conv_w.3) | copy-start | bytes 8847364
  7.9 2.6 %copy-start.4 = (bf16[192,128]{1,0:T(8,128)(2,1)S(1)}, bf16[192,128]{1,0:T(8,128)(2,1)}, u32[]{:S(2)}) copy-start(bf16[192,128]{1,0:T(8,128)(2,1)} %proj_a.3) | copy-start | bytes 147460
  7.9 2.6 %copy-start.5 = (bf16[192,128]{1,0:T(8,128)(2,1)S(1)}, bf16[192,128]{1,0:T(8,128)(2,1)}, u32[]{:S(2)}) copy-start(bf16[192,128]{1,0:T(8,128)(2,1)} %proj_b.3) | copy-start | bytes 147460
  12.3 5.3 %collective-permute-start.4 = (bf16[272,128]{1,0:T(8,128)(2,1)S(1)}, bf16[272,128]{1,0:T(8,128)(2,1)S(1)}, u32[]{:S(2)}, u32[]{:S(2)}) collective-permute-start(bf16[272,128]{1,0:T(8,128)(2,1)S(1)} %get-tuple-element.52), channel_id=1, source_target_pairs={{0,12},{2,14},{4,0},{6,2},{8,4},{10,6},{12,8},{14,10},{1,13},{3,15... | collective-permute-start | bytes 208904 | tf_op jit(solution)/shard_map/ppermute | solution.py:17
  15.4 5.7 %collective-permute-start.3 = (bf16[272,128]{1,0:T(8,128)(2,1)S(1)}, bf16[272,128]{1,0:T(8,128)(2,1)S(1)}, u32[]{:S(2)}, u32[]{:S(2)}) collective-permute-start(bf16[272,128]{1,0:T(8,128)(2,1)S(1)} %get-tuple-element.51), channel_id=1, source_target_pairs={{0,4},{2,6},{4,8},{6,10},{8,12},{10,14},{12,0},{14,2},{1,5},{3,7},... | collective-permute-start | bytes 208904 | tf_op jit(solution)/shard_map/ppermute | solution.py:17
  15.4 5.8 %collective-permute-start.2 = (bf16[80,128]{1,0:T(8,128)(2,1)S(1)}, bf16[80,128]{1,0:T(8,128)(2,1)S(1)}, u32[]{:S(2)}, u32[]{:S(2)}) collective-permute-start(bf16[80,128]{1,0:T(8,128)(2,1)S(1)} %slice.73), channel_id=1, source_target_pairs={{0,8},{2,10},{4,12},{6,14},{8,0},{10,2},{12,4},{14,6},{1,9},{3,11}... | collective-permute-start | bytes 61448 | tf_op jit(solution)/shard_map/ppermute | solution.py:17
  21.2 6.4 %collective-permute-start.5 = (bf16[464,128]{1,0:T(8,128)(2,1)S(1)}, bf16[464,128]{1,0:T(8,128)(2,1)S(1)}, u32[]{:S(2)}, u32[]{:S(2)}) collective-permute-start(bf16[464,128]{1,0:T(8,128)(2,1)S(1)} %pad_maximum_fusion.2), channel_id=1, source_target_pairs={{0,2},{2,0},{4,6},{6,4},{8,10},{10,8},{12,14},{14,12},{1,3},{3,1},... | collective-permute-start | bytes 356360 | tf_op jit(solution)/shard_map/ppermute | solution.py:22
  27.7 1.3 %collective-permute-start.6 = (bf16[35,128]{1,0:T(8,128)(2,1)S(1)}, bf16[35,128]{1,0:T(8,128)(2,1)S(1)}, u32[]{:S(2)}, u32[]{:S(2)}) collective-permute-start(bf16[35,128]{1,0:T(8,128)(2,1)S(1)} %slice_select_fusion.3), channel_id=1, source_target_pairs={{0,16},{16,0},{32,48},{48,32},{64,80},{80,64},{96,112},{112,96},{1... | collective-permute-start | bytes 26888 | tf_op jit(solution)/shard_map/ppermute | solution.py:22
  29.0 6.4 %collective-permute-start.10 = (bf16[70,128]{1,0:T(8,128)(2,1)S(1)}, bf16[70,128]{1,0:T(8,128)(2,1)S(1)}, u32[]{:S(2)}, u32[]{:S(2)}) collective-permute-start(bf16[70,128]{1,0:T(8,128)(2,1)S(1)} %pad_maximum_fusion.8), channel_id=1, source_target_pairs={{0,128},{2,18},{4,20},{6,22},{8,24},{10,26},{12,28},{14,30},{16,0}... | collective-permute-start | bytes 53768 | tf_op jit(solution)/shard_map/ppermute | solution.py:43
  33.9 5.0 %collective-permute-start.9 = (bf16[70,128]{1,0:T(8,128)(2,1)S(1)}, bf16[70,128]{1,0:T(8,128)(2,1)S(1)}, u32[]{:S(2)}, u32[]{:S(2)}) collective-permute-start(bf16[70,128]{1,0:T(8,128)(2,1)S(1)} %pad_maximum_fusion.8), channel_id=1, source_target_pairs={{0,96},{2,18},{4,20},{6,102},{8,24},{10,26},{12,28},{14,30},{16,17... | collective-permute-start | bytes 53768 | tf_op jit(solution)/shard_map/ppermute | solution.py:43
  33.9 5.0 %collective-permute-start.8 = (bf16[70,128]{1,0:T(8,128)(2,1)S(1)}, bf16[70,128]{1,0:T(8,128)(2,1)S(1)}, u32[]{:S(2)}, u32[]{:S(2)}) collective-permute-start(bf16[70,128]{1,0:T(8,128)(2,1)S(1)} %pad_maximum_fusion.8), channel_id=1, source_target_pairs={{0,64},{2,18},{4,68},{6,22},{8,24},{10,26},{12,28},{14,30},{16,208... | collective-permute-start | bytes 53768 | tf_op jit(solution)/shard_map/ppermute | solution.py:43
  33.9 5.0 %collective-permute-start.7 = (bf16[70,128]{1,0:T(8,128)(2,1)S(1)}, bf16[70,128]{1,0:T(8,128)(2,1)S(1)}, u32[]{:S(2)}, u32[]{:S(2)}) collective-permute-start(bf16[70,128]{1,0:T(8,128)(2,1)S(1)} %pad_maximum_fusion.8), channel_id=1, source_target_pairs={{0,32},{2,34},{4,20},{6,22},{8,24},{10,26},{12,28},{14,30},{16,240... | collective-permute-start | bytes 53768 | tf_op jit(solution)/shard_map/ppermute | solution.py:43
  38.9 1.3 %collective-permute-start.11 = (bf16[70,128]{1,0:T(8,128)(2,1)S(1)}, bf16[70,128]{1,0:T(8,128)(2,1)S(1)}, u32[]{:S(2)}, u32[]{:S(2)}) collective-permute-start(bf16[70,128]{1,0:T(8,128)(2,1)S(1)} %select_select_fusion), channel_id=1, source_target_pairs={{0,16},{16,0},{32,48},{48,32},{64,80},{80,64},{96,112},{112,96},{1... | collective-permute-start | bytes 53768 | tf_op jit(solution)/shard_map/ppermute | solution.py:22
  45.8 1.4 %collective-permute-start.12 = (bf16[616,128]{1,0:T(8,128)(2,1)S(1)}, bf16[616,128]{1,0:T(8,128)(2,1)S(1)}, u32[]{:S(2)}, u32[]{:S(2)}) collective-permute-start(bf16[616,128]{1,0:T(8,128)(2,1)S(1)} %get-tuple-element.64), channel_id=1, source_target_pairs={{0,16},{16,0},{32,48},{48,32},{64,80},{80,64},{96,112},{112,96},{1... | collective-permute-start | bytes 473096 | tf_op jit(solution)/shard_map/ppermute | solution.py:22
  47.3 4.7 %collective-permute-start.13 = (bf16[184,128]{1,0:T(8,128)(2,1)S(1)}, bf16[184,128]{1,0:T(8,128)(2,1)S(1)}, u32[]{:S(2)}, u32[]{:S(2)}) collective-permute-start(bf16[184,128]{1,0:T(8,128)(2,1)S(1)} %get-tuple-element.100), channel_id=1, source_target_pairs={{0,32},{16,48},{32,0},{48,16},{64,96},{80,112},{96,64},{112,80},{1... | collective-permute-start | bytes 141320 | tf_op jit(solution)/shard_map/ppermute | solution.py:22
  47.4 7.3 %collective-permute-start.14 = (bf16[184,128]{1,0:T(8,128)(2,1)S(1)}, bf16[184,128]{1,0:T(8,128)(2,1)S(1)}, u32[]{:S(2)}, u32[]{:S(2)}) collective-permute-start(bf16[184,128]{1,0:T(8,128)(2,1)S(1)} %get-tuple-element.101), channel_id=1, source_target_pairs={{0,64},{16,80},{32,96},{48,112},{64,0},{80,16},{96,32},{112,48},{1... | collective-permute-start | bytes 141320 | tf_op jit(solution)/shard_map/ppermute | solution.py:22
  48.7 6.0 %collective-permute-start.15 = (bf16[184,128]{1,0:T(8,128)(2,1)S(1)}, bf16[184,128]{1,0:T(8,128)(2,1)S(1)}, u32[]{:S(2)}, u32[]{:S(2)}) collective-permute-start(bf16[184,128]{1,0:T(8,128)(2,1)S(1)} %get-tuple-element.102), channel_id=1, source_target_pairs={{0,96},{16,112},{32,64},{48,80},{64,32},{80,48},{96,0},{112,16},{1... | collective-permute-start | bytes 141320 | tf_op jit(solution)/shard_map/ppermute | solution.py:22
  54.7 8.6 %collective-permute-start.16 = (bf16[184,128]{1,0:T(8,128)(2,1)S(1)}, bf16[184,128]{1,0:T(8,128)(2,1)S(1)}, u32[]{:S(2)}, u32[]{:S(2)}) collective-permute-start(bf16[184,128]{1,0:T(8,128)(2,1)S(1)} %add_convert_fusion.3), channel_id=1, source_target_pairs={{0,128},{16,144},{32,160},{48,176},{64,192},{80,208},{96,224},{112... | collective-permute-start | bytes 141320 | tf_op jit(solution)/shard_map/ppermute | solution.py:22
  63.3 5.5 %collective-permute-start.18 = (bf16[224,128]{1,0:T(8,128)(2,1)S(1)}, bf16[224,128]{1,0:T(8,128)(2,1)S(1)}, u32[]{:S(2)}, u32[]{:S(2)}) collective-permute-start(bf16[224,128]{1,0:T(8,128)(2,1)S(1)} %pad_maximum_fusion.7), channel_id=1, source_target_pairs={{0,4},{2,6},{4,8},{6,10},{8,12},{10,14},{12,0},{14,2},{1,5},{3,7},... | collective-permute-start | bytes 172040 | tf_op jit(solution)/shard_map/ppermute | solution.py:17
  64.1 5.7 %collective-permute-start.17 = (bf16[224,128]{1,0:T(8,128)(2,1)S(1)}, bf16[224,128]{1,0:T(8,128)(2,1)S(1)}, u32[]{:S(2)}, u32[]{:S(2)}) collective-permute-start(bf16[224,128]{1,0:T(8,128)(2,1)S(1)} %pad_maximum_fusion.7), channel_id=1, source_target_pairs={{0,8},{2,10},{4,12},{6,14},{8,0},{10,2},{12,4},{14,6},{1,9},{3,11}... | collective-permute-start | bytes 172040 | tf_op jit(solution)/shard_map/ppermute | solution.py:17
  64.6 5.6 %collective-permute-start.19 = (bf16[224,128]{1,0:T(8,128)(2,1)S(1)}, bf16[224,128]{1,0:T(8,128)(2,1)S(1)}, u32[]{:S(2)}, u32[]{:S(2)}) collective-permute-start(bf16[224,128]{1,0:T(8,128)(2,1)S(1)} %pad_maximum_fusion.7), channel_id=1, source_target_pairs={{0,12},{2,14},{4,0},{6,2},{8,4},{10,6},{12,8},{14,10},{1,13},{3,15... | collective-permute-start | bytes 172040 | tf_op jit(solution)/shard_map/ppermute | solution.py:17
  70.3 5.8 %collective-permute-start.20 = (bf16[224,128]{1,0:T(8,128)(2,1)S(1)}, bf16[224,128]{1,0:T(8,128)(2,1)S(1)}, u32[]{:S(2)}, u32[]{:S(2)}) collective-permute-start(bf16[224,128]{1,0:T(8,128)(2,1)S(1)} %add_convert_fusion.1), channel_id=1, source_target_pairs={{0,2},{2,0},{4,6},{6,4},{8,10},{10,8},{12,14},{14,12},{1,3},{3,1},... | collective-permute-start | bytes 172040 | tf_op jit(solution)/shard_map/ppermute | solution.py:22
  73.5 4.0 %collective-permute-start.21 = (bf16[144,128]{1,0:T(8,128)(2,1)S(1)}, bf16[144,128]{1,0:T(8,128)(2,1)S(1)}, u32[]{:S(2)}, u32[]{:S(2)}) collective-permute-start(bf16[144,128]{1,0:T(8,128)(2,1)S(1)} %slice.110), channel_id=1, source_target_pairs={{0,1},{1,0},{2,3},{3,2},{4,5},{5,4},{6,7},{7,6},{8,9},{9,8},{10,11... | collective-permute-start | bytes 110600 | tf_op jit(solution)/shard_map/ppermute | solution.py:22
  74.9 4.0 %collective-permute-start.22 = (bf16[144,128]{1,0:T(8,128)(2,1)S(1)}, bf16[144,128]{1,0:T(8,128)(2,1)S(1)}, u32[]{:S(2)}, u32[]{:S(2)}) collective-permute-start(bf16[144,128]{1,0:T(8,128)(2,1)S(1)} %slice.110), channel_id=1, source_target_pairs={{0,3},{1,2},{2,1},{3,0},{4,7},{5,6},{6,5},{7,4},{8,11},{9,10},{10,... | collective-permute-start | bytes 110600 | tf_op jit(solution)/shard_map/ppermute | solution.py:443
  78.9 6.4 %collective-permute-start.28 = (bf16[144,128]{1,0:T(8,128)(2,1)S(1)}, bf16[144,128]{1,0:T(8,128)(2,1)S(1)}, u32[]{:S(2)}, u32[]{:S(2)}) collective-permute-start(bf16[144,128]{1,0:T(8,128)(2,1)S(1)} %add_convert_fusion.4), channel_id=1, source_target_pairs={{0,96},{16,112},{32,64},{48,80},{64,32},{80,48},{96,0},{112,16},{1... | collective-permute-start | bytes 110600 | tf_op jit(solution)/shard_map/ppermute | solution.py:22
  80.8 8.7 %collective-permute-start.25 = (bf16[128,192]{1,0:T(8,128)(2,1)S(1)}, bf16[128,192]{1,0:T(8,128)(2,1)S(1)}, u32[]{:S(2)}, u32[]{:S(2)}) collective-permute-start(bf16[128,192]{1,0:T(8,128)(2,1)S(1)} %get-tuple-element.85), channel_id=1, source_target_pairs={{0,12},{2,14},{4,0},{6,2},{8,4},{10,6},{12,8},{14,10},{1,13},{3,15... | collective-permute-start | bytes 147464 | tf_op jit(solution)/shard_map/ppermute | solution.py:17
  83.3 6.3 %collective-permute-start.24 = (bf16[128,192]{1,0:T(8,128)(2,1)S(1)}, bf16[128,192]{1,0:T(8,128)(2,1)S(1)}, u32[]{:S(2)}, u32[]{:S(2)}) collective-permute-start(bf16[128,192]{1,0:T(8,128)(2,1)S(1)} %get-tuple-element.86), channel_id=1, source_target_pairs={{0,8},{2,10},{4,12},{6,14},{8,0},{10,2},{12,4},{14,6},{1,9},{3,11}... | collective-permute-start | bytes 147464 | tf_op jit(solution)/shard_map/ppermute | solution.py:17
  84.4 5.5 %collective-permute-start.23 = (bf16[128,192]{1,0:T(8,128)(2,1)S(1)}, bf16[128,192]{1,0:T(8,128)(2,1)S(1)}, u32[]{:S(2)}, u32[]{:S(2)}) collective-permute-start(bf16[128,192]{1,0:T(8,128)(2,1)S(1)} %get-tuple-element.87), channel_id=1, source_target_pairs={{0,4},{2,6},{4,8},{6,10},{8,12},{10,14},{12,0},{14,2},{1,5},{3,7},... | collective-permute-start | bytes 147464 | tf_op jit(solution)/shard_map/ppermute | solution.py:17
  84.4 5.0 %collective-permute-start.27 = (bf16[144,128]{1,0:T(8,128)(2,1)S(1)}, bf16[144,128]{1,0:T(8,128)(2,1)S(1)}, u32[]{:S(2)}, u32[]{:S(2)}) collective-permute-start(bf16[144,128]{1,0:T(8,128)(2,1)S(1)} %add_convert_fusion.4), channel_id=1, source_target_pairs={{0,64},{16,80},{32,96},{48,112},{64,0},{80,16},{96,32},{112,48},{1... | collective-permute-start | bytes 110600 | tf_op jit(solution)/shard_map/ppermute | solution.py:22
  85.2 4.4 %collective-permute-start.26 = (bf16[144,128]{1,0:T(8,128)(2,1)S(1)}, bf16[144,128]{1,0:T(8,128)(2,1)S(1)}, u32[]{:S(2)}, u32[]{:S(2)}) collective-permute-start(bf16[144,128]{1,0:T(8,128)(2,1)S(1)} %add_convert_fusion.4), channel_id=1, source_target_pairs={{0,32},{16,48},{32,0},{48,16},{64,96},{80,112},{96,64},{112,80},{1... | collective-permute-start | bytes 110600 | tf_op jit(solution)/shard_map/ppermute | solution.py:22
  89.9 5.5 %collective-permute-start.29 = (bf16[64,192]{1,0:T(8,128)(2,1)S(1)}, bf16[64,192]{1,0:T(8,128)(2,1)S(1)}, u32[]{:S(2)}, u32[]{:S(2)}) collective-permute-start(bf16[64,192]{1,0:T(8,128)(2,1)S(1)} %select_convert_fusion), channel_id=1, source_target_pairs={{0,2},{2,0},{4,6},{6,4},{8,10},{10,8},{12,14},{14,12},{1,3},{3,1},... | collective-permute-start | bytes 73736 | tf_op jit(solution)/shard_map/ppermute | solution.py:22
  91.5 4.6 %collective-permute-start.30 = (bf16[576,128]{1,0:T(8,128)(2,1)S(1)}, bf16[576,128]{1,0:T(8,128)(2,1)S(1)}, u32[]{:S(2)}, u32[]{:S(2)}) collective-permute-start(bf16[576,128]{1,0:T(8,128)(2,1)S(1)} %pad_maximum_fusion.1), channel_id=1, source_target_pairs={{0,16},{16,0},{32,48},{48,32},{64,80},{80,64},{96,112},{112,96},{1... | collective-permute-start | bytes 442376 | tf_op jit(solution)/shard_map/ppermute | solution.py:22

commit v7 on v6

--- a/solution.py
+++ b/solution.py
@@ -443,17 +443,18 @@
     crossed = lax.ppermute(quart, ("col", "batch"), [(i, i ^ 3) for i in range(16)])
     sums = (up(total[144:]) + up(across[144:])).astype(BF)
     parts = conv_backward(sums, proj_a, proj_b, conv_w)
+    parts, quart = lax.optimization_barrier((parts, quart))
     quart = ((up(quart) + up(across[:144])) + (up(others) + up(crossed))).astype(BF)
-    parts, quart = lax.optimization_barrier((parts, quart))
 
     parts = parts.reshape(4, 128, parts.shape[2])
     got = [shift(taken(parts, ahead[k]), "col", 2 * k) for k in (1, 2, 3)]
-    near = [flip(quart, "row", 2 * k) for k in (1, 2, 3)]
-    got, near = lax.optimization_barrier((got, near))
+    near = {k: flip(quart, "row", 2 * k) for k in (1,)}
+    got, quart, near = lax.optimization_barrier((got, quart, near))
     mine = (up(taken(parts, ahead[0])) + up(got[0])) + (up(got[1]) + up(got[2]))
-    near = jnp.stack([quart] + near)
+    near.update({k: flip(quart, "row", 2 * k) for k in (2, 3)})
+    near = jnp.stack([quart, near[1], near[2], near[3]])
+    other = flip(jnp.where(is_odd, mine[:64], mine[64:]).astype(BF), "col", 1)
     half = jnp.concatenate([taken(near, places[k]) for k in range(4)])
-    other = flip(jnp.where(is_odd, mine[:64], mine[64:]).astype(BF), "col", 1)
     theirs = flip(half, "row", 1)
     grad_pair_w = jnp.concatenate([jnp.where(is_first, half, theirs), jnp.where(is_first, theirs, half)])
     grad_pair_w = up(grad_pair_w).reshape(3, 3, pairs, pairs) / 512.0

time: 98.9 us -> 97.6 us (0.987)
  waiting for transfers between devices: 40.4 us -> 38.8 us
    ppermute x1, waiting for transfers between devices: 1.41 us -> 0.01 us  [local(): lax.ppermute(quart, ('col', 'batch'), [(i, i ^ 3) for i in range(16)])]
where the time goes in v7:
time: 97.6 us; the launch traced here: 96.4 us
  starting transfers between devices  44.1 us (45%)
  waiting for transfers between devices  38.8 us (40%)
  Pallas kernels  9.12 us (9%)
  other arithmetic  1.93 us (2%)
  local copies, waits for them, and re-layouts  1.33 us (1%)
  between operations  1.1 us (1%)
    ppermute x15, waiting for transfers between devices, flip(): return lax.ppermute(x, axis, [(i, i ^ bit) for i in range(count)])  23.6 us
    ppermute x15, starting transfers between devices, flip(): return lax.ppermute(x, axis, [(i, i ^ bit) for i in range(count)])  21.3 us
    ppermute x11, starting transfers between devices, shift(): lax.ppermute(x, axis, [(i, (i + step) % count) for i in range(count)])  17.8 us
    ppermute x11, waiting for transfers between devices, shift(): lax.ppermute(x, axis, [(i, (i + step) % count) for i in range(count)])  10.2 us
    pallas_call x1, Pallas kernels, pair_block(): pl.pallas_call(pair_kernel, out_shape=(jax.ShapeDtypeStruct((32, 64, chan...  5.57 us
    ppermute x4, waiting for transfers between devices, spread(): return lax.ppermute(x, ('row', 'col'), sorted(pairs.items()))  4.97 us
    ppermute x4, starting transfers between devices, spread(): return lax.ppermute(x, ('row', 'col'), sorted(pairs.items()))  4.93 us
  transfers between devices with their start and end apart: 31, of which 21 were waited for; matrix products, arithmetic and copies ran while one was open for 1% of the time, Pallas kernels for 1%

profile of v7, /device:TPU:2, one launch (start us, length us, event | category | flops | bytes accessed | tf_op | source)
XLA Modules:
  0.0 96.4 jit_solution(10205407818509645421)
XLA Ops:
  0.8 0.0 copy-start.1
  0.8 0.0 copy-start.2
  0.8 0.0 copy-start.3
  0.8 0.0 copy-start.6
  0.8 1.0 %copy-done.1 = bf16[1,32,64,128]{3,2,1,0:T(8,128)(2,1)S(1)} copy-done((bf16[1,32,64,128]{3,2,1,0:T(8,128)(2,1)S(1)}, bf16[1,32,64,128]{3,2,1,0:T(8,128)(2,1)}, u32[]{:S(2)}) %copy-start.1) | copy-done | bytes 524312
  1.8 0.2 copy-done.2
  2.0 0.0 copy-done.3
  2.0 0.5 shard_map.95
  2.6 0.0 collective-permute-start
  2.6 5.3 %collective-permute-start.1 = (bf16[8,64,128]{2,1,0:T(8,128)(2,1)S(1)}, bf16[8,64,128]{2,1,0:T(8,128)(2,1)S(1)}, u32[]{:S(2)}, u32[]{:S(2)}) collective-permute-start(bf16[8,64,128]{2,1,0:T(8,128)(2,1)S(1)} %get-tuple-element.45), channel_id=1, source_target_pairs={{0,240},{16,0},{32,16},{48,32},{64,48},{80,64},{96,80},{112,96},{1... | collective-permute-start | bytes 393224 | tf_op jit(solution)/shard_map/ppermute | solution.py:17
  7.9 0.3 shard_map.96
  8.2 2.3 %collective-permute-done.top = bf16[8,64,128]{2,1,0:T(8,128)(2,1)S(1)} collective-permute-done((bf16[8,64,128]{2,1,0:T(8,128)(2,1)S(1)}, bf16[8,64,128]{2,1,0:T(8,128)(2,1)S(1)}, u32[]{:S(2)}, u32[]{:S(2)}) %collective-permute-start) | collective-permute-done | bytes 131104 | tf_op jit(solution)/shard_map/ppermute | solution.py:17
  10.5 1.8 %shard_map.97 = (bf16[272,128]{1,0:T(8,128)(2,1)S(1)}, bf16[272,128]{1,0:T(8,128)(2,1)S(1)}) custom-call(s32[8]{0:T(128)S(1)} %select_convert_fusion.2.flags, bf16[64,1536]{1,0:T(8,128)(2,1)S(1)} %bitcast.48, bf16[8,64,128]{2,1,0:T(8,128)(2,1)S(1)} %collective-permute-done.top, bf16[8,64,128]{2,1,0:T(8,128)(2,1)S(1)} %collective-permute-done.1.bottom, ...), custom_call_target="tpu_custom_call" | custom-call | flops 120000000 | bytes 3500000 | tf_op jit(solution)/shard_map/pallas_call | solution.py:333
  12.3 3.1 %collective-permute-start.4 = (bf16[272,128]{1,0:T(8,128)(2,1)S(1)}, bf16[272,128]{1,0:T(8,128)(2,1)S(1)}, u32[]{:S(2)}, u32[]{:S(2)}) collective-permute-start(bf16[272,128]{1,0:T(8,128)(2,1)S(1)} %get-tuple-element.51), channel_id=1, source_target_pairs={{0,12},{2,14},{4,0},{6,2},{8,4},{10,6},{12,8},{14,10},{1,13},{3,15... | collective-permute-start | bytes 208904 | tf_op jit(solution)/shard_map/ppermute | solution.py:17
  15.4 2.2 %collective-permute-start.2 = (bf16[80,128]{1,0:T(8,128)(2,1)S(1)}, bf16[80,128]{1,0:T(8,128)(2,1)S(1)}, u32[]{:S(2)}, u32[]{:S(2)}) collective-permute-start(bf16[80,128]{1,0:T(8,128)(2,1)S(1)} %slice.73), channel_id=1, source_target_pairs={{0,8},{2,10},{4,12},{6,14},{8,0},{10,2},{12,4},{14,6},{1,9},{3,11}... | collective-permute-start | bytes 61448 | tf_op jit(solution)/shard_map/ppermute | solution.py:17
  17.6 0.0 collective-permute-done.4
  17.6 3.5 %collective-permute-done.3 = bf16[272,128]{1,0:T(8,128)(2,1)S(1)} collective-permute-done((bf16[272,128]{1,0:T(8,128)(2,1)S(1)}, bf16[272,128]{1,0:T(8,128)(2,1)S(1)}, u32[]{:S(2)}, u32[]{:S(2)}) %collective-permute-start.3) | collective-permute-done | bytes 69664 | tf_op jit(solution)/shard_map/ppermute | solution.py:17
  21.2 0.0 collective-permute-done.2
  21.2 2.2 %collective-permute-start.5 = (bf16[464,128]{1,0:T(8,128)(2,1)S(1)}, bf16[464,128]{1,0:T(8,128)(2,1)S(1)}, u32[]{:S(2)}, u32[]{:S(2)}) collective-permute-start(bf16[464,128]{1,0:T(8,128)(2,1)S(1)} %pad_maximum_fusion.2), channel_id=1, source_target_pairs={{0,2},{2,0},{4,6},{6,4},{8,10},{10,8},{12,14},{14,12},{1,3},{3,1},... | collective-permute-start | bytes 356360 | tf_op jit(solution)/shard_map/ppermute | solution.py:22
  23.4 4.2 %collective-permute-done.5 = bf16[464,128]{1,0:T(8,128)(2,1)S(1)} collective-permute-done((bf16[464,128]{1,0:T(8,128)(2,1)S(1)}, bf16[464,128]{1,0:T(8,128)(2,1)S(1)}, u32[]{:S(2)}, u32[]{:S(2)}) %collective-permute-start.5) | collective-permute-done | bytes 118816 | tf_op jit(solution)/shard_map/ppermute | solution.py:22
  27.7 0.1 collective-permute-start.6
  27.8 1.2 %collective-permute-done.6 = bf16[35,128]{1,0:T(8,128)(2,1)S(1)} collective-permute-done((bf16[35,128]{1,0:T(8,128)(2,1)S(1)}, bf16[35,128]{1,0:T(8,128)(2,1)S(1)}, u32[]{:S(2)}, u32[]{:S(2)}) %collective-permute-start.6) | collective-permute-done | bytes 8992 | tf_op jit(solution)/shard_map/ppermute | solution.py:22
  29.0 4.9 %collective-permute-start.10 = (bf16[70,128]{1,0:T(8,128)(2,1)S(1)}, bf16[70,128]{1,0:T(8,128)(2,1)S(1)}, u32[]{:S(2)}, u32[]{:S(2)}) collective-permute-start(bf16[70,128]{1,0:T(8,128)(2,1)S(1)} %pad_maximum_fusion.8), channel_id=1, source_target_pairs={{0,128},{2,18},{4,20},{6,22},{8,24},{10,26},{12,28},{14,30},{16,0}... | collective-permute-start | bytes 53768 | tf_op jit(solution)/shard_map/ppermute | solution.py:43
  33.9 0.0 collective-permute-start.9
  33.9 1.4 %collective-permute-done.10 = bf16[70,128]{1,0:T(8,128)(2,1)S(1)} collective-permute-done((bf16[70,128]{1,0:T(8,128)(2,1)S(1)}, bf16[70,128]{1,0:T(8,128)(2,1)S(1)}, u32[]{:S(2)}, u32[]{:S(2)}) %collective-permute-start.10) | collective-permute-done | bytes 17952 | tf_op jit(solution)/shard_map/ppermute | solution.py:43
  35.4 3.5 %collective-permute-done.9 = bf16[70,128]{1,0:T(8,128)(2,1)S(1)} collective-permute-done((bf16[70,128]{1,0:T(8,128)(2,1)S(1)}, bf16[70,128]{1,0:T(8,128)(2,1)S(1)}, u32[]{:S(2)}, u32[]{:S(2)}) %collective-permute-start.9) | collective-permute-done | bytes 17952 | tf_op jit(solution)/shard_map/ppermute | solution.py:43
  38.9 0.2 collective-permute-start.11
  39.1 1.1 %collective-permute-done.11 = bf16[70,128]{1,0:T(8,128)(2,1)S(1)} collective-permute-done((bf16[70,128]{1,0:T(8,128)(2,1)S(1)}, bf16[70,128]{1,0:T(8,128)(2,1)S(1)}, u32[]{:S(2)}, u32[]{:S(2)}) %collective-permute-start.11) | collective-permute-done | bytes 17952 | tf_op jit(solution)/shard_map/ppermute | solution.py:22
  40.2 5.6 %shard_map.98 = (bf16[32,64,128]{2,1,0:T(8,128)(2,1)}, f32[616,128]{1,0:T(8,128)S(1)}, bf16[616,128]{1,0:T(8,128)(2,1)S(1)}, bf16[40,128]{1,0:T(8,128)(2,1)S(1)}) custom-call(s32[8]{0:T(128)S(1)} %select_convert_fusion.2.flags, bf16[32,64,128]{2,1,0:T(8,128)(2,1)S(1)} %bitcast.41, bf16[32,64,128]{2,1,0:T(8,128)(2,1)S(1)} %bitcast.44, ...), custom_call_target="tpu_custom_call" | custom-call | flops 2500000000 | bytes 4000000 | tf_op jit(solution)/shard_map/pallas_call | solution.py:359
  45.8 0.2 collective-permute-start.12
  45.9 1.2 %collective-permute-done.12 = bf16[616,128]{1,0:T(8,128)(2,1)S(1)} collective-permute-done((bf16[616,128]{1,0:T(8,128)(2,1)S(1)}, bf16[616,128]{1,0:T(8,128)(2,1)S(1)}, u32[]{:S(2)}, u32[]{:S(2)}) %collective-permute-start.12) | collective-permute-done | bytes 157728 | tf_op jit(solution)/shard_map/ppermute | solution.py:22
  47.3 0.1 collective-permute-start.13
  47.4 1.3 %collective-permute-start.14 = (bf16[184,128]{1,0:T(8,128)(2,1)S(1)}, bf16[184,128]{1,0:T(8,128)(2,1)S(1)}, u32[]{:S(2)}, u32[]{:S(2)}) collective-permute-start(bf16[184,128]{1,0:T(8,128)(2,1)S(1)} %get-tuple-element.99), channel_id=1, source_target_pairs={{0,64},{16,80},{32,96},{48,112},{64,0},{80,16},{96,32},{112,48},{1... | collective-permute-start | bytes 141320 | tf_op jit(solution)/shard_map/ppermute | solution.py:22
  48.7 3.0 %collective-permute-start.15 = (bf16[184,128]{1,0:T(8,128)(2,1)S(1)}, bf16[184,128]{1,0:T(8,128)(2,1)S(1)}, u32[]{:S(2)}, u32[]{:S(2)}) collective-permute-start(bf16[184,128]{1,0:T(8,128)(2,1)S(1)} %get-tuple-element.100), channel_id=1, source_target_pairs={{0,96},{16,112},{32,64},{48,80},{64,32},{80,48},{96,0},{112,16},{1... | collective-permute-start | bytes 141320 | tf_op jit(solution)/shard_map/ppermute | solution.py:22
  51.8 0.2 collective-permute-done.13
  52.0 2.7 %collective-permute-done.14 = bf16[184,128]{1,0:T(8,128)(2,1)S(1)} collective-permute-done((bf16[184,128]{1,0:T(8,128)(2,1)S(1)}, bf16[184,128]{1,0:T(8,128)(2,1)S(1)}, u32[]{:S(2)}, u32[]{:S(2)}) %collective-permute-start.14) | collective-permute-done | bytes 47136 | tf_op jit(solution)/shard_map/ppermute | solution.py:22
  54.7 2.8 %collective-permute-start.16 = (bf16[184,128]{1,0:T(8,128)(2,1)S(1)}, bf16[184,128]{1,0:T(8,128)(2,1)S(1)}, u32[]{:S(2)}, u32[]{:S(2)}) collective-permute-start(bf16[184,128]{1,0:T(8,128)(2,1)S(1)} %add_convert_fusion.3), channel_id=1, source_target_pairs={{0,128},{16,144},{32,160},{48,176},{64,192},{80,208},{96,224},{112... | collective-permute-start | bytes 141320 | tf_op jit(solution)/shard_map/ppermute | solution.py:22
  57.5 5.8 %collective-permute-done.16 = bf16[184,128]{1,0:T(8,128)(2,1)S(1)} collective-permute-done((bf16[184,128]{1,0:T(8,128)(2,1)S(1)}, bf16[184,128]{1,0:T(8,128)(2,1)S(1)}, u32[]{:S(2)}, u32[]{:S(2)}) %collective-permute-start.16) | collective-permute-done | bytes 47136 | tf_op jit(solution)/shard_map/ppermute | solution.py:22
  63.3 0.8 collective-permute-start.18
  64.1 0.5 collective-permute-start.17
  64.6 2.3 %collective-permute-start.19 = (bf16[224,128]{1,0:T(8,128)(2,1)S(1)}, bf16[224,128]{1,0:T(8,128)(2,1)S(1)}, u32[]{:S(2)}, u32[]{:S(2)}) collective-permute-start(bf16[224,128]{1,0:T(8,128)(2,1)S(1)} %pad_maximum_fusion.7), channel_id=1, source_target_pairs={{0,12},{2,14},{4,0},{6,2},{8,4},{10,6},{12,8},{14,10},{1,13},{3,15... | collective-permute-start | bytes 172040 | tf_op jit(solution)/shard_map/ppermute | solution.py:17
  66.9 1.9 %collective-permute-done.18 = bf16[224,128]{1,0:T(8,128)(2,1)S(1)} collective-permute-done((bf16[224,128]{1,0:T(8,128)(2,1)S(1)}, bf16[224,128]{1,0:T(8,128)(2,1)S(1)}, u32[]{:S(2)}, u32[]{:S(2)}) %collective-permute-start.18) | collective-permute-done | bytes 57376 | tf_op jit(solution)/shard_map/ppermute | solution.py:17
  68.8 1.0 %collective-permute-done.17 = bf16[224,128]{1,0:T(8,128)(2,1)S(1)} collective-permute-done((bf16[224,128]{1,0:T(8,128)(2,1)S(1)}, bf16[224,128]{1,0:T(8,128)(2,1)S(1)}, u32[]{:S(2)}, u32[]{:S(2)}) %collective-permute-start.17) | collective-permute-done | bytes 57376 | tf_op jit(solution)/shard_map/ppermute | solution.py:17
  69.8 0.5 collective-permute-done.19
  70.3 3.2 %collective-permute-start.20 = (bf16[224,128]{1,0:T(8,128)(2,1)S(1)}, bf16[224,128]{1,0:T(8,128)(2,1)S(1)}, u32[]{:S(2)}, u32[]{:S(2)}) collective-permute-start(bf16[224,128]{1,0:T(8,128)(2,1)S(1)} %add_convert_fusion.1), channel_id=1, source_target_pairs={{0,2},{2,0},{4,6},{6,4},{8,10},{10,8},{12,14},{14,12},{1,3},{3,1},... | collective-permute-start | bytes 172040 | tf_op jit(solution)/shard_map/ppermute | solution.py:22
  73.5 1.6 %collective-permute-start.24 = (bf16[144,128]{1,0:T(8,128)(2,1)S(1)}, bf16[144,128]{1,0:T(8,128)(2,1)S(1)}, u32[]{:S(2)}, u32[]{:S(2)}) collective-permute-start(bf16[144,128]{1,0:T(8,128)(2,1)S(1)} %slice.110), channel_id=1, source_target_pairs={{0,1},{1,0},{2,3},{3,2},{4,5},{5,4},{6,7},{7,6},{8,9},{9,8},{10,11... | collective-permute-start | bytes 110600 | tf_op jit(solution)/shard_map/ppermute | solution.py:22
  75.1 1.0 %collective-permute-done.20 = bf16[224,128]{1,0:T(8,128)(2,1)S(1)} collective-permute-done((bf16[224,128]{1,0:T(8,128)(2,1)S(1)}, bf16[224,128]{1,0:T(8,128)(2,1)S(1)}, u32[]{:S(2)}, u32[]{:S(2)}) %collective-permute-start.20) | collective-permute-done | bytes 57376 | tf_op jit(solution)/shard_map/ppermute | solution.py:22
  76.1 0.9 shard_map.99
  77.0 2.7 %collective-permute-start.23 = (bf16[128,192]{1,0:T(8,128)(2,1)S(1)}, bf16[128,192]{1,0:T(8,128)(2,1)S(1)}, u32[]{:S(2)}, u32[]{:S(2)}) collective-permute-start(bf16[128,192]{1,0:T(8,128)(2,1)S(1)} %get-tuple-element.83), channel_id=1, source_target_pairs={{0,12},{2,14},{4,0},{6,2},{8,4},{10,6},{12,8},{14,10},{1,13},{3,15... | collective-permute-start | bytes 147464 | tf_op jit(solution)/shard_map/ppermute | solution.py:17
  79.7 0.9 collective-permute-start.22
  80.6 0.1 collective-permute-start.21
  80.7 0.8 collective-permute-start.26
  81.5 3.7 %collective-permute-done.26 = bf16[144,128]{1,0:T(8,128)(2,1)S(1)} collective-permute-done((bf16[144,128]{1,0:T(8,128)(2,1)S(1)}, bf16[144,128]{1,0:T(8,128)(2,1)S(1)}, u32[]{:S(2)}, u32[]{:S(2)}) %collective-permute-start.26) | collective-permute-done | bytes 36896 | tf_op jit(solution)/shard_map/ppermute | solution.py:22
  85.2 0.3 collective-permute-done.22
  85.5 0.7 collective-permute-done.21
  86.2 2.8 %collective-permute-start.29 = (bf16[144,128]{1,0:T(8,128)(2,1)S(1)}, bf16[144,128]{1,0:T(8,128)(2,1)S(1)}, u32[]{:S(2)}, u32[]{:S(2)}) collective-permute-start(bf16[144,128]{1,0:T(8,128)(2,1)S(1)} %add_convert_fusion.4), channel_id=1, source_target_pairs={{0,96},{16,112},{32,64},{48,80},{64,32},{80,48},{96,0},{112,16},{1... | collective-permute-start | bytes 110600 | tf_op jit(solution)/shard_map/ppermute | solution.py:22
  89.1 3.0 %collective-permute-start.27 = (bf16[64,192]{1,0:T(8,128)(2,1)S(1)}, bf16[64,192]{1,0:T(8,128)(2,1)S(1)}, u32[]{:S(2)}, u32[]{:S(2)}) collective-permute-start(bf16[64,192]{1,0:T(8,128)(2,1)S(1)} %select_convert_fusion), channel_id=1, source_target_pairs={{0,2},{2,0},{4,6},{6,4},{8,10},{10,8},{12,14},{14,12},{1,3},{3,1},... | collective-permute-start | bytes 73736 | tf_op jit(solution)/shard_map/ppermute | solution.py:22
  92.1 1.8 %collective-permute-done.28 = bf16[144,128]{1,0:T(8,128)(2,1)S(1)} collective-permute-done((bf16[144,128]{1,0:T(8,128)(2,1)S(1)}, bf16[144,128]{1,0:T(8,128)(2,1)S(1)}, u32[]{:S(2)}, u32[]{:S(2)}) %collective-permute-start.28) | collective-permute-done | bytes 36896 | tf_op jit(solution)/shard_map/ppermute | solution.py:22
  94.0 0.1 collective-permute-start.30
  94.1 0.5 collective-permute-done.27
  94.6 0.6 fusion.1
  95.2 0.2 collective-permute-done.30
  95.4 0.1 broadcast_select_fusion.1
  95.5 0.9 convert_multiply_fusion
  (56 shorter events, 0.5 us)
Async XLA Ops:
  0.8 1.0 %copy-start.1 = (bf16[1,32,64,128]{3,2,1,0:T(8,128)(2,1)S(1)}, bf16[1,32,64,128]{3,2,1,0:T(8,128)(2,1)}, u32[]{:S(2)}) copy-start(bf16[1,32,64,128]{3,2,1,0:T(8,128)(2,1)} %param.11) | copy-start | bytes 1572868
  0.8 1.2 %copy-start.2 = (bf16[1,32,64,128]{3,2,1,0:T(8,128)(2,1)S(1)}, bf16[1,32,64,128]{3,2,1,0:T(8,128)(2,1)}, u32[]{:S(2)}) copy-start(bf16[1,32,64,128]{3,2,1,0:T(8,128)(2,1)} %param.13) | copy-start | bytes 1572868
  0.8 1.2 %copy-start.3 = (bf16[1,64,1536]{2,1,0:T(8,128)(2,1)S(1)}, bf16[1,64,1536]{2,1,0:T(8,128)(2,1)}, u32[]{:S(2)}) copy-start(bf16[1,64,1536]{2,1,0:T(8,128)(2,1)} %param.7) | copy-start | bytes 589828
  0.8 7.1 %copy-start.6 = (bf16[3,3,128,128]{3,2,1,0:T(8,128)(2,1)S(1)}, bf16[3,3,128,128]{3,2,1,0:T(8,128)(2,1)}, u32[]{:S(2)}) copy-start(bf16[3,3,128,128]{3,2,1,0:T(8,128)(2,1)} %param.12) | copy-start | bytes 884740
  2.6 8.0 %collective-permute-start = (bf16[8,64,128]{2,1,0:T(8,128)(2,1)S(1)}, bf16[8,64,128]{2,1,0:T(8,128)(2,1)S(1)}, u32[]{:S(2)}, u32[]{:S(2)}) collective-permute-start(bf16[8,64,128]{2,1,0:T(8,128)(2,1)S(1)} %get-tuple-element.44), channel_id=1, source_target_pairs={{0,16},{16,32},{32,48},{48,64},{64,80},{80,96},{96,112},{112,128},... | collective-permute-start | bytes 393224 | tf_op jit(solution)/shard_map/ppermute | solution.py:17
  2.6 7.9 %collective-permute-start.1 = (bf16[8,64,128]{2,1,0:T(8,128)(2,1)S(1)}, bf16[8,64,128]{2,1,0:T(8,128)(2,1)S(1)}, u32[]{:S(2)}, u32[]{:S(2)}) collective-permute-start(bf16[8,64,128]{2,1,0:T(8,128)(2,1)S(1)} %get-tuple-element.45), channel_id=1, source_target_pairs={{0,240},{16,0},{32,16},{48,32},{64,48},{80,64},{96,80},{112,96},{1... | collective-permute-start | bytes 393224 | tf_op jit(solution)/shard_map/ppermute | solution.py:17
  7.9 2.6 %copy-start = (bf16[5,192,1536]{2,1,0:T(8,128)(2,1)S(1)}, bf16[5,192,1536]{2,1,0:T(8,128)(2,1)}, u32[]{:S(2)}) copy-start(bf16[5,192,1536]{2,1,0:T(8,128)(2,1)} %conv_w.3) | copy-start | bytes 8847364
  7.9 2.6 %copy-start.4 = (bf16[192,128]{1,0:T(8,128)(2,1)S(1)}, bf16[192,128]{1,0:T(8,128)(2,1)}, u32[]{:S(2)}) copy-start(bf16[192,128]{1,0:T(8,128)(2,1)} %proj_a.3) | copy-start | bytes 147460
  7.9 2.6 %copy-start.5 = (bf16[192,128]{1,0:T(8,128)(2,1)S(1)}, bf16[192,128]{1,0:T(8,128)(2,1)}, u32[]{:S(2)}) copy-start(bf16[192,128]{1,0:T(8,128)(2,1)} %proj_b.3) | copy-start | bytes 147460
  12.3 5.3 %collective-permute-start.4 = (bf16[272,128]{1,0:T(8,128)(2,1)S(1)}, bf16[272,128]{1,0:T(8,128)(2,1)S(1)}, u32[]{:S(2)}, u32[]{:S(2)}) collective-permute-start(bf16[272,128]{1,0:T(8,128)(2,1)S(1)} %get-tuple-element.51), channel_id=1, source_target_pairs={{0,12},{2,14},{4,0},{6,2},{8,4},{10,6},{12,8},{14,10},{1,13},{3,15... | collective-permute-start | bytes 208904 | tf_op jit(solution)/shard_map/ppermute | solution.py:17
  15.4 5.7 %collective-permute-start.3 = (bf16[272,128]{1,0:T(8,128)(2,1)S(1)}, bf16[272,128]{1,0:T(8,128)(2,1)S(1)}, u32[]{:S(2)}, u32[]{:S(2)}) collective-permute-start(bf16[272,128]{1,0:T(8,128)(2,1)S(1)} %get-tuple-element.50), channel_id=1, source_target_pairs={{0,4},{2,6},{4,8},{6,10},{8,12},{10,14},{12,0},{14,2},{1,5},{3,7},... | collective-permute-start | bytes 208904 | tf_op jit(solution)/shard_map/ppermute | solution.py:17
  15.4 5.8 %collective-permute-start.2 = (bf16[80,128]{1,0:T(8,128)(2,1)S(1)}, bf16[80,128]{1,0:T(8,128)(2,1)S(1)}, u32[]{:S(2)}, u32[]{:S(2)}) collective-permute-start(bf16[80,128]{1,0:T(8,128)(2,1)S(1)} %slice.73), channel_id=1, source_target_pairs={{0,8},{2,10},{4,12},{6,14},{8,0},{10,2},{12,4},{14,6},{1,9},{3,11}... | collective-permute-start | bytes 61448 | tf_op jit(solution)/shard_map/ppermute | solution.py:17
  21.2 6.4 %collective-permute-start.5 = (bf16[464,128]{1,0:T(8,128)(2,1)S(1)}, bf16[464,128]{1,0:T(8,128)(2,1)S(1)}, u32[]{:S(2)}, u32[]{:S(2)}) collective-permute-start(bf16[464,128]{1,0:T(8,128)(2,1)S(1)} %pad_maximum_fusion.2), channel_id=1, source_target_pairs={{0,2},{2,0},{4,6},{6,4},{8,10},{10,8},{12,14},{14,12},{1,3},{3,1},... | collective-permute-start | bytes 356360 | tf_op jit(solution)/shard_map/ppermute | solution.py:22
  27.7 1.3 %collective-permute-start.6 = (bf16[35,128]{1,0:T(8,128)(2,1)S(1)}, bf16[35,128]{1,0:T(8,128)(2,1)S(1)}, u32[]{:S(2)}, u32[]{:S(2)}) collective-permute-start(bf16[35,128]{1,0:T(8,128)(2,1)S(1)} %slice_select_fusion.3), channel_id=1, source_target_pairs={{0,16},{16,0},{32,48},{48,32},{64,80},{80,64},{96,112},{112,96},{1... | collective-permute-start | bytes 26888 | tf_op jit(solution)/shard_map/ppermute | solution.py:22
  29.0 6.4 %collective-permute-start.10 = (bf16[70,128]{1,0:T(8,128)(2,1)S(1)}, bf16[70,128]{1,0:T(8,128)(2,1)S(1)}, u32[]{:S(2)}, u32[]{:S(2)}) collective-permute-start(bf16[70,128]{1,0:T(8,128)(2,1)S(1)} %pad_maximum_fusion.8), channel_id=1, source_target_pairs={{0,128},{2,18},{4,20},{6,22},{8,24},{10,26},{12,28},{14,30},{16,0}... | collective-permute-start | bytes 53768 | tf_op jit(solution)/shard_map/ppermute | solution.py:43
  33.9 5.0 %collective-permute-start.9 = (bf16[70,128]{1,0:T(8,128)(2,1)S(1)}, bf16[70,128]{1,0:T(8,128)(2,1)S(1)}, u32[]{:S(2)}, u32[]{:S(2)}) collective-permute-start(bf16[70,128]{1,0:T(8,128)(2,1)S(1)} %pad_maximum_fusion.8), channel_id=1, source_target_pairs={{0,96},{2,18},{4,20},{6,102},{8,24},{10,26},{12,28},{14,30},{16,17... | collective-permute-start | bytes 53768 | tf_op jit(solution)/shard_map/ppermute | solution.py:43
  33.9 5.0 %collective-permute-start.8 = (bf16[70,128]{1,0:T(8,128)(2,1)S(1)}, bf16[70,128]{1,0:T(8,128)(2,1)S(1)}, u32[]{:S(2)}, u32[]{:S(2)}) collective-permute-start(bf16[70,128]{1,0:T(8,128)(2,1)S(1)} %pad_maximum_fusion.8), channel_id=1, source_target_pairs={{0,64},{2,18},{4,68},{6,22},{8,24},{10,26},{12,28},{14,30},{16,208... | collective-permute-start | bytes 53768 | tf_op jit(solution)/shard_map/ppermute | solution.py:43
  33.9 5.0 %collective-permute-start.7 = (bf16[70,128]{1,0:T(8,128)(2,1)S(1)}, bf16[70,128]{1,0:T(8,128)(2,1)S(1)}, u32[]{:S(2)}, u32[]{:S(2)}) collective-permute-start(bf16[70,128]{1,0:T(8,128)(2,1)S(1)} %pad_maximum_fusion.8), channel_id=1, source_target_pairs={{0,32},{2,34},{4,20},{6,22},{8,24},{10,26},{12,28},{14,30},{16,240... | collective-permute-start | bytes 53768 | tf_op jit(solution)/shard_map/ppermute | solution.py:43
  38.9 1.3 %collective-permute-start.11 = (bf16[70,128]{1,0:T(8,128)(2,1)S(1)}, bf16[70,128]{1,0:T(8,128)(2,1)S(1)}, u32[]{:S(2)}, u32[]{:S(2)}) collective-permute-start(bf16[70,128]{1,0:T(8,128)(2,1)S(1)} %select_select_fusion), channel_id=1, source_target_pairs={{0,16},{16,0},{32,48},{48,32},{64,80},{80,64},{96,112},{112,96},{1... | collective-permute-start | bytes 53768 | tf_op jit(solution)/shard_map/ppermute | solution.py:22
  45.8 1.4 %collective-permute-start.12 = (bf16[616,128]{1,0:T(8,128)(2,1)S(1)}, bf16[616,128]{1,0:T(8,128)(2,1)S(1)}, u32[]{:S(2)}, u32[]{:S(2)}) collective-permute-start(bf16[616,128]{1,0:T(8,128)(2,1)S(1)} %get-tuple-element.63), channel_id=1, source_target_pairs={{0,16},{16,0},{32,48},{48,32},{64,80},{80,64},{96,112},{112,96},{1... | collective-permute-start | bytes 473096 | tf_op jit(solution)/shard_map/ppermute | solution.py:22
  47.3 4.7 %collective-permute-start.13 = (bf16[184,128]{1,0:T(8,128)(2,1)S(1)}, bf16[184,128]{1,0:T(8,128)(2,1)S(1)}, u32[]{:S(2)}, u32[]{:S(2)}) collective-permute-start(bf16[184,128]{1,0:T(8,128)(2,1)S(1)} %get-tuple-element.98), channel_id=1, source_target_pairs={{0,32},{16,48},{32,0},{48,16},{64,96},{80,112},{96,64},{112,80},{1... | collective-permute-start | bytes 141320 | tf_op jit(solution)/shard_map/ppermute | solution.py:22
  47.4 7.3 %collective-permute-start.14 = (bf16[184,128]{1,0:T(8,128)(2,1)S(1)}, bf16[184,128]{1,0:T(8,128)(2,1)S(1)}, u32[]{:S(2)}, u32[]{:S(2)}) collective-permute-start(bf16[184,128]{1,0:T(8,128)(2,1)S(1)} %get-tuple-element.99), channel_id=1, source_target_pairs={{0,64},{16,80},{32,96},{48,112},{64,0},{80,16},{96,32},{112,48},{1... | collective-permute-start | bytes 141320 | tf_op jit(solution)/shard_map/ppermute | solution.py:22
  48.7 6.0 %collective-permute-start.15 = (bf16[184,128]{1,0:T(8,128)(2,1)S(1)}, bf16[184,128]{1,0:T(8,128)(2,1)S(1)}, u32[]{:S(2)}, u32[]{:S(2)}) collective-permute-start(bf16[184,128]{1,0:T(8,128)(2,1)S(1)} %get-tuple-element.100), channel_id=1, source_target_pairs={{0,96},{16,112},{32,64},{48,80},{64,32},{80,48},{96,0},{112,16},{1... | collective-permute-start | bytes 141320 | tf_op jit(solution)/shard_map/ppermute | solution.py:22
  54.7 8.6 %collective-permute-start.16 = (bf16[184,128]{1,0:T(8,128)(2,1)S(1)}, bf16[184,128]{1,0:T(8,128)(2,1)S(1)}, u32[]{:S(2)}, u32[]{:S(2)}) collective-permute-start(bf16[184,128]{1,0:T(8,128)(2,1)S(1)} %add_convert_fusion.3), channel_id=1, source_target_pairs={{0,128},{16,144},{32,160},{48,176},{64,192},{80,208},{96,224},{112... | collective-permute-start | bytes 141320 | tf_op jit(solution)/shard_map/ppermute | solution.py:22
  63.3 5.5 %collective-permute-start.18 = (bf16[224,128]{1,0:T(8,128)(2,1)S(1)}, bf16[224,128]{1,0:T(8,128)(2,1)S(1)}, u32[]{:S(2)}, u32[]{:S(2)}) collective-permute-start(bf16[224,128]{1,0:T(8,128)(2,1)S(1)} %pad_maximum_fusion.7), channel_id=1, source_target_pairs={{0,4},{2,6},{4,8},{6,10},{8,12},{10,14},{12,0},{14,2},{1,5},{3,7},... | collective-permute-start | bytes 172040 | tf_op jit(solution)/shard_map/ppermute | solution.py:17
  64.1 5.7 %collective-permute-start.17 = (bf16[224,128]{1,0:T(8,128)(2,1)S(1)}, bf16[224,128]{1,0:T(8,128)(2,1)S(1)}, u32[]{:S(2)}, u32[]{:S(2)}) collective-permute-start(bf16[224,128]{1,0:T(8,128)(2,1)S(1)} %pad_maximum_fusion.7), channel_id=1, source_target_pairs={{0,8},{2,10},{4,12},{6,14},{8,0},{10,2},{12,4},{14,6},{1,9},{3,11}... | collective-permute-start | bytes 172040 | tf_op jit(solution)/shard_map/ppermute | solution.py:17
  64.6 5.6 %collective-permute-start.19 = (bf16[224,128]{1,0:T(8,128)(2,1)S(1)}, bf16[224,128]{1,0:T(8,128)(2,1)S(1)}, u32[]{:S(2)}, u32[]{:S(2)}) collective-permute-start(bf16[224,128]{1,0:T(8,128)(2,1)S(1)} %pad_maximum_fusion.7), channel_id=1, source_target_pairs={{0,12},{2,14},{4,0},{6,2},{8,4},{10,6},{12,8},{14,10},{1,13},{3,15... | collective-permute-start | bytes 172040 | tf_op jit(solution)/shard_map/ppermute | solution.py:17
  70.3 5.8 %collective-permute-start.20 = (bf16[224,128]{1,0:T(8,128)(2,1)S(1)}, bf16[224,128]{1,0:T(8,128)(2,1)S(1)}, u32[]{:S(2)}, u32[]{:S(2)}) collective-permute-start(bf16[224,128]{1,0:T(8,128)(2,1)S(1)} %add_convert_fusion.1), channel_id=1, source_target_pairs={{0,2},{2,0},{4,6},{6,4},{8,10},{10,8},{12,14},{14,12},{1,3},{3,1},... | collective-permute-start | bytes 172040 | tf_op jit(solution)/shard_map/ppermute | solution.py:22
  73.5 7.2 %collective-permute-start.25 = (bf16[144,128]{1,0:T(8,128)(2,1)S(1)}, bf16[144,128]{1,0:T(8,128)(2,1)S(1)}, u32[]{:S(2)}, u32[]{:S(2)}) collective-permute-start(bf16[144,128]{1,0:T(8,128)(2,1)S(1)} %slice.110), channel_id=1, source_target_pairs={{0,3},{1,2},{2,1},{3,0},{4,7},{5,6},{6,5},{7,4},{8,11},{9,10},{10,... | collective-permute-start | bytes 110600 | tf_op jit(solution)/shard_map/ppermute | solution.py:443
  73.5 7.2 %collective-permute-start.24 = (bf16[144,128]{1,0:T(8,128)(2,1)S(1)}, bf16[144,128]{1,0:T(8,128)(2,1)S(1)}, u32[]{:S(2)}, u32[]{:S(2)}) collective-permute-start(bf16[144,128]{1,0:T(8,128)(2,1)S(1)} %slice.110), channel_id=1, source_target_pairs={{0,1},{1,0},{2,3},{3,2},{4,5},{5,4},{6,7},{7,6},{8,9},{9,8},{10,11... | collective-permute-start | bytes 110600 | tf_op jit(solution)/shard_map/ppermute | solution.py:22
  77.0 8.1 %collective-permute-start.23 = (bf16[128,192]{1,0:T(8,128)(2,1)S(1)}, bf16[128,192]{1,0:T(8,128)(2,1)S(1)}, u32[]{:S(2)}, u32[]{:S(2)}) collective-permute-start(bf16[128,192]{1,0:T(8,128)(2,1)S(1)} %get-tuple-element.83), channel_id=1, source_target_pairs={{0,12},{2,14},{4,0},{6,2},{8,4},{10,6},{12,8},{14,10},{1,13},{3,15... | collective-permute-start | bytes 147464 | tf_op jit(solution)/shard_map/ppermute | solution.py:17
  79.7 5.8 %collective-permute-start.22 = (bf16[128,192]{1,0:T(8,128)(2,1)S(1)}, bf16[128,192]{1,0:T(8,128)(2,1)S(1)}, u32[]{:S(2)}, u32[]{:S(2)}) collective-permute-start(bf16[128,192]{1,0:T(8,128)(2,1)S(1)} %get-tuple-element.84), channel_id=1, source_target_pairs={{0,8},{2,10},{4,12},{6,14},{8,0},{10,2},{12,4},{14,6},{1,9},{3,11}... | collective-permute-start | bytes 147464 | tf_op jit(solution)/shard_map/ppermute | solution.py:17
  80.6 5.6 %collective-permute-start.21 = (bf16[128,192]{1,0:T(8,128)(2,1)S(1)}, bf16[128,192]{1,0:T(8,128)(2,1)S(1)}, u32[]{:S(2)}, u32[]{:S(2)}) collective-permute-start(bf16[128,192]{1,0:T(8,128)(2,1)S(1)} %get-tuple-element.85), channel_id=1, source_target_pairs={{0,4},{2,6},{4,8},{6,10},{8,12},{10,14},{12,0},{14,2},{1,5},{3,7},... | collective-permute-start | bytes 147464 | tf_op jit(solution)/shard_map/ppermute | solution.py:17
  80.7 4.4 %collective-permute-start.26 = (bf16[144,128]{1,0:T(8,128)(2,1)S(1)}, bf16[144,128]{1,0:T(8,128)(2,1)S(1)}, u32[]{:S(2)}, u32[]{:S(2)}) collective-permute-start(bf16[144,128]{1,0:T(8,128)(2,1)S(1)} %add_convert_fusion.4), channel_id=1, source_target_pairs={{0,32},{16,48},{32,0},{48,16},{64,96},{80,112},{96,64},{112,80},{1... | collective-permute-start | bytes 110600 | tf_op jit(solution)/shard_map/ppermute | solution.py:22
  86.2 5.9 %collective-permute-start.29 = (bf16[144,128]{1,0:T(8,128)(2,1)S(1)}, bf16[144,128]{1,0:T(8,128)(2,1)S(1)}, u32[]{:S(2)}, u32[]{:S(2)}) collective-permute-start(bf16[144,128]{1,0:T(8,128)(2,1)S(1)} %add_convert_fusion.4), channel_id=1, source_target_pairs={{0,96},{16,112},{32,64},{48,80},{64,32},{80,48},{96,0},{112,16},{1... | collective-permute-start | bytes 110600 | tf_op jit(solution)/shard_map/ppermute | solution.py:22
  89.0 4.9 %collective-permute-start.28 = (bf16[144,128]{1,0:T(8,128)(2,1)S(1)}, bf16[144,128]{1,0:T(8,128)(2,1)S(1)}, u32[]{:S(2)}, u32[]{:S(2)}) collective-permute-start(bf16[144,128]{1,0:T(8,128)(2,1)S(1)} %add_convert_fusion.4), channel_id=1, source_target_pairs={{0,64},{16,80},{32,96},{48,112},{64,0},{80,16},{96,32},{112,48},{1... | collective-permute-start | bytes 110600 | tf_op jit(solution)/shard_map/ppermute | solution.py:22
  89.1 5.5 %collective-permute-start.27 = (bf16[64,192]{1,0:T(8,128)(2,1)S(1)}, bf16[64,192]{1,0:T(8,128)(2,1)S(1)}, u32[]{:S(2)}, u32[]{:S(2)}) collective-permute-start(bf16[64,192]{1,0:T(8,128)(2,1)S(1)} %select_convert_fusion), channel_id=1, source_target_pairs={{0,2},{2,0},{4,6},{6,4},{8,10},{10,8},{12,14},{14,12},{1,3},{3,1},... | collective-permute-start | bytes 73736 | tf_op jit(solution)/shard_map/ppermute | solution.py:22
  94.0 1.5 %collective-permute-start.30 = (bf16[576,128]{1,0:T(8,128)(2,1)S(1)}, bf16[576,128]{1,0:T(8,128)(2,1)S(1)}, u32[]{:S(2)}, u32[]{:S(2)}) collective-permute-start(bf16[576,128]{1,0:T(8,128)(2,1)S(1)} %pad_maximum_fusion.1), channel_id=1, source_target_pairs={{0,16},{16,0},{32,48},{48,32},{64,80},{80,64},{96,112},{112,96},{1... | collective-permute-start | bytes 442376 | tf_op jit(solution)/shard_map/ppermute | solution.py:22

commit v8 on v7

--- a/solution.py
+++ b/solution.py
@@ -458,6 +458,7 @@
     theirs = flip(half, "row", 1)
     grad_pair_w = jnp.concatenate([jnp.where(is_first, half, theirs), jnp.where(is_first, theirs, half)])
     grad_pair_w = up(grad_pair_w).reshape(3, 3, pairs, pairs) / 512.0
+    other, grad_pair_w = lax.optimization_barrier((other, grad_pair_w))
     grad_fine = (jnp.where(is_odd, mine[64:], mine[:64]) + up(other)).astype(BF)
     return out[None], grad_fine[None], grad_pair_w
 

time: 97.6 us -> 101 us (1.035)
  waiting for transfers between devices: 38.8 us -> 43.5 us
    ppermute x15, waiting for transfers between devices: 23.6 us -> 28.3 us  [flip(): return lax.ppermute(x, axis, [(i, i ^ bit) for i in range(count)])]
where the time goes in v8:
time: 101 us; the launch traced here: 100 us
  waiting for transfers between devices  43.5 us (43%)
  starting transfers between devices  43.2 us (43%)
  Pallas kernels  9.12 us (9%)
  other arithmetic  1.93 us (2%)
  local copies, waits for them, and re-layouts  1.33 us (1%)
  between operations  1.1 us (1%)
    ppermute x15, waiting for transfers between devices, flip(): return lax.ppermute(x, axis, [(i, i ^ bit) for i in range(count)])  28.3 us
    ppermute x15, starting transfers between devices, flip(): return lax.ppermute(x, axis, [(i, i ^ bit) for i in range(count)])  20.4 us
    ppermute x11, starting transfers between devices, shift(): lax.ppermute(x, axis, [(i, (i + step) % count) for i in range(count)])  17.8 us
    ppermute x11, waiting for transfers between devices, shift(): lax.ppermute(x, axis, [(i, (i + step) % count) for i in range(count)])  10.2 us
    pallas_call x1, Pallas kernels, pair_block(): pl.pallas_call(pair_kernel, out_shape=(jax.ShapeDtypeStruct((32, 64, chan...  5.57 us
    ppermute x4, waiting for transfers between devices, spread(): return lax.ppermute(x, ('row', 'col'), sorted(pairs.items()))  4.97 us
    ppermute x4, starting transfers between devices, spread(): return lax.ppermute(x, ('row', 'col'), sorted(pairs.items()))  4.93 us
  transfers between devices with their start and end apart: 31, of which 21 were waited for; matrix products, arithmetic and copies ran while one was open for 1% of the time, Pallas kernels for 1%

profile of v8, /device:TPU:2, one launch (start us, length us, event | category | flops | bytes accessed | tf_op | source)
XLA Modules:
  0.0 100.2 jit_solution(5502080254727938781)
XLA Ops:
  0.8 0.0 copy-start.1
  0.8 0.0 copy-start.2
  0.8 0.0 copy-start.3
  0.8 0.0 copy-start.6
  0.8 1.0 copy-done.1
  1.8 0.2 copy-done.2
  2.0 0.0 copy-done.3
  2.0 0.5 shard_map.95
  2.6 0.0 collective-permute-start
  2.6 5.3 %collective-permute-start.1 = (bf16[8,64,128]{2,1,0:T(8,128)(2,1)S(1)}, bf16[8,64,128]{2,1,0:T(8,128)(2,1)S(1)}, u32[]{:S(2)}, u32[]{:S(2)}) collective-permute-start(bf16[8,64,128]{2,1,0:T(8,128)(2,1)S(1)} %get-tuple-element.47), channel_id=1, source_target_pairs={{0,240},{16,0},{32,16},{48,32},{64,48},{80,64},{96,80},{112,96},{1... | collective-permute-start | bytes 393224 | tf_op jit(solution)/shard_map/ppermute | solution.py:17
  7.9 0.3 shard_map.96
  8.2 2.3 %collective-permute-done.top = bf16[8,64,128]{2,1,0:T(8,128)(2,1)S(1)} collective-permute-done((bf16[8,64,128]{2,1,0:T(8,128)(2,1)S(1)}, bf16[8,64,128]{2,1,0:T(8,128)(2,1)S(1)}, u32[]{:S(2)}, u32[]{:S(2)}) %collective-permute-start) | collective-permute-done | bytes 131104 | tf_op jit(solution)/shard_map/ppermute | solution.py:17
  10.5 1.8 %shard_map.97 = (bf16[272,128]{1,0:T(8,128)(2,1)S(1)}, bf16[272,128]{1,0:T(8,128)(2,1)S(1)}) custom-call(s32[8]{0:T(128)S(1)} %select_convert_fusion.2.flags, bf16[64,1536]{1,0:T(8,128)(2,1)S(1)} %bitcast.48, bf16[8,64,128]{2,1,0:T(8,128)(2,1)S(1)} %collective-permute-done.top, bf16[8,64,128]{2,1,0:T(8,128)(2,1)S(1)} %collective-permute-done.1.bottom, ...), custom_call_target="tpu_custom_call" | custom-call | flops 120000000 | bytes 3500000 | tf_op jit(solution)/shard_map/pallas_call | solution.py:333
  12.3 3.1 %collective-permute-start.4 = (bf16[272,128]{1,0:T(8,128)(2,1)S(1)}, bf16[272,128]{1,0:T(8,128)(2,1)S(1)}, u32[]{:S(2)}, u32[]{:S(2)}) collective-permute-start(bf16[272,128]{1,0:T(8,128)(2,1)S(1)} %get-tuple-element.53), channel_id=1, source_target_pairs={{0,12},{2,14},{4,0},{6,2},{8,4},{10,6},{12,8},{14,10},{1,13},{3,15... | collective-permute-start | bytes 208904 | tf_op jit(solution)/shard_map/ppermute | solution.py:17
  15.4 2.2 %collective-permute-start.2 = (bf16[80,128]{1,0:T(8,128)(2,1)S(1)}, bf16[80,128]{1,0:T(8,128)(2,1)S(1)}, u32[]{:S(2)}, u32[]{:S(2)}) collective-permute-start(bf16[80,128]{1,0:T(8,128)(2,1)S(1)} %slice.73), channel_id=1, source_target_pairs={{0,8},{2,10},{4,12},{6,14},{8,0},{10,2},{12,4},{14,6},{1,9},{3,11}... | collective-permute-start | bytes 61448 | tf_op jit(solution)/shard_map/ppermute | solution.py:17
  17.6 3.5 %collective-permute-done.3 = bf16[272,128]{1,0:T(8,128)(2,1)S(1)} collective-permute-done((bf16[272,128]{1,0:T(8,128)(2,1)S(1)}, bf16[272,128]{1,0:T(8,128)(2,1)S(1)}, u32[]{:S(2)}, u32[]{:S(2)}) %collective-permute-start.3) | collective-permute-done | bytes 69664 | tf_op jit(solution)/shard_map/ppermute | solution.py:17
  21.2 0.0 collective-permute-done.2
  21.2 2.2 %collective-permute-start.5 = (bf16[464,128]{1,0:T(8,128)(2,1)S(1)}, bf16[464,128]{1,0:T(8,128)(2,1)S(1)}, u32[]{:S(2)}, u32[]{:S(2)}) collective-permute-start(bf16[464,128]{1,0:T(8,128)(2,1)S(1)} %pad_maximum_fusion.2), channel_id=1, source_target_pairs={{0,2},{2,0},{4,6},{6,4},{8,10},{10,8},{12,14},{14,12},{1,3},{3,1},... | collective-permute-start | bytes 356360 | tf_op jit(solution)/shard_map/ppermute | solution.py:22
  23.4 4.2 %collective-permute-done.5 = bf16[464,128]{1,0:T(8,128)(2,1)S(1)} collective-permute-done((bf16[464,128]{1,0:T(8,128)(2,1)S(1)}, bf16[464,128]{1,0:T(8,128)(2,1)S(1)}, u32[]{:S(2)}, u32[]{:S(2)}) %collective-permute-start.5) | collective-permute-done | bytes 118816 | tf_op jit(solution)/shard_map/ppermute | solution.py:22
  27.7 0.1 collective-permute-start.6
  27.8 1.2 %collective-permute-done.6 = bf16[35,128]{1,0:T(8,128)(2,1)S(1)} collective-permute-done((bf16[35,128]{1,0:T(8,128)(2,1)S(1)}, bf16[35,128]{1,0:T(8,128)(2,1)S(1)}, u32[]{:S(2)}, u32[]{:S(2)}) %collective-permute-start.6) | collective-permute-done | bytes 8992 | tf_op jit(solution)/shard_map/ppermute | solution.py:22
  29.0 4.9 %collective-permute-start.10 = (bf16[70,128]{1,0:T(8,128)(2,1)S(1)}, bf16[70,128]{1,0:T(8,128)(2,1)S(1)}, u32[]{:S(2)}, u32[]{:S(2)}) collective-permute-start(bf16[70,128]{1,0:T(8,128)(2,1)S(1)} %pad_maximum_fusion.8), channel_id=1, source_target_pairs={{0,128},{2,18},{4,20},{6,22},{8,24},{10,26},{12,28},{14,30},{16,0}... | collective-permute-start | bytes 53768 | tf_op jit(solution)/shard_map/ppermute | solution.py:43
  33.9 1.4 %collective-permute-done.10 = bf16[70,128]{1,0:T(8,128)(2,1)S(1)} collective-permute-done((bf16[70,128]{1,0:T(8,128)(2,1)S(1)}, bf16[70,128]{1,0:T(8,128)(2,1)S(1)}, u32[]{:S(2)}, u32[]{:S(2)}) %collective-permute-start.10) | collective-permute-done | bytes 17952 | tf_op jit(solution)/shard_map/ppermute | solution.py:43
  35.4 3.5 %collective-permute-done.9 = bf16[70,128]{1,0:T(8,128)(2,1)S(1)} collective-permute-done((bf16[70,128]{1,0:T(8,128)(2,1)S(1)}, bf16[70,128]{1,0:T(8,128)(2,1)S(1)}, u32[]{:S(2)}, u32[]{:S(2)}) %collective-permute-start.9) | collective-permute-done | bytes 17952 | tf_op jit(solution)/shard_map/ppermute | solution.py:43
  38.9 0.0 collective-permute-done.7
  38.9 0.2 collective-permute-start.11
  39.1 1.1 %collective-permute-done.11 = bf16[70,128]{1,0:T(8,128)(2,1)S(1)} collective-permute-done((bf16[70,128]{1,0:T(8,128)(2,1)S(1)}, bf16[70,128]{1,0:T(8,128)(2,1)S(1)}, u32[]{:S(2)}, u32[]{:S(2)}) %collective-permute-start.11) | collective-permute-done | bytes 17952 | tf_op jit(solution)/shard_map/ppermute | solution.py:22
  40.2 5.6 %shard_map.98 = (bf16[32,64,128]{2,1,0:T(8,128)(2,1)}, f32[616,128]{1,0:T(8,128)S(1)}, bf16[616,128]{1,0:T(8,128)(2,1)S(1)}, bf16[40,128]{1,0:T(8,128)(2,1)S(1)}) custom-call(s32[8]{0:T(128)S(1)} %select_convert_fusion.2.flags, bf16[32,64,128]{2,1,0:T(8,128)(2,1)S(1)} %bitcast.41, bf16[32,64,128]{2,1,0:T(8,128)(2,1)S(1)} %bitcast.44, ...), custom_call_target="tpu_custom_call" | custom-call | flops 2500000000 | bytes 4000000 | tf_op jit(solution)/shard_map/pallas_call | solution.py:359
  45.8 0.2 collective-permute-start.12
  45.9 1.2 %collective-permute-done.12 = bf16[616,128]{1,0:T(8,128)(2,1)S(1)} collective-permute-done((bf16[616,128]{1,0:T(8,128)(2,1)S(1)}, bf16[616,128]{1,0:T(8,128)(2,1)S(1)}, u32[]{:S(2)}, u32[]{:S(2)}) %collective-permute-start.12) | collective-permute-done | bytes 157728 | tf_op jit(solution)/shard_map/ppermute | solution.py:22
  47.3 0.1 collective-permute-start.13
  47.4 1.3 %collective-permute-start.14 = (bf16[184,128]{1,0:T(8,128)(2,1)S(1)}, bf16[184,128]{1,0:T(8,128)(2,1)S(1)}, u32[]{:S(2)}, u32[]{:S(2)}) collective-permute-start(bf16[184,128]{1,0:T(8,128)(2,1)S(1)} %get-tuple-element.103), channel_id=1, source_target_pairs={{0,64},{16,80},{32,96},{48,112},{64,0},{80,16},{96,32},{112,48},{1... | collective-permute-start | bytes 141320 | tf_op jit(solution)/shard_map/ppermute | solution.py:22
  48.7 3.0 %collective-permute-start.15 = (bf16[184,128]{1,0:T(8,128)(2,1)S(1)}, bf16[184,128]{1,0:T(8,128)(2,1)S(1)}, u32[]{:S(2)}, u32[]{:S(2)}) collective-permute-start(bf16[184,128]{1,0:T(8,128)(2,1)S(1)} %get-tuple-element.104), channel_id=1, source_target_pairs={{0,96},{16,112},{32,64},{48,80},{64,32},{80,48},{96,0},{112,16},{1... | collective-permute-start | bytes 141320 | tf_op jit(solution)/shard_map/ppermute | solution.py:22
  51.8 0.2 collective-permute-done.13
  52.0 2.7 %collective-permute-done.14 = bf16[184,128]{1,0:T(8,128)(2,1)S(1)} collective-permute-done((bf16[184,128]{1,0:T(8,128)(2,1)S(1)}, bf16[184,128]{1,0:T(8,128)(2,1)S(1)}, u32[]{:S(2)}, u32[]{:S(2)}) %collective-permute-start.14) | collective-permute-done | bytes 47136 | tf_op jit(solution)/shard_map/ppermute | solution.py:22
  54.7 0.0 collective-permute-done.15
  54.7 2.8 %collective-permute-start.16 = (bf16[184,128]{1,0:T(8,128)(2,1)S(1)}, bf16[184,128]{1,0:T(8,128)(2,1)S(1)}, u32[]{:S(2)}, u32[]{:S(2)}) collective-permute-start(bf16[184,128]{1,0:T(8,128)(2,1)S(1)} %add_convert_fusion.3), channel_id=1, source_target_pairs={{0,128},{16,144},{32,160},{48,176},{64,192},{80,208},{96,224},{112... | collective-permute-start | bytes 141320 | tf_op jit(solution)/shard_map/ppermute | solution.py:22
  57.5 5.8 %collective-permute-done.16 = bf16[184,128]{1,0:T(8,128)(2,1)S(1)} collective-permute-done((bf16[184,128]{1,0:T(8,128)(2,1)S(1)}, bf16[184,128]{1,0:T(8,128)(2,1)S(1)}, u32[]{:S(2)}, u32[]{:S(2)}) %collective-permute-start.16) | collective-permute-done | bytes 47136 | tf_op jit(solution)/shard_map/ppermute | solution.py:22
  63.3 0.8 collective-permute-start.18
  64.1 0.5 collective-permute-start.17
  64.6 2.3 %collective-permute-start.19 = (bf16[224,128]{1,0:T(8,128)(2,1)S(1)}, bf16[224,128]{1,0:T(8,128)(2,1)S(1)}, u32[]{:S(2)}, u32[]{:S(2)}) collective-permute-start(bf16[224,128]{1,0:T(8,128)(2,1)S(1)} %pad_maximum_fusion.7), channel_id=1, source_target_pairs={{0,12},{2,14},{4,0},{6,2},{8,4},{10,6},{12,8},{14,10},{1,13},{3,15... | collective-permute-start | bytes 172040 | tf_op jit(solution)/shard_map/ppermute | solution.py:17
  66.9 1.9 %collective-permute-done.18 = bf16[224,128]{1,0:T(8,128)(2,1)S(1)} collective-permute-done((bf16[224,128]{1,0:T(8,128)(2,1)S(1)}, bf16[224,128]{1,0:T(8,128)(2,1)S(1)}, u32[]{:S(2)}, u32[]{:S(2)}) %collective-permute-start.18) | collective-permute-done | bytes 57376 | tf_op jit(solution)/shard_map/ppermute | solution.py:17
  68.8 1.0 %collective-permute-done.17 = bf16[224,128]{1,0:T(8,128)(2,1)S(1)} collective-permute-done((bf16[224,128]{1,0:T(8,128)(2,1)S(1)}, bf16[224,128]{1,0:T(8,128)(2,1)S(1)}, u32[]{:S(2)}, u32[]{:S(2)}) %collective-permute-start.17) | collective-permute-done | bytes 57376 | tf_op jit(solution)/shard_map/ppermute | solution.py:17
  69.8 0.5 collective-permute-done.19
  70.3 3.2 %collective-permute-start.20 = (bf16[224,128]{1,0:T(8,128)(2,1)S(1)}, bf16[224,128]{1,0:T(8,128)(2,1)S(1)}, u32[]{:S(2)}, u32[]{:S(2)}) collective-permute-start(bf16[224,128]{1,0:T(8,128)(2,1)S(1)} %add_convert_fusion.1), channel_id=1, source_target_pairs={{0,2},{2,0},{4,6},{6,4},{8,10},{10,8},{12,14},{14,12},{1,3},{3,1},... | collective-permute-start | bytes 172040 | tf_op jit(solution)/shard_map/ppermute | solution.py:22
  73.5 1.6 %collective-permute-start.24 = (bf16[144,128]{1,0:T(8,128)(2,1)S(1)}, bf16[144,128]{1,0:T(8,128)(2,1)S(1)}, u32[]{:S(2)}, u32[]{:S(2)}) collective-permute-start(bf16[144,128]{1,0:T(8,128)(2,1)S(1)} %slice.110), channel_id=1, source_target_pairs={{0,1},{1,0},{2,3},{3,2},{4,5},{5,4},{6,7},{7,6},{8,9},{9,8},{10,11... | collective-permute-start | bytes 110600 | tf_op jit(solution)/shard_map/ppermute | solution.py:22
  75.1 1.0 collective-permute-done.20
  76.1 0.9 shard_map.99
  77.0 2.7 %collective-permute-start.23 = (bf16[128,192]{1,0:T(8,128)(2,1)S(1)}, bf16[128,192]{1,0:T(8,128)(2,1)S(1)}, u32[]{:S(2)}, u32[]{:S(2)}) collective-permute-start(bf16[128,192]{1,0:T(8,128)(2,1)S(1)} %get-tuple-element.87), channel_id=1, source_target_pairs={{0,12},{2,14},{4,0},{6,2},{8,4},{10,6},{12,8},{14,10},{1,13},{3,15... | collective-permute-start | bytes 147464 | tf_op jit(solution)/shard_map/ppermute | solution.py:17
  79.7 0.9 collective-permute-start.22
  80.6 0.1 collective-permute-start.21
  80.7 0.8 collective-permute-start.26
  81.5 3.7 %collective-permute-done.26 = bf16[144,128]{1,0:T(8,128)(2,1)S(1)} collective-permute-done((bf16[144,128]{1,0:T(8,128)(2,1)S(1)}, bf16[144,128]{1,0:T(8,128)(2,1)S(1)}, u32[]{:S(2)}, u32[]{:S(2)}) %collective-permute-start.26) | collective-permute-done | bytes 36896 | tf_op jit(solution)/shard_map/ppermute | solution.py:22
  85.2 0.3 collective-permute-done.22
  85.5 0.7 collective-permute-done.21
  86.2 2.8 %collective-permute-start.29 = (bf16[144,128]{1,0:T(8,128)(2,1)S(1)}, bf16[144,128]{1,0:T(8,128)(2,1)S(1)}, u32[]{:S(2)}, u32[]{:S(2)}) collective-permute-start(bf16[144,128]{1,0:T(8,128)(2,1)S(1)} %add_convert_fusion.4), channel_id=1, source_target_pairs={{0,96},{16,112},{32,64},{48,80},{64,32},{80,48},{96,0},{112,16},{1... | collective-permute-start | bytes 110600 | tf_op jit(solution)/shard_map/ppermute | solution.py:22
  89.1 2.9 %collective-permute-done.29 = bf16[144,128]{1,0:T(8,128)(2,1)S(1)} collective-permute-done((bf16[144,128]{1,0:T(8,128)(2,1)S(1)}, bf16[144,128]{1,0:T(8,128)(2,1)S(1)}, u32[]{:S(2)}, u32[]{:S(2)}) %collective-permute-start.29) | collective-permute-done | bytes 36896 | tf_op jit(solution)/shard_map/ppermute | solution.py:22
  92.0 1.9 %collective-permute-done.28 = bf16[144,128]{1,0:T(8,128)(2,1)S(1)} collective-permute-done((bf16[144,128]{1,0:T(8,128)(2,1)S(1)}, bf16[144,128]{1,0:T(8,128)(2,1)S(1)}, u32[]{:S(2)}, u32[]{:S(2)}) %collective-permute-start.28) | collective-permute-done | bytes 36896 | tf_op jit(solution)/shard_map/ppermute | solution.py:22
  94.0 0.1 collective-permute-start.30
  94.1 2.0 %collective-permute-start.27 = (bf16[64,192]{1,0:T(8,128)(2,1)S(1)}, bf16[64,192]{1,0:T(8,128)(2,1)S(1)}, u32[]{:S(2)}, u32[]{:S(2)}) collective-permute-start(bf16[64,192]{1,0:T(8,128)(2,1)S(1)} %select_convert_fusion), channel_id=1, source_target_pairs={{0,2},{2,0},{4,6},{6,4},{8,10},{10,8},{12,14},{14,12},{1,3},{3,1},... | collective-permute-start | bytes 73736 | tf_op jit(solution)/shard_map/ppermute | solution.py:22
  96.1 0.1 broadcast_select_fusion.1
  96.2 0.9 convert_multiply_fusion
  97.1 2.5 %collective-permute-done.27 = bf16[64,192]{1,0:T(8,128)(2,1)S(1)} collective-permute-done((bf16[64,192]{1,0:T(8,128)(2,1)S(1)}, bf16[64,192]{1,0:T(8,128)(2,1)S(1)}, u32[]{:S(2)}, u32[]{:S(2)}) %collective-permute-start.27) | collective-permute-done | bytes 24608 | tf_op jit(solution)/shard_map/ppermute | solution.py:22
  99.6 0.6 fusion.1
  (56 shorter events, 0.5 us)
Async XLA Ops:
  0.8 1.0 %copy-start.1 = (bf16[1,32,64,128]{3,2,1,0:T(8,128)(2,1)S(1)}, bf16[1,32,64,128]{3,2,1,0:T(8,128)(2,1)}, u32[]{:S(2)}) copy-start(bf16[1,32,64,128]{3,2,1,0:T(8,128)(2,1)} %param.11) | copy-start | bytes 1572868
  0.8 1.2 %copy-start.2 = (bf16[1,32,64,128]{3,2,1,0:T(8,128)(2,1)S(1)}, bf16[1,32,64,128]{3,2,1,0:T(8,128)(2,1)}, u32[]{:S(2)}) copy-start(bf16[1,32,64,128]{3,2,1,0:T(8,128)(2,1)} %param.13) | copy-start | bytes 1572868
  0.8 1.2 %copy-start.3 = (bf16[1,64,1536]{2,1,0:T(8,128)(2,1)S(1)}, bf16[1,64,1536]{2,1,0:T(8,128)(2,1)}, u32[]{:S(2)}) copy-start(bf16[1,64,1536]{2,1,0:T(8,128)(2,1)} %param.7) | copy-start | bytes 589828
  0.8 7.1 %copy-start.6 = (bf16[3,3,128,128]{3,2,1,0:T(8,128)(2,1)S(1)}, bf16[3,3,128,128]{3,2,1,0:T(8,128)(2,1)}, u32[]{:S(2)}) copy-start(bf16[3,3,128,128]{3,2,1,0:T(8,128)(2,1)} %param.12) | copy-start | bytes 884740
  2.6 8.0 %collective-permute-start = (bf16[8,64,128]{2,1,0:T(8,128)(2,1)S(1)}, bf16[8,64,128]{2,1,0:T(8,128)(2,1)S(1)}, u32[]{:S(2)}, u32[]{:S(2)}) collective-permute-start(bf16[8,64,128]{2,1,0:T(8,128)(2,1)S(1)} %get-tuple-element.46), channel_id=1, source_target_pairs={{0,16},{16,32},{32,48},{48,64},{64,80},{80,96},{96,112},{112,128},... | collective-permute-start | bytes 393224 | tf_op jit(solution)/shard_map/ppermute | solution.py:17
  2.6 7.9 %collective-permute-start.1 = (bf16[8,64,128]{2,1,0:T(8,128)(2,1)S(1)}, bf16[8,64,128]{2,1,0:T(8,128)(2,1)S(1)}, u32[]{:S(2)}, u32[]{:S(2)}) collective-permute-start(bf16[8,64,128]{2,1,0:T(8,128)(2,1)S(1)} %get-tuple-element.47), channel_id=1, source_target_pairs={{0,240},{16,0},{32,16},{48,32},{64,48},{80,64},{96,80},{112,96},{1... | collective-permute-start | bytes 393224 | tf_op jit(solution)/shard_map/ppermute | solution.py:17
  7.9 2.6 %copy-start = (bf16[5,192,1536]{2,1,0:T(8,128)(2,1)S(1)}, bf16[5,192,1536]{2,1,0:T(8,128)(2,1)}, u32[]{:S(2)}) copy-start(bf16[5,192,1536]{2,1,0:T(8,128)(2,1)} %conv_w.3) | copy-start | bytes 8847364
  7.9 2.6 %copy-start.4 = (bf16[192,128]{1,0:T(8,128)(2,1)S(1)}, bf16[192,128]{1,0:T(8,128)(2,1)}, u32[]{:S(2)}) copy-start(bf16[192,128]{1,0:T(8,128)(2,1)} %proj_a.3) | copy-start | bytes 147460
  7.9 2.6 %copy-start.5 = (bf16[192,128]{1,0:T(8,128)(2,1)S(1)}, bf16[192,128]{1,0:T(8,128)(2,1)}, u32[]{:S(2)}) copy-start(bf16[192,128]{1,0:T(8,128)(2,1)} %proj_b.3) | copy-start | bytes 147460
  12.3 5.3 %collective-permute-start.4 = (bf16[272,128]{1,0:T(8,128)(2,1)S(1)}, bf16[272,128]{1,0:T(8,128)(2,1)S(1)}, u32[]{:S(2)}, u32[]{:S(2)}) collective-permute-start(bf16[272,128]{1,0:T(8,128)(2,1)S(1)} %get-tuple-element.53), channel_id=1, source_target_pairs={{0,12},{2,14},{4,0},{6,2},{8,4},{10,6},{12,8},{14,10},{1,13},{3,15... | collective-permute-start | bytes 208904 | tf_op jit(solution)/shard_map/ppermute | solution.py:17
  15.4 5.7 %collective-permute-start.3 = (bf16[272,128]{1,0:T(8,128)(2,1)S(1)}, bf16[272,128]{1,0:T(8,128)(2,1)S(1)}, u32[]{:S(2)}, u32[]{:S(2)}) collective-permute-start(bf16[272,128]{1,0:T(8,128)(2,1)S(1)} %get-tuple-element.52), channel_id=1, source_target_pairs={{0,4},{2,6},{4,8},{6,10},{8,12},{10,14},{12,0},{14,2},{1,5},{3,7},... | collective-permute-start | bytes 208904 | tf_op jit(solution)/shard_map/ppermute | solution.py:17
  15.4 5.8 %collective-permute-start.2 = (bf16[80,128]{1,0:T(8,128)(2,1)S(1)}, bf16[80,128]{1,0:T(8,128)(2,1)S(1)}, u32[]{:S(2)}, u32[]{:S(2)}) collective-permute-start(bf16[80,128]{1,0:T(8,128)(2,1)S(1)} %slice.73), channel_id=1, source_target_pairs={{0,8},{2,10},{4,12},{6,14},{8,0},{10,2},{12,4},{14,6},{1,9},{3,11}... | collective-permute-start | bytes 61448 | tf_op jit(solution)/shard_map/ppermute | solution.py:17
  21.2 6.4 %collective-permute-start.5 = (bf16[464,128]{1,0:T(8,128)(2,1)S(1)}, bf16[464,128]{1,0:T(8,128)(2,1)S(1)}, u32[]{:S(2)}, u32[]{:S(2)}) collective-permute-start(bf16[464,128]{1,0:T(8,128)(2,1)S(1)} %pad_maximum_fusion.2), channel_id=1, source_target_pairs={{0,2},{2,0},{4,6},{6,4},{8,10},{10,8},{12,14},{14,12},{1,3},{3,1},... | collective-permute-start | bytes 356360 | tf_op jit(solution)/shard_map/ppermute | solution.py:22
  27.7 1.3 %collective-permute-start.6 = (bf16[35,128]{1,0:T(8,128)(2,1)S(1)}, bf16[35,128]{1,0:T(8,128)(2,1)S(1)}, u32[]{:S(2)}, u32[]{:S(2)}) collective-permute-start(bf16[35,128]{1,0:T(8,128)(2,1)S(1)} %slice_select_fusion.3), channel_id=1, source_target_pairs={{0,16},{16,0},{32,48},{48,32},{64,80},{80,64},{96,112},{112,96},{1... | collective-permute-start | bytes 26888 | tf_op jit(solution)/shard_map/ppermute | solution.py:22
  29.0 6.4 %collective-permute-start.10 = (bf16[70,128]{1,0:T(8,128)(2,1)S(1)}, bf16[70,128]{1,0:T(8,128)(2,1)S(1)}, u32[]{:S(2)}, u32[]{:S(2)}) collective-permute-start(bf16[70,128]{1,0:T(8,128)(2,1)S(1)} %pad_maximum_fusion.8), channel_id=1, source_target_pairs={{0,128},{2,18},{4,20},{6,22},{8,24},{10,26},{12,28},{14,30},{16,0}... | collective-permute-start | bytes 53768 | tf_op jit(solution)/shard_map/ppermute | solution.py:43
  33.9 5.0 %collective-permute-start.9 = (bf16[70,128]{1,0:T(8,128)(2,1)S(1)}, bf16[70,128]{1,0:T(8,128)(2,1)S(1)}, u32[]{:S(2)}, u32[]{:S(2)}) collective-permute-start(bf16[70,128]{1,0:T(8,128)(2,1)S(1)} %pad_maximum_fusion.8), channel_id=1, source_target_pairs={{0,96},{2,18},{4,20},{6,102},{8,24},{10,26},{12,28},{14,30},{16,17... | collective-permute-start | bytes 53768 | tf_op jit(solution)/shard_map/ppermute | solution.py:43
  33.9 5.0 %collective-permute-start.8 = (bf16[70,128]{1,0:T(8,128)(2,1)S(1)}, bf16[70,128]{1,0:T(8,128)(2,1)S(1)}, u32[]{:S(2)}, u32[]{:S(2)}) collective-permute-start(bf16[70,128]{1,0:T(8,128)(2,1)S(1)} %pad_maximum_fusion.8), channel_id=1, source_target_pairs={{0,64},{2,18},{4,68},{6,22},{8,24},{10,26},{12,28},{14,30},{16,208... | collective-permute-start | bytes 53768 | tf_op jit(solution)/shard_map/ppermute | solution.py:43
  33.9 5.0 %collective-permute-start.7 = (bf16[70,128]{1,0:T(8,128)(2,1)S(1)}, bf16[70,128]{1,0:T(8,128)(2,1)S(1)}, u32[]{:S(2)}, u32[]{:S(2)}) collective-permute-start(bf16[70,128]{1,0:T(8,128)(2,1)S(1)} %pad_maximum_fusion.8), channel_id=1, source_target_pairs={{0,32},{2,34},{4,20},{6,22},{8,24},{10,26},{12,28},{14,30},{16,240... | collective-permute-start | bytes 53768 | tf_op jit(solution)/shard_map/ppermute | solution.py:43
  38.9 1.3 %collective-permute-start.11 = (bf16[70,128]{1,0:T(8,128)(2,1)S(1)}, bf16[70,128]{1,0:T(8,128)(2,1)S(1)}, u32[]{:S(2)}, u32[]{:S(2)}) collective-permute-start(bf16[70,128]{1,0:T(8,128)(2,1)S(1)} %select_select_fusion), channel_id=1, source_target_pairs={{0,16},{16,0},{32,48},{48,32},{64,80},{80,64},{96,112},{112,96},{1... | collective-permute-start | bytes 53768 | tf_op jit(solution)/shard_map/ppermute | solution.py:22
  45.8 1.4 %collective-permute-start.12 = (bf16[616,128]{1,0:T(8,128)(2,1)S(1)}, bf16[616,128]{1,0:T(8,128)(2,1)S(1)}, u32[]{:S(2)}, u32[]{:S(2)}) collective-permute-start(bf16[616,128]{1,0:T(8,128)(2,1)S(1)} %get-tuple-element.65), channel_id=1, source_target_pairs={{0,16},{16,0},{32,48},{48,32},{64,80},{80,64},{96,112},{112,96},{1... | collective-permute-start | bytes 473096 | tf_op jit(solution)/shard_map/ppermute | solution.py:22
  47.3 4.7 %collective-permute-start.13 = (bf16[184,128]{1,0:T(8,128)(2,1)S(1)}, bf16[184,128]{1,0:T(8,128)(2,1)S(1)}, u32[]{:S(2)}, u32[]{:S(2)}) collective-permute-start(bf16[184,128]{1,0:T(8,128)(2,1)S(1)} %get-tuple-element.102), channel_id=1, source_target_pairs={{0,32},{16,48},{32,0},{48,16},{64,96},{80,112},{96,64},{112,80},{1... | collective-permute-start | bytes 141320 | tf_op jit(solution)/shard_map/ppermute | solution.py:22
  47.4 7.3 %collective-permute-start.14 = (bf16[184,128]{1,0:T(8,128)(2,1)S(1)}, bf16[184,128]{1,0:T(8,128)(2,1)S(1)}, u32[]{:S(2)}, u32[]{:S(2)}) collective-permute-start(bf16[184,128]{1,0:T(8,128)(2,1)S(1)} %get-tuple-element.103), channel_id=1, source_target_pairs={{0,64},{16,80},{32,96},{48,112},{64,0},{80,16},{96,32},{112,48},{1... | collective-permute-start | bytes 141320 | tf_op jit(solution)/shard_map/ppermute | solution.py:22
  48.7 6.0 %collective-permute-start.15 = (bf16[184,128]{1,0:T(8,128)(2,1)S(1)}, bf16[184,128]{1,0:T(8,128)(2,1)S(1)}, u32[]{:S(2)}, u32[]{:S(2)}) collective-permute-start(bf16[184,128]{1,0:T(8,128)(2,1)S(1)} %get-tuple-element.104), channel_id=1, source_target_pairs={{0,96},{16,112},{32,64},{48,80},{64,32},{80,48},{96,0},{112,16},{1... | collective-permute-start | bytes 141320 | tf_op jit(solution)/shard_map/ppermute | solution.py:22
  54.7 8.6 %collective-permute-start.16 = (bf16[184,128]{1,0:T(8,128)(2,1)S(1)}, bf16[184,128]{1,0:T(8,128)(2,1)S(1)}, u32[]{:S(2)}, u32[]{:S(2)}) collective-permute-start(bf16[184,128]{1,0:T(8,128)(2,1)S(1)} %add_convert_fusion.3), channel_id=1, source_target_pairs={{0,128},{16,144},{32,160},{48,176},{64,192},{80,208},{96,224},{112... | collective-permute-start | bytes 141320 | tf_op jit(solution)/shard_map/ppermute | solution.py:22
  63.3 5.5 %collective-permute-start.18 = (bf16[224,128]{1,0:T(8,128)(2,1)S(1)}, bf16[224,128]{1,0:T(8,128)(2,1)S(1)}, u32[]{:S(2)}, u32[]{:S(2)}) collective-permute-start(bf16[224,128]{1,0:T(8,128)(2,1)S(1)} %pad_maximum_fusion.7), channel_id=1, source_target_pairs={{0,4},{2,6},{4,8},{6,10},{8,12},{10,14},{12,0},{14,2},{1,5},{3,7},... | collective-permute-start | bytes 172040 | tf_op jit(solution)/shard_map/ppermute | solution.py:17
  64.1 5.7 %collective-permute-start.17 = (bf16[224,128]{1,0:T(8,128)(2,1)S(1)}, bf16[224,128]{1,0:T(8,128)(2,1)S(1)}, u32[]{:S(2)}, u32[]{:S(2)}) collective-permute-start(bf16[224,128]{1,0:T(8,128)(2,1)S(1)} %pad_maximum_fusion.7), channel_id=1, source_target_pairs={{0,8},{2,10},{4,12},{6,14},{8,0},{10,2},{12,4},{14,6},{1,9},{3,11}... | collective-permute-start | bytes 172040 | tf_op jit(solution)/shard_map/ppermute | solution.py:17
  64.6 5.6 %collective-permute-start.19 = (bf16[224,128]{1,0:T(8,128)(2,1)S(1)}, bf16[224,128]{1,0:T(8,128)(2,1)S(1)}, u32[]{:S(2)}, u32[]{:S(2)}) collective-permute-start(bf16[224,128]{1,0:T(8,128)(2,1)S(1)} %pad_maximum_fusion.7), channel_id=1, source_target_pairs={{0,12},{2,14},{4,0},{6,2},{8,4},{10,6},{12,8},{14,10},{1,13},{3,15... | collective-permute-start | bytes 172040 | tf_op jit(solution)/shard_map/ppermute | solution.py:17
  70.3 5.8 %collective-permute-start.20 = (bf16[224,128]{1,0:T(8,128)(2,1)S(1)}, bf16[224,128]{1,0:T(8,128)(2,1)S(1)}, u32[]{:S(2)}, u32[]{:S(2)}) collective-permute-start(bf16[224,128]{1,0:T(8,128)(2,1)S(1)} %add_convert_fusion.1), channel_id=1, source_target_pairs={{0,2},{2,0},{4,6},{6,4},{8,10},{10,8},{12,14},{14,12},{1,3},{3,1},... | collective-permute-start | bytes 172040 | tf_op jit(solution)/shard_map/ppermute | solution.py:22
  73.5 7.2 %collective-permute-start.25 = (bf16[144,128]{1,0:T(8,128)(2,1)S(1)}, bf16[144,128]{1,0:T(8,128)(2,1)S(1)}, u32[]{:S(2)}, u32[]{:S(2)}) collective-permute-start(bf16[144,128]{1,0:T(8,128)(2,1)S(1)} %slice.110), channel_id=1, source_target_pairs={{0,3},{1,2},{2,1},{3,0},{4,7},{5,6},{6,5},{7,4},{8,11},{9,10},{10,... | collective-permute-start | bytes 110600 | tf_op jit(solution)/shard_map/ppermute | solution.py:443
  73.5 7.2 %collective-permute-start.24 = (bf16[144,128]{1,0:T(8,128)(2,1)S(1)}, bf16[144,128]{1,0:T(8,128)(2,1)S(1)}, u32[]{:S(2)}, u32[]{:S(2)}) collective-permute-start(bf16[144,128]{1,0:T(8,128)(2,1)S(1)} %slice.110), channel_id=1, source_target_pairs={{0,1},{1,0},{2,3},{3,2},{4,5},{5,4},{6,7},{7,6},{8,9},{9,8},{10,11... | collective-permute-start | bytes 110600 | tf_op jit(solution)/shard_map/ppermute | solution.py:22
  77.0 8.1 %collective-permute-start.23 = (bf16[128,192]{1,0:T(8,128)(2,1)S(1)}, bf16[128,192]{1,0:T(8,128)(2,1)S(1)}, u32[]{:S(2)}, u32[]{:S(2)}) collective-permute-start(bf16[128,192]{1,0:T(8,128)(2,1)S(1)} %get-tuple-element.87), channel_id=1, source_target_pairs={{0,12},{2,14},{4,0},{6,2},{8,4},{10,6},{12,8},{14,10},{1,13},{3,15... | collective-permute-start | bytes 147464 | tf_op jit(solution)/shard_map/ppermute | solution.py:17
  79.7 5.8 %collective-permute-start.22 = (bf16[128,192]{1,0:T(8,128)(2,1)S(1)}, bf16[128,192]{1,0:T(8,128)(2,1)S(1)}, u32[]{:S(2)}, u32[]{:S(2)}) collective-permute-start(bf16[128,192]{1,0:T(8,128)(2,1)S(1)} %get-tuple-element.88), channel_id=1, source_target_pairs={{0,8},{2,10},{4,12},{6,14},{8,0},{10,2},{12,4},{14,6},{1,9},{3,11}... | collective-permute-start | bytes 147464 | tf_op jit(solution)/shard_map/ppermute | solution.py:17
  80.6 5.6 %collective-permute-start.21 = (bf16[128,192]{1,0:T(8,128)(2,1)S(1)}, bf16[128,192]{1,0:T(8,128)(2,1)S(1)}, u32[]{:S(2)}, u32[]{:S(2)}) collective-permute-start(bf16[128,192]{1,0:T(8,128)(2,1)S(1)} %get-tuple-element.89), channel_id=1, source_target_pairs={{0,4},{2,6},{4,8},{6,10},{8,12},{10,14},{12,0},{14,2},{1,5},{3,7},... | collective-permute-start | bytes 147464 | tf_op jit(solution)/shard_map/ppermute | solution.py:17
  80.7 4.4 %collective-permute-start.26 = (bf16[144,128]{1,0:T(8,128)(2,1)S(1)}, bf16[144,128]{1,0:T(8,128)(2,1)S(1)}, u32[]{:S(2)}, u32[]{:S(2)}) collective-permute-start(bf16[144,128]{1,0:T(8,128)(2,1)S(1)} %add_convert_fusion.4), channel_id=1, source_target_pairs={{0,32},{16,48},{32,0},{48,16},{64,96},{80,112},{96,64},{112,80},{1... | collective-permute-start | bytes 110600 | tf_op jit(solution)/shard_map/ppermute | solution.py:22
  86.2 5.8 %collective-permute-start.29 = (bf16[144,128]{1,0:T(8,128)(2,1)S(1)}, bf16[144,128]{1,0:T(8,128)(2,1)S(1)}, u32[]{:S(2)}, u32[]{:S(2)}) collective-permute-start(bf16[144,128]{1,0:T(8,128)(2,1)S(1)} %add_convert_fusion.4), channel_id=1, source_target_pairs={{0,96},{16,112},{32,64},{48,80},{64,32},{80,48},{96,0},{112,16},{1... | collective-permute-start | bytes 110600 | tf_op jit(solution)/shard_map/ppermute | solution.py:22
  89.0 4.9 %collective-permute-start.28 = (bf16[144,128]{1,0:T(8,128)(2,1)S(1)}, bf16[144,128]{1,0:T(8,128)(2,1)S(1)}, u32[]{:S(2)}, u32[]{:S(2)}) collective-permute-start(bf16[144,128]{1,0:T(8,128)(2,1)S(1)} %add_convert_fusion.4), channel_id=1, source_target_pairs={{0,64},{16,80},{32,96},{48,112},{64,0},{80,16},{96,32},{112,48},{1... | collective-permute-start | bytes 110600 | tf_op jit(solution)/shard_map/ppermute | solution.py:22
  94.0 2.2 %collective-permute-start.30 = (bf16[576,128]{1,0:T(8,128)(2,1)S(1)}, bf16[576,128]{1,0:T(8,128)(2,1)S(1)}, u32[]{:S(2)}, u32[]{:S(2)}) collective-permute-start(bf16[576,128]{1,0:T(8,128)(2,1)S(1)} %pad_maximum_fusion.1), channel_id=1, source_target_pairs={{0,16},{16,0},{32,48},{48,32},{64,80},{80,64},{96,112},{112,96},{1... | collective-permute-start | bytes 442376 | tf_op jit(solution)/shard_map/ppermute | solution.py:22
  94.1 5.5 %collective-permute-start.27 = (bf16[64,192]{1,0:T(8,128)(2,1)S(1)}, bf16[64,192]{1,0:T(8,128)(2,1)S(1)}, u32[]{:S(2)}, u32[]{:S(2)}) collective-permute-start(bf16[64,192]{1,0:T(8,128)(2,1)S(1)} %select_convert_fusion), channel_id=1, source_target_pairs={{0,2},{2,0},{4,6},{6,4},{8,10},{10,8},{12,14},{14,12},{1,3},{3,1},... | collective-permute-start | bytes 73736 | tf_op jit(solution)/shard_map/ppermute | solution.py:22
